TPU v7x, 32 devices: a whole 2x2x4 slice. The times are simulated.
32 devices in a mesh: head: 4 (over x, core), blk: 8 (over z, y).
Axes of the slice: x: 2, y: 2, z: 4, core: 2. Of those that a mesh axis runs over, the one named last changes fastest.
Arguments:
- block_input: bfloat16 [8, 512, 2048], P('blk', 'head'), may hold values from -6 to 6
- out_cotangent: bfloat16 [8, 512, 2048], P('blk', 'head'), may hold values from -6 to 6
- start_flags: int32 [8, 512], P('blk'), may hold values from 0 to 1, as said below
- in_weight: float32 [2048, 8240], P(('head', 'blk'))
- out_weight: float32 [4096, 2048], P(('head', 'blk'))
- gate_up_weight: float32 [2048, 8192], P(('head', 'blk')), may hold values from -0.125 to 0.125
- down_weight: float32 [4096, 2048], P(('head', 'blk')), may hold values from -0.09375 to 0.09375
- first_gain: float32 [2048], replicated, may hold values from 0.5 to 1.5
- second_gain: float32 [2048], replicated, may hold values from 0.5 to 1.5
- conv_weight: float32 [4, 3584], replicated, may hold values from -0.5 to 0.5
- conv_bias: float32 [3584], replicated, may hold values from -0.3 to 0.3
- step_bias: float32 [48], replicated, may hold values from -1 to 1
- decay_log: float32 [48], replicated, may hold values from -9.5 to -3
- skip_gain: float32 [48], replicated, may hold values from 0.5 to 1.5
Outputs:
- block_output: bfloat16 [8, 512, 2048], P('blk', 'head')
- grad_input: bfloat16 [8, 512, 2048], P('blk', 'head')
- grad_in_weight: float32 [2048, 8240], P(('head', 'blk'))
- grad_out_weight: float32 [4096, 2048], P(('head', 'blk'))
- grad_gate_up_weight: float32 [2048, 8192], P(('head', 'blk'))
- grad_down_weight: float32 [4096, 2048], P(('head', 'blk'))
- grad_first_gain: float32 [2048], replicated
- grad_second_gain: float32 [2048], replicated
- grad_conv_weight: float32 [4, 3584], replicated
- grad_conv_bias: float32 [3584], replicated
- grad_step_bias: float32 [48], replicated
- grad_decay_log: float32 [48], replicated
- grad_skip_gain: float32 [48], replicated
Inputs may be any that keep to these rules, and one draw needn't show every extreme that they name: `start_flags`: token 0 starts a sequence; besides it, one start lies within 1024 tokens of each k * 8192 for 1 <= k < 4096/8192, and a few more lie in the last eighth of the tokens.
All inputs are finite; a program needn't handle non-finite values.
Results may differ from a plain program's by a relative error of at most 0.017.
Values may be sent and summed in bfloat16 or wider, within the bound.
No kernel may reach another device: no remote copies, remote signals or barrier semaphores. Data moves between devices by JAX's collectives and lax.ppermute only.
A program may use at most 576 MiB of HBM per device.

v0:
```python
from functools import partial

import jax
import jax.numpy as jnp
from jax import lax
from jax.sharding import PartitionSpec as P

QH = 8
KVH = 2
HD = 128
MH = 48
MP = 64
NS = 256
FF = 4096
KW = 4


precise = lax.Precision.HIGHEST
epsilon = 1e-05
rope_base = 100000000000.0
masked_score = -1e30


def passed_along(shard, axis, by):
    peers = lax.axis_size(axis)
    pairs = [(i, i + by) for i in range(peers) if 0 <= i + by < peers]
    return lax.ppermute(shard, axis, pairs)


def prefix(shard, axis, combine, identity):
    peers, mine = (lax.axis_size(axis), lax.axis_index(axis))
    everything = jax.tree.map(
        lambda part, kind: lax.all_gather(part.astype(kind), axis),
        shard,
        (jnp.bfloat16, jnp.bfloat16, jnp.bfloat16),
    )
    start = jax.tree.map(
        lambda part, zero: jnp.broadcast_to(jnp.asarray(zero, part.dtype), part.shape),
        shard,
        identity,
    )

    def step(k, before):
        reached = k < mine
        new = combine(
            before, jax.tree.map(lambda part, own: part[k].astype(own.dtype), everything, shard)
        )
        return jax.tree.map(lambda a, b: jnp.where(reached, a, b), new, before)

    return lax.fori_loop(0, peers, step, start)


def carried_in(shard, axis, join, neutral):
    count = lax.axis_size(axis)
    place = lax.axis_index(axis)
    ahead = count - 1 - place
    gathered = jax.tree.map(
        lambda a, kind: lax.all_gather(a.astype(kind), axis),
        shard,
        jax.tree.map(lambda a: jnp.bfloat16 if a.dtype == jnp.float32 else a.dtype, shard),
    )
    state = jax.tree.map(lambda a, e: jnp.zeros_like(a) + jnp.asarray(e, a.dtype), shard, neutral)

    def one(step, state):
        source = count - 1 - step
        return join(
            state,
            jax.tree.map(
                lambda a, own: lax.dynamic_index_in_dim(a, source, 0, False).astype(own.dtype),
                gathered,
                shard,
            ),
        )

    return lax.fori_loop(0, ahead, one, state)


def fetch_weights(first, second):
    return (
        lax.all_gather(first, ("head", "blk"), axis=0, tiled=True),
        lax.all_gather(second, ("head", "blk"), axis=0, tiled=True),
    )


def refetch_weights(first, second):
    return (
        lax.all_gather(first, ("head", "blk"), axis=0, tiled=True),
        lax.all_gather(second, ("head", "blk"), axis=0, tiled=True),
    )


def reduce_grads(first, second):
    return (
        lax.psum_scatter(first, ("head", "blk"), scatter_dimension=0, tiled=True),
        lax.psum_scatter(second, ("head", "blk"), scatter_dimension=0, tiled=True),
    )


def outer_grad(left_side, grad_side):
    return lax.dot_general(
        left_side, grad_side, (((0,), (0,)), ((), ())), preferred_element_type=jnp.float32
    )


def times_transposed(grad_side, weight):
    return lax.dot_general(
        grad_side, weight, (((1,), (1,)), ((), ())), preferred_element_type=jnp.float32
    )


def to_heads(packed):
    return lax.all_to_all(packed, "head", split_axis=1, concat_axis=0, tiled=True)[:, 0, :]


def to_tokens(packed):
    return lax.all_to_all(packed[:, None, :], "head", split_axis=0, concat_axis=1, tiled=True)


def rotate(values_in, positions, direction):
    half_width = values_in.shape[-1] // 2
    frequencies = rope_base ** (
        -jnp.arange(half_width, dtype=jnp.float32) * 2.0 / values_in.shape[-1]
    )
    angles = positions.astype(jnp.float32)[:, None] * frequencies[None, :]
    cosine = jnp.cos(angles)[:, None, :]
    sine_part = direction * jnp.sin(angles)[:, None, :]
    first_half = values_in[..., :half_width]
    second_half = values_in[..., half_width:]
    return jnp.concatenate(
        [
            first_half * cosine - second_half * sine_part,
            second_half * cosine + first_half * sine_part,
        ],
        axis=-1,
    )


def norm_back(values_in, inverse, gain_vector, grad_side):
    scaled = grad_side * gain_vector
    mean_term = jnp.mean(scaled * values_in, axis=-1, keepdims=True)
    return inverse * scaled - values_in * inverse**3 * mean_term


def combine_states(earlier, later):
    return (
        later[1][:, None, None] * earlier[0] + later[0],
        earlier[1] * later[1],
        jnp.maximum(earlier[2], later[2]),
    )


def combine_grads(earlier, later):
    return (later[0] * earlier[0], later[1] + later[0][:, None, None] * earlier[1])


def mamba_prepare(extended, conv_taps, conv_shift, step_raw, step_shift, decay_rate, keep_masks):
    length = step_raw.shape[0]
    lag_total = conv_taps.shape[0]
    result = conv_shift + conv_taps[0] * extended[lag_total - 1 :]
    for lag_index in range(1, lag_total):
        begin = lag_total - 1 - lag_index
        result = (
            result
            + conv_taps[lag_index]
            * keep_masks[lag_index][:, None]
            * extended[begin : begin + length]
        )
    active = jax.nn.silu(result)
    inner_width = active.shape[1] - 2 * NS
    inner_act = active[:, :inner_width].reshape(length, inner_width // MP, MP)
    into_act = active[:, inner_width : inner_width + NS]
    outof_act = active[:, inner_width + NS :]
    step_size = jax.nn.softplus(step_raw + step_shift)
    cumulative = jnp.cumsum(-step_size * jnp.exp(decay_rate), axis=0)
    return (inner_act, into_act, outof_act, step_size, cumulative)


def mamba_state(inner_act, into_act, step_size, cumulative, segment):
    ending = jnp.where(
        (segment == segment[-1])[:, None], jnp.exp(cumulative[-1][None, :] - cumulative), 0.0
    )
    local_state = jnp.einsum(
        "sm,smp,sn->mpn", ending * step_size, inner_act, into_act, precision=precise
    )
    span_factor = jnp.exp(cumulative[-1]) * (segment[-1] == 0).astype(jnp.float32)
    return (local_state, span_factor)


def mamba_output(
    inner_act, into_act, outof_act, step_size, cumulative, gate_act, skip_local, state_in, segment
):
    length = step_size.shape[0]
    index_line = jnp.arange(length, dtype=jnp.int32)
    related = (segment[:, None] == segment[None, :]) & (index_line[:, None] >= index_line[None, :])
    scores = jnp.dot(outof_act, into_act.T, precision=precise)

    def one_head(head_items):
        cum_head, step_head, inner_head = head_items
        spread = cum_head[:, None] - cum_head[None, :]
        decays = jnp.where(related, jnp.exp(jnp.where(related, spread, 0.0)), 0.0)
        weights = decays * scores * step_head[None, :]
        return jnp.dot(weights, inner_head, precision=precise)

    within = lax.map(
        jax.checkpoint(one_head), (cumulative.T, step_size.T, jnp.transpose(inner_act, (1, 0, 2)))
    )
    within = jnp.transpose(within, (1, 0, 2))
    entering = jnp.exp(cumulative) * (segment == 0).astype(jnp.float32)[:, None]
    carried = entering[:, :, None] * jnp.einsum(
        "mpn,tn->tmp", state_in, outof_act, precision=precise
    )
    return (within + carried + skip_local[None, :, None] * inner_act) * jax.nn.silu(gate_act)


def per_device(
    block_input,
    out_cotangent,
    start_flags,
    in_weight,
    out_weight,
    gate_up_weight,
    down_weight,
    first_gain,
    second_gain,
    conv_weight,
    conv_bias,
    step_bias,
    decay_log,
    skip_gain,
):
    head_count = lax.axis_size("head")
    blocks = lax.axis_size("blk")
    head_index = lax.axis_index("head")
    block_index = lax.axis_index("blk")
    tokens = block_input[0].astype(jnp.float32)
    row_count = tokens.shape[0]
    span_rows = row_count * head_count
    query_group = QH // head_count
    mamba_group = MH // head_count
    kv_spread = head_count // KVH
    query_width = QH * HD
    kv_width = KVH * HD
    mamba_width = MH * MP
    group_query = query_group * HD
    group_inner = mamba_group * MP
    score_scale = HD ** (-0.5)
    weights_in = in_weight.astype(jnp.bfloat16)
    weights_out = out_weight.astype(jnp.bfloat16)
    weights_ffn = gate_up_weight.astype(jnp.bfloat16)
    weights_down = down_weight.astype(jnp.bfloat16)
    positions = (
        block_index * span_rows + head_index * row_count + jnp.arange(row_count, dtype=jnp.int32)
    )
    gathered_in, gathered_out = fetch_weights(weights_in, weights_out)
    inverse_one = lax.rsqrt(jnp.mean(tokens * tokens, axis=-1, keepdims=True) + epsilon)
    normed_one = (tokens * inverse_one * first_gain).astype(jnp.bfloat16)
    projected = jnp.dot(normed_one, gathered_in, preferred_element_type=jnp.float32)
    offset_z = query_width + 2 * kv_width
    offset_x = offset_z + mamba_width
    offset_b = offset_x + mamba_width
    offset_dt = offset_b + 2 * NS
    query_rot = rotate(projected[:, :query_width].reshape(row_count, QH, HD), positions, 1.0)
    key_rot = rotate(
        projected[:, query_width : query_width + kv_width].reshape(row_count, KVH, HD),
        positions,
        1.0,
    )
    value_part = projected[:, query_width + kv_width : offset_z].reshape(row_count, KVH, HD)
    key_value = jnp.concatenate([key_rot, value_part], axis=2).astype(jnp.bfloat16)
    packed = jnp.concatenate(
        [
            query_rot.astype(jnp.bfloat16).reshape(row_count, head_count, group_query),
            jnp.repeat(key_value, kv_spread, axis=1),
            projected[:, offset_z:offset_x]
            .astype(jnp.bfloat16)
            .reshape(row_count, head_count, group_inner),
            projected[:, offset_x:offset_b]
            .astype(jnp.bfloat16)
            .reshape(row_count, head_count, group_inner),
            jnp.broadcast_to(
                projected[:, offset_b:offset_dt].astype(jnp.bfloat16)[:, None, :],
                (row_count, head_count, 2 * NS),
            ),
            projected[:, offset_dt:]
            .astype(jnp.bfloat16)
            .reshape(row_count, head_count, mamba_group),
        ],
        axis=2,
    )
    regrouped = to_heads(packed)
    cut_z = group_query + 2 * HD
    cut_x = cut_z + group_inner
    cut_b = cut_x + group_inner
    cut_dt = cut_b + 2 * NS
    query_local = regrouped[:, :group_query].reshape(span_rows, query_group, HD)
    query_float = query_local.astype(jnp.float32)
    kv_local = regrouped[:, group_query:cut_z]
    gate_act = regrouped[:, cut_z:cut_x].astype(jnp.float32).reshape(span_rows, mamba_group, MP)
    conv_local = regrouped[:, cut_x:cut_dt]
    step_local = regrouped[:, cut_dt:].astype(jnp.float32)
    flags_local = start_flags[0]
    rim_rows, rim_flags = passed_along(
        (
            conv_local[span_rows - (KW - 1) :],
            flags_local[span_rows - (KW - 2) :].astype(jnp.bfloat16),
        ),
        "blk",
        1,
    )
    flag_ext = jnp.concatenate([rim_flags.astype(jnp.float32), flags_local.astype(jnp.float32)])
    keep_masks = [jnp.ones((span_rows,), jnp.float32)]
    for lag_index in range(1, KW):
        begin = KW - 1 - lag_index
        keep_masks.append(keep_masks[-1] * (1.0 - flag_ext[begin : begin + span_rows]))
    extended = jnp.concatenate([rim_rows, conv_local], axis=0).astype(jnp.float32)
    conv_taps = jnp.concatenate(
        [
            lax.dynamic_slice_in_dim(conv_weight, head_index * group_inner, group_inner, 1),
            conv_weight[:, mamba_width:],
        ],
        axis=1,
    )
    conv_shift = jnp.concatenate(
        [
            lax.dynamic_slice_in_dim(conv_bias, head_index * group_inner, group_inner, 0),
            conv_bias[mamba_width:],
        ]
    )
    step_shift = lax.dynamic_slice_in_dim(step_bias, head_index * mamba_group, mamba_group, 0)
    decay_rate = lax.dynamic_slice_in_dim(decay_log, head_index * mamba_group, mamba_group, 0)
    skip_local = lax.dynamic_slice_in_dim(skip_gain, head_index * mamba_group, mamba_group, 0)
    prepared, prepare_back = jax.vjp(
        partial(mamba_prepare, keep_masks=keep_masks),
        extended,
        conv_taps,
        conv_shift,
        step_local,
        step_shift,
        decay_rate,
    )
    inner_act, into_act, outof_act, step_size, cumulative = prepared
    segment = jnp.cumsum(flags_local)
    state_pair, state_back = jax.vjp(
        partial(mamba_state, segment=segment), inner_act, into_act, step_size, cumulative
    )
    local_state, span_factor = state_pair
    query_pos = block_index * span_rows + jnp.arange(span_rows, dtype=jnp.int32)
    last_start = jnp.max(jnp.where(flags_local > 0, query_pos, -1)).astype(jnp.float32)
    identity = (jnp.zeros_like(local_state), jnp.ones_like(span_factor), jnp.float32(-1.0))
    state_in, factor_in, start_in = prefix(
        (local_state, span_factor, last_start), "blk", combine_states, identity
    )
    mamba_out, output_back = jax.vjp(
        partial(mamba_output, segment=segment),
        inner_act,
        into_act,
        outof_act,
        step_size,
        cumulative,
        gate_act,
        skip_local,
        state_in,
    )
    local_start = lax.cummax(jnp.where(flags_local > 0, query_pos, -1), axis=0)
    first_visible = jnp.maximum(local_start, start_in.astype(jnp.int32))
    earliest_visible = jnp.min(first_visible)
    last_query = block_index * span_rows + span_rows - 1

    def visible_mask(key_start, key_total):
        key_pos = key_start + jnp.arange(key_total, dtype=jnp.int32)
        return (key_pos[None, :] <= query_pos[:, None]) & (
            key_pos[None, :] >= first_visible[:, None]
        )

    def attend_block(carried_state, key_block, key_start):
        running_top, running_total, summed = carried_state
        scores = (
            jnp.einsum(
                "tqd,sd->tqs", query_local, key_block[:, :HD], preferred_element_type=jnp.float32
            )
            * score_scale
        )
        visible = visible_mask(key_start, key_block.shape[0])[:, None, :]
        scores = jnp.where(visible, scores, masked_score)
        new_top = jnp.maximum(running_top, jnp.max(scores, axis=-1))
        probabilities = jnp.where(visible, jnp.exp(scores - new_top[..., None]), 0.0)
        rescale = jnp.exp(running_top - new_top)
        running_total = running_total * rescale + jnp.sum(probabilities, axis=-1)
        summed = summed * rescale[..., None] + jnp.einsum(
            "tqs,sd->tqd", probabilities, key_block[:, HD:].astype(jnp.float32), precision=precise
        )
        return (new_top, running_total, summed)

    def make_piece(block_fn):

        def one_block(carried_state, key_block, key_start):
            needed = (key_start <= last_query) & (key_start + key_block.shape[0] > earliest_visible)
            return lax.cond(
                needed,
                lambda unchanged: block_fn(unchanged, key_block, key_start),
                lambda unchanged: unchanged,
                carried_state,
            )

        def piece_fn(carried_state, shard_piece, first_row):
            piece_rows = shard_piece.shape[0]
            stacked = shard_piece.reshape(piece_rows // span_rows, span_rows, shard_piece.shape[1])
            begins = span_rows * jnp.arange(piece_rows // span_rows, dtype=jnp.int32)

            def scan_step(inner_state, pair_items):
                return (one_block(inner_state, pair_items[0], pair_items[1]), None)

            return lax.scan(scan_step, carried_state, (stacked, begins))[0]

        return piece_fn

    initial = (
        jnp.full((span_rows, query_group), masked_score, jnp.float32),
        jnp.zeros((span_rows, query_group), jnp.float32),
        jnp.zeros((span_rows, query_group, HD), jnp.float32),
    )
    running_top, running_total, summed = make_piece(attend_block)(
        initial, lax.all_gather(kv_local, "blk", axis=0, tiled=True), jnp.int32(0)
    )
    attended = summed / running_total[..., None]
    log_total = running_top + jnp.log(running_total)
    mixer_heads = jnp.concatenate(
        [
            attended.reshape(span_rows, group_query).astype(jnp.bfloat16),
            mamba_out.reshape(span_rows, group_inner).astype(jnp.bfloat16),
        ],
        axis=1,
    )
    mixer_tokens = to_tokens(mixer_heads)
    mixer = jnp.concatenate(
        [
            mixer_tokens[:, :, :group_query].reshape(row_count, query_width),
            mixer_tokens[:, :, group_query:].reshape(row_count, mamba_width),
        ],
        axis=1,
    )
    hidden_one = tokens + jnp.dot(mixer, gathered_out, preferred_element_type=jnp.float32)
    gathered_ffn, gathered_down = fetch_weights(weights_ffn, weights_down)
    inverse_two = lax.rsqrt(jnp.mean(hidden_one * hidden_one, axis=-1, keepdims=True) + epsilon)
    normed_two = (hidden_one * inverse_two * second_gain).astype(jnp.bfloat16)
    gate_up = jnp.dot(normed_two, gathered_ffn, preferred_element_type=jnp.float32)
    gate_part = gate_up[:, :FF]
    up_part = gate_up[:, FF:]
    activated = (jax.nn.silu(gate_part) * up_part).astype(jnp.bfloat16)
    block_output = hidden_one + jnp.dot(
        activated, gathered_down, preferred_element_type=jnp.float32
    )
    cotangent = out_cotangent[0]
    back_ffn, back_down = refetch_weights(weights_ffn, weights_down)
    grad_down_full = outer_grad(activated, cotangent)
    grad_activated = times_transposed(cotangent, back_down)
    sigmoid_gate = jax.nn.sigmoid(gate_part)
    grad_gate_up = jnp.concatenate(
        [
            grad_activated * up_part * sigmoid_gate * (1.0 + gate_part * (1.0 - sigmoid_gate)),
            grad_activated * jax.nn.silu(gate_part),
        ],
        axis=1,
    ).astype(jnp.bfloat16)
    grad_ffn_full = outer_grad(normed_two, grad_gate_up)
    grad_normed_two = times_transposed(grad_gate_up, back_ffn)
    grad_ffn, grad_down = reduce_grads(grad_ffn_full, grad_down_full)
    grad_hidden = cotangent.astype(jnp.float32) + norm_back(
        hidden_one, inverse_two, second_gain, grad_normed_two
    )
    grad_second = jnp.sum(grad_normed_two * hidden_one * inverse_two, axis=0)
    grad_hidden_low = grad_hidden.astype(jnp.bfloat16)
    back_out, back_in = refetch_weights(weights_out, weights_in)
    grad_mix_full = outer_grad(mixer, grad_hidden_low)
    grad_mixer = times_transposed(grad_hidden_low, back_out).astype(jnp.bfloat16)
    grad_heads = to_heads(
        jnp.concatenate(
            [
                grad_mixer[:, :query_width].reshape(row_count, head_count, group_query),
                grad_mixer[:, query_width:].reshape(row_count, head_count, group_inner),
            ],
            axis=2,
        )
    )
    grad_attended = grad_heads[:, :group_query].reshape(span_rows, query_group, HD)
    grad_attended_float = grad_attended.astype(jnp.float32)
    grad_mamba = grad_heads[:, group_query:].astype(jnp.float32).reshape(span_rows, mamba_group, MP)
    row_delta = jnp.sum(grad_attended_float * attended, axis=-1)

    def grad_block(pair_items, key_block, key_start):
        grad_query, grad_keys_all = pair_items
        keys_float = key_block[:, :HD].astype(jnp.float32)
        scores = (
            jnp.einsum(
                "tqd,sd->tqs", query_local, key_block[:, :HD], preferred_element_type=jnp.float32
            )
            * score_scale
        )
        visible = visible_mask(key_start, key_block.shape[0])[:, None, :]
        probabilities = jnp.where(
            visible, jnp.exp(jnp.where(visible, scores, 0.0) - log_total[..., None]), 0.0
        )
        grad_probs = jnp.einsum(
            "tqd,sd->tqs", grad_attended, key_block[:, HD:], preferred_element_type=jnp.float32
        )
        grad_scores = probabilities * (grad_probs - row_delta[..., None])
        grad_query = grad_query + score_scale * jnp.einsum(
            "tqs,sd->tqd", grad_scores, keys_float, precision=precise
        )
        grad_key = score_scale * jnp.einsum(
            "tqs,tqd->sd", grad_scores, query_float, precision=precise
        )
        grad_value = jnp.einsum(
            "tqs,tqd->sd", probabilities, grad_attended_float, precision=precise
        )
        current = lax.dynamic_slice_in_dim(grad_keys_all, key_start, key_block.shape[0], 0)
        grad_keys_all = lax.dynamic_update_slice_in_dim(
            grad_keys_all, current + jnp.concatenate([grad_key, grad_value], axis=1), key_start, 0
        )
        return (grad_query, grad_keys_all)

    initial_back = (
        jnp.zeros((span_rows, query_group, HD), jnp.float32),
        jnp.zeros((blocks * span_rows, 2 * HD), jnp.float32),
    )
    grad_query_all, grad_keys_all = make_piece(grad_block)(
        initial_back, lax.all_gather(kv_local, "blk", axis=0, tiled=True), jnp.int32(0)
    )
    grad_keys_own = lax.psum_scatter(
        grad_keys_all.astype(jnp.bfloat16), "blk", scatter_dimension=0, tiled=True
    )
    out_grads = output_back(grad_mamba)
    (
        grad_inner_b,
        grad_into_b,
        grad_outof,
        grad_step_b,
        grad_cum_b,
        grad_gate,
        grad_skip,
        grad_state_in,
    ) = out_grads
    suffix = carried_in(
        (span_factor, grad_state_in),
        "blk",
        combine_grads,
        (jnp.ones_like(span_factor), jnp.zeros_like(grad_state_in)),
    )
    later_grad = suffix[1]
    grad_factor = jnp.sum(later_grad * state_in, axis=(1, 2))
    grad_inner_a, grad_into_a, grad_step_a, grad_cum_a = state_back((later_grad, grad_factor))
    prep_grads = prepare_back(
        (
            grad_inner_a + grad_inner_b,
            grad_into_a + grad_into_b,
            grad_outof,
            grad_step_a + grad_step_b,
            grad_cum_a + grad_cum_b,
        )
    )
    grad_extended, grad_taps, grad_shift, grad_raw, grad_step_shift, grad_rate = prep_grads
    rim_back = passed_along(grad_extended[: KW - 1], "blk", -1)
    conv_grad = grad_extended[KW - 1 :] + jnp.pad(rim_back, ((span_rows - (KW - 1), 0), (0, 0)))
    back_packed = jnp.concatenate(
        [
            grad_query_all.reshape(span_rows, group_query).astype(jnp.bfloat16),
            grad_keys_own,
            grad_gate.reshape(span_rows, group_inner).astype(jnp.bfloat16),
            conv_grad.astype(jnp.bfloat16),
            grad_raw.astype(jnp.bfloat16),
        ],
        axis=1,
    )
    back_tokens = to_tokens(back_packed)
    grad_query_seq = rotate(
        back_tokens[:, :, :group_query].astype(jnp.float32).reshape(row_count, QH, HD),
        positions,
        -1.0,
    ).reshape(row_count, query_width)
    grad_kv_seq = jnp.sum(
        back_tokens[:, :, group_query:cut_z]
        .astype(jnp.float32)
        .reshape(row_count, KVH, kv_spread, 2 * HD),
        axis=2,
    )
    grad_key_seq = rotate(grad_kv_seq[:, :, :HD], positions, -1.0).reshape(row_count, kv_width)
    grad_value_seq = grad_kv_seq[:, :, HD:].reshape(row_count, kv_width)
    grad_gate_seq = (
        back_tokens[:, :, cut_z:cut_x].astype(jnp.float32).reshape(row_count, mamba_width)
    )
    grad_inner_seq = (
        back_tokens[:, :, cut_x:cut_b].astype(jnp.float32).reshape(row_count, mamba_width)
    )
    grad_bc_seq = jnp.sum(back_tokens[:, :, cut_b:cut_dt].astype(jnp.float32), axis=1)
    grad_step_seq = back_tokens[:, :, cut_dt:].astype(jnp.float32).reshape(row_count, MH)
    grad_projected = jnp.concatenate(
        [
            grad_query_seq,
            grad_key_seq,
            grad_value_seq,
            grad_gate_seq,
            grad_inner_seq,
            grad_bc_seq,
            grad_step_seq,
        ],
        axis=1,
    ).astype(jnp.bfloat16)
    grad_proj_full = outer_grad(normed_one, grad_projected)
    grad_normed_one = times_transposed(grad_projected, back_in)
    grad_proj_weight, grad_mix_weight = reduce_grads(grad_proj_full, grad_mix_full)
    grad_input = (grad_hidden + norm_back(tokens, inverse_one, first_gain, grad_normed_one)).astype(
        jnp.bfloat16
    )
    grad_first = jnp.sum(grad_normed_one * tokens * inverse_one, axis=0)
    grad_conv_weight = jnp.concatenate(
        [
            lax.dynamic_update_slice_in_dim(
                jnp.zeros((KW, mamba_width), jnp.float32),
                grad_taps[:, :group_inner],
                head_index * group_inner,
                1,
            ),
            grad_taps[:, group_inner:],
        ],
        axis=1,
    )
    grad_conv_bias = jnp.concatenate(
        [
            lax.dynamic_update_slice_in_dim(
                jnp.zeros((mamba_width,), jnp.float32),
                grad_shift[:group_inner],
                head_index * group_inner,
                0,
            ),
            grad_shift[group_inner:],
        ]
    )
    grad_step_bias = lax.dynamic_update_slice_in_dim(
        jnp.zeros((MH,), jnp.float32), grad_step_shift, head_index * mamba_group, 0
    )
    grad_decay = lax.dynamic_update_slice_in_dim(
        jnp.zeros((MH,), jnp.float32), grad_rate, head_index * mamba_group, 0
    )
    grad_skip_full = lax.dynamic_update_slice_in_dim(
        jnp.zeros((MH,), jnp.float32), grad_skip, head_index * mamba_group, 0
    )
    summed_small = lax.psum(
        (
            grad_first,
            grad_second,
            grad_conv_weight,
            grad_conv_bias,
            grad_step_bias,
            grad_decay,
            grad_skip_full,
        ),
        ("head", "blk"),
    )
    return (
        block_output.astype(jnp.bfloat16)[None],
        grad_input[None],
        grad_proj_weight,
        grad_mix_weight,
        grad_ffn,
        grad_down,
        summed_small[0],
        summed_small[1],
        summed_small[2],
        summed_small[3],
        summed_small[4],
        summed_small[5],
        summed_small[6],
    )


def solution(mesh):
    placed = (
        P("blk", "head", None),
        P("blk", "head", None),
        P("blk", None),
        P(("head", "blk"), None),
        P(("head", "blk"), None),
        P(("head", "blk"), None),
        P(("head", "blk"), None),
        P(),
        P(),
        P(),
        P(),
        P(),
        P(),
        P(),
    )
    return jax.shard_map(
        per_device,
        mesh=mesh,
        in_specs=placed,
        out_specs=(
            P("blk", "head", None),
            P("blk", "head", None),
            P(("head", "blk"), None),
            P(("head", "blk"), None),
            P(("head", "blk"), None),
            P(("head", "blk"), None),
            P(),
            P(),
            P(),
            P(),
            P(),
            P(),
            P(),
        ),
        check_vma=False,
    )
```

profile of v0, /device:TPU:16, one launch (start us, length us, event | category | flops | bytes accessed | tf_op | source)
XLA Modules:
  0.0 5778.7 jit_solution(1432854145474083989)
XLA Ops:
  12.4 196.7 %all-gather.11.cloned.1.call-done = bf16[2048,8240]{1,0:T(8,128)(2,1)} async-done(((bf16[64,8240]{1,0:T(8,128)(2,1)}), bf16[2048,8240]{1,0:T(8,128)(2,1)}) %all-gather.11.cloned.1.call-update) | async-done | bytes 33751056 | tf_op jit(solution)/shard_map/all_gather | solution.py:80
  209.1 19.5 fusion.176
  242.9 3.8 all-to-all-start
  256.2 22.0 all-to-all-done
  303.5 3.6 fusion.85
  319.1 15.7 all-reduce.14
  336.6 17.2 all-gather.2
  366.7 45.8 while.94
  413.5 19.8 while.96
  434.1 52.3 while.93
  436.6 6.3 conditional.6
  445.5 6.4 conditional.6
  454.5 6.3 conditional.6
  463.4 6.3 conditional.6
  472.3 6.3 conditional.6
  486.8 5.9 multiply_convert_fusion.3
  497.1 26.0 all_to_all.66
  527.3 14.1 all-gather.15.cloned.1.call-done
  541.3 8.2 multiply_reduce_fusion.10
  549.6 190.1 %all-gather.17.cloned.1.call-done = bf16[2048,8192]{1,0:T(8,128)(2,1)} async-done(((bf16[64,8192]{1,0:T(8,128)(2,1)}), bf16[2048,8192]{1,0:T(8,128)(2,1)}) %all-gather.17.cloned.1.call-update) | async-done | bytes 33554448 | tf_op jit(solution)/shard_map/all_gather | solution.py:80
  739.7 17.2 fusion.162
  757.0 99.4 %all-gather.19.cloned.1.call-done = bf16[4096,2048]{1,0:T(8,128)(2,1)} async-done(((bf16[128,2048]{1,0:T(8,128)(2,1)}), bf16[4096,2048]{1,0:T(8,128)(2,1)}) %all-gather.19.cloned.1.call-update) | async-done | bytes 16777232 | tf_op jit(solution)/shard_map/all_gather | solution.py:81
  856.3 14.5 multiply_convert_fusion.1
  870.8 18.3 multiply_reduce_fusion.8
  890.7 11.7 convolution_convert_fusion
  908.3 13.4 all-to-all-done.2
  927.0 130.6 %while.95 = (s32[]{:T(128)}, f32[512,2,128]{2,0,1:T(8,128)}, f32[4096,256]{0,1:T(8,128)}, s32[8]{0:T(128)S(1)}, s32[]{:T(128)}, /*index=5*/s32[]{:T(128)}, s32[5...) while((s32[]{:T(128)}, f32[512,2,128]{2,0,1:T(8,128)}, ...), condition=%wide.region_25.26_spmd.clone, body=%wide.region_22.25_spmd.clone.sunk | while | flops 2688877568 | bytes 19814812 | solution.py:413
  929.7 22.0 conditional.7
  948.1 3.6 fusion.24
  954.2 22.0 conditional.7
  972.6 3.6 fusion.24
  978.8 22.0 conditional.7
  997.1 3.6 fusion.24
  1003.3 22.0 conditional.7
  1021.7 3.6 fusion.24
  1027.9 22.0 conditional.7
  1042.7 3.5 dynamic_update_slice.45
  1046.3 3.6 fusion.24
  1057.6 4.6 copy.483
  1067.9 4.3 multiply_reduce_fusion.7
  1078.6 98.3 %while.97 = (s32[]{:T(128)}, f32[512,512]{1,0:T(8,128)S(1)}, f32[12,512]{1,0:T(8,128)S(1)}, f32[12,512]{1,0:T(8,128)}, f32[12,512,64]{1,2,0:T(8,128)}, /*index=5...) while((s32[]{:T(128)}, f32[512,512]{1,0:T(8,128)S(1)}, ...), condition=%wide.region_31.32_spmd.clone, body=%wide.region_27.31_spmd.clone.sunk | while | flops 408944128 | bytes 8560819 | solution.py:204
  1196.1 59.6 %all-gather.23.cloned.1.call-done = bf16[96,64,256]{2,1,0:T(8,128)(2,1)} async-done(((bf16[12,64,256]{2,1,0:T(8,128)(2,1)}), bf16[96,64,256]{2,1,0:T(8,128)(2,1)}) %all-gather.23.cloned.1.call-update) | async-done | bytes 3145744 | tf_op jit(solution)/shard_map/all_gather | solution.py:58
  1255.7 4.0 while.92
  1262.7 3.8 convolution_add_fusion.2
  1266.5 4.0 multiply_reduce_fusion.5
  1273.7 4.4 multiply_reduce_fusion.4
  1285.2 5.0 reduce-window.48
  1291.3 4.5 collective-permute-start.2
  1299.3 4.6 reduce.28
  1303.9 8.2 reshape.685
  1312.0 4.8 all-to-all-start.3
  1321.6 26.8 all-to-all-done.3
  1348.4 8.3 reshape.686
  1367.5 18.8 fusion.106
  1386.4 13.8 fusion.111
  1401.6 13.3 fusion.113
  1416.1 24.8 fusion.82
  1441.0 25.2 fusion.143
  1466.2 9.3 fusion.66
  1476.9 35.7 all-reduce.18.cloned.1.call-done
  1512.6 709.0 %reduce-scatter.10.cloned.1.call-done = f32[128,2048]{1,0:T(8,128)} async-done(((f32[4096,2048]{1,0:T(8,128)}), f32[128,2048]{1,0:T(8,128)}) %reduce-scatter.10.cloned.1.call-update) | async-done | bytes 1048592 | tf_op jit(solution)/shard_map/reduce_scatter | solution.py:95
  2221.6 708.9 %reduce-scatter.14.cloned.1.call-done = f32[128,2048]{1,0:T(8,128)} async-done(((f32[4096,2048]{1,0:T(8,128)}), f32[128,2048]{1,0:T(8,128)}) %reduce-scatter.14.cloned.1.call-update) | async-done | bytes 1048592 | tf_op jit(solution)/shard_map/reduce_scatter | solution.py:95
  2930.5 1405.4 %reduce-scatter.12.cloned.1.call-done = f32[64,8192]{1,0:T(8,128)} async-done(((f32[2048,8192]{1,0:T(8,128)}), f32[64,8192]{1,0:T(8,128)}) %reduce-scatter.12.cloned.1.call-update) | async-done | bytes 2097168 | tf_op jit(solution)/shard_map/reduce_scatter | solution.py:94
  4335.9 1427.3 %reduce-scatter.8.cloned.1.call-done = f32[64,8240]{1,0:T(8,128)} async-done(((f32[2048,8240]{1,0:T(8,128)}), f32[64,8240]{1,0:T(8,128)}) %reduce-scatter.8.cloned.1.call-update) | async-done | bytes 2109456 | tf_op jit(solution)/shard_map/reduce_scatter | solution.py:94
  (777 shorter events, 459.8 us)
Async XLA Ops:
  7.2 201.9 %copy-start.49 = (f32[2048]{0:T(1024)S(1)}, f32[2048]{0:T(1024)}, u32[]{:S(2)}) copy-start(f32[2048]{0:T(1024)} %param.37) | copy-start | bytes 24580
  7.2 201.9 %all-gather.11.cloned.1.call-start = ((), (), s32[]{:S(2)}) async-start(), calls=%async_computation.9 | async-start | bytes 35143680 | tf_op jit(solution)/shard_map/all_gather | solution.py:80
  10.9 224.8 %copy-start.47 = (f32[128,64]{0,1:T(8,128)}, f32[128,64]{0,1:T(8,128)S(1)}, u32[]{:S(2)}) copy-start(f32[128,64]{0,1:T(8,128)S(1)} %get-tuple-element.1611) | copy-start | bytes 98308
  11.0 223.6 %copy-start.42 = (f32[128,64]{1,0:T(8,128)}, f32[128,64]{1,0:T(8,128)S(1)}, u32[]{:S(2)}) copy-start(f32[128,64]{1,0:T(8,128)S(1)} %copy.454) | copy-start | bytes 98308
  12.4 216.2 %copy-start.66 = (f32[128]{0:T(128)}, f32[128]{0:T(128)S(1)}, u32[]{:S(2)}) copy-start(f32[128]{0:T(128)S(1)} %get-tuple-element.1613) | copy-start | bytes 1540
  242.9 9.8 copy-start.84
  242.9 9.9 copy-start.94
  242.9 10.0 copy-start.77
  242.9 10.0 slice-start
  242.9 10.6 copy-start.92
  242.9 10.7 slice-start.1
  242.9 35.3 all-to-all-start
  246.7 165.8 %all-gather.21.cloned.1.call-start = ((), (), s32[]{:S(2)}) async-start(), calls=%async_computation.19 | async-start | bytes 3538944 | tf_op jit(solution)/shard_map/all_gather | solution.py:33
  246.9 8.6 collective-permute-start.1
  252.8 30.8 copy-start.79
  253.5 41.9 copy-start.55
  253.6 30.1 copy-start.85
  256.2 39.3 copy-start.68
  283.0 9.7 copy-start.19
  285.5 69.7 %copy-start.24 = (f32[12,4,128]{0,2,1:T(8,128)}, f32[12,4,128]{0,2,1:T(8,128)S(1)}, u32[]{:S(2)}) copy-start(f32[12,4,128]{0,2,1:T(8,128)S(1)} %copy.461) | copy-start | bytes 73732
  285.5 8.3 collective-permute-start
  293.8 9.6 copy-start.44
  303.4 183.4 %copy-start.2 = (f32[512,768]{0,1:T(8,128)}, f32[512,768]{0,1:T(8,128)S(1)}, u32[]{:S(2)}) copy-start(f32[512,768]{0,1:T(8,128)S(1)} %copy.463) | copy-start | bytes 4718596
  307.1 126.9 %all-gather.13.cloned.1.call-start = ((), (), s32[]{:S(2)}) async-start(), calls=%async_computation.10 | async-start | bytes 2359296 | tf_op jit(solution)/shard_map/all_gather | solution.py:423
  309.1 232.3 %all-gather.15.cloned.1.call-start = ((), (), s32[]{:S(2)}) async-start(), calls=%async_computation.11 | async-start | bytes 17301504 | tf_op jit(solution)/shard_map/all_gather | solution.py:81
  311.2 428.5 %all-gather.17.cloned.1.call-start = ((), (), s32[]{:S(2)}) async-start(), calls=%async_computation.12 | async-start | bytes 34603008 | tf_op jit(solution)/shard_map/all_gather | solution.py:80
  314.0 21.3 copy-start.95
  314.0 22.6 copy-start.86
  314.0 542.3 %all-gather.19.cloned.1.call-start = ((), (), s32[]{:S(2)}) async-start(), calls=%async_computation.13 | async-start | bytes 17301504 | tf_op jit(solution)/shard_map/all_gather | solution.py:81
  366.7 45.8 copy-start.98
  412.5 20.8 copy-start.87
  412.5 21.6 copy-start.96
  433.2 53.6 copy-start.4
  526.6 14.8 copy-start.17
  527.1 22.5 copy-start.29
  527.3 22.3 copy-start.36
  541.3 198.4 %copy-start.51 = (f32[2048]{0:T(1024)S(1)}, f32[2048]{0:T(1024)}, u32[]{:S(2)}) copy-start(f32[2048]{0:T(1024)} %param.38) | copy-start | bytes 24580
  549.6 339.5 %copy-start.9 = (f32[128,2048]{1,0:T(8,128)}, f32[128,2048]{1,0:T(8,128)S(1)}, u32[]{:S(2)}) copy-start(f32[128,2048]{1,0:T(8,128)S(1)} %get-tuple-element.1620) | copy-start | bytes 3145732
  549.6 339.5 %copy-start.64 = (f32[128]{0:T(128)}, f32[128]{0:T(128)S(1)}, u32[]{:S(2)}) copy-start(f32[128]{0:T(128)S(1)} %get-tuple-element.1615) | copy-start | bytes 1540
  739.7 116.6 %copy-start.38 = (bf16[1,128,2048]{2,1,0:T(8,128)(2,1)S(1)}, bf16[1,128,2048]{2,1,0:T(8,128)(2,1)}, u32[]{:S(2)}) copy-start(bf16[1,128,2048]{2,1,0:T(8,128)(2,1)} %param.31) | copy-start | bytes 1572868
  870.8 18.3 copy-start.32
  890.7 11.8 copy-start.20
  903.8 18.0 all-to-all-start.2
  907.3 286.0 %reduce-scatter.6.cloned.1.call-start = ((), (), s32[]{:S(2)}) async-start(), calls=%async_computation.14 | async-start | bytes 2359296 | tf_op jit(solution)/shard_map/reduce_scatter | solution.py:529
  1062.3 193.3 %all-gather.23.cloned.1.call-start = ((), (), s32[]{:S(2)}) async-start(), calls=%async_computation.20 | async-start | bytes 3538944 | tf_op jit(solution)/shard_map/all_gather | solution.py:58
  1078.6 99.2 %copy-start.78 = (f32[512]{0:T(512)S(1)}, f32[512]{0:T(512)}, u32[]{:S(2)}) copy-start(f32[512]{0:T(512)} %get-tuple-element.1552) | copy-start | bytes 6148
  1177.0 5.6 copy-start.14
  1185.2 9.9 copy-start.34
  1280.8 15.0 copy-start.41
  1291.3 5.9 collective-permute-start.2
  1312.0 36.4 all-to-all-start.3
  1316.9 195.7 %all-reduce.18.cloned.1.call-start = ((), (), s32[]{:S(2)}) async-start(), calls=%async_computation.21 | async-start | bytes 183296 | tf_op jit(solution)/shard_map/psum | solution.py:647
  1319.5 37.2 copy-start.90
  1319.8 36.9 copy-start.91
  1320.9 35.7 copy-start.89
  1367.5 18.9 copy-start.21
  1367.5 18.9 copy-start.30
  1367.5 18.9 copy-start.37
  1386.3 835.3 %reduce-scatter.10.cloned.1.call-start = ((), (), s32[]{:S(2)}) async-start(), calls=%async_computation.16 | async-start | bytes 34603008 | tf_op jit(solution)/shard_map/reduce_scatter | solution.py:95
  1400.2 1530.2 %reduce-scatter.14.cloned.1.call-start = ((), (), s32[]{:S(2)}) async-start(), calls=%async_computation.18 | async-start | bytes 34603008 | tf_op jit(solution)/shard_map/reduce_scatter | solution.py:95
  1414.9 2921.0 %reduce-scatter.12.cloned.1.call-start = ((), (), s32[]{:S(2)}) async-start(), calls=%async_computation.17 | async-start | bytes 69206016 | tf_op jit(solution)/shard_map/reduce_scatter | solution.py:94
  1440.9 4322.3 %reduce-scatter.8.cloned.1.call-start = ((), (), s32[]{:S(2)}) async-start(), calls=%async_computation.15 | async-start | bytes 70287360 | tf_op jit(solution)/shard_map/reduce_scatter | solution.py:94
  1466.2 9.4 copy-start.33
  1466.2 9.3 copy-start.88
  (56 other events, 167.8 us)
Sparse Core Ops, SparseCore 0:
  11.5 197.5 all-gather.10
  307.2 58.2 all-gather.20
  367.7 47.7 all-gather.12
  419.0 122.2 all-gather.14
  544.7 194.9 all-gather.16
  743.2 113.0 all-gather.18
  1062.4 130.8 reduce-scatter.5
  1195.5 60.0 all-gather.22
  1386.4 126.1 all-reduce.17
  1515.4 706.1 reduce-scatter.9
  2224.5 705.9 reduce-scatter.13
  2933.4 1402.4 reduce-scatter.11
  4339.0 1424.2 reduce-scatter.7
where the time goes:
time: 5800 us; the launch traced here: 5780 us
  waiting for transfers between devices  4910 us (85%)
  matrix products  391 us (7%)
  local copies, waits for them, and re-layouts  217 us (4%)
  other arithmetic  109 us (2%)
  blocking collectives  59 us (1%)
    reduce_scatter x2, waiting for transfers between devices, reduce_grads(): lax.psum_scatter(first, ('head', 'blk'), scatter_dimension=0, tiled=True)  2830 us
    reduce_scatter x2, waiting for transfers between devices, reduce_grads(): lax.psum_scatter(second, ('head', 'blk'), scatter_dimension=0, tiled=True)  1420 us
    all_gather x2, waiting for transfers between devices, fetch_weights(): lax.all_gather(first, ('head', 'blk'), axis=0, tiled=True)  387 us
  transfers between devices with their start and end apart: 19, of which 14 were waited for; matrix products, arithmetic and copies ran while one was open for 7% of the time, Pallas kernels for 0%

commit v1 on v0

--- a/solution.py
+++ b/solution.py
@@ -75,25 +75,170 @@
     return lax.fori_loop(0, ahead, one, state)
 
 
-def fetch_weights(first, second):
-    return (
-        lax.all_gather(first, ("head", "blk"), axis=0, tiled=True),
-        lax.all_gather(second, ("head", "blk"), axis=0, tiled=True),
-    )
-
-
-def refetch_weights(first, second):
-    return (
-        lax.all_gather(first, ("head", "blk"), axis=0, tiled=True),
-        lax.all_gather(second, ("head", "blk"), axis=0, tiled=True),
-    )
-
-
-def reduce_grads(first, second):
-    return (
-        lax.psum_scatter(first, ("head", "blk"), scatter_dimension=0, tiled=True),
-        lax.psum_scatter(second, ("head", "blk"), scatter_dimension=0, tiled=True),
-    )
+def ring_of(axis):
+    peers = lax.axis_size(axis)
+    if peers != 8:
+        return list(range(peers))
+    return [0, 2, 4, 6, 7, 5, 3, 1]
+
+
+def gather_blocks(shard):
+    return lax.all_gather(
+        shard, "blk", axis=0, tiled=True, axis_index_groups=[ring_of("blk")]
+    )
+
+
+def scatter_blocks(partial_sums):
+    return lax.psum_scatter(
+        partial_sums,
+        "blk",
+        scatter_dimension=0,
+        tiled=True,
+        axis_index_groups=[ring_of("blk")],
+    )
+
+
+def from_head(shard, distance):
+    peers = lax.axis_size("head")
+    return lax.ppermute(shard, "head", [(i, i ^ distance) for i in range(peers)])
+
+
+def by_distance(parts):
+    mine = lax.axis_index("head")
+    stacked = jnp.stack(parts)
+    return [
+        lax.dynamic_index_in_dim(stacked, jnp.bitwise_xor(mine, j), 0, False)
+        for j in range(len(parts))
+    ]
+
+
+def gather_heads(shard):
+    across = from_head(shard, 2)
+    beside = from_head(jnp.stack([shard, across]), 1)
+    return by_distance([shard, beside[0], across, beside[1]])
+
+
+def scatter_heads(chunks):
+    mine = lax.axis_index("head")
+
+    def chunk(distance):
+        return lax.dynamic_index_in_dim(chunks, jnp.bitwise_xor(mine, distance), 0, False)
+
+    got = from_head(jnp.stack([chunk(1), chunk(3)]), 1)
+    near = chunk(0) + got[0]
+    far = (chunk(2) + got[1]).astype(jnp.bfloat16)
+    return near + from_head(far, 2).astype(jnp.float32)
+
+
+def ring_features(values_in):
+    heads, ring = lax.axis_size("head"), ring_of("blk")
+    rows, width = values_in.shape
+    cut = values_in.reshape(rows, heads, len(ring), width // (heads * len(ring)))
+    return jnp.concatenate([cut[:, :, k, :].reshape(rows, -1) for k in ring], axis=1)
+
+
+def plain_features(values_in):
+    heads, ring = lax.axis_size("head"), ring_of("blk")
+    rows, width = values_in.shape
+    cut = values_in.reshape(rows, len(ring), heads, width // (heads * len(ring)))
+    places = [ring.index(k) for k in range(len(ring))]
+    return jnp.concatenate(
+        [cut[:, places[k], j, :] for j in range(heads) for k in range(len(ring))], axis=1
+    )
+
+
+def mixer_place():
+    heads, ring = lax.axis_size("head"), ring_of("blk")
+    peers = heads * len(ring)
+    rows = (QH * HD + MH * MP) // peers
+    query_blocks, mamba_blocks = QH * HD // rows // heads, MH * MP // rows // heads
+    pairs = []
+    for r in range(peers):
+        if r < query_blocks * heads:
+            group, slot = divmod(r, query_blocks)
+        else:
+            group, slot = divmod(r - query_blocks * heads, mamba_blocks)
+            slot += query_blocks
+        pairs.append((r, group * len(ring) + ring[slot]))
+    return pairs
+
+
+def column_cuts():
+    query_end = QH * HD
+    z_begin = query_end + 2 * KVH * HD
+    x_begin = z_begin + MH * MP
+    b_begin = x_begin + MH * MP
+    dt_begin = b_begin + 2 * NS
+    heads = lax.axis_size("head")
+    cuts = []
+    for j in range(heads):
+        kind, kv_head = j % 2, j // 2
+        kv_begin = query_end + kind * KVH * HD + kv_head * HD
+        cuts.append(
+            [
+                (j * QH * HD // heads, QH * HD // heads),
+                (kv_begin, HD),
+                (z_begin + j * MH * MP // heads, MH * MP // heads),
+                (x_begin + j * MH * MP // heads, MH * MP // heads),
+                (b_begin + j * 2 * NS // heads, 2 * NS // heads),
+                (dt_begin + j * MH // heads, MH // heads),
+            ]
+        )
+    return cuts
+
+
+step_pad = 128
+
+
+def pack_in(weight):
+    groups = []
+    for cuts in column_cuts():
+        pieces = [weight[:, begin : begin + size] for begin, size in cuts]
+        pad = jnp.zeros((weight.shape[0], step_pad - cuts[-1][1]), weight.dtype)
+        groups.append(jnp.concatenate(pieces + [pad], axis=1))
+    return jnp.stack(groups)
+
+
+def unpack_in(groups):
+    pieces = []
+    for j, cuts in enumerate(column_cuts()):
+        at = 0
+        for begin, size in cuts:
+            pieces.append((begin, groups[j][:, at : at + size]))
+            at += size
+    pieces.sort(key=lambda item: item[0])
+    return jnp.concatenate([piece for _, piece in pieces], axis=1)
+
+
+def pack_ffn(weight):
+    heads, ring = lax.axis_size("head"), ring_of("blk")
+    unit = FF // (heads * len(ring))
+    cut = weight.reshape(weight.shape[0], 2, heads, len(ring), unit)
+    return jnp.stack(
+        [
+            jnp.concatenate([cut[:, half, j, k] for half in range(2) for k in ring], axis=1)
+            for j in range(heads)
+        ]
+    )
+
+
+def unpack_ffn(groups):
+    heads, ring = lax.axis_size("head"), ring_of("blk")
+    rows = groups.shape[1]
+    cut = groups.reshape(heads, rows, 2, len(ring), FF // (heads * len(ring)))
+    return jnp.concatenate(
+        [
+            cut[j, :, half, ring.index(k)]
+            for half in range(2)
+            for j in range(heads)
+            for k in range(len(ring))
+        ],
+        axis=1,
+    )
+
+
+def swap_groups(groups):
+    return lax.all_to_all(groups, "head", split_axis=0, concat_axis=0, tiled=True)
 
 
 def outer_grad(left_side, grad_side):
@@ -106,14 +251,6 @@
     return lax.dot_general(
         grad_side, weight, (((1,), (1,)), ((), ())), preferred_element_type=jnp.float32
     )
-
-
-def to_heads(packed):
-    return lax.all_to_all(packed, "head", split_axis=1, concat_axis=0, tiled=True)[:, 0, :]
-
-
-def to_tokens(packed):
-    return lax.all_to_all(packed[:, None, :], "head", split_axis=0, concat_axis=1, tiled=True)
 
 
 def rotate(values_in, positions, direction):
@@ -237,67 +374,65 @@
     span_rows = row_count * head_count
     query_group = QH // head_count
     mamba_group = MH // head_count
-    kv_spread = head_count // KVH
-    query_width = QH * HD
-    kv_width = KVH * HD
     mamba_width = MH * MP
     group_query = query_group * HD
     group_inner = mamba_group * MP
     score_scale = HD ** (-0.5)
-    weights_in = in_weight.astype(jnp.bfloat16)
-    weights_out = out_weight.astype(jnp.bfloat16)
-    weights_ffn = gate_up_weight.astype(jnp.bfloat16)
-    weights_down = down_weight.astype(jnp.bfloat16)
-    positions = (
-        block_index * span_rows + head_index * row_count + jnp.arange(row_count, dtype=jnp.int32)
-    )
-    gathered_in, gathered_out = fetch_weights(weights_in, weights_out)
+    out_pairs = mixer_place()
+    weights_in = gather_blocks(
+        swap_groups(pack_in(in_weight.astype(jnp.bfloat16))).reshape(
+            head_count * in_weight.shape[0], -1
+        )
+    )
+    weights_out = gather_blocks(
+        lax.ppermute(out_weight.astype(jnp.bfloat16), ("head", "blk"), out_pairs)
+    )
+    weights_ffn = gather_blocks(
+        swap_groups(pack_ffn(gate_up_weight.astype(jnp.bfloat16))).reshape(
+            head_count * gate_up_weight.shape[0], -1
+        )
+    )
+    weights_down = gather_blocks(down_weight.astype(jnp.bfloat16))
+    positions = block_index * span_rows + jnp.arange(span_rows, dtype=jnp.int32)
+    span_tokens = jnp.concatenate(gather_heads(block_input[0]), axis=0).astype(jnp.float32)
+    span_inverse = lax.rsqrt(jnp.mean(span_tokens * span_tokens, axis=-1, keepdims=True) + epsilon)
+    normed_one = ring_features((span_tokens * span_inverse * first_gain).astype(jnp.bfloat16))
+    projected = jnp.dot(normed_one, weights_in, preferred_element_type=jnp.float32)
     inverse_one = lax.rsqrt(jnp.mean(tokens * tokens, axis=-1, keepdims=True) + epsilon)
-    normed_one = (tokens * inverse_one * first_gain).astype(jnp.bfloat16)
-    projected = jnp.dot(normed_one, gathered_in, preferred_element_type=jnp.float32)
-    offset_z = query_width + 2 * kv_width
-    offset_x = offset_z + mamba_width
-    offset_b = offset_x + mamba_width
-    offset_dt = offset_b + 2 * NS
-    query_rot = rotate(projected[:, :query_width].reshape(row_count, QH, HD), positions, 1.0)
-    key_rot = rotate(
-        projected[:, query_width : query_width + kv_width].reshape(row_count, KVH, HD),
-        positions,
-        1.0,
-    )
-    value_part = projected[:, query_width + kv_width : offset_z].reshape(row_count, KVH, HD)
-    key_value = jnp.concatenate([key_rot, value_part], axis=2).astype(jnp.bfloat16)
-    packed = jnp.concatenate(
-        [
-            query_rot.astype(jnp.bfloat16).reshape(row_count, head_count, group_query),
-            jnp.repeat(key_value, kv_spread, axis=1),
-            projected[:, offset_z:offset_x]
-            .astype(jnp.bfloat16)
-            .reshape(row_count, head_count, group_inner),
-            projected[:, offset_x:offset_b]
-            .astype(jnp.bfloat16)
-            .reshape(row_count, head_count, group_inner),
-            jnp.broadcast_to(
-                projected[:, offset_b:offset_dt].astype(jnp.bfloat16)[:, None, :],
-                (row_count, head_count, 2 * NS),
-            ),
-            projected[:, offset_dt:]
-            .astype(jnp.bfloat16)
-            .reshape(row_count, head_count, mamba_group),
-        ],
-        axis=2,
-    )
-    regrouped = to_heads(packed)
-    cut_z = group_query + 2 * HD
+    cut_kv = group_query
+    cut_z = cut_kv + HD
     cut_x = cut_z + group_inner
     cut_b = cut_x + group_inner
-    cut_dt = cut_b + 2 * NS
-    query_local = regrouped[:, :group_query].reshape(span_rows, query_group, HD)
+    cut_dt = cut_b + 2 * NS // head_count
+    even = head_index % 2 == 0
+    query_local = rotate(
+        projected[:, :group_query].reshape(span_rows, query_group, HD), positions, 1.0
+    ).astype(jnp.bfloat16)
     query_float = query_local.astype(jnp.float32)
-    kv_local = regrouped[:, group_query:cut_z]
-    gate_act = regrouped[:, cut_z:cut_x].astype(jnp.float32).reshape(span_rows, mamba_group, MP)
-    conv_local = regrouped[:, cut_x:cut_dt]
-    step_local = regrouped[:, cut_dt:].astype(jnp.float32)
+    kv_plain = projected[:, cut_kv:cut_z]
+    kv_mine = jnp.where(
+        even, rotate(kv_plain.reshape(span_rows, 1, HD), positions, 1.0)[:, 0], kv_plain
+    ).astype(jnp.bfloat16)
+    kv_beside = from_head(kv_mine, 1)
+    kv_local = jnp.where(
+        even,
+        jnp.concatenate([kv_mine, kv_beside], axis=1),
+        jnp.concatenate([kv_beside, kv_mine], axis=1),
+    )
+    gate_act = (
+        projected[:, cut_z:cut_x]
+        .astype(jnp.bfloat16)
+        .astype(jnp.float32)
+        .reshape(span_rows, mamba_group, MP)
+    )
+    conv_local = jnp.concatenate(
+        [projected[:, cut_x:cut_b].astype(jnp.bfloat16)]
+        + gather_heads(projected[:, cut_b:cut_dt].astype(jnp.bfloat16)),
+        axis=1,
+    )
+    step_local = (
+        projected[:, cut_dt : cut_dt + mamba_group].astype(jnp.bfloat16).astype(jnp.float32)
+    )
     flags_local = start_flags[0]
     rim_rows, rim_flags = passed_along(
         (
@@ -431,29 +566,26 @@
         ],
         axis=1,
     )
-    mixer_tokens = to_tokens(mixer_heads)
-    mixer = jnp.concatenate(
-        [
-            mixer_tokens[:, :, :group_query].reshape(row_count, query_width),
-            mixer_tokens[:, :, group_query:].reshape(row_count, mamba_width),
-        ],
-        axis=1,
-    )
-    hidden_one = tokens + jnp.dot(mixer, gathered_out, preferred_element_type=jnp.float32)
-    gathered_ffn, gathered_down = fetch_weights(weights_ffn, weights_down)
+    mixed = jnp.dot(mixer_heads, weights_out, preferred_element_type=jnp.float32)
+    hidden_one = tokens + scatter_heads(mixed.reshape(head_count, row_count, -1))
     inverse_two = lax.rsqrt(jnp.mean(hidden_one * hidden_one, axis=-1, keepdims=True) + epsilon)
-    normed_two = (hidden_one * inverse_two * second_gain).astype(jnp.bfloat16)
-    gate_up = jnp.dot(normed_two, gathered_ffn, preferred_element_type=jnp.float32)
-    gate_part = gate_up[:, :FF]
-    up_part = gate_up[:, FF:]
+    normed_two = jnp.concatenate(
+        gather_heads(ring_features((hidden_one * inverse_two * second_gain).astype(jnp.bfloat16))),
+        axis=0,
+    )
+    gate_up = jnp.dot(normed_two, weights_ffn, preferred_element_type=jnp.float32)
+    group_units = FF // head_count
+    gate_part = gate_up[:, :group_units]
+    up_part = gate_up[:, group_units:]
     activated = (jax.nn.silu(gate_part) * up_part).astype(jnp.bfloat16)
-    block_output = hidden_one + jnp.dot(
-        activated, gathered_down, preferred_element_type=jnp.float32
-    )
+    downed = jnp.dot(activated, weights_down, preferred_element_type=jnp.float32)
+    block_output = hidden_one + scatter_heads(downed.reshape(head_count, row_count, -1))
     cotangent = out_cotangent[0]
-    back_ffn, back_down = refetch_weights(weights_ffn, weights_down)
-    grad_down_full = outer_grad(activated, cotangent)
-    grad_activated = times_transposed(cotangent, back_down)
+    span_cotangent = jnp.concatenate(gather_heads(cotangent), axis=0)
+    grad_down = scatter_blocks(outer_grad(activated, span_cotangent).astype(jnp.bfloat16)).astype(
+        jnp.float32
+    )
+    grad_activated = times_transposed(span_cotangent, weights_down)
     sigmoid_gate = jax.nn.sigmoid(gate_part)
     grad_gate_up = jnp.concatenate(
         [
@@ -462,26 +594,26 @@
         ],
         axis=1,
     ).astype(jnp.bfloat16)
-    grad_ffn_full = outer_grad(normed_two, grad_gate_up)
-    grad_normed_two = times_transposed(grad_gate_up, back_ffn)
-    grad_ffn, grad_down = reduce_grads(grad_ffn_full, grad_down_full)
+    grad_ffn = scatter_blocks(outer_grad(normed_two, grad_gate_up).astype(jnp.bfloat16))
+    grad_ffn = unpack_ffn(swap_groups(grad_ffn.reshape(head_count, -1, 2 * group_units))).astype(
+        jnp.float32
+    )
+    grad_normed_two = plain_features(
+        scatter_heads(
+            times_transposed(grad_gate_up, weights_ffn).reshape(head_count, row_count, -1)
+        )
+    )
     grad_hidden = cotangent.astype(jnp.float32) + norm_back(
         hidden_one, inverse_two, second_gain, grad_normed_two
     )
     grad_second = jnp.sum(grad_normed_two * hidden_one * inverse_two, axis=0)
-    grad_hidden_low = grad_hidden.astype(jnp.bfloat16)
-    back_out, back_in = refetch_weights(weights_out, weights_in)
-    grad_mix_full = outer_grad(mixer, grad_hidden_low)
-    grad_mixer = times_transposed(grad_hidden_low, back_out).astype(jnp.bfloat16)
-    grad_heads = to_heads(
-        jnp.concatenate(
-            [
-                grad_mixer[:, :query_width].reshape(row_count, head_count, group_query),
-                grad_mixer[:, query_width:].reshape(row_count, head_count, group_inner),
-            ],
-            axis=2,
-        )
-    )
+    span_grad_hidden = jnp.concatenate(gather_heads(grad_hidden.astype(jnp.bfloat16)), axis=0)
+    grad_mix_weight = lax.ppermute(
+        scatter_blocks(outer_grad(mixer_heads, span_grad_hidden).astype(jnp.bfloat16)),
+        ("head", "blk"),
+        [(there, here) for here, there in out_pairs],
+    ).astype(jnp.float32)
+    grad_heads = times_transposed(span_grad_hidden, weights_out).astype(jnp.bfloat16)
     grad_attended = grad_heads[:, :group_query].reshape(span_rows, query_group, HD)
     grad_attended_float = grad_attended.astype(jnp.float32)
     grad_mamba = grad_heads[:, group_query:].astype(jnp.float32).reshape(span_rows, mamba_group, MP)
@@ -561,53 +693,40 @@
     grad_extended, grad_taps, grad_shift, grad_raw, grad_step_shift, grad_rate = prep_grads
     rim_back = passed_along(grad_extended[: KW - 1], "blk", -1)
     conv_grad = grad_extended[KW - 1 :] + jnp.pad(rim_back, ((span_rows - (KW - 1), 0), (0, 0)))
-    back_packed = jnp.concatenate(
-        [
-            grad_query_all.reshape(span_rows, group_query).astype(jnp.bfloat16),
-            grad_keys_own,
-            grad_gate.reshape(span_rows, group_inner).astype(jnp.bfloat16),
-            conv_grad.astype(jnp.bfloat16),
-            grad_raw.astype(jnp.bfloat16),
-        ],
-        axis=1,
-    )
-    back_tokens = to_tokens(back_packed)
+    keys_mine = jnp.where(even, grad_keys_own[:, :HD], grad_keys_own[:, HD:])
+    keys_other = jnp.where(even, grad_keys_own[:, HD:], grad_keys_own[:, :HD])
+    grad_kv = keys_mine.astype(jnp.float32) + from_head(keys_other, 1).astype(jnp.float32)
+    grad_kv = jnp.where(
+        even, rotate(grad_kv.reshape(span_rows, 1, HD), positions, -1.0)[:, 0], grad_kv
+    )
     grad_query_seq = rotate(
-        back_tokens[:, :, :group_query].astype(jnp.float32).reshape(row_count, QH, HD),
-        positions,
-        -1.0,
-    ).reshape(row_count, query_width)
-    grad_kv_seq = jnp.sum(
-        back_tokens[:, :, group_query:cut_z]
-        .astype(jnp.float32)
-        .reshape(row_count, KVH, kv_spread, 2 * HD),
-        axis=2,
-    )
-    grad_key_seq = rotate(grad_kv_seq[:, :, :HD], positions, -1.0).reshape(row_count, kv_width)
-    grad_value_seq = grad_kv_seq[:, :, HD:].reshape(row_count, kv_width)
-    grad_gate_seq = (
-        back_tokens[:, :, cut_z:cut_x].astype(jnp.float32).reshape(row_count, mamba_width)
-    )
-    grad_inner_seq = (
-        back_tokens[:, :, cut_x:cut_b].astype(jnp.float32).reshape(row_count, mamba_width)
-    )
-    grad_bc_seq = jnp.sum(back_tokens[:, :, cut_b:cut_dt].astype(jnp.float32), axis=1)
-    grad_step_seq = back_tokens[:, :, cut_dt:].astype(jnp.float32).reshape(row_count, MH)
+        grad_query_all.astype(jnp.bfloat16).astype(jnp.float32), positions, -1.0
+    ).reshape(span_rows, group_query)
+    grad_bc = conv_grad[:, group_inner:].astype(jnp.bfloat16).astype(jnp.float32)
+    grad_bc = scatter_heads(
+        jnp.stack(jnp.split(grad_bc, head_count, axis=1))
+    )
     grad_projected = jnp.concatenate(
         [
             grad_query_seq,
-            grad_key_seq,
-            grad_value_seq,
-            grad_gate_seq,
-            grad_inner_seq,
-            grad_bc_seq,
-            grad_step_seq,
+            grad_kv,
+            grad_gate.reshape(span_rows, group_inner),
+            conv_grad[:, :group_inner],
+            grad_bc,
+            grad_raw,
+            jnp.zeros((span_rows, step_pad - mamba_group), jnp.float32),
         ],
         axis=1,
     ).astype(jnp.bfloat16)
-    grad_proj_full = outer_grad(normed_one, grad_projected)
-    grad_normed_one = times_transposed(grad_projected, back_in)
-    grad_proj_weight, grad_mix_weight = reduce_grads(grad_proj_full, grad_mix_full)
+    grad_proj_weight = scatter_blocks(outer_grad(normed_one, grad_projected).astype(jnp.bfloat16))
+    grad_proj_weight = unpack_in(
+        swap_groups(grad_proj_weight.reshape(head_count, -1, grad_projected.shape[1]))
+    ).astype(jnp.float32)
+    grad_normed_one = plain_features(
+        scatter_heads(
+            times_transposed(grad_projected, weights_in).reshape(head_count, row_count, -1)
+        )
+    )
     grad_input = (grad_hidden + norm_back(tokens, inverse_one, first_gain, grad_normed_one)).astype(
         jnp.bfloat16
     )

time: 5800 us -> 1390 us (0.24)
  waiting for transfers between devices: 4910 us -> 497 us
  matrix products: 391 us -> 294 us
    reduce_scatter x4, waiting for transfers between devices: 4250 us -> 153 us  [scatter_blocks(): lax.psum_scatter(partial_sums, 'blk', scatter_dimension=0, tiled=True, ax...]
    all_gather x4, waiting for transfers between devices: 500 us -> 91.4 us  [gather_blocks(): lax.all_gather(shard, 'blk', axis=0, tiled=True, axis_index_groups=[ring_...]
    ppermute x0 -> x24, waiting for transfers between devices: none -> 75.3 us  [the longest x22 75.3 us: from_head(): lax.ppermute(shard, 'head', [(i, i ^ distance) for i in range(peers)])]
    psum x1, waiting for transfers between devices: 35.7 us -> 109 us  [per_device(): lax.psum((grad_first, grad_second, grad_conv_weight, grad_conv_bias, grad...]
  transfers between devices with their start and end apart: 19 -> 42, of which waited for: 14 -> 25; matrix products, arithmetic and copies ran while one was open for 7% -> 37% of each run, Pallas kernels for 0% -> 0%
where the time goes in v1:
time: 1390 us; the launch traced here: 1370 us
  waiting for transfers between devices  497 us (36%)
  matrix products  294 us (21%)
  local copies, waits for them, and re-layouts  252 us (18%)
  other arithmetic  136 us (10%)
  blocking collectives  67 us (5%)
  starting transfers between devices  54.5 us (4%)
  loops' own time  47.3 us (3%)
  between operations  19.4 us (1%)
    reduce_scatter x4, waiting for transfers between devices, scatter_blocks(): lax.psum_scatter(partial_sums, 'blk', scatter_dimension=0, tiled=True, ax...  153 us
    psum x1, waiting for transfers between devices, per_device(): lax.psum((grad_first, grad_second, grad_conv_weight, grad_conv_bias, grad...  109 us
    dot_general x36, matrix products, one_head(): return jnp.dot(weights, inner_head, precision=precise)  98.6 us
    all_gather x4, waiting for transfers between devices, gather_blocks(): lax.all_gather(shard, 'blk', axis=0, tiled=True, axis_index_groups=[ring_...  91.4 us
    unnamed x541, local copies, waits for them, and re-layouts  85.7 us
    ppermute x22, waiting for transfers between devices, from_head(): lax.ppermute(shard, 'head', [(i, i ^ distance) for i in range(peers)])  75.3 us
    all_gather x1, waiting for transfers between devices, carried_in(): lax.all_gather(a.astype(kind), axis)  44.4 us
    all_to_all x2, blocking collectives, swap_groups(): lax.all_to_all(groups, 'head', split_axis=0, concat_axis=0, tiled=True)  36.2 us
  transfers between devices with their start and end apart: 42, of which 25 were waited for; matrix products, arithmetic and copies ran while one was open for 37% of the time, Pallas kernels for 0%

profile of v1, /device:TPU:16, one launch (start us, length us, event | category | flops | bytes accessed | tf_op | source)
XLA Modules:
  0.0 1366.7 jit_solution(767820914881014858)
XLA Ops:
  9.8 18.5 %all_to_all.20 = bf16[4,64,2176]{2,1,0:T(8,128)(2,1)} all-to-all(bf16[4,64,2176]{2,1,0:T(8,128)(2,1)S(1)} %pad_maximum_fusion.14), channel_id=1, replica_groups=mesh['head'=4,'blk'=8] {'head'}, dimensions={0} | all-to-all | bytes 2228224 | tf_op jit(solution)/shard_map/all_to_all | solution.py:241
  52.8 82.3 %all-gather.11.cloned.1.call-done = bf16[2048,2176]{1,0:T(8,128)(2,1)} async-done(((bf16[256,2176]{1,0:T(8,128)(2,1)}), bf16[2048,2176]{1,0:T(8,128)(2,1)}) %all-gather.11.cloned.1.call-update) | async-done | bytes 8912912 | tf_op jit(solution)/shard_map/all_gather | solution.py:86
  135.1 10.5 fusion.221
  149.1 3.6 collective-permute-done.2
  181.3 4.0 fusion.208
  185.3 3.8 fusion.206
  226.9 17.7 %all_to_all.21 = bf16[4,64,2048]{2,1,0:T(8,128)(2,1)} all-to-all(bf16[4,64,2048]{2,1,0:T(8,128)(2,1)S(1)} %pad_maximum_fusion.18), channel_id=1, replica_groups=mesh['head'=4,'blk'=8] {'head'}, dimensions={0} | all-to-all | bytes 2097152 | tf_op jit(solution)/shard_map/all_to_all | solution.py:241
  247.4 15.7 %all-reduce.14 = bf16[8]{0:T(256)(128)(2,1)S(1)} all-reduce(bf16[8]{0:T(256)(128)(2,1)S(1)} %dynamic-update-slice), channel_id=1, replica_groups=mesh['head'=4,'blk'=8] {'blk'}, use_global_device_ids=true, to_apply=%add.14 | all-reduce | flops 8 | bytes 32
  272.7 15.1 %all-gather.2 = bf16[8,1,12]{2,1,0:T(2,128)(2,1)S(1)} all-gather(bf16[1,1,12]{2,1,0:T(2,128)(2,1)S(1)} %copy-done.134), channel_id=1, replica_groups=mesh['head'=4,'blk'=8] {'blk'}, dimensions={0}, use_global_device_ids=true | all-gather | bytes 216 | tf_op jit(solution)/shard_map/all_gather | solution.py:33
  299.4 46.0 %while.94 = (s32[]{:T(128)}, f32[12,512,64]{1,2,0:T(8,128)}, f32[12,512]{1,0:T(8,128)}, f32[512,512]{1,0:T(8,128)S(1)}, f32[12,512]{1,0:T(8,128)}, /*index=5*/f32[12,512,64]{2,1,0:T(8,128)}, s32[512]{0:T(512)S(1)}, s32[]{:T(128)}) while((s32[]{:T(128)}, f32[12,512,64]{1,2,0:T(8,128)}, f32[12,512]{1,0:T(8,128)}, ...), condition=%wide.region_18.19_spmd.clone, body=%wide.region_17.18_spmd.clone.sunk | while | flops 203423744 | bytes 1461337 | solution.py:341
  346.3 19.8 %while.96 = (s32[]{:T(128)}, f32[12,64,256]{2,1,0:T(8,128)S(1)}, f32[]{:T(128)}, s32[]{:T(128)}, bf16[8,12]{1,0:T(8,128)(2,1)S(1)}, /*index=5*/bf16[8,12,64,256]...) while((s32[]{:T(128)}, f32[12,64,256]{2,1,0:T(8,128)S(1)}, f32[]{:T(128)}, ...), condition=%wide.region_9.10_spmd.clone, body=%wide.region_8.9_spmd.clone.sunk | while | flops 983058 | bytes 1966352 | solution.py:50
  367.5 52.1 %while.93 = (s32[]{:T(128)}, f32[512,2]{0,1:T(2,128)S(1)}, f32[512,2]{0,1:T(2,128)S(1)}, f32[512,2,128]{2,0,1:T(8,128)S(1)}, s32[8]{0:T(128)S(1)}, /*index=5*/s3...) while((s32[]{:T(128)}, f32[512,2]{0,1:T(2,128)S(1)}, ...), condition=%wide.region_16.17_spmd.clone, body=%wide.region_11.16_spmd.clone.sunk | while | flops 946867200 | bytes 9517379 | solution.py:548
  370.0 6.3 conditional.6
  378.9 6.3 conditional.6
  387.8 6.3 conditional.6
  396.7 6.3 conditional.6
  405.5 6.3 conditional.6
  422.6 5.6 multiply_convert_fusion.4
  428.3 4.9 fusion.111
  449.5 11.3 collective-permute-done.9
  464.4 7.6 collective-permute-done.14
  473.2 9.1 collective-permute-done.10
  487.1 10.7 fusion.137
  497.8 9.1 all-gather.19.cloned.1.call-done
  506.9 8.3 multiply_convert_fusion.2
  515.2 5.0 fusion.80
  520.7 4.1 collective-permute-done.16
  530.1 11.2 collective-permute-done.17
  545.0 11.7 collective-permute-done.18
  572.1 129.6 %while.95 = (s32[]{:T(128)}, f32[512,2,128]{2,0,1:T(8,128)}, f32[4096,256]{0,1:T(8,128)}, s32[8]{0:T(128)S(1)}, s32[]{:T(128)}, /*index=5*/s32[]{:T(128)}, s32[5...) while((s32[]{:T(128)}, f32[512,2,128]{2,0,1:T(8,128)}, ...), condition=%wide.region_26.27_spmd.clone, body=%wide.region_23.26_spmd.clone.sunk | while | flops 2688877568 | bytes 19814812 | solution.py:548
  574.7 21.9 %conditional.7 = ((f32[512,2,128]{2,0,1:T(8,128)}, f32[4096,256]{0,1:T(8,128)})) conditional(s32[]{:T(128)} %convert_element_type.493, (f32[512,2,128]{2,0,1:T(8,128)}, f32[4096,256]{0,1:T(8,128)}) %tuple.580, (s32[]{:T(128)}, s32[]{:T(128)}, s32[512]{0:T(512)S(1)}, bf16[8,512,256]{2,1,0:T(8,128)(2,1)}, s32[]{:T(128)}, ...), branch_computations={%region_24.24_spmd, %region_25.25_spmd} | conditional | flops 2688877568 | bytes 19812428 | solution.py:533
  592.9 3.6 fusion.24
  599.1 21.9 %conditional.7 = ((f32[512,2,128]{2,0,1:T(8,128)}, f32[4096,256]{0,1:T(8,128)})) conditional(s32[]{:T(128)} %convert_element_type.493, (f32[512,2,128]{2,0,1:T(8,128)}, f32[4096,256]{0,1:T(8,128)}) %tuple.580, (s32[]{:T(128)}, s32[]{:T(128)}, s32[512]{0:T(512)S(1)}, bf16[8,512,256]{2,1,0:T(8,128)(2,1)}, s32[]{:T(128)}, ...), branch_computations={%region_24.24_spmd, %region_25.25_spmd} | conditional | flops 2688877568 | bytes 19812428 | solution.py:533
  617.3 3.6 fusion.24
  623.4 21.9 %conditional.7 = ((f32[512,2,128]{2,0,1:T(8,128)}, f32[4096,256]{0,1:T(8,128)})) conditional(s32[]{:T(128)} %convert_element_type.493, (f32[512,2,128]{2,0,1:T(8,128)}, f32[4096,256]{0,1:T(8,128)}) %tuple.580, (s32[]{:T(128)}, s32[]{:T(128)}, s32[512]{0:T(512)S(1)}, bf16[8,512,256]{2,1,0:T(8,128)(2,1)}, s32[]{:T(128)}, ...), branch_computations={%region_24.24_spmd, %region_25.25_spmd} | conditional | flops 2688877568 | bytes 19812428 | solution.py:533
  641.7 3.6 fusion.24
  647.8 21.9 %conditional.7 = ((f32[512,2,128]{2,0,1:T(8,128)}, f32[4096,256]{0,1:T(8,128)})) conditional(s32[]{:T(128)} %convert_element_type.493, (f32[512,2,128]{2,0,1:T(8,128)}, f32[4096,256]{0,1:T(8,128)}) %tuple.580, (s32[]{:T(128)}, s32[]{:T(128)}, s32[512]{0:T(512)S(1)}, bf16[8,512,256]{2,1,0:T(8,128)(2,1)}, s32[]{:T(128)}, ...), branch_computations={%region_24.24_spmd, %region_25.25_spmd} | conditional | flops 2688877568 | bytes 19812428 | solution.py:533
  666.0 3.6 fusion.24
  672.2 21.9 %conditional.7 = ((f32[512,2,128]{2,0,1:T(8,128)}, f32[4096,256]{0,1:T(8,128)})) conditional(s32[]{:T(128)} %convert_element_type.493, (f32[512,2,128]{2,0,1:T(8,128)}, f32[4096,256]{0,1:T(8,128)}) %tuple.580, (s32[]{:T(128)}, s32[]{:T(128)}, s32[512]{0:T(512)S(1)}, bf16[8,512,256]{2,1,0:T(8,128)(2,1)}, s32[]{:T(128)}, ...), branch_computations={%region_24.24_spmd, %region_25.25_spmd} | conditional | flops 2688877568 | bytes 19812428 | solution.py:533
  690.4 3.6 fusion.24
  701.6 4.6 copy.4737
  709.3 4.4 multiply_reduce_fusion.8
  718.2 4.4 convolution_convert_fusion.2
  724.4 4.0 convolution_convert_fusion.3
  729.9 8.3 convolution_convert_fusion.1
  740.1 109.9 %while.97 = (s32[]{:T(128)}, f32[512,512]{1,0:T(8,128)S(1)}, f32[12,512]{1,0:T(8,128)S(1)}, f32[12,512]{1,0:T(8,128)S(1)}, f32[12,512,64]{1,2,0:T(8,128)}, /*ind...) while((s32[]{:T(128)}, f32[512,512]{1,0:T(8,128)S(1)}, ...), condition=%wide.region_32.33_spmd.clone, body=%wide.region_28.32_spmd.clone.sunk | while | flops 408944128 | bytes 9609423 | solution.py:341
  850.0 4.1 fusion.90
  867.8 44.4 %all-gather.23.cloned.1.call-done = bf16[96,64,256]{2,1,0:T(8,128)(2,1)} async-done(((bf16[12,64,256]{2,1,0:T(8,128)(2,1)}), bf16[96,64,256]{2,1,0:T(8,128)(2,1)}) %all-gather.23.cloned.1.call-update) | async-done | bytes 3145744 | tf_op jit(solution)/shard_map/all_gather | solution.py:58
  912.3 6.0 while.92
  918.4 5.2 multiply_reduce_fusion.6
  933.2 4.7 multiply_reduce_fusion.5
  938.8 4.6 collective-permute-start.21
  948.6 5.2 reduce-window.48
  966.3 9.4 convolution_convert_fusion
  976.9 4.7 fusion.222
  985.2 5.1 fusion.223
  1013.6 8.9 collective-permute-start.26
  1022.5 5.2 collective-permute-done.25
  1030.5 81.9 %reduce-scatter.12.cloned.1.call-done = bf16[256,2048]{1,0:T(8,128)(2,1)} async-done(((bf16[2048,2048]{1,0:T(8,128)(2,1)}), bf16[256,2048]{1,0:T(8,128)(2,1)}) %reduce-scatter.12.cloned.1.call-update) | async-done | bytes 1048592 | tf_op jit(solution)/shard_map/reduce_scatter | solution.py:92
  1112.4 14.7 %all-to-all-start.3 = ((bf16[4,64,2048]{2,1,0:T(8,128)(2,1)}), bf16[4,64,2048]{2,1,0:T(8,128)(2,1)}, u32[]{:S(2)}, u32[]{:S(2)}) async-start(bf16[4,64,2048]{2,1,0:T(8,128)(2,1)} %bitcast.1091), calls=%async_computation.7 | async-start | bytes 2097152 | tf_op jit(solution)/shard_map/all_to_all | solution.py:241
  1136.4 6.2 all-to-all-done.3
  1147.2 71.4 %reduce-scatter.8.cloned.1.call-done = bf16[256,2176]{1,0:T(8,128)(2,1)} async-done(((bf16[2048,2176]{1,0:T(8,128)(2,1)}), bf16[256,2176]{1,0:T(8,128)(2,1)}) %reduce-scatter.8.cloned.1.call-update) | async-done | bytes 1114128 | tf_op jit(solution)/shard_map/reduce_scatter | solution.py:92
  1223.7 14.0 %all-to-all-done.2 = bf16[4,64,2176]{2,1,0:T(8,128)(2,1)S(1)} async-done(((bf16[4,64,2176]{2,1,0:T(8,128)(2,1)}), bf16[4,64,2176]{2,1,0:T(8,128)(2,1)S(1)}, u32[]{:S(2)}, u32[]{:S(2)}) %all-to-all-start.2) | async-done | bytes 1114144 | tf_op jit(solution)/shard_map/all_to_all | solution.py:241
  1241.6 109.3 %all-reduce.18.cloned.1.call-done = (f32[2048]{0:T(1024)}, f32[2048]{0:T(1024)}, f32[4,3584]{1,0:T(4,128)}, f32[3584]{0:T(1024)}, f32[48]{0:T(128)}, /*index=5*/f32[48]{0:T(128)}, f32[48]{0:T(128)}) async-done(((f32[2048]{0:T(1024)}, f32[2048]{0:T(1024)}, f32[4,3584]{1,0:T(4,128)}, f32[3584]{0:T(1024)}, f32[48]{0:T(128)}, /*index=5*/f32[48]{0:T(128)}, f32[48]{0:T(128)}), (f32[2048]{0:T(1024)}, ...) | async-done | bytes 88656 | tf_op jit(solution)/shard_map/psum | solution.py:766
  (1221 shorter events, 587.1 us)
Async XLA Ops:
  7.2 127.9 %all-gather.11.cloned.1.call-start = ((), (), s32[]{:S(2)}) async-start(), calls=%async_computation.9 | async-start | bytes 10027008 | tf_op jit(solution)/shard_map/all_gather | solution.py:86
  28.2 317.1 %all-gather.21.cloned.1.call-start = ((), (), s32[]{:S(2)}) async-start(), calls=%async_computation.19 | async-start | bytes 3538944 | tf_op jit(solution)/shard_map/all_gather | solution.py:33
  28.6 13.7 collective-permute-start
  29.1 15.5 %collective-permute-start.5 = (bf16[2]{0:T(256)(128)(2,1)S(1)}, bf16[2]{0:T(256)(128)(2,1)S(1)}, u32[]{:S(2)}, u32[]{:S(2)}) collective-permute-start(bf16[2]{0:T(256)(128)(2,1)S(1)} %fusion.173), channel_id=1, source_target_pairs={{0,1},{1,2},{2,3},{3,4},{4,5},{5,6},{6,7},{8,9},{9,10},{10,11},{11... | collective-permute-start | bytes 20 | tf_op jit(solution)/shard_map/ppermute | solution.py:27
  34.6 170.5 %collective-permute-start.7 = (bf16[128,2048]{1,0:T(8,128)(2,1)}, bf16[128,2048]{1,0:T(8,128)(2,1)}, u32[]{:S(2)}, u32[]{:S(2)}) collective-permute-start(bf16[128,2048]{1,0:T(8,128)(2,1)} %convert_element_type.324), channel_id=1, source_target_pairs={{0,0},{1,2},{2,8},{3,10},{4,16},{5,18},{6,24},{7,26},{8,4},{9,6},{... | collective-permute-start | bytes 1572872 | tf_op jit(solution)/shard_map/ppermute | solution.py:388
  38.7 122.8 %copy-start.116 = (f32[512]{0:T(512)}, f32[512]{0:T(512)S(1)}, u32[]{:S(2)}) copy-start(f32[512]{0:T(512)S(1)} %get-tuple-element.2643) | copy-start | bytes 6148
  40.8 120.6 %copy-start.118 = (f32[12]{0:T(128)}, f32[12]{0:T(128)S(1)}, u32[]{:S(2)}) copy-start(f32[12]{0:T(128)S(1)} %dynamic_slice.258) | copy-start | bytes 148
  40.9 126.0 %copy-start.95 = (f32[1280]{0:T(1024)}, f32[1280]{0:T(1024)S(1)}, u32[]{:S(2)}) copy-start(f32[1280]{0:T(1024)S(1)} %get-tuple-element.2507) | copy-start | bytes 15364
  40.9 126.0 %copy-start.97 = (f32[1280]{0:T(1024)}, f32[1280]{0:T(1024)S(1)}, u32[]{:S(2)}) copy-start(f32[1280]{0:T(1024)S(1)} %get-tuple-element.2508) | copy-start | bytes 15364
  40.9 126.0 %copy-start.99 = (f32[1280]{0:T(1024)}, f32[1280]{0:T(1024)S(1)}, u32[]{:S(2)}) copy-start(f32[1280]{0:T(1024)S(1)} %get-tuple-element.2509) | copy-start | bytes 15364
  40.9 126.0 %copy-start.101 = (f32[1280]{0:T(1024)}, f32[1280]{0:T(1024)S(1)}, u32[]{:S(2)}) copy-start(f32[1280]{0:T(1024)S(1)} %get-tuple-element.2510) | copy-start | bytes 15364
  41.0 222.7 %copy-start.106 = (f32[512]{0:T(512)}, f32[512]{0:T(512)S(1)}, u32[]{:S(2)}) copy-start(f32[512]{0:T(512)S(1)} %fusion.170) | copy-start | bytes 6148
  42.4 2.7 collective-permute-start.1
  42.5 104.9 %copy-start.129 = (f32[12]{0:T(128)}, f32[12]{0:T(128)S(1)}, u32[]{:S(2)}) copy-start(f32[12]{0:T(128)S(1)} %dynamic-slice_exponential_fusion) | copy-start | bytes 148
  43.2 118.3 %copy-start.120 = (pred[512]{0:T(512)(128)(4,1)}, pred[512]{0:T(512)(128)(4,1)S(1)}, u32[]{:S(2)}) copy-start(pred[512]{0:T(512)(128)(4,1)S(1)} %broadcast_compare_fusion) | copy-start | bytes 1540
  44.7 122.2 %copy-start.108 = (f32[512]{0:T(512)}, f32[512]{0:T(512)S(1)}, u32[]{:S(2)}) copy-start(f32[512]{0:T(512)S(1)} %get-tuple-element.2647) | copy-start | bytes 6148
  44.7 122.2 %copy-start.110 = (f32[512]{0:T(512)}, f32[512]{0:T(512)S(1)}, u32[]{:S(2)}) copy-start(f32[512]{0:T(512)S(1)} %get-tuple-element.2648) | copy-start | bytes 6148
  44.7 122.2 %copy-start.112 = (f32[512]{0:T(512)}, f32[512]{0:T(512)S(1)}, u32[]{:S(2)}) copy-start(f32[512]{0:T(512)S(1)} %get-tuple-element.2936) | copy-start | bytes 6148
  147.4 5.3 collective-permute-start.2
  152.7 1.6 collective-permute-start.3
  153.0 136.5 %copy-start.24 = (f32[12,4,128]{0,2,1:T(8,128)}, f32[12,4,128]{0,2,1:T(8,128)S(1)}, u32[]{:S(2)}) copy-start(f32[12,4,128]{0,2,1:T(8,128)S(1)} %copy.4710) | copy-start | bytes 73732
  157.9 7.4 collective-permute-start.4
  174.9 247.6 %copy-start.2 = (f32[512,768]{0,1:T(8,128)}, f32[512,768]{0,1:T(8,128)S(1)}, u32[]{:S(2)}) copy-start(f32[512,768]{0,1:T(8,128)S(1)} %copy.4712) | copy-start | bytes 4718596
  178.7 188.7 %all-gather.13.cloned.1.call-start = ((), (), s32[]{:S(2)}) async-start(), calls=%async_computation.10 | async-start | bytes 2359296 | tf_op jit(solution)/shard_map/all_gather | solution.py:558
  192.8 1.4 collective-permute-start.6
  195.0 233.2 %all-gather.15.cloned.1.call-start = ((), (), s32[]{:S(2)}) async-start(), calls=%async_computation.11 | async-start | bytes 4718592 | tf_op jit(solution)/shard_map/all_gather | solution.py:86
  205.1 281.9 %all-gather.17.cloned.1.call-start = ((), (), s32[]{:S(2)}) async-start(), calls=%async_computation.12 | async-start | bytes 9437184 | tf_op jit(solution)/shard_map/all_gather | solution.py:86
  244.7 262.2 %all-gather.19.cloned.1.call-start = ((), (), s32[]{:S(2)}) async-start(), calls=%async_computation.13 | async-start | bytes 4718592 | tf_op jit(solution)/shard_map/all_gather | solution.py:86
  263.6 159.0 %copy-start.130 = (f32[12]{0:T(128)}, f32[12]{0:T(128)S(1)}, u32[]{:S(2)}) copy-start(f32[12]{0:T(128)S(1)} %dynamic_slice.266) | copy-start | bytes 148
  436.6 4.4 collective-permute-start.8
  437.7 421.7 %reduce-scatter.6.cloned.1.call-start = ((), (), s32[]{:S(2)}) async-start(), calls=%async_computation.14 | async-start | bytes 2359296 | tf_op jit(solution)/shard_map/reduce_scatter | solution.py:661
  445.7 15.1 %collective-permute-start.9 = (bf16[128,2048]{0,1:T(8,128)(2,1)}, bf16[128,2048]{0,1:T(8,128)(2,1)}, u32[]{:S(2)}, u32[]{:S(2)}) collective-permute-start(bf16[128,2048]{0,1:T(8,128)(2,1)} %bitcast.72), channel_id=1, source_target_pairs={{0,16},{8,24},{16,0},{24,8},{1,17},{9,25},{17,1},{25,9},{2,18},{10... | collective-permute-start | bytes 1572872 | tf_op jit(solution)/shard_map/ppermute | solution.py:103
  448.1 23.9 %collective-permute-start.14 = (bf16[128,2048]{0,1:T(8,128)(2,1)S(1)}, bf16[128,2048]{0,1:T(8,128)(2,1)}, u32[]{:S(2)}, u32[]{:S(2)}) collective-permute-start(bf16[128,2048]{0,1:T(8,128)(2,1)S(1)} %bitcast.965), channel_id=1, source_target_pairs={{0,16},{8,24},{16,0},{24,8},{1,17},{9,25},{17,1},{25,9},{2,18},{10... | collective-permute-start | bytes 1572872 | tf_op jit(solution)/shard_map/ppermute | solution.py:103
  463.3 19.1 %collective-permute-start.10 = (bf16[128,2048]{0,1:T(8,128)(2,1)S(1)}, bf16[128,2048]{0,1:T(8,128)(2,1)S(1)}, u32[]{:S(2)}, u32[]{:S(2)}) collective-permute-start(bf16[128,2048]{0,1:T(8,128)(2,1)S(1)} %constant_dynamic-update-slice_fusion.12), channel_id=1, source_target_pairs={{0,16},{8,24},{16,0},{24,8},{1,17},{9,25},{17,1},{25,9},{2,18},{10... | collective-permute-start | bytes 1572872 | tf_op jit(solution)/shard_map/ppermute | solution.py:103
  473.2 9.4 collective-permute-start.15
  482.4 2.7 collective-permute-start.11
  520.7 4.2 collective-permute-start.16
  527.1 14.2 %collective-permute-start.17 = (bf16[128,2048]{0,1:T(8,128)(2,1)}, bf16[128,2048]{0,1:T(8,128)(2,1)S(1)}, u32[]{:S(2)}, u32[]{:S(2)}) collective-permute-start(bf16[128,2048]{0,1:T(8,128)(2,1)} %bitcast.105), channel_id=1, source_target_pairs={{0,16},{8,24},{16,0},{24,8},{1,17},{9,25},{17,1},{25,9},{2,18},{10... | collective-permute-start | bytes 1572872 | tf_op jit(solution)/shard_map/ppermute | solution.py:103
  543.5 13.2 collective-permute-start.18
  556.8 2.7 collective-permute-start.19
  706.3 206.0 %all-gather.23.cloned.1.call-start = ((), (), s32[]{:S(2)}) async-start(), calls=%async_computation.20 | async-start | bytes 3538944 | tf_op jit(solution)/shard_map/all_gather | solution.py:58
  718.1 287.4 %reduce-scatter.14.cloned.1.call-start = ((), (), s32[]{:S(2)}) async-start(), calls=%async_computation.18 | async-start | bytes 4718592 | tf_op jit(solution)/shard_map/reduce_scatter | solution.py:92
  722.6 290.9 %reduce-scatter.10.cloned.1.call-start = ((), (), s32[]{:S(2)}) async-start(), calls=%async_computation.16 | async-start | bytes 4718592 | tf_op jit(solution)/shard_map/reduce_scatter | solution.py:92
  728.4 384.0 %reduce-scatter.12.cloned.1.call-start = ((), (), s32[]{:S(2)}) async-start(), calls=%async_computation.17 | async-start | bytes 9437184 | tf_op jit(solution)/shard_map/reduce_scatter | solution.py:92
  738.2 480.4 %reduce-scatter.8.cloned.1.call-start = ((), (), s32[]{:S(2)}) async-start(), calls=%async_computation.15 | async-start | bytes 10027008 | tf_op jit(solution)/shard_map/reduce_scatter | solution.py:92
  740.1 109.9 %copy-start.5 = (f32[12,64,256]{2,1,0:T(8,128)S(1)}, f32[12,64,256]{2,1,0:T(8,128)}, u32[]{:S(2)}) copy-start(f32[12,64,256]{2,1,0:T(8,128)} %copy-done.4) | copy-start | bytes 2359300
  860.4 5.3 collective-permute-start.20
  938.8 7.0 collective-permute-start.21
  947.2 6.9 collective-permute-start.22
  955.1 5.9 collective-permute-start.23
  985.2 9.0 collective-permute-start.12
  993.7 15.5 %collective-permute-start.24 = (f32[2,128,2048]{2,1,0:T(8,128)}, f32[2,128,2048]{2,1,0:T(8,128)}, u32[]{:S(2)}, u32[]{:S(2)}) collective-permute-start(f32[2,128,2048]{2,1,0:T(8,128)} %pad_maximum_fusion.11), channel_id=1, source_target_pairs={{0,8},{8,0},{16,24},{24,16},{1,9},{9,1},{17,25},{25,17},{2,10},{10... | collective-permute-start | bytes 6291464 | tf_op jit(solution)/shard_map/ppermute | solution.py:103
  998.7 128.5 %collective-permute-start.13 = (bf16[128,2048]{0,1:T(8,128)(2,1)}, bf16[128,2048]{0,1:T(8,128)(2,1)}, u32[]{:S(2)}, u32[]{:S(2)}) collective-permute-start(bf16[128,2048]{0,1:T(8,128)(2,1)} %bitcast.1095), channel_id=1, source_target_pairs={{0,16},{8,24},{16,0},{24,8},{1,17},{9,25},{17,1},{25,9},{2,18},{10... | collective-permute-start | bytes 1572872 | tf_op jit(solution)/shard_map/ppermute | solution.py:103
  1012.0 15.8 %collective-permute-start.25 = (bf16[128,2048]{0,1:T(8,128)(2,1)S(1)}, bf16[128,2048]{0,1:T(8,128)(2,1)S(1)}, u32[]{:S(2)}, u32[]{:S(2)}) collective-permute-start(bf16[128,2048]{0,1:T(8,128)(2,1)S(1)} %bitcast.1096), channel_id=1, source_target_pairs={{0,16},{8,24},{16,0},{24,8},{1,17},{9,25},{17,1},{25,9},{2,18},{10... | collective-permute-start | bytes 1572872 | tf_op jit(solution)/shard_map/ppermute | solution.py:103
  1013.6 120.7 %collective-permute-start.26 = (bf16[128,2048]{1,0:T(8,128)(2,1)}, bf16[128,2048]{1,0:T(8,128)(2,1)}, u32[]{:S(2)}, u32[]{:S(2)}) collective-permute-start(bf16[128,2048]{1,0:T(8,128)(2,1)} %reduce-scatter.10.cloned.1.call-done), channel_id=1, source_target_pairs={{0,0},{2,1},{8,2},{10,3},{16,4},{18,5},{24,6},{26,7},{4,8},{6,9},{... | collective-permute-start | bytes 1572872 | tf_op jit(solution)/shard_map/ppermute | solution.py:611
  1028.1 99.0 %copy-start.14 = (f32[128,2048]{0,1:T(8,128)S(1)}, f32[128,2048]{0,1:T(8,128)}, u32[]{:S(2)}) copy-start(f32[128,2048]{0,1:T(8,128)} %copy-done.13) | copy-start | bytes 3145732
  1028.1 99.0 %copy-start.20 = (bf16[1,128,2048]{1,2,0:T(8,128)(2,1)S(1)}, bf16[1,128,2048]{1,2,0:T(8,128)(2,1)}, u32[]{:S(2)}) copy-start(bf16[1,128,2048]{1,2,0:T(8,128)(2,1)} %copy-done.19) | copy-start | bytes 1572868
  1028.1 99.0 %copy-start.23 = (f32[128,2048]{0,1:T(8,128)S(1)}, f32[128,2048]{0,1:T(8,128)}, u32[]{:S(2)}) copy-start(f32[128,2048]{0,1:T(8,128)} %copy-done.22) | copy-start | bytes 3145732
  1028.2 99.0 %copy-start.77 = (f32[2048]{0:T(1024)S(1)}, f32[2048]{0:T(1024)}, u32[]{:S(2)}) copy-start(f32[2048]{0:T(1024)} %param.38) | copy-start | bytes 24580
  1028.2 99.0 %copy-start.126 = (f32[128]{0:T(128)S(1)}, f32[128]{0:T(128)}, u32[]{:S(2)}) copy-start(f32[128]{0:T(128)} %copy-done.125) | copy-start | bytes 1540
  1028.2 99.0 %copy-start.136 = (f32[128]{0:T(128)S(1)}, f32[128]{0:T(128)}, u32[]{:S(2)}) copy-start(f32[128]{0:T(128)} %copy-done.135) | copy-start | bytes 1540
  1112.4 30.1 %all-to-all-start.3 = ((bf16[4,64,2048]{2,1,0:T(8,128)(2,1)}), bf16[4,64,2048]{2,1,0:T(8,128)(2,1)}, u32[]{:S(2)}, u32[]{:S(2)}) async-start(bf16[4,64,2048]{2,1,0:T(8,128)(2,1)} %bitcast.1091), calls=%async_computation.7 | async-start | bytes 2097152 | tf_op jit(solution)/shard_map/all_to_all | solution.py:241
  1127.1 223.8 %all-reduce.18.cloned.1.call-start = ((), (), s32[]{:S(2)}) async-start(), calls=%async_computation.21 | async-start | bytes 183296 | tf_op jit(solution)/shard_map/psum | solution.py:766
  1218.6 19.0 %all-to-all-start.2 = ((bf16[4,64,2176]{2,1,0:T(8,128)(2,1)}), bf16[4,64,2176]{2,1,0:T(8,128)(2,1)S(1)}, u32[]{:S(2)}, u32[]{:S(2)}) async-start(bf16[4,64,2176]{2,1,0:T(8,128)(2,1)} %bitcast.1079), calls=%async_computation.4 | async-start | bytes 2228224 | tf_op jit(solution)/shard_map/all_to_all | solution.py:241
  (149 other events, 1461.8 us)
Sparse Core Ops, SparseCore 0:
  28.4 106.7 all-gather.10
  178.8 58.7 all-gather.20
  240.3 48.0 all-gather.12
  289.7 46.9 all-gather.14
  338.1 87.2 all-gather.16
  437.8 69.0 all-gather.18
  706.4 143.5 reduce-scatter.5
  852.2 60.0 all-gather.22
  914.5 47.9 reduce-scatter.13
  964.6 48.0 reduce-scatter.9
  1015.0 97.4 reduce-scatter.11
  1114.6 103.9 reduce-scatter.7
  1226.2 124.7 all-reduce.17

commit v2 on v1

v2 whole, which is shorter than its diff:
```python
import math
from functools import partial

import jax
import jax.numpy as jnp
from jax import lax
from jax.experimental import pallas as pl
from jax.experimental.pallas import tpu as pltpu
from jax.sharding import PartitionSpec as P

QH = 8
KVH = 2
HD = 128
MH = 48
MP = 64
NS = 256
FF = 4096
KW = 4


epsilon = 1e-05
rope_base = 100000000000.0
masked_score = -1e30


def passed_along(shard, axis, by):
    peers = lax.axis_size(axis)
    pairs = [(i, i + by) for i in range(peers) if 0 <= i + by < peers]
    return lax.ppermute(shard, axis, pairs)


def ring_of(axis):
    peers = lax.axis_size(axis)
    if peers != 8:
        return list(range(peers))
    return [0, 2, 4, 6, 7, 5, 3, 1]


def gather_blocks(shard):
    return lax.all_gather(
        shard, "blk", axis=0, tiled=True, axis_index_groups=[ring_of("blk")]
    )


def scatter_blocks(partial_sums):
    return lax.psum_scatter(
        partial_sums,
        "blk",
        scatter_dimension=0,
        tiled=True,
        axis_index_groups=[ring_of("blk")],
    )


def from_head(shard, distance):
    peers = lax.axis_size("head")
    return lax.ppermute(shard, "head", [(i, i ^ distance) for i in range(peers)])


def by_distance(parts):
    mine = lax.axis_index("head")
    stacked = jnp.stack(parts)
    return [
        lax.dynamic_index_in_dim(stacked, jnp.bitwise_xor(mine, j), 0, False)
        for j in range(len(parts))
    ]


def gather_heads(shard):
    across = from_head(shard, 2)
    beside = from_head(jnp.stack([shard, across]), 1)
    return by_distance([shard, beside[0], across, beside[1]])


def scatter_heads(chunks):
    mine = lax.axis_index("head")

    def chunk(distance):
        return lax.dynamic_index_in_dim(chunks, jnp.bitwise_xor(mine, distance), 0, False)

    got = from_head(jnp.stack([chunk(1), chunk(3)]), 1)
    near = chunk(0) + got[0]
    far = (chunk(2) + got[1]).astype(jnp.bfloat16)
    return near + from_head(far, 2).astype(jnp.float32)


def ring_features(values_in):
    heads, ring = lax.axis_size("head"), ring_of("blk")
    rows, width = values_in.shape
    cut = values_in.reshape(rows, heads, len(ring), width // (heads * len(ring)))
    return jnp.concatenate([cut[:, :, k, :].reshape(rows, -1) for k in ring], axis=1)


def plain_features(values_in):
    heads, ring = lax.axis_size("head"), ring_of("blk")
    rows, width = values_in.shape
    cut = values_in.reshape(rows, len(ring), heads, width // (heads * len(ring)))
    places = [ring.index(k) for k in range(len(ring))]
    return jnp.concatenate(
        [cut[:, places[k], j, :] for j in range(heads) for k in range(len(ring))], axis=1
    )


def mixer_place():
    heads, ring = lax.axis_size("head"), ring_of("blk")
    peers = heads * len(ring)
    rows = (QH * HD + MH * MP) // peers
    query_blocks, mamba_blocks = QH * HD // rows // heads, MH * MP // rows // heads
    pairs = []
    for r in range(peers):
        if r < query_blocks * heads:
            group, slot = divmod(r, query_blocks)
        else:
            group, slot = divmod(r - query_blocks * heads, mamba_blocks)
            slot += query_blocks
        pairs.append((r, group * len(ring) + ring[slot]))
    return pairs


def column_cuts():
    query_end = QH * HD
    z_begin = query_end + 2 * KVH * HD
    x_begin = z_begin + MH * MP
    b_begin = x_begin + MH * MP
    dt_begin = b_begin + 2 * NS
    heads = lax.axis_size("head")
    cuts = []
    for j in range(heads):
        kind, kv_head = j % 2, j // 2
        kv_begin = query_end + kind * KVH * HD + kv_head * HD
        cuts.append(
            [
                (x_begin + j * MH * MP // heads, MH * MP // heads),
                (b_begin + j * 2 * NS // heads, 2 * NS // heads),
                (dt_begin + j * MH // heads, MH // heads),
                (0, MH // heads - step_pad),
                (j * QH * HD // heads, QH * HD // heads),
                (kv_begin, HD),
                (z_begin + j * MH * MP // heads, MH * MP // heads),
            ]
        )
    return cuts


step_pad = 128


def pack_in(weight):
    groups = []
    for cuts in column_cuts():
        pieces = [
            weight[:, begin : begin + size]
            if size > 0
            else jnp.zeros((weight.shape[0], -size), weight.dtype)
            for begin, size in cuts
        ]
        groups.append(jnp.concatenate(pieces, axis=1))
    return jnp.stack(groups)


def unpack_in(groups):
    pieces = []
    for j, cuts in enumerate(column_cuts()):
        at = 0
        for begin, size in cuts:
            if size > 0:
                pieces.append((begin, groups[j][:, at : at + size]))
            at += abs(size)
    pieces.sort(key=lambda item: item[0])
    return jnp.concatenate([piece for _, piece in pieces], axis=1)


def pack_ffn(weight):
    heads, ring = lax.axis_size("head"), ring_of("blk")
    unit = FF // (heads * len(ring))
    cut = weight.reshape(weight.shape[0], 2, heads, len(ring), unit)
    return jnp.stack(
        [
            jnp.concatenate([cut[:, half, j, k] for half in range(2) for k in ring], axis=1)
            for j in range(heads)
        ]
    )


def unpack_ffn(groups):
    heads, ring = lax.axis_size("head"), ring_of("blk")
    rows = groups.shape[1]
    cut = groups.reshape(heads, rows, 2, len(ring), FF // (heads * len(ring)))
    return jnp.concatenate(
        [
            cut[j, :, half, ring.index(k)]
            for half in range(2)
            for j in range(heads)
            for k in range(len(ring))
        ],
        axis=1,
    )


def swap_groups(groups):
    return lax.all_to_all(groups, "head", split_axis=0, concat_axis=0, tiled=True)


def outer_grad(left_side, grad_side):
    return lax.dot_general(
        left_side, grad_side, (((0,), (0,)), ((), ())), preferred_element_type=jnp.float32
    )


def times_transposed(grad_side, weight):
    return lax.dot_general(
        grad_side, weight, (((1,), (1,)), ((), ())), preferred_element_type=jnp.float32
    )


def rotate(values_in, positions, direction):
    half_width = values_in.shape[-1] // 2
    frequencies = rope_base ** (
        -jnp.arange(half_width, dtype=jnp.float32) * 2.0 / values_in.shape[-1]
    )
    angles = positions.astype(jnp.float32)[:, None] * frequencies[None, :]
    cosine = jnp.cos(angles)[:, None, :]
    sine_part = direction * jnp.sin(angles)[:, None, :]
    first_half = values_in[..., :half_width]
    second_half = values_in[..., half_width:]
    return jnp.concatenate(
        [
            first_half * cosine - second_half * sine_part,
            second_half * cosine + first_half * sine_part,
        ],
        axis=-1,
    )


def norm_back(values_in, inverse, gain_vector, grad_side):
    scaled = grad_side * gain_vector
    mean_term = jnp.mean(scaled * values_in, axis=-1, keepdims=True)
    return inverse * scaled - values_in * inverse**3 * mean_term


chunk = 128
lanes = 128
low = jnp.bfloat16
exact = lax.Precision.HIGHEST


def dot_nn(a, b, precision=None):
    return lax.dot_general(
        a, b, (((1,), (0,)), ((), ())), precision=precision, preferred_element_type=jnp.float32
    )


def dot_nt(a, b):
    return lax.dot_general(a, b, (((1,), (1,)), ((), ())), preferred_element_type=jnp.float32)


def dot_tn(a, b):
    return lax.dot_general(a, b, (((0,), (0,)), ((), ())), preferred_element_type=jnp.float32)


def iota(shape, dim):
    return lax.broadcasted_iota(jnp.int32, shape, dim)


def spread(per_head, pair):
    rows = per_head.shape[0]
    first = per_head[:, 2 * pair : 2 * pair + 1]
    second = per_head[:, 2 * pair + 1 : 2 * pair + 2]
    return jnp.where(iota((rows, lanes), 1) < MP, first, second)


def head_sums(products, pair):
    mine = 2 * pair + (iota((lanes, lanes), 0) >= MP).astype(jnp.int32)
    ones = (mine == iota((lanes, lanes), 1)).astype(jnp.float32)
    return dot_nn(products, ones, exact)


def chunk_terms(decay, segment, segment_before):
    lower = iota((chunk, chunk), 0) >= iota((chunk, chunk), 1)
    cumulative = dot_nn(lower.astype(jnp.float32), decay, exact)
    total = cumulative[chunk - 1 :, :]
    segment_end = segment[chunk - 1 :, :]
    related = lower & (segment == segment.T)
    entering = jnp.where(segment == segment_before, jnp.exp(cumulative), 0.0)
    ending = jnp.where(segment == segment_end, jnp.exp(total - cumulative), 0.0)
    whole = jnp.where(segment_end == segment_before, jnp.exp(total), 0.0)
    return cumulative, cumulative.T, related, entering, ending, whole, total, segment_end


def decays_of(cumulative, transposed, related, head):
    apart = cumulative[:, head : head + 1] - transposed[head : head + 1, :]
    return jnp.exp(jnp.where(related, apart, masked_score))


def row_factor(whole, pair, width):
    first = whole[:, 2 * pair : 2 * pair + 1]
    second = whole[:, 2 * pair + 1 : 2 * pair + 2]
    return jnp.where(iota((lanes, width), 0) < MP, first, second)


def chunk_rows(index):
    return pl.ds(pl.multiple_of(index * chunk, chunk), chunk)


def ssd_local(x_ref, b_ref, c_ref, step_ref, decay_ref, seg_ref, y_ref, state_ref, enter_ref, fac_ref):
    pairs = x_ref.shape[1] // lanes
    state_ref[...] = jnp.zeros_like(state_ref)

    def body(index, carry):
        segment_before, base = carry
        rows = chunk_rows(index)
        segment = seg_ref[rows, :]
        cumulative, transposed, related, entering, ending, whole, total, segment_end = chunk_terms(
            decay_ref[rows, :], segment, segment_before
        )
        enter_ref[rows, :] = jnp.where(segment == 0.0, jnp.exp(base + cumulative), 0.0)
        into = b_ref[rows, :].astype(low)
        outof = c_ref[rows, :].astype(low)
        step = step_ref[rows, :]
        scores = dot_nt(outof, into)
        left = iota((chunk, lanes), 1) < MP
        for pair in range(pairs):
            cols = slice(pair * lanes, (pair + 1) * lanes)
            taken = x_ref[rows, cols] * spread(step, pair)
            taken_low = taken.astype(low)
            parts = []
            for head in (2 * pair, 2 * pair + 1):
                weights = decays_of(cumulative, transposed, related, head) * scores
                parts.append(dot_nn(weights.astype(low), taken_low))
            state = state_ref[cols, :]
            y_ref[rows, cols] = jnp.where(left, parts[0], parts[1]) + spread(
                entering, pair
            ) * dot_nt(outof, state.astype(low))
            kept = (taken * spread(ending, pair)).astype(low)
            state_ref[cols, :] = row_factor(whole, pair, state.shape[1]) * state + dot_tn(
                kept, into
            )
        return segment_end, base + total

    start = jnp.zeros((1, lanes), jnp.float32)
    segment_end, base = lax.fori_loop(0, x_ref.shape[0] // chunk, body, (start, start))
    fac_ref[...] = jnp.broadcast_to(
        jnp.where(segment_end == 0.0, jnp.exp(base), 0.0), fac_ref.shape
    )


def ssd_finish(y_ref, enter_ref, c_ref, state_ref, x_ref, z_ref, skip_ref, ssd_ref, out_ref):
    pairs = x_ref.shape[1] // lanes

    def body(index, carry):
        rows = chunk_rows(index)
        outof = c_ref[rows, :].astype(low)
        entering = enter_ref[rows, :]
        for pair in range(pairs):
            cols = slice(pair * lanes, (pair + 1) * lanes)
            ssd = y_ref[rows, cols] + spread(entering, pair) * dot_nt(outof, state_ref[cols, :])
            ssd_ref[rows, cols] = ssd
            gate = z_ref[rows, cols].astype(jnp.float32)
            total = ssd + skip_ref[:, cols] * x_ref[rows, cols]
            out_ref[rows, cols] = (total * gate / (1.0 + jnp.exp(-gate))).astype(low)
        return carry

    lax.fori_loop(0, x_ref.shape[0] // chunk, body, 0)


def ssd_gate_back(
    grad_ref, z_ref, ssd_ref, x_ref, skip_ref, enter_ref, c_ref, dy_ref, dz_ref, dstate_ref, dskip_ref
):
    pairs = x_ref.shape[1] // lanes
    dstate_ref[...] = jnp.zeros_like(dstate_ref)
    dskip_ref[...] = jnp.zeros_like(dskip_ref)

    def body(index, carry):
        rows = chunk_rows(index)
        outof = c_ref[rows, :].astype(low)
        entering = enter_ref[rows, :]
        for pair in range(pairs):
            cols = slice(pair * lanes, (pair + 1) * lanes)
            gate = z_ref[rows, cols].astype(jnp.float32)
            sigmoid = 1.0 / (1.0 + jnp.exp(-gate))
            grad = grad_ref[rows, cols].astype(jnp.float32)
            x = x_ref[rows, cols]
            total = ssd_ref[rows, cols] + skip_ref[:, cols] * x
            dz_ref[rows, cols] = (
                grad * total * sigmoid * (1.0 + gate * (1.0 - sigmoid))
            ).astype(low)
            dy = grad * gate * sigmoid
            dy_ref[rows, cols] = dy
            dskip_ref[:, cols] += jnp.broadcast_to(
                jnp.sum(dy * x, axis=0, keepdims=True), (dskip_ref.shape[0], lanes)
            )
            dstate_ref[cols, :] += dot_tn((dy * spread(entering, pair)).astype(low), outof)
        return carry

    lax.fori_loop(0, x_ref.shape[0] // chunk, body, 0)


def ssd_back(
    x_ref, b_ref, c_ref, step_ref, decay_ref, seg_ref, dy_ref, ssd_ref, skip_ref, state_ref, later_ref,
    dx_ref, db_ref, dc_ref, dstep_ref, ddecay_ref, states, grads,
):
    pairs = x_ref.shape[1] // lanes
    chunks = x_ref.shape[0] // chunk
    zero_row = jnp.zeros((1, lanes), jnp.float32)

    def before(index):
        rows = pl.ds(pl.multiple_of(jnp.maximum(index - 1, 0) * chunk, chunk), chunk)
        return jnp.where(index == 0, 0.0, seg_ref[rows, :][chunk - 1 :, :])

    states[0] = state_ref[...].astype(jnp.float32)

    def forward(index, carry):
        rows = chunk_rows(index)
        _, _, _, _, ending, whole, _, _ = chunk_terms(
            decay_ref[rows, :], seg_ref[rows, :], before(index)
        )
        into = b_ref[rows, :].astype(low)
        step = step_ref[rows, :]
        for pair in range(pairs):
            cols = slice(pair * lanes, (pair + 1) * lanes)
            kept = (x_ref[rows, cols] * spread(step, pair) * spread(ending, pair)).astype(low)
            state = states[index, cols, :]
            states[index + 1, cols, :] = row_factor(
                whole, pair, state.shape[1]
            ) * state + dot_tn(kept, into)
        return carry

    lax.fori_loop(0, chunks, forward, 0)
    grads[...] = later_ref[...].astype(jnp.float32)
    last = jnp.zeros((8, lanes), jnp.float32)
    for pair in range(pairs):
        cols = slice(pair * lanes, (pair + 1) * lanes)
        product = grads[cols, :] * states[chunks, cols, :]
        along = lax.dot_general(
            jnp.ones((8, product.shape[1]), jnp.float32),
            product,
            (((1,), (1,)), ((), ())),
            precision=exact,
            preferred_element_type=jnp.float32,
        )
        last = last + head_sums(along, pair)

    def backward(at, carry):
        index = chunks - 1 - at
        rows = chunk_rows(index)
        cumulative, transposed, related, entering, ending, whole, _, _ = chunk_terms(
            decay_ref[rows, :], seg_ref[rows, :], before(index)
        )
        into = b_ref[rows, :].astype(low)
        outof = c_ref[rows, :].astype(low)
        step = step_ref[rows, :]
        scores = dot_nt(outof, into)
        left = iota((chunk, lanes), 1) < MP
        grad_scores = jnp.zeros((chunk, chunk), jnp.float32)
        grad_into = jnp.zeros((chunk, b_ref.shape[1]), jnp.float32)
        grad_outof = jnp.zeros((chunk, b_ref.shape[1]), jnp.float32)
        grad_cum = jnp.zeros((chunk, lanes), jnp.float32)
        grad_step = jnp.zeros((chunk, lanes), jnp.float32)
        for pair in range(pairs):
            cols = slice(pair * lanes, (pair + 1) * lanes)
            x = x_ref[rows, cols]
            step_pair = spread(step, pair)
            taken = x * step_pair
            taken_low = taken.astype(low)
            dy = dy_ref[rows, cols]
            dy_low = dy.astype(low)
            parts = []
            for half, head in enumerate((2 * pair, 2 * pair + 1)):
                decays = decays_of(cumulative, transposed, related, head)
                parts.append(dot_tn((decays * scores).astype(low), dy_low))
                own = jnp.where(left if half == 0 else ~left, dy_low, jnp.zeros_like(dy_low))
                grad_scores = grad_scores + decays * dot_nt(own, taken_low)
            later = grads[cols, :]
            later_low = later.astype(low)
            ending_pair = spread(ending, pair)
            grad_taken = jnp.where(left, parts[0], parts[1]) + ending_pair * dot_nt(
                into, later_low
            )
            grad_into = grad_into + dot_nn((taken * ending_pair).astype(low), later_low)
            dy_enter = (dy * spread(entering, pair)).astype(low)
            grad_outof = grad_outof + dot_nn(dy_enter, states[index, cols, :].astype(low))
            grads[cols, :] = row_factor(whole, pair, later.shape[1]) * later + dot_tn(
                dy_enter, outof
            )
            grad_cum = grad_cum + head_sums(dy * ssd_ref[rows, cols] - taken * grad_taken, pair)
            grad_step = grad_step + head_sums(x * grad_taken, pair)
            dx_ref[rows, cols] = step_pair * grad_taken + skip_ref[:, cols] * dy
        grad_scores_low = grad_scores.astype(low)
        db_ref[rows, :] = grad_into + dot_tn(grad_scores_low, outof)
        dc_ref[rows, :] = grad_outof + dot_nn(grad_scores_low, into)
        dstep_ref[rows, :] = grad_step
        upper = (iota((chunk, chunk), 0) <= iota((chunk, chunk), 1)).astype(jnp.float32)
        ddecay_ref[rows, :] = dot_nn(upper, grad_cum, exact) + carry
        return carry + jnp.sum(grad_cum, axis=0, keepdims=True)

    lax.fori_loop(0, chunks, backward, last[:1, :] + zero_row)


def attend(place_ref, q_ref, first_ref, k_ref, v_ref, out_ref, lse_ref, top, total, summed):
    away = pl.program_id(0)
    mine, earliest, latest = place_ref[0], place_ref[1], place_ref[2]
    span = q_ref.shape[0]
    heads = q_ref.shape[1] // HD
    key_start = (mine - away) * span

    @pl.when(away == 0)
    def _():
        top[...] = jnp.full_like(top, masked_score)
        total[...] = jnp.zeros_like(total)
        summed[...] = jnp.zeros_like(summed)

    def one(masked):
        keys = k_ref[0]
        values = v_ref[0]
        if masked:
            key_pos = key_start + iota((span, span), 1)
            query_pos = mine * span + iota((span, span), 0)
            visible = (key_pos <= query_pos) & (key_pos >= first_ref[:, :1])
        for head in range(heads):
            cols = slice(head * HD, (head + 1) * HD)
            scores = dot_nt(q_ref[:, cols], keys) * HD**-0.5
            if masked:
                scores = jnp.where(visible, scores, masked_score)
            old_top = top[head][:, :1]
            new_top = jnp.maximum(old_top, jnp.max(scores, axis=1, keepdims=True))
            weights = jnp.exp(scores - new_top)
            scale = jnp.exp(old_top - new_top)
            total[head] = total[head] * scale + jnp.sum(weights, axis=1, keepdims=True)
            top[head] = jnp.broadcast_to(new_top, (span, lanes))
            summed[head] = summed[head] * scale + dot_nn(weights.astype(low), values)

    needed = (away <= mine) & (key_start + span > earliest)
    plain = (away > 0) & (key_start >= latest)
    pl.when(needed & plain)(lambda: one(False))
    pl.when(needed & jnp.logical_not(plain))(lambda: one(True))

    @pl.when(away == pl.num_programs(0) - 1)
    def _():
        for head in range(heads):
            cols = slice(head * HD, (head + 1) * HD)
            out_ref[:, cols] = summed[head] / total[head]
            lse_ref[head] = top[head] + jnp.log(total[head])


def attend_back(
    place_ref, q_ref, first_ref, k_ref, v_ref, grad_ref, out_ref, lse_ref, dq_ref, dk_ref, dv_ref
):
    away = pl.program_id(0)
    mine, earliest, latest = place_ref[0], place_ref[1], place_ref[2]
    span = q_ref.shape[0]
    heads = q_ref.shape[1] // HD
    key_start = (mine - away) * span

    @pl.when(away == 0)
    def _():
        dq_ref[...] = jnp.zeros_like(dq_ref)

    def one(masked):
        keys = k_ref[0]
        values = v_ref[0]
        if masked:
            key_pos = key_start + iota((span, span), 1)
            query_pos = mine * span + iota((span, span), 0)
            visible = (key_pos <= query_pos) & (key_pos >= first_ref[:, :1])
        grad_keys = jnp.zeros(keys.shape, jnp.float32)
        grad_values = jnp.zeros(keys.shape, jnp.float32)
        for head in range(heads):
            cols = slice(head * HD, (head + 1) * HD)
            query = q_ref[:, cols]
            grad = grad_ref[:, cols]
            delta = jnp.sum(
                grad.astype(jnp.float32) * out_ref[:, cols], axis=1, keepdims=True
            )
            scores = dot_nt(query, keys) * HD**-0.5
            if masked:
                scores = jnp.where(visible, scores, masked_score)
            weights = jnp.exp(scores - lse_ref[head][:, :1])
            changes = weights * (dot_nt(grad, values) - delta)
            weights_low = weights.astype(low)
            changes_low = (changes * HD**-0.5).astype(low)
            grad_values = grad_values + dot_tn(weights_low, grad)
            grad_keys = grad_keys + dot_tn(changes_low, query)
            dq_ref[:, cols] += dot_nn(changes_low, keys)
        dk_ref[0] = grad_keys.astype(low)
        dv_ref[0] = grad_values.astype(low)

    needed = (away <= mine) & (key_start + span > earliest)
    plain = (away > 0) & (key_start >= latest)
    pl.when(needed & plain)(lambda: one(False))
    pl.when(needed & jnp.logical_not(plain))(lambda: one(True))

    @pl.when(jnp.logical_not(needed))
    def _():
        dk_ref[...] = jnp.zeros_like(dk_ref)
        dv_ref[...] = jnp.zeros_like(dv_ref)


def shaped(shape, kind):
    return jax.ShapeDtypeStruct(shape, kind)


def whole_call(kernel, outputs, scratch, flops, *operands):
    sizes = sum(math.prod(a.shape) * a.dtype.itemsize for a in (*operands, *outputs))
    return pl.pallas_call(
        kernel,
        out_shape=outputs,
        in_specs=[pl.BlockSpec(memory_space=pltpu.VMEM)] * len(operands),
        out_specs=[pl.BlockSpec(memory_space=pltpu.VMEM)] * len(outputs),
        scratch_shapes=scratch,
        compiler_params=pltpu.CompilerParams(vmem_limit_bytes=kernel_memory),
        cost_estimate=pl.CostEstimate(flops=flops, bytes_accessed=sizes, transcendentals=0),
    )(*operands)


kernel_memory = 44 * 1024 * 1024


def attention(place, query, first_visible, keys, values):
    away, span = keys.shape[0], query.shape[0]
    heads = query.shape[1] // HD
    same = lambda d, place: (0, 0)
    block = lambda d, place: (d, 0, 0)
    return pl.pallas_call(
        attend,
        grid_spec=pltpu.PrefetchScalarGridSpec(
            num_scalar_prefetch=1,
            grid=(away,),
            in_specs=[
                pl.BlockSpec(query.shape, same),
                pl.BlockSpec(first_visible.shape, same),
                pl.BlockSpec((1, span, HD), block),
                pl.BlockSpec((1, span, HD), block),
            ],
            out_specs=[
                pl.BlockSpec(query.shape, same),
                pl.BlockSpec((heads, span, lanes), lambda d, place: (0, 0, 0)),
            ],
            scratch_shapes=[
                pltpu.VMEM((heads, span, lanes), jnp.float32),
                pltpu.VMEM((heads, span, lanes), jnp.float32),
                pltpu.VMEM((heads, span, HD), jnp.float32),
            ],
        ),
        out_shape=[
            shaped(query.shape, jnp.float32),
            shaped((heads, span, lanes), jnp.float32),
        ],
        compiler_params=pltpu.CompilerParams(vmem_limit_bytes=kernel_memory),
        cost_estimate=pl.CostEstimate(
            flops=20 * 10**9, bytes_accessed=4 * 10**6, transcendentals=0
        ),
    )(place, query, first_visible, keys, values)


def attention_back(place, query, first_visible, keys, values, grad, out, lse):
    away, span = keys.shape[0], query.shape[0]
    same = lambda d, place: (0, 0)
    block = lambda d, place: (d, 0, 0)
    return pl.pallas_call(
        attend_back,
        grid_spec=pltpu.PrefetchScalarGridSpec(
            num_scalar_prefetch=1,
            grid=(away,),
            in_specs=[
                pl.BlockSpec(query.shape, same),
                pl.BlockSpec(first_visible.shape, same),
                pl.BlockSpec((1, span, HD), block),
                pl.BlockSpec((1, span, HD), block),
                pl.BlockSpec(query.shape, same),
                pl.BlockSpec(query.shape, same),
                pl.BlockSpec(lse.shape, lambda d, place: (0, 0, 0)),
            ],
            out_specs=[
                pl.BlockSpec(query.shape, same),
                pl.BlockSpec((1, span, HD), block),
                pl.BlockSpec((1, span, HD), block),
            ],
        ),
        out_shape=[
            shaped(query.shape, jnp.float32),
            shaped(keys.shape, low),
            shaped(keys.shape, low),
        ],
        compiler_params=pltpu.CompilerParams(vmem_limit_bytes=kernel_memory),
        cost_estimate=pl.CostEstimate(
            flops=30 * 10**9, bytes_accessed=4 * 10**6, transcendentals=0
        ),
    )(place, query, first_visible, keys, values, grad, out, lse)


def conv_act(extended, conv_taps, conv_shift, keep_masks):
    length = keep_masks[0].shape[0]
    result = conv_shift + conv_taps[0] * extended[KW - 1 :]
    for lag_index in range(1, KW):
        begin = KW - 1 - lag_index
        result = (
            result
            + conv_taps[lag_index]
            * keep_masks[lag_index][:, None]
            * extended[begin : begin + length]
        )
    return jax.nn.silu(result)


def step_and_decay(step_raw, step_shift, decay_rate):
    step_size = jax.nn.softplus(step_raw + step_shift)
    return step_size, -step_size * jnp.exp(decay_rate)


def in_lanes(per_head):
    return jnp.pad(per_head, ((0, 0), (0, lanes - per_head.shape[1])))


def chained(local, factor, backwards):
    blocks = lax.axis_size("blk")
    share = local.shape[0] // blocks
    per_row = jnp.repeat(factor, MP).reshape(blocks, 1, share)
    rough = per_row.astype(low)
    rest = (per_row - rough.astype(jnp.float32)).astype(low)
    extra = jnp.pad(
        jnp.concatenate([rough, rest], axis=1), ((0, 0), (0, 14), (0, local.shape[1] - share))
    )
    sent = jnp.concatenate([local.reshape(blocks, share, -1).astype(low), extra], axis=1)
    got = lax.all_to_all(sent, "blk", split_axis=0, concat_axis=0, tiled=True)
    parts = got[:, :share].astype(jnp.float32)
    factors = (
        got[:, share, :share].astype(jnp.float32) + got[:, share + 1, :share].astype(jnp.float32)
    )[:, :, None]
    state = jnp.zeros_like(parts[0])
    states = [None] * blocks
    for k in range(blocks - 1, -1, -1) if backwards else range(blocks):
        states[k] = state.astype(low)
        state = factors[k] * state + parts[k]
    back = lax.all_to_all(jnp.stack(states), "blk", split_axis=0, concat_axis=0, tiled=True)
    return back.reshape(local.shape)


def summed_over(values_in, axis):
    peers = lax.axis_size(axis)
    by = 1
    while by < peers:
        values_in = values_in + lax.ppermute(values_in, axis, [(i, i ^ by) for i in range(peers)])
        by *= 2
    return values_in


def per_device(
    block_input,
    out_cotangent,
    start_flags,
    in_weight,
    out_weight,
    gate_up_weight,
    down_weight,
    first_gain,
    second_gain,
    conv_weight,
    conv_bias,
    step_bias,
    decay_log,
    skip_gain,
):
    head_count = lax.axis_size("head")
    blocks = lax.axis_size("blk")
    head_index = lax.axis_index("head")
    block_index = lax.axis_index("blk")
    tokens = block_input[0].astype(jnp.float32)
    row_count = tokens.shape[0]
    span_rows = row_count * head_count
    query_group = QH // head_count
    mamba_group = MH // head_count
    mamba_width = MH * MP
    group_query = query_group * HD
    group_inner = mamba_group * MP
    even = head_index % 2 == 0
    out_pairs = mixer_place()

    flags_all = lax.all_gather(start_flags[0], "blk", axis=0, tiled=True)
    packed_in = swap_groups(pack_in(in_weight.astype(low))).reshape(
        head_count * in_weight.shape[0], -1
    )
    conv_columns = group_inner + 2 * NS // head_count + step_pad
    weights_conv = gather_blocks(packed_in[:, :conv_columns])
    weights_rest = gather_blocks(packed_in[:, conv_columns:])
    weights_out = gather_blocks(
        lax.ppermute(out_weight.astype(low), ("head", "blk"), out_pairs)
    )
    weights_ffn = gather_blocks(
        swap_groups(pack_ffn(gate_up_weight.astype(low))).reshape(
            head_count * gate_up_weight.shape[0], -1
        )
    )
    weights_down = gather_blocks(down_weight.astype(low))
    cotangent = out_cotangent[0]
    span_tokens = jnp.concatenate(gather_heads(block_input[0]), axis=0).astype(jnp.float32)
    span_cotangent = jnp.concatenate(gather_heads(cotangent), axis=0)

    positions = block_index * span_rows + jnp.arange(span_rows, dtype=jnp.int32)
    all_positions = jnp.arange(blocks * span_rows, dtype=jnp.int32)
    starts_all = lax.cummax(jnp.where(flags_all > 0, all_positions, 0), axis=0)
    first_visible = lax.dynamic_slice_in_dim(starts_all, block_index * span_rows, span_rows, 0)
    flags_before = jnp.concatenate([jnp.zeros((KW - 2,), jnp.int32), flags_all])
    flag_ext = lax.dynamic_slice_in_dim(
        flags_before, block_index * span_rows, span_rows + KW - 2, 0
    ).astype(jnp.float32)
    segment = jnp.broadcast_to(
        jnp.cumsum(start_flags[0]).astype(jnp.float32)[:, None], (span_rows, lanes)
    )
    place = jnp.stack([block_index, jnp.min(first_visible), jnp.max(first_visible)])
    first_wide = jnp.broadcast_to(first_visible[:, None], (span_rows, lanes))
    keep_masks = [jnp.ones((span_rows,), jnp.float32)]
    for lag_index in range(1, KW):
        begin = KW - 1 - lag_index
        keep_masks.append(keep_masks[-1] * (1.0 - flag_ext[begin : begin + span_rows]))
    conv_taps = jnp.concatenate(
        [
            lax.dynamic_slice_in_dim(conv_weight, head_index * group_inner, group_inner, 1),
            conv_weight[:, mamba_width:],
        ],
        axis=1,
    )
    conv_shift = jnp.concatenate(
        [
            lax.dynamic_slice_in_dim(conv_bias, head_index * group_inner, group_inner, 0),
            conv_bias[mamba_width:],
        ]
    )
    step_shift = lax.dynamic_slice_in_dim(step_bias, head_index * mamba_group, mamba_group, 0)
    decay_rate = lax.dynamic_slice_in_dim(decay_log, head_index * mamba_group, mamba_group, 0)
    skip_local = lax.dynamic_slice_in_dim(skip_gain, head_index * mamba_group, mamba_group, 0)
    skip_wide = jnp.repeat(skip_local, MP)[None, :]

    span_inverse = lax.rsqrt(jnp.mean(span_tokens * span_tokens, axis=-1, keepdims=True) + epsilon)
    normed_one = ring_features((span_tokens * span_inverse * first_gain).astype(low))
    inverse_one = lax.rsqrt(jnp.mean(tokens * tokens, axis=-1, keepdims=True) + epsilon)

    projected = jnp.dot(normed_one, weights_conv, preferred_element_type=jnp.float32)
    cut_b = group_inner
    cut_dt = cut_b + 2 * NS // head_count
    conv_local = jnp.concatenate(
        [projected[:, :cut_b].astype(low)]
        + gather_heads(projected[:, cut_b:cut_dt].astype(low)),
        axis=1,
    )
    step_local = projected[:, cut_dt : cut_dt + mamba_group].astype(low).astype(jnp.float32)
    rim_rows = passed_along(conv_local[span_rows - (KW - 1) :], "blk", 1)
    extended = jnp.concatenate([rim_rows, conv_local], axis=0).astype(jnp.float32)
    active, conv_back = jax.vjp(
        partial(conv_act, keep_masks=keep_masks), extended, conv_taps, conv_shift
    )
    (step_size, log_decay), step_back = jax.vjp(
        step_and_decay, step_local, step_shift, decay_rate
    )
    inner_act = active[:, :group_inner]
    into_act = active[:, group_inner : group_inner + NS]
    outof_act = active[:, group_inner + NS :]
    step_wide = in_lanes(step_size)
    decay_wide = in_lanes(log_decay)
    tall = shaped((span_rows, group_inner), jnp.float32)
    narrow = shaped((span_rows, lanes), jnp.float32)
    state_shape = (group_inner, NS)
    within, local_state, entering, factor = whole_call(
        ssd_local,
        [tall, shaped(state_shape, jnp.float32), narrow, shaped((8, lanes), jnp.float32)],
        [],
        6 * 10**9,
        inner_act,
        into_act,
        outof_act,
        step_wide,
        decay_wide,
        segment,
    )
    span_factor = factor[0, :mamba_group]
    state_in = chained(local_state, span_factor, False)

    cut_kv = group_query
    cut_z = cut_kv + HD
    projected_rest = jnp.dot(normed_one, weights_rest, preferred_element_type=jnp.float32)
    query_local = (
        rotate(
            projected_rest[:, :group_query].reshape(span_rows, query_group, HD), positions, 1.0
        )
        .astype(low)
        .reshape(span_rows, group_query)
    )
    kv_plain = projected_rest[:, cut_kv:cut_z]
    kv_mine = jnp.where(
        even, rotate(kv_plain.reshape(span_rows, 1, HD), positions, 1.0)[:, 0], kv_plain
    ).astype(low)
    gate_act = projected_rest[:, cut_z:].astype(low)
    kv_blocks = jnp.stack([kv_mine] + [passed_along(kv_mine, "blk", d) for d in range(1, blocks)])
    kv_beside = from_head(kv_blocks, 1)
    keys = jnp.where(even, kv_blocks, kv_beside)
    values = jnp.where(even, kv_beside, kv_blocks)
    attended, lse = attention(place, query_local, first_wide, keys, values)

    ssd, mamba_out = whole_call(
        ssd_finish,
        [tall, shaped((span_rows, group_inner), low)],
        [],
        2 * 10**9,
        within,
        entering,
        outof_act,
        state_in,
        inner_act,
        gate_act,
        skip_wide,
    )
    mixer_heads = jnp.concatenate([attended.astype(low), mamba_out], axis=1)
    mixed = jnp.dot(mixer_heads, weights_out, preferred_element_type=jnp.float32)
    hidden_one = tokens + scatter_heads(mixed.reshape(head_count, row_count, -1))
    inverse_two = lax.rsqrt(jnp.mean(hidden_one * hidden_one, axis=-1, keepdims=True) + epsilon)
    normed_two = jnp.concatenate(
        gather_heads(ring_features((hidden_one * inverse_two * second_gain).astype(low))),
        axis=0,
    )
    gate_up = jnp.dot(normed_two, weights_ffn, preferred_element_type=jnp.float32)
    group_units = FF // head_count
    gate_part = gate_up[:, :group_units]
    up_part = gate_up[:, group_units:]
    activated = (jax.nn.silu(gate_part) * up_part).astype(low)
    downed = jnp.dot(activated, weights_down, preferred_element_type=jnp.float32)
    block_output = hidden_one + scatter_heads(downed.reshape(head_count, row_count, -1))
    grad_down = scatter_blocks(outer_grad(activated, span_cotangent).astype(low)).astype(
        jnp.float32
    )
    grad_activated = times_transposed(span_cotangent, weights_down)
    sigmoid_gate = jax.nn.sigmoid(gate_part)
    grad_gate_up = jnp.concatenate(
        [
            grad_activated * up_part * sigmoid_gate * (1.0 + gate_part * (1.0 - sigmoid_gate)),
            grad_activated * jax.nn.silu(gate_part),
        ],
        axis=1,
    ).astype(low)
    grad_ffn = scatter_blocks(outer_grad(normed_two, grad_gate_up).astype(low))
    grad_ffn = unpack_ffn(swap_groups(grad_ffn.reshape(head_count, -1, 2 * group_units))).astype(
        jnp.float32
    )
    grad_normed_two = plain_features(
        scatter_heads(
            times_transposed(grad_gate_up, weights_ffn).reshape(head_count, row_count, -1)
        )
    )
    grad_hidden = cotangent.astype(jnp.float32) + norm_back(
        hidden_one, inverse_two, second_gain, grad_normed_two
    )
    grad_second = jnp.sum(grad_normed_two * hidden_one * inverse_two, axis=0)
    span_grad_hidden = jnp.concatenate(gather_heads(grad_hidden.astype(low)), axis=0)
    grad_mix_weight = lax.ppermute(
        scatter_blocks(outer_grad(mixer_heads, span_grad_hidden).astype(low)),
        ("head", "blk"),
        [(there, here) for here, there in out_pairs],
    ).astype(jnp.float32)
    grad_heads = times_transposed(span_grad_hidden, weights_out).astype(low)

    grad_ssd, grad_gate, grad_state_in, grad_skip_wide = whole_call(
        ssd_gate_back,
        [
            tall,
            shaped((span_rows, group_inner), low),
            shaped(state_shape, jnp.float32),
            shaped((8, group_inner), jnp.float32),
        ],
        [],
        2 * 10**9,
        grad_heads[:, group_query:],
        gate_act,
        ssd,
        inner_act,
        skip_wide,
        entering,
        outof_act,
    )
    grad_skip = grad_skip_wide[0].reshape(mamba_group, MP).sum(axis=1)
    later_grad = chained(grad_state_in, span_factor, True)

    grad_query, grad_keys, grad_values = attention_back(
        place,
        query_local,
        first_wide,
        keys,
        values,
        grad_heads[:, :group_query],
        attended,
        lse,
    )
    kept_kv = jnp.where(even, grad_keys, grad_values)
    given_kv = jnp.where(even, grad_values, grad_keys)
    kv_sums = (kept_kv.astype(jnp.float32) + from_head(given_kv, 1).astype(jnp.float32)).astype(
        low
    )
    grad_kv = kv_sums[0].astype(jnp.float32)
    for d in range(1, blocks):
        grad_kv = grad_kv + passed_along(kv_sums[d], "blk", -d).astype(jnp.float32)
    grad_kv = jnp.where(
        even, rotate(grad_kv.reshape(span_rows, 1, HD), positions, -1.0)[:, 0], grad_kv
    )
    grad_query_seq = rotate(
        grad_query.reshape(span_rows, query_group, HD), positions, -1.0
    ).reshape(span_rows, group_query)
    grad_rest = jnp.concatenate(
        [grad_query_seq.astype(low), grad_kv.astype(low), grad_gate], axis=1
    )
    grad_rest_weight = scatter_blocks(outer_grad(normed_one, grad_rest).astype(low))

    grad_inner, grad_into, grad_outof, grad_step, grad_decay_line = whole_call(
        ssd_back,
        [
            tall,
            shaped((span_rows, NS), jnp.float32),
            shaped((span_rows, NS), jnp.float32),
            narrow,
            narrow,
        ],
        [
            pltpu.VMEM((span_rows // chunk + 1, group_inner, NS), jnp.float32),
            pltpu.VMEM((group_inner, NS), jnp.float32),
        ],
        10 * 10**9,
        inner_act,
        into_act,
        outof_act,
        step_wide,
        decay_wide,
        segment,
        grad_ssd,
        ssd,
        skip_wide,
        state_in,
        later_grad,
    )
    grad_raw, grad_step_shift, grad_rate = step_back(
        (grad_step[:, :mamba_group], grad_decay_line[:, :mamba_group])
    )
    grad_extended, grad_taps, grad_shift = conv_back(
        jnp.concatenate([grad_inner, grad_into, grad_outof], axis=1)
    )
    rim_back = passed_along(grad_extended[: KW - 1], "blk", -1)
    conv_grad = grad_extended[KW - 1 :] + jnp.pad(rim_back, ((span_rows - (KW - 1), 0), (0, 0)))
    grad_bc = conv_grad[:, group_inner:].astype(low).astype(jnp.float32)
    grad_bc = scatter_heads(jnp.stack(jnp.split(grad_bc, head_count, axis=1)))
    grad_conv = jnp.concatenate(
        [
            conv_grad[:, :group_inner],
            grad_bc,
            grad_raw,
            jnp.zeros((span_rows, step_pad - mamba_group), jnp.float32),
        ],
        axis=1,
    ).astype(low)
    grad_conv_in = scatter_blocks(outer_grad(normed_one, grad_conv).astype(low))
    grad_proj_weight = unpack_in(
        jnp.concatenate(
            [
                swap_groups(part.reshape(head_count, in_weight.shape[0], -1))
                for part in (grad_conv_in, grad_rest_weight)
            ],
            axis=2,
        )
    ).astype(jnp.float32)
    grad_normed_one = times_transposed(grad_rest, weights_rest) + times_transposed(
        grad_conv, weights_conv
    )
    grad_normed_one = plain_features(
        scatter_heads(grad_normed_one.reshape(head_count, row_count, -1))
    )
    grad_input = (grad_hidden + norm_back(tokens, inverse_one, first_gain, grad_normed_one)).astype(
        low
    )
    grad_first = jnp.sum(grad_normed_one * tokens * inverse_one, axis=0)

    def own_part(values_in, total):
        return lax.dynamic_update_slice_in_dim(
            jnp.zeros(values_in.shape[:-1] + (total,), jnp.float32),
            values_in,
            head_index * values_in.shape[-1],
            values_in.ndim - 1,
        )

    small = [
        grad_first,
        grad_second,
        jnp.concatenate(
            [own_part(grad_taps[:, :group_inner], mamba_width), grad_taps[:, group_inner:]], axis=1
        ),
        jnp.concatenate(
            [own_part(grad_shift[:group_inner], mamba_width), grad_shift[group_inner:]]
        ),
        own_part(grad_step_shift, MH),
        own_part(grad_rate, MH),
        own_part(grad_skip, MH),
    ]
    line = jnp.concatenate([part.reshape(-1) for part in small])
    line = jnp.pad(line, (0, -line.shape[0] % 1024)).reshape(-1, 128)
    line = summed_over(summed_over(line, "head"), "blk").reshape(-1)
    summed_small = []
    at = 0
    for part in small:
        summed_small.append(line[at : at + part.size].reshape(part.shape))
        at += part.size
    return (
        block_output.astype(low)[None],
        grad_input[None],
        grad_proj_weight,
        grad_mix_weight,
        grad_ffn,
        grad_down,
        *summed_small,
    )


def solution(mesh):
    placed = (
        P("blk", "head", None),
        P("blk", "head", None),
        P("blk", None),
        P(("head", "blk"), None),
        P(("head", "blk"), None),
        P(("head", "blk"), None),
        P(("head", "blk"), None),
        P(),
        P(),
        P(),
        P(),
        P(),
        P(),
        P(),
    )
    return jax.shard_map(
        per_device,
        mesh=mesh,
        in_specs=placed,
        out_specs=(
            P("blk", "head", None),
            P("blk", "head", None),
            P(("head", "blk"), None),
            P(("head", "blk"), None),
            P(("head", "blk"), None),
            P(("head", "blk"), None),
            P(),
            P(),
            P(),
            P(),
            P(),
            P(),
            P(),
        ),
        check_vma=False,
    )
```

time: 1390 us -> 854 us (0.61)
  waiting for transfers between devices: 497 us -> 278 us
  matrix products: 294 us -> 89.1 us
  local copies, waits for them, and re-layouts: 252 us -> 126 us
  starting transfers between devices: 54.5 us -> 123 us
  Pallas kernels: 0 us -> 60.8 us
  other arithmetic: 136 us -> 80.4 us
  loops' own time: 47.3 us -> 0 us
    dot_general x81 -> x2, matrix products: 227 us -> 11.2 us  [the longest x1 5.96 us: per_device(): jnp.dot(normed_one, weights_rest, preferred_element_type=jnp.float32)]
    psum x1 -> x0, waiting for transfers between devices: 109 us -> none  [per_device(): lax.psum((grad_first, grad_second, grad_conv_weight, grad_conv_bias, grad...]
    all_gather x4 -> x5, waiting for transfers between devices: 91.4 us -> 25.7 us  [gather_blocks(): lax.all_gather(shard, 'blk', axis=0, tiled=True, axis_index_groups=[ring_...]
    pallas_call x0 -> x6, Pallas kernels: none -> 60.8 us  [the longest x4 29.3 us: whole_call(): pl.pallas_call(kernel, out_shape=outputs, in_specs=[pl.BlockSpec(memory_s...]
    reduce_scatter x4 -> x5, waiting for transfers between devices: 153 us -> 99.7 us  [scatter_blocks(): lax.psum_scatter(partial_sums, 'blk', scatter_dimension=0, tiled=True, ax...]
    another operation x22 -> x0, loops' own time: 47.3 us -> none  [the longest x2 30.8 us: piece_fn(): return lax.scan(scan_step, carried_state, (stacked, begins))[0]]
    ppermute x3 -> x16, waiting for transfers between devices: 2.58 us -> 49.2 us  [passed_along(): return lax.ppermute(shard, axis, pairs)]
    dynamic_slice x72 -> x0, local copies, waits for them, and re-layouts: 44.7 us -> none  [the longest x48 30.4 us: mamba_output(): lax.map(jax.checkpoint(one_head), (cumulative.T, step_size.T, jnp.transpo...]
  transfers between devices with their start and end apart: 42 -> 62, of which waited for: 25 -> 33; matrix products, arithmetic and copies ran while one was open for 37% -> 28% of each run, Pallas kernels for 0% -> 7%
where the time goes in v2:
time: 854 us; the launch traced here: 840 us
  waiting for transfers between devices  278 us (33%)
  local copies, waits for them, and re-layouts  126 us (15%)
  starting transfers between devices  123 us (14%)
  matrix products  89.1 us (10%)
  other arithmetic  80.4 us (9%)
  blocking collectives  63.9 us (7%)
  Pallas kernels  60.8 us (7%)
  between operations  18.3 us (2%)
    reduce_scatter x5, waiting for transfers between devices, scatter_blocks(): lax.psum_scatter(partial_sums, 'blk', scatter_dimension=0, tiled=True, ax...  99.7 us
    ppermute x22, waiting for transfers between devices, from_head(): lax.ppermute(shard, 'head', [(i, i ^ distance) for i in range(peers)])  80.3 us
    unnamed x500, local copies, waits for them, and re-layouts  74.7 us
    ppermute x16, waiting for transfers between devices, passed_along(): return lax.ppermute(shard, axis, pairs)  49.2 us
    dot_general x5, matrix products, outer_grad(): lax.dot_general(left_side, grad_side, (((0,), (0,)), ((), ())), preferred...  32.7 us
    pallas_call x4, Pallas kernels, whole_call(): pl.pallas_call(kernel, out_shape=outputs, in_specs=[pl.BlockSpec(memory_s...  29.3 us
    ppermute x16, starting transfers between devices, passed_along(): return lax.ppermute(shard, axis, pairs)  28.5 us
    all_to_all x4, starting transfers between devices, swap_groups(): lax.all_to_all(groups, 'head', split_axis=0, concat_axis=0, tiled=True)  26.5 us
  transfers between devices with their start and end apart: 62, of which 33 were waited for; matrix products, arithmetic and copies ran while one was open for 28% of the time, Pallas kernels for 7%

profile of v2, /device:TPU:16, one launch (start us, length us, event | category | flops | bytes accessed | tf_op | source)
XLA Modules:
  0.0 839.6 jit_solution(249426383906668544)
XLA Ops:
  9.7 17.9 %all_to_all.45 = bf16[4,64,2176]{2,1,0:T(8,128)(2,1)S(1)} all-to-all(bf16[4,64,2176]{2,1,0:T(8,128)(2,1)S(1)} %pad_maximum_fusion.15), channel_id=1, replica_groups=mesh['head'=4,'blk'=8] {'head'}, dimensions={0} | all-to-all | bytes 2228224 | tf_op jit(solution)/shard_map/all_to_all | solution.py:201
  30.1 3.3 collective-permute-start.13
  72.1 3.7 all-to-all-start.3
  75.9 24.7 %all-gather = s32[1,4096]{1,0:T(1,128)S(1)} all-gather(s32[1,512]{1,0:T(1,128)S(1)} %copy-done.111), channel_id=2, replica_groups=mesh['head'=4,'blk'=8] {'blk'}, dimensions={1}, use_global_device_ids=true | all-gather | bytes 18432 | tf_op jit(solution)/shard_map/all_gather | solution.py:778
  112.9 5.2 convolution_convert_fusion.6
  128.8 4.2 collective-permute-done.12
  133.3 3.4 fusion.6
  137.0 6.7 shard_map.238
  145.8 6.0 fusion.132
  156.9 5.8 all-to-all-start.1
  162.6 3.4 collective-permute-start.3
  171.5 13.0 %collective-permute-done.3 = bf16[512,128]{1,0:T(8,128)(2,1)S(1)} collective-permute-done((bf16[512,128]{1,0:T(8,128)(2,1)S(1)}, bf16[512,128]{1,0:T(8,128)(2,1)S(1)}, u32[]{:S(2)}, u32[]{:S(2)}) %collective-permute-start.3) | collective-permute-done | bytes 131104 | tf_op jit(solution)/shard_map/ppermute | solution.py:29
  185.8 7.2 collective-permute-done.4
  203.6 21.4 %all-to-all-start.2 = ((bf16[8,96,256]{2,1,0:T(8,128)(2,1)}), bf16[8,96,256]{2,1,0:T(8,128)(2,1)S(1)}, u32[]{:S(2)}, u32[]{:S(2)}) async-start(bf16[8,96,256]{2,1,0:T(8,128)(2,1)} %constant_dynamic-update-slice_fusion.20), calls=%async_computation.2 | async-start | bytes 786432 | tf_op jit(solution)/shard_map/all_to_all | solution.py:734
  244.9 21.5 %shard_map.237 = (f32[512,256]{1,0:T(8,128)S(1)}, f32[2,512,128]{2,1,0:T(8,128)S(1)}) custom-call(s32[3]{0:T(128)S(1)} %pad_add_fusion.4.place_ref, bf16[512,256]{1,0:T(8,128)(2,1)S(1)} %bitcast.803, s32[512,128]{1,0:T(8,128)S(1)} %broadcast_in_dim.20.first_ref, bf16[8,512,128]{2,1,0:T(8,128)(2,1)S(1)} %get-tuple-element.531.k_ref, ...), custom_call_target="tpu_custom_call" | custom-call | flops 20000000000 | bytes 4000000 | tf_op jit(solution)/shard_map/pallas_call | solution.py:623
  268.7 4.9 fusion.23
  277.1 3.6 collective-permute-done.14
  280.7 3.7 slice_add_fusion.8
  290.6 2.6 copy.3660
  293.2 8.4 %collective-permute-done.15 = bf16[128,2048]{0,1:T(8,128)(2,1)} collective-permute-done((bf16[128,2048]{0,1:T(8,128)(2,1)}, bf16[128,2048]{0,1:T(8,128)(2,1)}, u32[]{:S(2)}, u32[]{:S(2)}) %collective-permute-start.15) | collective-permute-done | bytes 524320 | tf_op jit(solution)/shard_map/ppermute | solution.py:57
  306.2 6.6 collective-permute-done.20
  314.0 9.1 %collective-permute-done.16 = bf16[128,2048]{0,1:T(8,128)(2,1)S(1)} collective-permute-done((bf16[128,2048]{0,1:T(8,128)(2,1)S(1)}, bf16[128,2048]{0,1:T(8,128)(2,1)S(1)}, u32[]{:S(2)}, u32[]{:S(2)}) %collective-permute-start.16) | collective-permute-done | bytes 524320 | tf_op jit(solution)/shard_map/ppermute | solution.py:57
  328.4 10.6 %fusion.34 = f32[512,2048]{1,0:T(8,128)} fusion(bf16[2048,2048]{1,0:T(8,128)(2,1)} %all-gather.13.cloned.1.call-done, bf16[128,2048]{0,1:T(8,128)(2,1)} %get-tuple-element.794, bf16[128,2048]{0,1:T(8,128)(2,1)} %get-tuple-element.793, bf16[128,2048]{0,1:T(8,128)(2,1)} %get-tuple-element.792, bf16[128,2048]{0,1:T(8,128)(2,1)} %get-tuple-element.795), kind=kOutput, calls=%fused_computation.386 | convolution fusion | flops 4303355904 | bytes 14680064 | tf_op jit(solution)/shard_map/dot_general | solution.py:919
  339.0 25.6 %all-gather.15.cloned.1.call-done = bf16[1024,2048]{1,0:T(8,128)(2,1)} async-done(((bf16[128,2048]{1,0:T(8,128)(2,1)}), bf16[1024,2048]{1,0:T(8,128)(2,1)}) %all-gather.15.cloned.1.call-update) | async-done | bytes 4194320 | tf_op jit(solution)/shard_map/all_gather | solution.py:40
  364.6 8.5 %multiply_convert_fusion.2 = (bf16[512,1024]{1,0:T(8,128)(2,1)S(1)}, bf16[512,1024]{1,0:T(8,128)(2,1)S(1)}, bf16[512,1024]{1,0:T(8,128)(2,1)}) fusion(f32[512,2048]{1,0:T(8,128)} %fusion.34, bf16[1024,2048]{1,0:T(8,128)(2,1)} %all-gather.15.cloned.1.call-done, bf16[128,2048]{0,1:T(8,128)(2,1)} %get-tuple-element.523, ...), kind=kOutput, calls=%fused_computation.43 | convolution fusion | flops 2163736576 | bytes 13631488 | tf_op jit(solution)/shard_map/dot_general | solution.py:211
  373.2 4.5 fusion.8
  378.3 4.1 collective-permute-done.22
  389.9 10.3 %collective-permute-done.23 = bf16[128,2048]{0,1:T(8,128)(2,1)} collective-permute-done((bf16[128,2048]{0,1:T(8,128)(2,1)}, bf16[128,2048]{0,1:T(8,128)(2,1)}, u32[]{:S(2)}, u32[]{:S(2)}) %collective-permute-start.23) | collective-permute-done | bytes 524320 | tf_op jit(solution)/shard_map/ppermute | solution.py:57
  405.2 11.7 %collective-permute-done.24 = bf16[128,2048]{0,1:T(8,128)(2,1)S(1)} collective-permute-done((bf16[128,2048]{0,1:T(8,128)(2,1)S(1)}, bf16[128,2048]{0,1:T(8,128)(2,1)S(1)}, u32[]{:S(2)}, u32[]{:S(2)}) %collective-permute-start.24) | collective-permute-done | bytes 524320 | tf_op jit(solution)/shard_map/ppermute | solution.py:57
  417.1 2.6 collective-permute-done.25
  431.8 5.1 all-to-all-start.4
  437.4 6.2 convolution_convert_fusion.2
  443.6 4.2 all-to-all-done.4
  450.3 21.4 %all_to_all.46 = bf16[8,96,256]{2,1,0:T(8,128)(2,1)S(1)} all-to-all(bf16[8,96,256]{2,1,0:T(8,128)(2,1)S(1)} %constant_dynamic-update-slice_fusion.132), channel_id=1, replica_groups=mesh['head'=4,'blk'=8] {'blk'}, dimensions={0} | all-to-all | bytes 786432 | tf_op jit(solution)/shard_map/all_to_all | solution.py:734
  471.8 18.6 %shard_map.242 = (f32[512,768]{1,0:T(8,128)S(1)}, f32[512,256]{1,0:T(8,128)S(1)}, f32[512,256]{1,0:T(8,128)S(1)}, f32[512,128]{1,0:T(8,128)S(1)}, f32[512,128]{1,0:T(8,128)S(1)}) custom-call(f32[512,768]{1,0:T(8,128)S(1)} %slice.1697.x_ref, f32[512,256]{1,0:T(8,128)S(1)} %copy-done.9, f32[512,256]{1,0:T(8,128)S(1)} %copy-done.7, f32[512,128]{1,0:T(8,128)S(1)} %copy-done.13, ...), custom_call_target="tpu_custom_call" | custom-call | flops 10000000000 | bytes 10488832 | tf_op jit(solution)/shard_map/pallas_call | solution.py:604
  492.2 3.4 multiply_reduce_fusion.4
  496.6 4.6 collective-permute-start.34
  511.4 5.9 convolution_convert_fusion.4
  518.8 5.7 convolution_convert_fusion.3
  528.0 10.0 %shard_map.240 = (f32[512,256]{1,0:T(8,128)S(1)}, bf16[8,512,128]{2,1,0:T(8,128)(2,1)S(1)}, bf16[8,512,128]{2,1,0:T(8,128)(2,1)S(1)}) custom-call(s32[3]{0:T(128)S(1)} %pad_add_fusion.4.place_ref, bf16[512,256]{1,0:T(8,128)(2,1)S(1)} %bitcast.804, s32[512,128]{1,0:T(8,128)S(1)} %copy-done.21, bf16[8,512,128]{2,1,0:T(8,128)(2,1)S(1)} %copy-done.1, ...), custom_call_target="tpu_custom_call" | custom-call | flops 30000001024 | bytes 4000000 | tf_op jit(solution)/shard_map/pallas_call | solution.py:659
  538.3 2.6 collective-permute-done.26
  541.4 3.5 collective-permute-start.27
  552.2 8.7 %collective-permute-done.28 = bf16[512,128]{1,0:T(8,128)(2,1)} collective-permute-done((bf16[512,128]{1,0:T(8,128)(2,1)S(1)}, bf16[512,128]{1,0:T(8,128)(2,1)}, u32[]{:S(2)}, u32[]{:S(2)}) %collective-permute-start.28) | collective-permute-done | bytes 131104 | tf_op jit(solution)/shard_map/ppermute | solution.py:29
  565.1 11.2 %collective-permute-done.30 = bf16[512,128]{1,0:T(8,128)(2,1)S(1)} collective-permute-done((bf16[512,128]{1,0:T(8,128)(2,1)S(1)}, bf16[512,128]{1,0:T(8,128)(2,1)S(1)}, u32[]{:S(2)}, u32[]{:S(2)}) %collective-permute-start.30) | collective-permute-done | bytes 131104 | tf_op jit(solution)/shard_map/ppermute | solution.py:29
  578.7 6.6 convolution_convert_fusion.1
  586.9 8.3 convolution_convert_fusion
  596.4 4.8 fusion.37
  601.2 4.9 convolution_add_fusion
  608.3 4.6 fusion.133
  623.4 11.6 %collective-permute-done.38 = bf16[128,2048]{0,1:T(8,128)(2,1)S(1)} collective-permute-done((bf16[128,2048]{0,1:T(8,128)(2,1)}, bf16[128,2048]{0,1:T(8,128)(2,1)S(1)}, u32[]{:S(2)}, u32[]{:S(2)}) %collective-permute-start.38) | collective-permute-done | bytes 524320 | tf_op jit(solution)/shard_map/ppermute | solution.py:57
  640.1 3.4 slice_add_fusion.6
  645.2 2.8 collective-permute-start.42
  648.0 2.7 copy.3662
  652.9 4.9 collective-permute-start.43
  657.8 5.0 collective-permute-done.43
  662.8 6.3 collective-permute-start.44
  669.1 4.4 all-to-all-start.6
  673.6 2.9 fusion.25
  683.2 24.7 %reduce-scatter.8.cloned.1.call-done = bf16[256,1152]{1,0:T(8,128)(2,1)} async-done(((bf16[2048,1152]{1,0:T(8,128)(2,1)}), bf16[256,1152]{1,0:T(8,128)(2,1)}) %reduce-scatter.8.cloned.1.call-update) | async-done | bytes 589840 | tf_op jit(solution)/shard_map/reduce_scatter | solution.py:46
  707.9 14.9 %all-to-all-start.7 = ((bf16[4,64,1152]{2,1,0:T(8,128)(2,1)}), bf16[4,64,1152]{2,1,0:T(8,128)(2,1)S(1)}, u32[]{:S(2)}, u32[]{:S(2)}) async-start(bf16[4,64,1152]{2,1,0:T(8,128)(2,1)} %bitcast.928), calls=%async_computation.9 | async-start | bytes 1179648 | tf_op jit(solution)/shard_map/all_to_all | solution.py:201
  726.8 5.5 all-to-all-done.7
  734.4 75.0 %reduce-scatter.12.cloned.1.call-done = bf16[256,2048]{1,0:T(8,128)(2,1)} async-done(((bf16[2048,2048]{1,0:T(8,128)(2,1)}), bf16[256,2048]{1,0:T(8,128)(2,1)}) %reduce-scatter.12.cloned.1.call-update) | async-done | bytes 1048592 | tf_op jit(solution)/shard_map/reduce_scatter | solution.py:46
  809.4 3.5 all-to-all-start.8
  820.0 7.4 all-to-all-done.8
  (853 shorter events, 242.0 us)
Async XLA Ops:
  7.2 105.7 %all-gather.9.cloned.1.call-start = ((), (), s32[]{:S(2)}) async-start(), calls=%async_computation.15 | async-start | bytes 4718592 | tf_op jit(solution)/shard_map/all_gather | solution.py:40
  28.5 117.4 %all-gather.7.cloned.1.call-start = ((), (), s32[]{:S(2)}) async-start(), calls=%async_computation.14 | async-start | bytes 5308416 | tf_op jit(solution)/shard_map/all_gather | solution.py:40
  28.8 72.4 %collective-permute-start = (bf16[128,2048]{0,1:T(8,128)(2,1)S(1)}, bf16[128,2048]{0,1:T(8,128)(2,1)S(1)}, u32[]{:S(2)}, u32[]{:S(2)}) collective-permute-start(bf16[128,2048]{0,1:T(8,128)(2,1)S(1)} %bitcast.805), channel_id=1, source_target_pairs={{0,16},{8,24},{16,0},{24,8},{1,17},{9,25},{17,1},{25,9},{2,18},{10... | collective-permute-start | bytes 1572872 | tf_op jit(solution)/shard_map/ppermute | solution.py:57
  30.1 36.9 %collective-permute-start.13 = (bf16[128,2048]{1,0:T(8,128)(2,1)}, bf16[128,2048]{1,0:T(8,128)(2,1)S(1)}, u32[]{:S(2)}, u32[]{:S(2)}) collective-permute-start(bf16[128,2048]{1,0:T(8,128)(2,1)} %convert_element_type.380), channel_id=1, source_target_pairs={{0,0},{1,2},{2,8},{3,10},{4,16},{5,18},{6,24},{7,26},{8,4},{9,6},{... | collective-permute-start | bytes 1572872 | tf_op jit(solution)/shard_map/ppermute | solution.py:786
  41.6 227.2 %all-gather.11.cloned.1.call-start = ((), (), s32[]{:S(2)}) async-start(), calls=%async_computation.16 | async-start | bytes 4718592 | tf_op jit(solution)/shard_map/all_gather | solution.py:40
  72.1 49.5 %all-to-all-start.3 = ((bf16[4,64,2048]{2,1,0:T(8,128)(2,1)}), bf16[4,64,2048]{2,1,0:T(8,128)(2,1)S(1)}, u32[]{:S(2)}, u32[]{:S(2)}) async-start(bf16[4,64,2048]{2,1,0:T(8,128)(2,1)} %pad_maximum_fusion.19), calls=%async_computation.3 | async-start | bytes 2097152 | tf_op jit(solution)/shard_map/all_to_all | solution.py:201
  75.8 252.6 %all-gather.13.cloned.1.call-start = ((), (), s32[]{:S(2)}) async-start(), calls=%async_computation.17 | async-start | bytes 9437184 | tf_op jit(solution)/shard_map/all_gather | solution.py:40
  101.0 125.4 %copy-start.101 = (f32[512]{0:T(512)}, f32[512]{0:T(512)S(1)}, u32[]{:S(2)}) copy-start(f32[512]{0:T(512)S(1)} %add_convert_fusion.3) | copy-start | bytes 6148
  102.2 2.9 collective-permute-start.1
  102.3 124.1 %copy-start.115 = (f32[64]{0:T(128)}, f32[64]{0:T(128)S(1)}, u32[]{:S(2)}) copy-start(f32[64]{0:T(128)S(1)} %multiply_power_fusion) | copy-start | bytes 772
  118.2 6.2 collective-permute-start.10
  124.4 1.6 collective-permute-start.11
  126.3 6.7 collective-permute-start.12
  153.8 16.3 %collective-permute-start.2 = (bf16[512,128]{1,0:T(8,128)(2,1)S(1)}, bf16[512,128]{1,0:T(8,128)(2,1)S(1)}, u32[]{:S(2)}, u32[]{:S(2)}) collective-permute-start(bf16[512,128]{1,0:T(8,128)(2,1)S(1)} %get-tuple-element.481), channel_id=1, source_target_pairs={{0,1},{1,2},{2,3},{3,4},{4,5},{5,6},{6,7},{8,9},{9,10},{10,11},{11... | collective-permute-start | bytes 393224 | tf_op jit(solution)/shard_map/ppermute | solution.py:29
  156.9 41.7 %all-to-all-start.1 = ((bf16[8,112,256]{2,1,0:T(8,128)(2,1)}), bf16[8,112,256]{2,1,0:T(8,128)(2,1)S(1)}, u32[]{:S(2)}, u32[]{:S(2)}) async-start(bf16[8,112,256]{2,1,0:T(8,128)(2,1)} %pad_maximum_fusion.26), calls=%async_computation.1 | async-start | bytes 917504 | tf_op jit(solution)/shard_map/all_to_all | solution.py:724
  162.6 21.9 %collective-permute-start.3 = (bf16[512,128]{1,0:T(8,128)(2,1)S(1)}, bf16[512,128]{1,0:T(8,128)(2,1)S(1)}, u32[]{:S(2)}, u32[]{:S(2)}) collective-permute-start(bf16[512,128]{1,0:T(8,128)(2,1)S(1)} %get-tuple-element.481), channel_id=1, source_target_pairs={{0,2},{1,3},{2,4},{3,5},{4,6},{5,7},{8,10},{9,11},{10,12},{11,13},... | collective-permute-start | bytes 393224 | tf_op jit(solution)/shard_map/ppermute | solution.py:29
  166.0 27.0 %collective-permute-start.4 = (bf16[512,128]{1,0:T(8,128)(2,1)S(1)}, bf16[512,128]{1,0:T(8,128)(2,1)S(1)}, u32[]{:S(2)}, u32[]{:S(2)}) collective-permute-start(bf16[512,128]{1,0:T(8,128)(2,1)S(1)} %get-tuple-element.481), channel_id=1, source_target_pairs={{0,3},{1,4},{2,5},{3,6},{4,7},{8,11},{9,12},{10,13},{11,14},{12,15... | collective-permute-start | bytes 393224 | tf_op jit(solution)/shard_map/ppermute | solution.py:29
  168.2 27.7 %collective-permute-start.5 = (bf16[512,128]{1,0:T(8,128)(2,1)S(1)}, bf16[512,128]{1,0:T(8,128)(2,1)S(1)}, u32[]{:S(2)}, u32[]{:S(2)}) collective-permute-start(bf16[512,128]{1,0:T(8,128)(2,1)S(1)} %get-tuple-element.481), channel_id=1, source_target_pairs={{0,4},{1,5},{2,6},{3,7},{8,12},{9,13},{10,14},{11,15},{16,20},{17,... | collective-permute-start | bytes 393224 | tf_op jit(solution)/shard_map/ppermute | solution.py:29
  169.5 27.1 %collective-permute-start.6 = (bf16[512,128]{1,0:T(8,128)(2,1)S(1)}, bf16[512,128]{1,0:T(8,128)(2,1)S(1)}, u32[]{:S(2)}, u32[]{:S(2)}) collective-permute-start(bf16[512,128]{1,0:T(8,128)(2,1)S(1)} %get-tuple-element.481), channel_id=1, source_target_pairs={{0,5},{1,6},{2,7},{8,13},{9,14},{10,15},{16,21},{17,22},{18,23},{2... | collective-permute-start | bytes 393224 | tf_op jit(solution)/shard_map/ppermute | solution.py:29
  170.2 27.1 %collective-permute-start.7 = (bf16[512,128]{1,0:T(8,128)(2,1)S(1)}, bf16[512,128]{1,0:T(8,128)(2,1)S(1)}, u32[]{:S(2)}, u32[]{:S(2)}) collective-permute-start(bf16[512,128]{1,0:T(8,128)(2,1)S(1)} %get-tuple-element.481), channel_id=1, source_target_pairs={{0,6},{1,7},{8,14},{9,15},{16,22},{17,23},{24,30},{25,31}} | collective-permute-start | bytes 393224 | tf_op jit(solution)/shard_map/ppermute | solution.py:29
  184.5 13.4 %collective-permute-start.8 = (bf16[512,128]{1,0:T(8,128)(2,1)S(1)}, bf16[512,128]{1,0:T(8,128)(2,1)S(1)}, u32[]{:S(2)}, u32[]{:S(2)}) collective-permute-start(bf16[512,128]{1,0:T(8,128)(2,1)S(1)} %get-tuple-element.481), channel_id=1, source_target_pairs={{0,7},{8,15},{16,23},{24,31}} | collective-permute-start | bytes 393224 | tf_op jit(solution)/shard_map/ppermute | solution.py:29
  198.6 44.1 %collective-permute-start.9 = (bf16[8,512,128]{2,1,0:T(8,128)(2,1)}, bf16[8,512,128]{2,1,0:T(8,128)(2,1)}, u32[]{:S(2)}, u32[]{:S(2)}) collective-permute-start(bf16[8,512,128]{2,1,0:T(8,128)(2,1)} %constant_dynamic-update-slice_fusion.8), channel_id=1, source_target_pairs={{0,8},{8,0},{16,24},{24,16},{1,9},{9,1},{17,25},{25,17},{2,10},{10... | collective-permute-start | bytes 3145736 | tf_op jit(solution)/shard_map/ppermute | solution.py:57
  203.6 33.9 %all-to-all-start.2 = ((bf16[8,96,256]{2,1,0:T(8,128)(2,1)}), bf16[8,96,256]{2,1,0:T(8,128)(2,1)S(1)}, u32[]{:S(2)}, u32[]{:S(2)}) async-start(bf16[8,96,256]{2,1,0:T(8,128)(2,1)} %constant_dynamic-update-slice_fusion.20), calls=%async_computation.2 | async-start | bytes 786432 | tf_op jit(solution)/shard_map/all_to_all | solution.py:734
  225.0 139.6 %all-gather.15.cloned.1.call-start = ((), (), s32[]{:S(2)}) async-start(), calls=%async_computation.18 | async-start | bytes 4718592 | tf_op jit(solution)/shard_map/all_gather | solution.py:40
  276.2 4.5 collective-permute-start.14
  286.5 15.1 %collective-permute-start.15 = (bf16[128,2048]{0,1:T(8,128)(2,1)}, bf16[128,2048]{0,1:T(8,128)(2,1)}, u32[]{:S(2)}, u32[]{:S(2)}) collective-permute-start(bf16[128,2048]{0,1:T(8,128)(2,1)} %bitcast.930), channel_id=1, source_target_pairs={{0,16},{8,24},{16,0},{24,8},{1,17},{9,25},{17,1},{25,9},{2,18},{10... | collective-permute-start | bytes 1572872 | tf_op jit(solution)/shard_map/ppermute | solution.py:57
  290.2 22.6 %collective-permute-start.20 = (bf16[128,2048]{0,1:T(8,128)(2,1)}, bf16[128,2048]{0,1:T(8,128)(2,1)}, u32[]{:S(2)}, u32[]{:S(2)}) collective-permute-start(bf16[128,2048]{0,1:T(8,128)(2,1)} %bitcast.806), channel_id=1, source_target_pairs={{0,16},{8,24},{16,0},{24,8},{1,17},{9,25},{17,1},{25,9},{2,18},{10... | collective-permute-start | bytes 1572872 | tf_op jit(solution)/shard_map/ppermute | solution.py:57
  304.5 18.7 %collective-permute-start.16 = (bf16[128,2048]{0,1:T(8,128)(2,1)S(1)}, bf16[128,2048]{0,1:T(8,128)(2,1)S(1)}, u32[]{:S(2)}, u32[]{:S(2)}) collective-permute-start(bf16[128,2048]{0,1:T(8,128)(2,1)S(1)} %constant_dynamic-update-slice_fusion.28), channel_id=1, source_target_pairs={{0,16},{8,24},{16,0},{24,8},{1,17},{9,25},{17,1},{25,9},{2,18},{10... | collective-permute-start | bytes 1572872 | tf_op jit(solution)/shard_map/ppermute | solution.py:57
  314.0 9.4 %collective-permute-start.21 = (bf16[2,128,2048]{1,2,0:T(8,128)(2,1)S(1)}, bf16[2,128,2048]{1,2,0:T(8,128)(2,1)S(1)}, u32[]{:S(2)}, u32[]{:S(2)}) collective-permute-start(bf16[2,128,2048]{1,2,0:T(8,128)(2,1)S(1)} %pad_maximum_fusion.20), channel_id=1, source_target_pairs={{0,8},{8,0},{16,24},{24,16},{1,9},{9,1},{17,25},{25,17},{2,10},{10... | collective-permute-start | bytes 3145736 | tf_op jit(solution)/shard_map/ppermute | solution.py:57
  323.2 2.7 collective-permute-start.17
  378.2 4.2 collective-permute-start.22
  385.9 14.3 %collective-permute-start.23 = (bf16[128,2048]{0,1:T(8,128)(2,1)}, bf16[128,2048]{0,1:T(8,128)(2,1)}, u32[]{:S(2)}, u32[]{:S(2)}) collective-permute-start(bf16[128,2048]{0,1:T(8,128)(2,1)} %bitcast.931), channel_id=1, source_target_pairs={{0,16},{8,24},{16,0},{24,8},{1,17},{9,25},{17,1},{25,9},{2,18},{10... | collective-permute-start | bytes 1572872 | tf_op jit(solution)/shard_map/ppermute | solution.py:57
  403.7 13.2 %collective-permute-start.24 = (bf16[128,2048]{0,1:T(8,128)(2,1)S(1)}, bf16[128,2048]{0,1:T(8,128)(2,1)S(1)}, u32[]{:S(2)}, u32[]{:S(2)}) collective-permute-start(bf16[128,2048]{0,1:T(8,128)(2,1)S(1)} %fusion.95), channel_id=1, source_target_pairs={{0,16},{8,24},{16,0},{24,8},{1,17},{9,25},{17,1},{25,9},{2,18},{10... | collective-permute-start | bytes 1572872 | tf_op jit(solution)/shard_map/ppermute | solution.py:57
  417.0 2.7 collective-permute-start.25
  431.8 16.0 %all-to-all-start.4 = ((bf16[8,112,256]{2,1,0:T(8,128)(2,1)}), bf16[8,112,256]{2,1,0:T(8,128)(2,1)}, u32[]{:S(2)}, u32[]{:S(2)}) async-start(bf16[8,112,256]{2,1,0:T(8,128)(2,1)} %pad_maximum_fusion.25), calls=%async_computation.4 | async-start | bytes 917504 | tf_op jit(solution)/shard_map/all_to_all | solution.py:724
  436.9 213.8 %reduce-scatter.14.cloned.1.call-start = ((), (), s32[]{:S(2)}) async-start(), calls=%async_computation.23 | async-start | bytes 4718592 | tf_op jit(solution)/shard_map/reduce_scatter | solution.py:46
  443.6 225.5 %reduce-scatter.6.cloned.1.call-start = ((), (), s32[]{:S(2)}) async-start(), calls=%async_computation.19 | async-start | bytes 4718592 | tf_op jit(solution)/shard_map/reduce_scatter | solution.py:46
  496.6 5.9 collective-permute-start.34
  503.1 2.0 collective-permute-start.35
  505.1 5.6 collective-permute-start.36
  517.3 163.2 %reduce-scatter.10.cloned.1.call-start = ((), (), s32[]{:S(2)}) async-start(), calls=%async_computation.21 | async-start | bytes 4718592 | tf_op jit(solution)/shard_map/reduce_scatter | solution.py:46
  524.5 183.4 %reduce-scatter.8.cloned.1.call-start = ((), (), s32[]{:S(2)}) async-start(), calls=%async_computation.20 | async-start | bytes 5308416 | tf_op jit(solution)/shard_map/reduce_scatter | solution.py:46
  538.2 2.7 collective-permute-start.26
  541.4 10.1 %collective-permute-start.27 = (bf16[512,128]{1,0:T(8,128)(2,1)S(1)}, bf16[512,128]{1,0:T(8,128)(2,1)}, u32[]{:S(2)}, u32[]{:S(2)}) collective-permute-start(bf16[512,128]{1,0:T(8,128)(2,1)S(1)} %get-tuple-element.643), channel_id=1, source_target_pairs={{1,0},{2,1},{3,2},{4,3},{5,4},{6,5},{7,6},{9,8},{10,9},{11,10},{12... | collective-permute-start | bytes 393224 | tf_op jit(solution)/shard_map/ppermute | solution.py:29
  544.9 16.0 %collective-permute-start.28 = (bf16[512,128]{1,0:T(8,128)(2,1)S(1)}, bf16[512,128]{1,0:T(8,128)(2,1)}, u32[]{:S(2)}, u32[]{:S(2)}) collective-permute-start(bf16[512,128]{1,0:T(8,128)(2,1)S(1)} %get-tuple-element.649), channel_id=1, source_target_pairs={{2,0},{3,1},{4,2},{5,3},{6,4},{7,5},{10,8},{11,9},{12,10},{13,11},... | collective-permute-start | bytes 393224 | tf_op jit(solution)/shard_map/ppermute | solution.py:29
  547.1 18.0 %collective-permute-start.29 = (bf16[512,128]{1,0:T(8,128)(2,1)S(1)}, bf16[512,128]{1,0:T(8,128)(2,1)S(1)}, u32[]{:S(2)}, u32[]{:S(2)}) collective-permute-start(bf16[512,128]{1,0:T(8,128)(2,1)S(1)} %get-tuple-element.648), channel_id=1, source_target_pairs={{3,0},{4,1},{5,2},{6,3},{7,4},{11,8},{12,9},{13,10},{14,11},{15,12... | collective-permute-start | bytes 393224 | tf_op jit(solution)/shard_map/ppermute | solution.py:29
  549.0 27.2 %collective-permute-start.30 = (bf16[512,128]{1,0:T(8,128)(2,1)S(1)}, bf16[512,128]{1,0:T(8,128)(2,1)S(1)}, u32[]{:S(2)}, u32[]{:S(2)}) collective-permute-start(bf16[512,128]{1,0:T(8,128)(2,1)S(1)} %get-tuple-element.647), channel_id=1, source_target_pairs={{4,0},{5,1},{6,2},{7,3},{12,8},{13,9},{14,10},{15,11},{20,16},{21,... | collective-permute-start | bytes 393224 | tf_op jit(solution)/shard_map/ppermute | solution.py:29
  550.3 25.9 %collective-permute-start.31 = (bf16[512,128]{1,0:T(8,128)(2,1)S(1)}, bf16[512,128]{1,0:T(8,128)(2,1)S(1)}, u32[]{:S(2)}, u32[]{:S(2)}) collective-permute-start(bf16[512,128]{1,0:T(8,128)(2,1)S(1)} %get-tuple-element.646), channel_id=1, source_target_pairs={{5,0},{6,1},{7,2},{13,8},{14,9},{15,10},{21,16},{22,17},{23,18},{2... | collective-permute-start | bytes 393224 | tf_op jit(solution)/shard_map/ppermute | solution.py:29
  551.6 24.7 %collective-permute-start.32 = (bf16[512,128]{1,0:T(8,128)(2,1)S(1)}, bf16[512,128]{1,0:T(8,128)(2,1)S(1)}, u32[]{:S(2)}, u32[]{:S(2)}) collective-permute-start(bf16[512,128]{1,0:T(8,128)(2,1)S(1)} %get-tuple-element.645), channel_id=1, source_target_pairs={{6,0},{7,1},{14,8},{15,9},{22,16},{23,17},{30,24},{31,25}} | collective-permute-start | bytes 393224 | tf_op jit(solution)/shard_map/ppermute | solution.py:29
  560.9 15.3 %collective-permute-start.33 = (bf16[512,128]{1,0:T(8,128)(2,1)S(1)}, bf16[512,128]{1,0:T(8,128)(2,1)S(1)}, u32[]{:S(2)}, u32[]{:S(2)}) collective-permute-start(bf16[512,128]{1,0:T(8,128)(2,1)S(1)} %get-tuple-element.644), channel_id=1, source_target_pairs={{7,0},{15,8},{23,16},{31,24}} | collective-permute-start | bytes 393224 | tf_op jit(solution)/shard_map/ppermute | solution.py:29
  585.3 224.0 %reduce-scatter.12.cloned.1.call-start = ((), (), s32[]{:S(2)}) async-start(), calls=%async_computation.22 | async-start | bytes 9437184 | tf_op jit(solution)/shard_map/reduce_scatter | solution.py:46
  608.0 9.2 %collective-permute-start.37 = (f32[2,128,2048]{2,1,0:T(8,128)S(1)}, f32[2,128,2048]{2,1,0:T(8,128)}, u32[]{:S(2)}, u32[]{:S(2)}) collective-permute-start(f32[2,128,2048]{2,1,0:T(8,128)S(1)} %pad_maximum_fusion.11), channel_id=1, source_target_pairs={{0,8},{8,0},{16,24},{24,16},{1,9},{9,1},{17,25},{25,17},{2,10},{10... | collective-permute-start | bytes 6291464 | tf_op jit(solution)/shard_map/ppermute | solution.py:57
  615.6 24.6 %collective-permute-start.18 = (f32[2,128,2048]{2,1,0:T(8,128)}, f32[2,128,2048]{2,1,0:T(8,128)}, u32[]{:S(2)}, u32[]{:S(2)}) collective-permute-start(f32[2,128,2048]{2,1,0:T(8,128)} %pad_maximum_fusion.4), channel_id=1, source_target_pairs={{0,8},{8,0},{16,24},{24,16},{1,9},{9,1},{17,25},{25,17},{2,10},{10... | collective-permute-start | bytes 6291464 | tf_op jit(solution)/shard_map/ppermute | solution.py:57
  620.7 14.3 %collective-permute-start.38 = (bf16[128,2048]{0,1:T(8,128)(2,1)}, bf16[128,2048]{0,1:T(8,128)(2,1)S(1)}, u32[]{:S(2)}, u32[]{:S(2)}) collective-permute-start(bf16[128,2048]{0,1:T(8,128)(2,1)} %bitcast.159), channel_id=1, source_target_pairs={{0,16},{8,24},{16,0},{24,8},{1,17},{9,25},{17,1},{25,9},{2,18},{10... | collective-permute-start | bytes 1572872 | tf_op jit(solution)/shard_map/ppermute | solution.py:57
  637.2 1.4 collective-permute-start.40
  638.6 6.5 collective-permute-start.41
  644.6 29.0 %collective-permute-start.19 = (bf16[128,2048]{0,1:T(8,128)(2,1)}, bf16[128,2048]{0,1:T(8,128)(2,1)}, u32[]{:S(2)}, u32[]{:S(2)}) collective-permute-start(bf16[128,2048]{0,1:T(8,128)(2,1)} %bitcast.82), channel_id=1, source_target_pairs={{0,16},{8,24},{16,0},{24,8},{1,17},{9,25},{17,1},{25,9},{2,18},{10... | collective-permute-start | bytes 1572872 | tf_op jit(solution)/shard_map/ppermute | solution.py:57
  645.2 7.7 collective-permute-start.42
  652.9 9.9 %collective-permute-start.43 = (f32[176,128]{1,0:T(8,128)S(1)}, f32[176,128]{1,0:T(8,128)S(1)}, u32[]{:S(2)}, u32[]{:S(2)}) collective-permute-start(f32[176,128]{1,0:T(8,128)S(1)} %add.524), channel_id=1, source_target_pairs={{0,2},{1,3},{2,0},{3,1},{4,6},{5,7},{6,4},{7,5},{8,10},{9,11},{10,... | collective-permute-start | bytes 270344 | tf_op jit(solution)/shard_map/ppermute | solution.py:742
  662.8 17.7 %collective-permute-start.44 = (f32[176,128]{1,0:T(8,128)S(1)}, f32[176,128]{1,0:T(8,128)S(1)}, u32[]{:S(2)}, u32[]{:S(2)}) collective-permute-start(f32[176,128]{1,0:T(8,128)S(1)} %add.525), channel_id=1, source_target_pairs={{0,4},{1,5},{2,6},{3,7},{4,0},{5,1},{6,2},{7,3},{8,12},{9,13},{10,... | collective-permute-start | bytes 270344 | tf_op jit(solution)/shard_map/ppermute | solution.py:742
  669.1 38.8 %all-to-all-start.6 = ((bf16[4,64,1024]{2,1,0:T(8,128)(2,1)}), bf16[4,64,1024]{2,1,0:T(8,128)(2,1)}, u32[]{:S(2)}, u32[]{:S(2)}) async-start(bf16[4,64,1024]{2,1,0:T(8,128)(2,1)} %bitcast.929), calls=%async_computation.7 | async-start | bytes 1048576 | tf_op jit(solution)/shard_map/all_to_all | solution.py:201
  680.6 44.1 %collective-permute-start.39 = (bf16[128,2048]{1,0:T(8,128)(2,1)}, bf16[128,2048]{1,0:T(8,128)(2,1)S(1)}, u32[]{:S(2)}, u32[]{:S(2)}) collective-permute-start(bf16[128,2048]{1,0:T(8,128)(2,1)} %reduce-scatter.10.cloned.1.call-done), channel_id=1, source_target_pairs={{0,0},{2,1},{8,2},{10,3},{16,4},{18,5},{24,6},{26,7},{4,8},{6,9},{... | collective-permute-start | bytes 1572872 | tf_op jit(solution)/shard_map/ppermute | solution.py:952
  707.9 24.5 %all-to-all-start.7 = ((bf16[4,64,1152]{2,1,0:T(8,128)(2,1)}), bf16[4,64,1152]{2,1,0:T(8,128)(2,1)S(1)}, u32[]{:S(2)}, u32[]{:S(2)}) async-start(bf16[4,64,1152]{2,1,0:T(8,128)(2,1)} %bitcast.928), calls=%async_computation.9 | async-start | bytes 1179648 | tf_op jit(solution)/shard_map/all_to_all | solution.py:201
  809.4 18.0 %all-to-all-start.8 = ((bf16[4,64,2048]{2,1,0:T(8,128)(2,1)}), bf16[4,64,2048]{2,1,0:T(8,128)(2,1)S(1)}, u32[]{:S(2)}, u32[]{:S(2)}) async-start(bf16[4,64,2048]{2,1,0:T(8,128)(2,1)} %bitcast.927), calls=%async_computation.12 | async-start | bytes 2097152 | tf_op jit(solution)/shard_map/all_to_all | solution.py:201
  (139 other events, 1559.8 us)
Sparse Core Ops, SparseCore 0:
  28.6 61.7 all-gather.8
  92.0 52.5 all-gather.6
  146.1 79.5 all-gather.10
  227.6 87.1 all-gather.12
  316.2 48.4 all-gather.14
  443.7 56.7 reduce-scatter.13
  517.5 69.7 reduce-scatter.5
  589.6 49.3 reduce-scatter.9
  641.3 66.6 reduce-scatter.7
  710.0 99.2 reduce-scatter.11

commit v3 on v2

v3 whole, which is shorter than its diff:
```python
import math
from functools import partial

import jax
import jax.numpy as jnp
from jax import lax
from jax.experimental import pallas as pl
from jax.experimental.pallas import tpu as pltpu
from jax.sharding import PartitionSpec as P

D = 2048
QH = 8
KVH = 2
HD = 128
MH = 48
MP = 64
NS = 256
FF = 4096
KW = 4


epsilon = 1e-05
rope_base = 100000000000.0
masked_score = -1e30


def after(value, *others):
    return lax.optimization_barrier((value, *others))[0]


def passed_along(shard, axis, by):
    peers = lax.axis_size(axis)
    pairs = [(i, i + by) for i in range(peers) if 0 <= i + by < peers]
    return lax.ppermute(shard, axis, pairs)


def ring_of(axis):
    peers = lax.axis_size(axis)
    if peers != 8:
        return list(range(peers))
    return [0, 2, 4, 6, 7, 5, 3, 1]


def gather_blocks(shard):
    return lax.all_gather(shard, "blk", axis=0, tiled=True, axis_index_groups=[ring_of("blk")])


def scatter_blocks(partial_sums):
    return lax.psum_scatter(
        partial_sums,
        "blk",
        scatter_dimension=0,
        tiled=True,
        axis_index_groups=[ring_of("blk")],
    )


def from_head(shard, distance):
    peers = lax.axis_size("head")
    return lax.ppermute(shard, "head", [(i, i ^ distance) for i in range(peers)])


def gather_heads(shard):
    across = from_head(shard, 2)
    return [shard, across, from_head(shard, 1), from_head(across, 1)]


def in_head_order(parts):
    mine = lax.axis_index("head")
    stacked = jnp.stack([parts[0], parts[2], parts[1], parts[3]])
    return [
        lax.dynamic_index_in_dim(stacked, jnp.bitwise_xor(mine, j), 0, False) for j in range(4)
    ]


def scatter_pairs(own, other, middle=jnp.float32):
    rows = own.shape[0] // 2
    got = from_head(other.astype(middle), 1).astype(jnp.float32)
    far = from_head((own[rows:] + got[rows:]).astype(low), 2)
    return own[:rows] + got[:rows] + far.astype(jnp.float32)


def swap_heads(pieces):
    return lax.all_to_all(pieces, "head", split_axis=0, concat_axis=0, tiled=True)


def mixer_place():
    heads, ring = lax.axis_size("head"), ring_of("blk")
    peers = heads * len(ring)
    rows = (QH * HD + MH * MP) // peers
    query_blocks, mamba_blocks = QH * HD // rows // heads, MH * MP // rows // heads
    pairs = []
    for r in range(peers):
        if r < query_blocks * heads:
            group, slot = divmod(r, query_blocks)
        else:
            group, slot = divmod(r - query_blocks * heads, mamba_blocks)
            slot += query_blocks
        pairs.append((r, group * len(ring) + ring[slot]))
    return pairs


kv_begin = QH * HD
z_begin = kv_begin + 2 * KVH * HD
x_begin = z_begin + MH * MP
b_begin = x_begin + MH * MP
dt_begin = b_begin + 2 * NS
query_columns = QH * HD // 4
inner_columns = MH * MP // 4
bc_columns = 2 * NS // 4
step_heads = MH // 4
step_at = inner_columns + bc_columns
kv_at = step_at + 128
conv_columns = kv_at + HD
rest_columns = query_columns + inner_columns


def column_parts(head):
    conv = [
        (x_begin + head * inner_columns, 0, inner_columns),
        (b_begin + head * bc_columns, inner_columns, bc_columns),
        (kv_begin + (head % 2) * KVH * HD + (head // 2) * HD, kv_at, HD),
    ]
    rest = [
        (head * query_columns, 0, query_columns),
        (z_begin + head * inner_columns, query_columns, inner_columns),
    ]
    return conv, rest


def pack_in(place_ref, weight_ref, conv_ref, rest_ref, tail_ref):
    tail_ref[...] = jnp.zeros_like(tail_ref)
    tail_ref[:, :MH] = weight_ref[:, dt_begin : dt_begin + MH]
    last = tail_ref[...]
    lane = iota(last.shape, 1)
    for head in range(4):
        for parts, ref in zip(column_parts(head), (conv_ref, rest_ref)):
            for begin, at, size in parts:
                ref[head, :, at : at + size] = weight_ref[:, begin : begin + size].astype(low)
        steps = pltpu.roll(last, lanes - step_heads * head, 1) if head else last
        conv_ref[head, :, step_at:kv_at] = jnp.where(lane < step_heads, steps, 0.0).astype(low)


def unpack_in(place_ref, conv_ref, rest_ref, out_ref):
    total = jnp.zeros((out_ref.shape[0], lanes), jnp.float32)
    lane = iota(total.shape, 1)
    for head in range(4):
        for parts, ref in zip(column_parts(head), (conv_ref, rest_ref)):
            for begin, at, size in parts:
                out_ref[:, begin : begin + size] = ref[head, :, at : at + size].astype(jnp.float32)
        steps = conv_ref[head, :, step_at:kv_at].astype(jnp.float32)
        steps = jnp.where(lane < step_heads, steps, 0.0)
        total = total + (pltpu.roll(steps, step_heads * head, 1) if head else steps)
    out_ref[:, dt_begin : dt_begin + MH] = total[:, :MH]


def ffn_moves(ring):
    unit = FF // (4 * len(ring))
    return unit, [
        (
            head,
            half * FF + (head * len(ring) + k) * unit,
            half * (FF // 4) + i * unit,
        )
        for half in range(2)
        for head in range(4)
        for i, k in enumerate(ring)
    ]


def pack_ffn(place_ref, weight_ref, out_ref, *, ring):
    unit, moves = ffn_moves(ring)
    for head, begin, at in moves:
        out_ref[head, :, at : at + unit] = weight_ref[:, begin : begin + unit].astype(low)


def unpack_ffn(place_ref, in_ref, out_ref, *, ring):
    unit, moves = ffn_moves(ring)
    for head, begin, at in moves:
        out_ref[:, begin : begin + unit] = in_ref[head, :, at : at + unit].astype(jnp.float32)


def inverse_rms(values_in):
    return lax.rsqrt(jnp.mean(values_in * values_in, axis=1, keepdims=True) + epsilon)


def feature_moves(ring):
    piece = D // 4 // len(ring)
    return piece, [
        ((e * len(ring) + k) * piece, (4 * i + e) * piece)
        for e in range(4)
        for i, k in enumerate(ring)
    ]


def whole_lanes(begin, size):
    return pl.ds(pl.multiple_of(begin, 128), size)


def norm_one(place_ref, own, across, beside, both, gain_ref, out_ref, line_ref, *, ring):
    rows = own.shape[0]
    piece, moves = feature_moves(ring)
    for distance, ref in ((0, own), (2, across), (1, beside), (3, both)):
        x = ref[...].astype(jnp.float32)
        line_ref[...] = (x * inverse_rms(x) * gain_ref[...]).astype(low)
        there = jnp.bitwise_xor(place_ref[0], distance) * rows
        there = pl.ds(pl.multiple_of(there, rows), rows)
        for source, at in moves:
            out_ref[there, at : at + piece] = line_ref[:, source : source + piece]


def norm_two(place_ref, mixed_ref, tokens_ref, gain_ref, hidden_ref, out_ref, line_ref, *, ring):
    hidden = tokens_ref[...].astype(jnp.float32) + mixed_ref[...]
    hidden_ref[...] = hidden
    line_ref[...] = (hidden * inverse_rms(hidden) * gain_ref[...]).astype(low)
    piece, moves = feature_moves(ring)
    for source, at in moves:
        out_ref[:, at : at + piece] = line_ref[:, source : source + piece]


def back_two(
    place_ref, grad_ref, hidden_ref, cotangent_ref, gain_ref, out_ref, low_ref, sum_ref, plain_ref,
    *, ring,
):
    piece, moves = feature_moves(ring)
    for source, at in moves:
        plain_ref[:, source : source + piece] = grad_ref[:, at : at + piece]
    grad = plain_ref[...]
    hidden = hidden_ref[...]
    inverse = inverse_rms(hidden)
    scaled = grad * gain_ref[...]
    total = (
        cotangent_ref[...].astype(jnp.float32)
        + inverse * scaled
        - hidden * (inverse * inverse * inverse * jnp.mean(scaled * hidden, axis=1, keepdims=True))
    )
    out_ref[...] = total
    low_ref[...] = total.astype(low)
    sum_ref[...] = jnp.broadcast_to(
        jnp.sum(grad * hidden * inverse, axis=0, keepdims=True), sum_ref.shape
    )


def back_one(
    place_ref, grad_ref, tokens_ref, hidden_ref, gain_ref, out_ref, plain_ref, *, ring
):
    piece, moves = feature_moves(ring)
    for source, at in moves:
        plain_ref[:, source : source + piece] = grad_ref[:, at : at + piece]
    grad = plain_ref[...]
    x = tokens_ref[...].astype(jnp.float32)
    inverse = inverse_rms(x)
    scaled = grad * gain_ref[...]
    out_ref[...] = (
        hidden_ref[...]
        + inverse * scaled
        - x * (inverse * inverse * inverse * jnp.mean(scaled * x, axis=1, keepdims=True))
    ).astype(low)


def turned(values_in, cosine, sine):
    return values_in * cosine + pltpu.roll(values_in, HD // 2, 1) * sine


def rope_kv(place_ref, in_ref, cosine_ref, sine_ref, out_ref):
    kv = in_ref[...]
    kv = jnp.where(place_ref[1] == 0, turned(kv, cosine_ref[...], sine_ref[...]), kv).astype(low)
    for k in range(out_ref.shape[0]):
        out_ref[k] = kv


def rope_query(place_ref, in_ref, cosine_ref, sine_ref, query_ref, gate_ref):
    cosine, sine = cosine_ref[...], sine_ref[...]
    for begin in range(0, query_columns, HD):
        query_ref[:, begin : begin + HD] = turned(
            in_ref[:, begin : begin + HD], cosine, sine
        ).astype(low)
    gate_ref[...] = in_ref[:, query_columns:].astype(low)


def query_back(place_ref, query_ref, gate_ref, cosine_ref, sine_ref, out_ref):
    cosine, sine = cosine_ref[...], -sine_ref[...]
    for begin in range(0, query_columns, HD):
        rounded = query_ref[:, begin : begin + HD].astype(low).astype(jnp.float32)
        out_ref[:, begin : begin + HD] = turned(rounded, cosine, sine).astype(low)
    out_ref[:, query_columns:] = gate_ref[...]


def join_conv(place_ref, inner_ref, own, across, beside, both, out_ref):
    out_ref[:, :inner_columns] = inner_ref[...].astype(low)
    for distance, ref in ((0, own), (2, across), (1, beside), (3, both)):
        at = inner_columns + jnp.bitwise_xor(place_ref[0], distance) * lanes
        out_ref[:, whole_lanes(at, lanes)] = ref[...]


def conv_joined(
    place_ref, inner_ref, near_ref, far_ref, step_ref, cosine_ref, sine_ref, kv_ref, out_ref
):
    out_ref[:, :inner_columns] = inner_ref[...].astype(low)
    out_ref[:, inner_columns:step_at] = (near_ref[...] + far_ref[...].astype(jnp.float32)).astype(low)
    out_ref[:, step_at:kv_at] = step_ref[...].astype(low)
    kv = kv_ref[0].astype(jnp.float32)
    for k in range(1, kv_ref.shape[0]):
        kv = kv + kv_ref[k].astype(jnp.float32)
    out_ref[:, kv_at:] = jnp.where(
        place_ref[1] == 0, turned(kv, cosine_ref[...], -sine_ref[...]), kv
    ).astype(low)


def relative_order(place_ref, first_ref, second_ref, first_out, second_out):
    for at, distance in enumerate((0, 2, 1, 3)):
        there = jnp.bitwise_xor(place_ref[0], distance) * chunk
        there = pl.ds(pl.multiple_of(there, chunk), chunk)
        rows = slice(at * chunk, (at + 1) * chunk)
        first_out[rows, :] = first_ref[there, :]
        second_out[rows, :] = second_ref[there, :]


def outer_grad(left_side, grad_side):
    return lax.dot_general(
        left_side, grad_side, (((0,), (0,)), ((), ())), preferred_element_type=jnp.float32
    )


def times_transposed(grad_side, weight):
    return lax.dot_general(
        grad_side, weight, (((1,), (1,)), ((), ())), preferred_element_type=jnp.float32
    )


chunk = 128
lanes = 128
low = jnp.bfloat16
exact = lax.Precision.HIGHEST


def dot_nn(a, b, precision=None):
    return lax.dot_general(
        a, b, (((1,), (0,)), ((), ())), precision=precision, preferred_element_type=jnp.float32
    )


def dot_nt(a, b):
    return lax.dot_general(a, b, (((1,), (1,)), ((), ())), preferred_element_type=jnp.float32)


def dot_tn(a, b):
    return lax.dot_general(a, b, (((0,), (0,)), ((), ())), preferred_element_type=jnp.float32)


def iota(shape, dim):
    return lax.broadcasted_iota(jnp.int32, shape, dim)


def spread(per_head, pair):
    rows = per_head.shape[0]
    first = per_head[:, 2 * pair : 2 * pair + 1]
    second = per_head[:, 2 * pair + 1 : 2 * pair + 2]
    return jnp.where(iota((rows, lanes), 1) < MP, first, second)


def head_sums(products, pair):
    mine = 2 * pair + (iota((lanes, lanes), 0) >= MP).astype(jnp.int32)
    ones = (mine == iota((lanes, lanes), 1)).astype(jnp.float32)
    return dot_nn(products, ones, exact)


def chunk_terms(decay, segment, segment_before):
    lower = iota((chunk, chunk), 0) >= iota((chunk, chunk), 1)
    cumulative = dot_nn(lower.astype(jnp.float32), decay, exact)
    total = cumulative[chunk - 1 :, :]
    segment_end = segment[chunk - 1 :, :]
    related = lower & (segment == segment.T)
    entering = jnp.where(segment == segment_before, jnp.exp(cumulative), 0.0)
    ending = jnp.where(segment == segment_end, jnp.exp(total - cumulative), 0.0)
    whole = jnp.where(segment_end == segment_before, jnp.exp(total), 0.0)
    return cumulative, cumulative.T, related, entering, ending, whole, total, segment_end


def decays_of(cumulative, transposed, related, head):
    apart = cumulative[:, head : head + 1] - transposed[head : head + 1, :]
    return jnp.exp(jnp.where(related, apart, masked_score))


def row_factor(whole, pair, width):
    first = whole[:, 2 * pair : 2 * pair + 1]
    second = whole[:, 2 * pair + 1 : 2 * pair + 2]
    return jnp.where(iota((lanes, width), 0) < MP, first, second)


def chunk_rows(index):
    return pl.ds(pl.multiple_of(index * chunk, chunk), chunk)


def pack_states(state_ref, factor, out_ref):
    blocks, rows, width = out_ref.shape
    share = rows - extra_rows
    row = iota((extra_rows, width), 0)
    for k in range(blocks):
        extra = jnp.zeros((extra_rows, width), jnp.float32)
        for e in range(4):
            head = k * share // MP + e
            if head * MP < state_ref.shape[0]:
                whole = factor[:, head : head + 1]
                rough = whole.astype(low).astype(jnp.float32)
                extra = jnp.where(row == e, rough, extra)
                extra = jnp.where(row == 4 + e, whole - rough, extra)
        out_ref[k, :extra_rows, :] = extra.astype(low)
        out_ref[k, extra_rows:, :] = state_ref[k * share : (k + 1) * share, :].astype(low)


extra_rows = 16


def chain(place_ref, got_ref, out_ref, backwards):
    blocks, rows, width = got_ref.shape
    share = rows - extra_rows
    row = iota((share, width), 0) + lax.rem(place_ref[4] * share, MP)
    state = jnp.zeros((share, width), jnp.float32)
    for k in range(blocks - 1, -1, -1) if backwards else range(blocks):
        out_ref[k] = state.astype(low)
        extra = got_ref[k, :extra_rows, :].astype(jnp.float32)
        factor = extra[0:1, :] + extra[4:5, :]
        for e in range(1, 4):
            factor = jnp.where(row >= e * MP, extra[e : e + 1, :] + extra[4 + e : 5 + e, :], factor)
        state = factor * state + got_ref[k, extra_rows:, :].astype(jnp.float32)


def ssd_local(
    place_ref, x_ref, b_ref, c_ref, step_ref, decay_ref, seg_ref,
    y_ref, sent_ref, enter_ref, fac_ref, state_ref,
):
    pairs = x_ref.shape[1] // lanes
    state_ref[...] = jnp.zeros_like(state_ref)

    def body(index, carry):
        segment_before, base = carry
        rows = chunk_rows(index)
        segment = seg_ref[rows, :]
        cumulative, transposed, related, entering, ending, whole, total, segment_end = chunk_terms(
            decay_ref[rows, :], segment, segment_before
        )
        enter_ref[rows, :] = jnp.where(segment == 0.0, jnp.exp(base + cumulative), 0.0)
        into = b_ref[rows, :].astype(low)
        outof = c_ref[rows, :].astype(low)
        step = step_ref[rows, :]
        scores = dot_nt(outof, into)
        left = iota((chunk, lanes), 1) < MP
        for pair in range(pairs):
            cols = slice(pair * lanes, (pair + 1) * lanes)
            taken = x_ref[rows, cols] * spread(step, pair)
            taken_low = taken.astype(low)
            parts = []
            for head in (2 * pair, 2 * pair + 1):
                weights = decays_of(cumulative, transposed, related, head) * scores
                parts.append(dot_nn(weights.astype(low), taken_low))
            state = state_ref[cols, :]
            y_ref[rows, cols] = jnp.where(left, parts[0], parts[1]) + spread(
                entering, pair
            ) * dot_nt(outof, state.astype(low))
            kept = (taken * spread(ending, pair)).astype(low)
            state_ref[cols, :] = row_factor(whole, pair, state.shape[1]) * state + dot_tn(
                kept, into
            )
        return segment_end, base + total

    start = jnp.zeros((1, lanes), jnp.float32)
    segment_end, base = lax.fori_loop(0, x_ref.shape[0] // chunk, body, (start, start))
    factor = jnp.where(segment_end == 0.0, jnp.exp(base), 0.0)
    fac_ref[...] = jnp.broadcast_to(factor, fac_ref.shape)
    pack_states(state_ref, factor, sent_ref)


def relative_rows(place_ref, index):
    distance = jnp.bitwise_xor(place_ref[0], index)
    at = (distance % 2) * 2 + distance // 2
    return pl.ds(pl.multiple_of(at * chunk, chunk), chunk)


def ssd_finish(
    place_ref, y_ref, enter_ref, c_ref, state_ref, x_ref, z_ref, skip_ref, attended_ref,
    ssd_ref, mixer_ref,
):
    pairs = x_ref.shape[1] // lanes
    width = attended_ref.shape[1]

    def body(index, carry):
        rows = chunk_rows(index)
        there = relative_rows(place_ref, index)
        outof = c_ref[rows, :].astype(low)
        entering = enter_ref[rows, :]
        mixer_ref[there, :width] = attended_ref[rows, :].astype(low)
        for pair in range(pairs):
            cols = slice(pair * lanes, (pair + 1) * lanes)
            ssd = y_ref[rows, cols] + spread(entering, pair) * dot_nt(outof, state_ref[cols, :])
            ssd_ref[rows, cols] = ssd
            gate = z_ref[rows, cols].astype(jnp.float32)
            total = ssd + skip_ref[:, cols] * x_ref[rows, cols]
            mixer_ref[there, width + pair * lanes : width + (pair + 1) * lanes] = (
                total * gate / (1.0 + jnp.exp(-gate))
            ).astype(low)
        return carry

    lax.fori_loop(0, x_ref.shape[0] // chunk, body, 0)


def ssd_gate_back(
    place_ref, grad_ref, z_ref, ssd_ref, x_ref, skip_ref, enter_ref, c_ref, fac_ref,
    dy_ref, dz_ref, sent_ref, dskip_ref, datt_ref, dstate_ref,
):
    pairs = x_ref.shape[1] // lanes
    width = datt_ref.shape[1]
    dstate_ref[...] = jnp.zeros_like(dstate_ref)
    dskip_ref[...] = jnp.zeros_like(dskip_ref)

    def body(index, carry):
        rows = chunk_rows(index)
        there = relative_rows(place_ref, index)
        outof = c_ref[rows, :].astype(low)
        entering = enter_ref[rows, :]
        datt_ref[rows, :] = grad_ref[there, :width]
        for pair in range(pairs):
            cols = slice(pair * lanes, (pair + 1) * lanes)
            gate = z_ref[rows, cols].astype(jnp.float32)
            sigmoid = 1.0 / (1.0 + jnp.exp(-gate))
            grad = grad_ref[
                there, width + pair * lanes : width + (pair + 1) * lanes
            ].astype(jnp.float32)
            x = x_ref[rows, cols]
            total = ssd_ref[rows, cols] + skip_ref[:, cols] * x
            dz_ref[rows, cols] = (
                grad * total * sigmoid * (1.0 + gate * (1.0 - sigmoid))
            ).astype(low)
            dy = grad * gate * sigmoid
            dy_ref[rows, cols] = dy
            dskip_ref[:, cols] += jnp.broadcast_to(
                jnp.sum(dy * x, axis=0, keepdims=True), (dskip_ref.shape[0], lanes)
            )
            dstate_ref[cols, :] += dot_tn((dy * spread(entering, pair)).astype(low), outof)
        return carry

    lax.fori_loop(0, x_ref.shape[0] // chunk, body, 0)
    pack_states(dstate_ref, fac_ref[:1, :], sent_ref)


def ssd_back(
    place_ref, x_ref, b_ref, c_ref, step_ref, decay_ref, seg_ref, dy_ref, ssd_ref, skip_ref, state_ref, later_ref,
    dx_ref, db_ref, dc_ref, dstep_ref, ddecay_ref, states, grads,
):
    pairs = x_ref.shape[1] // lanes
    chunks = x_ref.shape[0] // chunk
    zero_row = jnp.zeros((1, lanes), jnp.float32)

    def before(index):
        rows = pl.ds(pl.multiple_of(jnp.maximum(index - 1, 0) * chunk, chunk), chunk)
        return jnp.where(index == 0, 0.0, seg_ref[rows, :][chunk - 1 :, :])

    states[0] = state_ref[...].astype(jnp.float32)

    def forward(index, carry):
        rows = chunk_rows(index)
        _, _, _, _, ending, whole, _, _ = chunk_terms(
            decay_ref[rows, :], seg_ref[rows, :], before(index)
        )
        into = b_ref[rows, :].astype(low)
        step = step_ref[rows, :]
        for pair in range(pairs):
            cols = slice(pair * lanes, (pair + 1) * lanes)
            kept = (x_ref[rows, cols] * spread(step, pair) * spread(ending, pair)).astype(low)
            state = states[index, cols, :]
            states[index + 1, cols, :] = row_factor(
                whole, pair, state.shape[1]
            ) * state + dot_tn(kept, into)
        return carry

    lax.fori_loop(0, chunks, forward, 0)
    grads[...] = later_ref[...].astype(jnp.float32)
    last = jnp.zeros((8, lanes), jnp.float32)
    for pair in range(pairs):
        cols = slice(pair * lanes, (pair + 1) * lanes)
        product = grads[cols, :] * states[chunks, cols, :]
        along = lax.dot_general(
            jnp.ones((8, product.shape[1]), jnp.float32),
            product,
            (((1,), (1,)), ((), ())),
            precision=exact,
            preferred_element_type=jnp.float32,
        )
        last = last + head_sums(along, pair)

    def backward(at, carry):
        index = chunks - 1 - at
        rows = chunk_rows(index)
        cumulative, transposed, related, entering, ending, whole, _, _ = chunk_terms(
            decay_ref[rows, :], seg_ref[rows, :], before(index)
        )
        into = b_ref[rows, :].astype(low)
        outof = c_ref[rows, :].astype(low)
        step = step_ref[rows, :]
        scores = dot_nt(outof, into)
        left = iota((chunk, lanes), 1) < MP
        grad_scores = jnp.zeros((chunk, chunk), jnp.float32)
        grad_into = jnp.zeros((chunk, b_ref.shape[1]), jnp.float32)
        grad_outof = jnp.zeros((chunk, b_ref.shape[1]), jnp.float32)
        grad_cum = jnp.zeros((chunk, lanes), jnp.float32)
        grad_step = jnp.zeros((chunk, lanes), jnp.float32)
        for pair in range(pairs):
            cols = slice(pair * lanes, (pair + 1) * lanes)
            x = x_ref[rows, cols]
            step_pair = spread(step, pair)
            taken = x * step_pair
            taken_low = taken.astype(low)
            dy = dy_ref[rows, cols]
            dy_low = dy.astype(low)
            parts = []
            for half, head in enumerate((2 * pair, 2 * pair + 1)):
                decays = decays_of(cumulative, transposed, related, head)
                parts.append(dot_tn((decays * scores).astype(low), dy_low))
                own = jnp.where(left if half == 0 else ~left, dy_low, jnp.zeros_like(dy_low))
                grad_scores = grad_scores + decays * dot_nt(own, taken_low)
            later = grads[cols, :]
            later_low = later.astype(low)
            ending_pair = spread(ending, pair)
            grad_taken = jnp.where(left, parts[0], parts[1]) + ending_pair * dot_nt(
                into, later_low
            )
            grad_into = grad_into + dot_nn((taken * ending_pair).astype(low), later_low)
            dy_enter = (dy * spread(entering, pair)).astype(low)
            grad_outof = grad_outof + dot_nn(dy_enter, states[index, cols, :].astype(low))
            grads[cols, :] = row_factor(whole, pair, later.shape[1]) * later + dot_tn(
                dy_enter, outof
            )
            grad_cum = grad_cum + head_sums(dy * ssd_ref[rows, cols] - taken * grad_taken, pair)
            grad_step = grad_step + head_sums(x * grad_taken, pair)
            dx_ref[rows, cols] = step_pair * grad_taken + skip_ref[:, cols] * dy
        grad_scores_low = grad_scores.astype(low)
        db_ref[rows, :] = grad_into + dot_tn(grad_scores_low, outof)
        dc_ref[rows, :] = grad_outof + dot_nn(grad_scores_low, into)
        dstep_ref[rows, :] = grad_step
        upper = (iota((chunk, chunk), 0) <= iota((chunk, chunk), 1)).astype(jnp.float32)
        ddecay_ref[rows, :] = dot_nn(upper, grad_cum, exact) + carry
        return carry + jnp.sum(grad_cum, axis=0, keepdims=True)

    lax.fori_loop(0, chunks, backward, last[:1, :] + zero_row)


def needed_and_plain(place_ref, block, span):
    mine, earliest, latest = place_ref[0], place_ref[1], place_ref[2]
    needed = (block <= mine) & ((block + 1) * span > earliest)
    return needed, (block < mine) & (block * span >= latest)


def visible_keys(place_ref, first_ref, block, span):
    key_pos = block * span + iota((span, span), 1)
    query_pos = place_ref[0] * span + iota((span, span), 0)
    return (key_pos <= query_pos) & (key_pos >= first_ref[:, :1])


def attend(place_ref, q_ref, first_ref, k_ref, v_ref, out_ref, lse_ref, top, total, summed):
    block = pl.program_id(0)
    span = q_ref.shape[0]
    heads = q_ref.shape[1] // HD

    @pl.when(block == 0)
    def _():
        top[...] = jnp.full_like(top, masked_score)
        total[...] = jnp.zeros_like(total)
        summed[...] = jnp.zeros_like(summed)

    def one(masked):
        keys = k_ref[0]
        values = v_ref[0]
        if masked:
            visible = visible_keys(place_ref, first_ref, block, span)
        for head in range(heads):
            cols = slice(head * HD, (head + 1) * HD)
            scores = dot_nt(q_ref[:, cols], keys) * HD**-0.5
            if masked:
                scores = jnp.where(visible, scores, masked_score)
            old_top = top[head][:, :1]
            new_top = jnp.maximum(old_top, jnp.max(scores, axis=1, keepdims=True))
            weights = jnp.exp(scores - new_top)
            if masked:
                weights = jnp.where(visible, weights, 0.0)
            scale = jnp.exp(old_top - new_top)
            total[head] = total[head] * scale + jnp.sum(weights, axis=1, keepdims=True)
            top[head] = jnp.broadcast_to(new_top, (span, lanes))
            summed[head] = summed[head] * scale + dot_nn(weights.astype(low), values)

    needed, plain = needed_and_plain(place_ref, block, span)
    pl.when(needed & plain)(lambda: one(False))
    pl.when(needed & jnp.logical_not(plain))(lambda: one(True))

    @pl.when(block == pl.num_programs(0) - 1)
    def _():
        for head in range(heads):
            cols = slice(head * HD, (head + 1) * HD)
            out_ref[:, cols] = summed[head] / total[head]
            lse_ref[head] = top[head] + jnp.log(total[head])


def attend_back(
    place_ref, q_ref, first_ref, k_ref, v_ref, grad_ref, out_ref, lse_ref, dq_ref, dk_ref, dv_ref
):
    block = pl.program_id(0)
    span = q_ref.shape[0]
    heads = q_ref.shape[1] // HD

    @pl.when(block == 0)
    def _():
        dq_ref[...] = jnp.zeros_like(dq_ref)

    def one(masked):
        keys = k_ref[0]
        values = v_ref[0]
        if masked:
            visible = visible_keys(place_ref, first_ref, block, span)
        grad_keys = jnp.zeros(keys.shape, jnp.float32)
        grad_values = jnp.zeros(keys.shape, jnp.float32)
        for head in range(heads):
            cols = slice(head * HD, (head + 1) * HD)
            query = q_ref[:, cols]
            grad = grad_ref[:, cols]
            delta = jnp.sum(
                grad.astype(jnp.float32) * out_ref[:, cols], axis=1, keepdims=True
            )
            scores = dot_nt(query, keys) * HD**-0.5
            if masked:
                scores = jnp.where(visible, scores, masked_score)
            weights = jnp.exp(scores - lse_ref[head][:, :1])
            changes = weights * (dot_nt(grad, values) - delta)
            weights_low = weights.astype(low)
            changes_low = (changes * HD**-0.5).astype(low)
            grad_values = grad_values + dot_tn(weights_low, grad)
            grad_keys = grad_keys + dot_tn(changes_low, query)
            dq_ref[:, cols] += dot_nn(changes_low, keys)
        dk_ref[0] = grad_keys.astype(low)
        dv_ref[0] = grad_values.astype(low)

    needed, plain = needed_and_plain(place_ref, block, span)
    pl.when(needed & plain)(lambda: one(False))
    pl.when(needed & jnp.logical_not(plain))(lambda: one(True))

    @pl.when(jnp.logical_not(needed))
    def _():
        dk_ref[...] = jnp.zeros_like(dk_ref)
        dv_ref[...] = jnp.zeros_like(dv_ref)


def shaped(shape, kind):
    return jax.ShapeDtypeStruct(shape, kind)


def call(kernel, outputs, place, operands, after=(), scratch=(), flops=10**6):
    count, skipped = len(operands), len(operands) + len(after)
    sizes = sum(math.prod(a.shape) * a.dtype.itemsize for a in (*operands, *outputs))

    def body(place_ref, *refs):
        kernel(place_ref, *refs[:count], *refs[skipped:])

    return pl.pallas_call(
        body,
        out_shape=outputs,
        in_specs=[pl.BlockSpec(memory_space=pltpu.SMEM)]
        + [pl.BlockSpec(memory_space=pltpu.VMEM)] * count
        + [pl.BlockSpec(memory_space=pl.ANY)] * len(after),
        out_specs=[pl.BlockSpec(memory_space=pltpu.VMEM)] * len(outputs),
        scratch_shapes=list(scratch),
        compiler_params=pltpu.CompilerParams(vmem_limit_bytes=kernel_memory),
        cost_estimate=pl.CostEstimate(flops=flops, bytes_accessed=sizes, transcendentals=0),
    )(place, *operands, *after)


kernel_memory = 44 * 1024 * 1024


def attention(place, query, first_visible, keys, values, after):
    away, span = keys.shape[0], query.shape[0]
    heads = query.shape[1] // HD
    same = lambda d, place: (0, 0)
    block = lambda d, place: (d, 0, 0)
    def body(*refs):
        attend(*refs[:5], *refs[5 + len(after) :])

    return pl.pallas_call(
        body,
        grid_spec=pltpu.PrefetchScalarGridSpec(
            num_scalar_prefetch=1,
            grid=(away,),
            in_specs=[
                pl.BlockSpec(query.shape, same),
                pl.BlockSpec(first_visible.shape, same),
                pl.BlockSpec((1, span, HD), block),
                pl.BlockSpec((1, span, HD), block),
            ]
            + [pl.BlockSpec(memory_space=pl.ANY)] * len(after),
            out_specs=[
                pl.BlockSpec(query.shape, same),
                pl.BlockSpec((heads, span, lanes), lambda d, place: (0, 0, 0)),
            ],
            scratch_shapes=[
                pltpu.VMEM((heads, span, lanes), jnp.float32),
                pltpu.VMEM((heads, span, lanes), jnp.float32),
                pltpu.VMEM((heads, span, HD), jnp.float32),
            ],
        ),
        out_shape=[
            shaped(query.shape, jnp.float32),
            shaped((heads, span, lanes), jnp.float32),
        ],
        compiler_params=pltpu.CompilerParams(vmem_limit_bytes=kernel_memory),
        cost_estimate=pl.CostEstimate(
            flops=20 * 10**9, bytes_accessed=4 * 10**6, transcendentals=0
        ),
    )(place, query, first_visible, keys, values, *after)


def attention_back(place, query, first_visible, keys, values, grad, out, lse, after):
    away, span = keys.shape[0], query.shape[0]
    same = lambda d, place: (0, 0)
    block = lambda d, place: (d, 0, 0)
    def body(*refs):
        attend_back(*refs[:8], *refs[8 + len(after) :])

    return pl.pallas_call(
        body,
        grid_spec=pltpu.PrefetchScalarGridSpec(
            num_scalar_prefetch=1,
            grid=(away,),
            in_specs=[
                pl.BlockSpec(query.shape, same),
                pl.BlockSpec(first_visible.shape, same),
                pl.BlockSpec((1, span, HD), block),
                pl.BlockSpec((1, span, HD), block),
                pl.BlockSpec(query.shape, same),
                pl.BlockSpec(query.shape, same),
                pl.BlockSpec(lse.shape, lambda d, place: (0, 0, 0)),
            ]
            + [pl.BlockSpec(memory_space=pl.ANY)] * len(after),
            out_specs=[
                pl.BlockSpec(query.shape, same),
                pl.BlockSpec((1, span, HD), block),
                pl.BlockSpec((1, span, HD), block),
            ],
        ),
        out_shape=[
            shaped(query.shape, jnp.float32),
            shaped(keys.shape, low),
            shaped(keys.shape, low),
        ],
        compiler_params=pltpu.CompilerParams(vmem_limit_bytes=kernel_memory),
        cost_estimate=pl.CostEstimate(
            flops=30 * 10**9, bytes_accessed=4 * 10**6, transcendentals=0
        ),
    )(place, query, first_visible, keys, values, grad, out, lse, *after)


def conv_act(extended, conv_taps, conv_shift, keep_masks):
    length = keep_masks[0].shape[0]
    result = conv_shift + conv_taps[0] * extended[KW - 1 :]
    for lag_index in range(1, KW):
        begin = KW - 1 - lag_index
        result = (
            result
            + conv_taps[lag_index]
            * keep_masks[lag_index][:, None]
            * extended[begin : begin + length]
        )
    return jax.nn.silu(result)


def step_and_decay(step_raw, step_shift, decay_rate):
    step_size = jax.nn.softplus(step_raw + step_shift)
    return step_size, -step_size * jnp.exp(decay_rate)


def in_lanes(per_head):
    return jnp.pad(per_head, ((0, 0), (0, lanes - per_head.shape[1])))


def summed_over(values_in, axis):
    peers = lax.axis_size(axis)
    by = 1
    while by < peers:
        values_in = values_in + lax.ppermute(values_in, axis, [(i, i ^ by) for i in range(peers)])
        by *= 2
    return values_in


def per_device(
    block_input,
    out_cotangent,
    start_flags,
    in_weight,
    out_weight,
    gate_up_weight,
    down_weight,
    first_gain,
    second_gain,
    conv_weight,
    conv_bias,
    step_bias,
    decay_log,
    skip_gain,
):
    head_count = lax.axis_size("head")
    blocks = lax.axis_size("blk")
    head_index = lax.axis_index("head")
    block_index = lax.axis_index("blk")
    ring = ring_of("blk")
    tokens = block_input[0]
    cotangent = out_cotangent[0]
    row_count = tokens.shape[0]
    span_rows = row_count * head_count
    mamba_width = MH * MP
    even = head_index % 2 == 0
    out_pairs = mixer_place()
    place = jnp.stack(
        [head_index, head_index % 2, 0, 0, block_index, 0, 0, 0]
    ).astype(jnp.int32)

    rows_in = in_weight.shape[0]
    flags_all = summed_over(
        lax.dynamic_update_slice_in_dim(
            jnp.zeros((blocks * span_rows,), jnp.int32),
            start_flags[0],
            block_index * span_rows,
            0,
        ),
        "blk",
    )
    packed_conv, packed_rest = call(
        pack_in,
        [
            shaped((4, rows_in, conv_columns), low),
            shaped((4, rows_in, rest_columns), low),
        ],
        place,
        [in_weight],
        scratch=[pltpu.VMEM((rows_in, lanes), jnp.float32)],
    )
    conv_rows = swap_heads(packed_conv).reshape(-1, conv_columns)
    weights_conv = gather_blocks(conv_rows)
    rest_rows = swap_heads(after(packed_rest, conv_rows)).reshape(-1, rest_columns)
    weights_rest = gather_blocks(rest_rows)
    gathered_tokens = gather_heads(after(tokens, conv_rows))
    out_rows = lax.ppermute(after(out_weight.astype(low), rest_rows), ("head", "blk"), out_pairs)
    weights_out = gather_blocks(out_rows)
    rows_ffn = gate_up_weight.shape[0]
    units = FF // 4
    packed_ffn = call(
        partial(pack_ffn, ring=ring),
        [shaped((4, rows_ffn, 2 * units), low)],
        place,
        [after(gate_up_weight, rest_rows)],
    )[0]
    ffn_rows = swap_heads(packed_ffn).reshape(-1, 2 * units)
    weights_ffn = gather_blocks(after(ffn_rows, out_rows))
    weights_down = gather_blocks(after(down_weight.astype(low), ffn_rows))
    model_cotangent = jnp.concatenate(gather_heads(after(cotangent, ffn_rows)))

    positions = block_index * span_rows + jnp.arange(span_rows, dtype=jnp.int32)
    all_positions = jnp.arange(blocks * span_rows, dtype=jnp.int32)
    starts_all = lax.cummax(jnp.where(flags_all > 0, all_positions, 0), axis=0)
    first_visible = lax.dynamic_slice_in_dim(starts_all, block_index * span_rows, span_rows, 0)
    flags_before = jnp.concatenate([jnp.zeros((KW - 2,), jnp.int32), flags_all])
    flag_ext = lax.dynamic_slice_in_dim(
        flags_before, block_index * span_rows, span_rows + KW - 2, 0
    ).astype(jnp.float32)
    segment = jnp.broadcast_to(
        jnp.cumsum(start_flags[0]).astype(jnp.float32)[:, None], (span_rows, lanes)
    )
    view = jnp.stack([block_index, jnp.min(first_visible), jnp.max(first_visible)])
    first_wide = jnp.broadcast_to(first_visible[:, None], (span_rows, lanes))
    keep_masks = [jnp.ones((span_rows,), jnp.float32)]
    for lag_index in range(1, KW):
        begin = KW - 1 - lag_index
        keep_masks.append(keep_masks[-1] * (1.0 - flag_ext[begin : begin + span_rows]))
    frequencies = rope_base ** (-jnp.arange(HD // 2, dtype=jnp.float32) * 2.0 / HD)
    angles = positions.astype(jnp.float32)[:, None] * frequencies[None, :]
    cosine = jnp.cos(angles)
    sine = jnp.sin(angles)
    cosine_wide = jnp.concatenate([cosine, cosine], axis=1)
    sine_wide = jnp.concatenate([-sine, sine], axis=1)
    conv_taps = jnp.concatenate(
        [
            lax.dynamic_slice_in_dim(conv_weight, head_index * inner_columns, inner_columns, 1),
            conv_weight[:, mamba_width:],
        ],
        axis=1,
    )
    conv_shift = jnp.concatenate(
        [
            lax.dynamic_slice_in_dim(conv_bias, head_index * inner_columns, inner_columns, 0),
            conv_bias[mamba_width:],
        ]
    )
    step_shift = lax.dynamic_slice_in_dim(step_bias, head_index * step_heads, step_heads, 0)
    decay_rate = lax.dynamic_slice_in_dim(decay_log, head_index * step_heads, step_heads, 0)
    skip_local = lax.dynamic_slice_in_dim(skip_gain, head_index * step_heads, step_heads, 0)
    skip_wide = jnp.repeat(skip_local, MP)[None, :]

    normed_one = call(
        partial(norm_one, ring=ring),
        [shaped((span_rows, D), low)],
        place,
        [*gathered_tokens, first_gain[None, :]],
        scratch=[pltpu.VMEM((row_count, D), low)],
    )[0]

    projected = jnp.dot(normed_one, weights_conv, preferred_element_type=jnp.float32)
    kv_mine = call(
        rope_kv,
        [shaped((blocks, span_rows, HD), low)],
        place,
        [projected[:, kv_at:], cosine_wide, sine_wide],
    )[0]
    pair_bc = projected[:, inner_columns:step_at].astype(low)
    conv_local = call(
        join_conv,
        [shaped((span_rows, inner_columns + 2 * NS), low)],
        place,
        [projected[:, :inner_columns], *gather_heads(pair_bc)],
    )[0]
    step_local = projected[:, step_at : step_at + step_heads].astype(low).astype(jnp.float32)
    rim_rows = passed_along(conv_local[span_rows - (KW - 1) :], "blk", 1)
    extended = jnp.concatenate([rim_rows, conv_local], axis=0).astype(jnp.float32)
    active, conv_back = jax.vjp(
        partial(conv_act, keep_masks=keep_masks), extended, conv_taps, conv_shift
    )
    (step_size, log_decay), step_back = jax.vjp(
        step_and_decay, step_local, step_shift, decay_rate
    )
    inner_act = active[:, :inner_columns]
    into_act = active[:, inner_columns : inner_columns + NS]
    outof_act = active[:, inner_columns + NS :]
    step_wide = in_lanes(step_size)
    decay_wide = in_lanes(log_decay)
    tall = shaped((span_rows, inner_columns), jnp.float32)
    tall_low = shaped((span_rows, inner_columns), low)
    narrow = shaped((span_rows, lanes), jnp.float32)
    share = inner_columns // blocks
    sent = shaped((blocks, extra_rows + share, NS), low)
    state_scratch = pltpu.VMEM((inner_columns, NS), jnp.float32)

    def chained(payload, backwards, after=()):
        got = lax.all_to_all(payload, "blk", split_axis=0, concat_axis=0, tiled=True)
        states = call(
            partial(chain, backwards=backwards),
            [shaped((blocks, share, NS), low)],
            place,
            [got],
            after=after,
        )[0]
        moved = lax.all_to_all(states, "blk", split_axis=0, concat_axis=0, tiled=True)
        return moved.reshape(inner_columns, NS), states

    within, state_sent, entering, factor = call(
        ssd_local,
        [tall, sent, narrow, shaped((8, lanes), jnp.float32)],
        place,
        [inner_act, into_act, outof_act, step_wide, decay_wide, segment],
        after=[ffn_rows],
        scratch=[state_scratch],
        flops=6 * 10**9,
    )
    state_in, states_mine = chained(state_sent, False)

    normed_after = after(normed_one, states_mine)
    projected_rest = jnp.dot(normed_after, weights_rest, preferred_element_type=jnp.float32)
    query_local, gate_act = call(
        rope_query,
        [shaped((span_rows, query_columns), low), tall_low],
        place,
        [projected_rest, cosine_wide, sine_wide],
    )
    kv_blocks = lax.all_to_all(
        after(kv_mine, state_sent), "blk", split_axis=0, concat_axis=0, tiled=True
    )
    kv_beside = from_head(kv_blocks, 1)
    keys = jnp.where(even, kv_blocks, kv_beside)
    values = jnp.where(even, kv_beside, kv_blocks)
    attended, lse = attention(
        view, query_local, first_wide, keys, values, [states_mine, model_cotangent]
    )

    ssd, mixer = call(
        ssd_finish,
        [tall, shaped((span_rows, query_columns + inner_columns), low)],
        place,
        [within, entering, outof_act, state_in, inner_act, gate_act, skip_wide, attended],
        flops=2 * 10**9,
    )
    pair_rows = 2 * row_count
    mixed_other = jnp.dot(mixer[pair_rows:], weights_out, preferred_element_type=jnp.float32)
    mixed_own = jnp.dot(mixer[:pair_rows], weights_out, preferred_element_type=jnp.float32)
    mixed = scatter_pairs(mixed_own, mixed_other)
    hidden_one, normed_two = call(
        partial(norm_two, ring=ring),
        [shaped((row_count, D), jnp.float32), shaped((row_count, D), low)],
        place,
        [mixed, tokens, second_gain[None, :]],
        scratch=[pltpu.VMEM((row_count, D), low)],
    )
    model_normed = jnp.concatenate(gather_heads(normed_two))
    gate_up = jnp.dot(model_normed, weights_ffn, preferred_element_type=jnp.float32)
    gate_part, up_part = gate_up[:, :units], gate_up[:, units:]
    activated = (jax.nn.silu(gate_part) * up_part).astype(low)
    grad_activated = times_transposed(model_cotangent, weights_down)
    sigmoid_gate = jax.nn.sigmoid(gate_part)
    grad_gate_up = jnp.concatenate(
        [
            grad_activated * up_part * sigmoid_gate * (1.0 + gate_part * (1.0 - sigmoid_gate)),
            grad_activated * jax.nn.silu(gate_part),
        ],
        axis=1,
    ).astype(low)
    grad_down_low = outer_grad(activated, model_cotangent).astype(low)
    grad_down = scatter_blocks(grad_down_low)
    gate_up_late = after(grad_gate_up, grad_down_low)
    grad_norm_other = times_transposed(gate_up_late[pair_rows:], weights_ffn).astype(low)
    grad_norm_own = times_transposed(gate_up_late[:pair_rows], weights_ffn)
    grad_normed_two = scatter_pairs(grad_norm_own, grad_norm_other, low)
    grad_ffn_low = outer_grad(model_normed, after(grad_gate_up, grad_norm_own)).astype(low)
    grad_ffn = scatter_blocks(after(grad_ffn_low, grad_down))

    grad_hidden, grad_hidden_low, grad_second = call(
        partial(back_two, ring=ring),
        [
            shaped((row_count, D), jnp.float32),
            shaped((row_count, D), low),
            shaped((8, D), jnp.float32),
        ],
        place,
        [
            grad_normed_two,
            hidden_one,
            cotangent,
            second_gain[None, :],
        ],
        after=[grad_down_low, grad_ffn_low],
        scratch=[pltpu.VMEM((row_count, D), jnp.float32)],
    )
    span_grad_hidden = jnp.concatenate(gather_heads(after(grad_hidden_low, grad_down)))
    grad_heads = times_transposed(span_grad_hidden, weights_out).astype(low)
    grad_ssd, grad_gate, grad_sent, grad_skip_wide, grad_attended = call(
        ssd_gate_back,
        [
            tall,
            tall_low,
            sent,
            shaped((8, inner_columns), jnp.float32),
            shaped((span_rows, query_columns), low),
        ],
        place,
        [grad_heads, gate_act, ssd, inner_act, skip_wide, entering, outof_act, factor],
        scratch=[state_scratch],
        flops=2 * 10**9,
    )
    grad_ffn_weight = call(
        partial(unpack_ffn, ring=ring),
        [shaped(gate_up_weight.shape, jnp.float32)],
        place,
        [swap_heads(grad_ffn.reshape(4, rows_ffn, 2 * units))],
    )[0]
    activated_late = after(activated, span_grad_hidden)
    downed_other = jnp.dot(
        activated_late[pair_rows:], weights_down, preferred_element_type=jnp.float32
    )
    downed_own = jnp.dot(
        activated_late[:pair_rows], weights_down, preferred_element_type=jnp.float32
    )
    block_output = (hidden_one + scatter_pairs(downed_own, downed_other, low)).astype(low)

    grad_skip = grad_skip_wide[0].reshape(step_heads, MP).sum(axis=1)
    grad_out_low = outer_grad(mixer, span_grad_hidden).astype(low)
    grad_out_sum = scatter_blocks(after(grad_out_low, grad_ffn))
    grad_mix_weight = lax.ppermute(
        grad_out_sum, ("head", "blk"), [(there, here) for here, there in out_pairs]
    ).astype(jnp.float32)
    later_grad, _ = chained(grad_sent, True)

    grad_query, grad_keys, grad_values = attention_back(
        view,
        query_local,
        first_wide,
        keys,
        values,
        grad_attended,
        attended,
        lse,
        [grad_out_low],
    )
    kept_kv = jnp.where(even, grad_keys, grad_values)
    given_kv = jnp.where(even, grad_values, grad_keys)
    kv_sums = (kept_kv.astype(jnp.float32) + from_head(given_kv, 1).astype(jnp.float32)).astype(
        low
    )
    grad_rest = call(
        query_back,
        [shaped((span_rows, rest_columns), low)],
        place,
        [grad_query, grad_gate, cosine_wide, sine_wide],
    )[0]
    grad_rest_low = outer_grad(normed_one, grad_rest).astype(low)
    grad_rest_in = scatter_blocks(after(grad_rest_low, grad_out_sum))
    grad_kv_parts = lax.all_to_all(kv_sums, "blk", split_axis=0, concat_axis=0, tiled=True)

    grad_inner, grad_into, grad_outof, grad_step, grad_decay_line = call(
        ssd_back,
        [
            tall,
            shaped((span_rows, NS), jnp.float32),
            shaped((span_rows, NS), jnp.float32),
            narrow,
            narrow,
        ],
        place,
        [
            inner_act,
            into_act,
            outof_act,
            step_wide,
            decay_wide,
            segment,
            grad_ssd,
            ssd,
            skip_wide,
            state_in,
            later_grad,
        ],
        after=[kv_sums, grad_rest_low, block_output],
        scratch=[
            pltpu.VMEM((span_rows // chunk + 1, inner_columns, NS), jnp.float32),
            state_scratch,
        ],
        flops=10 * 10**9,
    )
    grad_raw, grad_step_shift, grad_rate = step_back(
        (grad_step[:, :step_heads], grad_decay_line[:, :step_heads])
    )
    grad_inner = after(grad_inner, grad_ffn)
    grad_extended, grad_taps, grad_shift = conv_back(
        jnp.concatenate([grad_inner, grad_into, grad_outof], axis=1)
    )
    rim_back = passed_along(grad_extended[: KW - 1], "blk", -1)
    conv_grad = grad_extended[KW - 1 :] + jnp.pad(rim_back, ((span_rows - (KW - 1), 0), (0, 0)))
    grad_bc = conv_grad[:, inner_columns:].astype(low).astype(jnp.float32)

    def tile_at(distance):
        at = jnp.bitwise_xor(head_index, distance) * lanes
        return lax.dynamic_slice_in_dim(grad_bc, at, lanes, 1)

    bc_beside = from_head(jnp.stack([tile_at(1), tile_at(3)]).astype(low), 1).astype(jnp.float32)
    bc_far = from_head((tile_at(2) + bc_beside[1]).astype(low), 2)
    bc_near = tile_at(0) + bc_beside[0]
    grad_conv = call(
        conv_joined,
        [shaped((span_rows, conv_columns), low)],
        place,
        [
            conv_grad[:, :inner_columns],
            bc_near,
            bc_far,
            in_lanes(grad_raw),
            cosine_wide,
            sine_wide,
            grad_kv_parts,
        ],
    )[0]
    grad_conv_low = outer_grad(normed_one, grad_conv).astype(low)
    grad_conv_in = scatter_blocks(after(grad_conv_low, grad_rest_in))
    grad_proj_weight = call(
        unpack_in,
        [shaped(in_weight.shape, jnp.float32)],
        place,
        [
            swap_heads(part.reshape(4, rows_in, -1))
            for part in (grad_conv_in, grad_rest_in)
        ],
    )[0]
    conv_moved, rest_moved = call(
        relative_order,
        [shaped((span_rows, conv_columns), low), shaped((span_rows, rest_columns), low)],
        place,
        [grad_conv, grad_rest],
        after=[grad_conv_low],
    )

    def back_in(part):
        return times_transposed(rest_moved[part], weights_rest) + times_transposed(
            conv_moved[part], weights_conv
        )

    grad_normed_other = back_in(slice(pair_rows, span_rows)).astype(low)
    grad_normed_own = back_in(slice(0, pair_rows))
    grad_normed_other = after(grad_normed_other, grad_out_sum)
    grad_input = call(
        partial(back_one, ring=ring),
        [shaped((row_count, D), low)],
        place,
        [
            scatter_pairs(grad_normed_own, grad_normed_other, low),
            tokens,
            grad_hidden,
            first_gain[None, :],
        ],
        scratch=[pltpu.VMEM((row_count, D), jnp.float32)],
    )[0]
    first_line = jnp.sum(
        weights_conv.astype(jnp.float32) * grad_conv_low.astype(jnp.float32), axis=1
    ) + jnp.sum(weights_rest.astype(jnp.float32) * grad_rest_low.astype(jnp.float32), axis=1)
    first_line = first_line.reshape(blocks, 4, -1)
    first_line = jnp.stack([first_line[ring.index(k)] for k in range(blocks)], axis=1).reshape(D)

    def own_part(values_in, total):
        return lax.dynamic_update_slice_in_dim(
            jnp.zeros(values_in.shape[:-1] + (total,), jnp.float32),
            values_in,
            head_index * values_in.shape[-1],
            values_in.ndim - 1,
        )

    small = [
        first_line / first_gain,
        grad_second[0],
        jnp.concatenate(
            [own_part(grad_taps[:, :inner_columns], mamba_width), grad_taps[:, inner_columns:]],
            axis=1,
        ),
        jnp.concatenate(
            [own_part(grad_shift[:inner_columns], mamba_width), grad_shift[inner_columns:]]
        ),
        own_part(grad_step_shift, MH),
        own_part(grad_rate, MH),
        own_part(grad_skip, MH),
    ]
    line = jnp.concatenate([part.reshape(-1) for part in small])
    line = jnp.pad(line, (0, -line.shape[0] % 1024)).reshape(-1, 128)
    line = summed_over(summed_over(line, "head"), "blk").reshape(-1)
    summed_small = []
    at = 0
    for part in small:
        summed_small.append(line[at : at + part.size].reshape(part.shape))
        at += part.size
    return (
        block_output[None],
        grad_input[None],
        grad_proj_weight,
        grad_mix_weight,
        grad_ffn_weight,
        grad_down.astype(jnp.float32),
        *summed_small,
    )


def own_first(chunks, mine, order=(0, 1, 2, 3)):
    return [lax.dynamic_index_in_dim(chunks, jnp.bitwise_xor(mine, d), 0, False) for d in order]


def solution(mesh):
    placed = (
        P("blk", "head", None),
        P("blk", "head", None),
        P("blk", None),
        P(("head", "blk"), None),
        P(("head", "blk"), None),
        P(("head", "blk"), None),
        P(("head", "blk"), None),
        P(),
        P(),
        P(),
        P(),
        P(),
        P(),
        P(),
    )
    return jax.shard_map(
        per_device,
        mesh=mesh,
        in_specs=placed,
        out_specs=(
            P("blk", "head", None),
            P("blk", "head", None),
            P(("head", "blk"), None),
            P(("head", "blk"), None),
            P(("head", "blk"), None),
            P(("head", "blk"), None),
            P(),
            P(),
            P(),
            P(),
            P(),
            P(),
            P(),
        ),
        check_vma=False,
    )
```

time: 854 us -> 787 us (0.922)
  waiting for transfers between devices: 278 us -> 342 us
  local copies, waits for them, and re-layouts: 126 us -> 74.7 us
  starting transfers between devices: 123 us -> 76.7 us
  other arithmetic: 80.4 us -> 40.9 us
  blocking collectives: 63.9 us -> 42.5 us
  Pallas kernels: 60.8 us -> 77.3 us
  matrix products: 89.1 us -> 103 us
    ppermute x16 -> x2, waiting for transfers between devices: 49.2 us -> 3.78 us  [passed_along(): return lax.ppermute(shard, axis, pairs)]
    ppermute x2, waiting for transfers between devices: 0.01 us -> 44 us  [the longest x1 28.8 us: per_device(): lax.ppermute(after(out_weight.astype(low), rest_rows), ('head', 'blk'), o...]
    all_gather x5, waiting for transfers between devices: 25.7 us -> 58.9 us  [gather_blocks(): lax.all_gather(shard, 'blk', axis=0, tiled=True, axis_index_groups=[ring_...]
    all_to_all x7 -> x9, waiting for transfers between devices: 17.1 us -> 48.9 us  [the longest x1 19.5 us: per_device(): lax.all_to_all(after(kv_mine, state_sent), 'blk', split_axis=0, concat_ax...]
    all_gather x1 -> x0, blocking collectives: 24.7 us -> none  [per_device(): flags_all = lax.all_gather(start_flags[0], 'blk', axis=0, tiled=True)]
    ppermute x16 -> x2, starting transfers between devices: 28.5 us -> 5.78 us  [passed_along(): return lax.ppermute(shard, axis, pairs)]
    slice x48 -> x20, local copies, waits for them, and re-layouts: 19.4 us -> 2.85 us  [the longest x1 0.93 us: per_device(): grad_second[0]]
    pallas_call x6 -> x22, Pallas kernels: 60.8 us -> 77.3 us  [the longest x20 54.6 us: call(): pl.pallas_call(body, out_shape=outputs, in_specs=[pl.BlockSpec(memory_spa...]
  transfers between devices with their start and end apart: 62 -> 58, of which waited for: 33 -> 32; matrix products, arithmetic and copies ran while one was open for 28% -> 19% of each run, Pallas kernels for 7% -> 10%
where the time goes in v3:
time: 787 us; the launch traced here: 773 us
  waiting for transfers between devices  342 us (43%)
  matrix products  103 us (13%)
  Pallas kernels  77.3 us (10%)
  starting transfers between devices  76.7 us (10%)
  local copies, waits for them, and re-layouts  74.7 us (9%)
  blocking collectives  42.5 us (5%)
  other arithmetic  40.9 us (5%)
  between operations  16.3 us (2%)
    ppermute x27, waiting for transfers between devices, from_head(): lax.ppermute(shard, 'head', [(i, i ^ distance) for i in range(peers)])  90.1 us
    reduce_scatter x5, waiting for transfers between devices, scatter_blocks(): lax.psum_scatter(partial_sums, 'blk', scatter_dimension=0, tiled=True, ax...  88.9 us
    unnamed x295, local copies, waits for them, and re-layouts  63.2 us
    all_gather x5, waiting for transfers between devices, gather_blocks(): lax.all_gather(shard, 'blk', axis=0, tiled=True, axis_index_groups=[ring_...  58.9 us
    pallas_call x20, Pallas kernels, call(): pl.pallas_call(body, out_shape=outputs, in_specs=[pl.BlockSpec(memory_spa...  54.6 us
    all_to_all x3, blocking collectives, swap_heads(): lax.all_to_all(pieces, 'head', split_axis=0, concat_axis=0, tiled=True)  42.5 us
    dot_general x8, matrix products, times_transposed(): lax.dot_general(grad_side, weight, (((1,), (1,)), ((), ())), preferred_el...  38.5 us
    dot_general x5, matrix products, outer_grad(): lax.dot_general(left_side, grad_side, (((0,), (0,)), ((), ())), preferred...  29 us
  transfers between devices with their start and end apart: 58, of which 32 were waited for; matrix products, arithmetic and copies ran while one was open for 19% of the time, Pallas kernels for 10%

profile of v3, /device:TPU:16, one launch (start us, length us, event | category | flops | bytes accessed | tf_op | source)
XLA Modules:
  0.0 773.3 jit_solution(14287665365537258465)
XLA Ops:
  9.6 12.8 %all_to_all.60 = bf16[4,64,1152]{2,1,0:T(8,128)(2,1)} all-to-all(bf16[4,64,1152]{2,1,0:T(8,128)(2,1)S(1)} %get-tuple-element.64), channel_id=1, replica_groups=mesh['head'=4,'blk'=8] {'head'}, dimensions={0} | all-to-all | bytes 1179648 | tf_op jit(solution)/shard_map/all_to_all | solution.py:84
  22.5 11.9 %all_to_all.61 = bf16[4,64,1024]{2,1,0:T(8,128)(2,1)} all-to-all(bf16[4,64,1024]{2,1,0:T(8,128)(2,1)S(1)} %get-tuple-element.67), channel_id=1, replica_groups=mesh['head'=4,'blk'=8] {'head'}, dimensions={0} | all-to-all | bytes 1048576 | tf_op jit(solution)/shard_map/all_to_all | solution.py:84
  37.7 28.8 %collective-permute-done.14 = bf16[128,2048]{1,0:T(8,128)(2,1)S(1)} collective-permute-done((bf16[128,2048]{1,0:T(8,128)(2,1)S(1)}, bf16[128,2048]{1,0:T(8,128)(2,1)S(1)}, u32[]{:S(2)}, u32[]{:S(2)}) %collective-permute-start.14) | collective-permute-done | bytes 524320 | tf_op jit(solution)/shard_map/ppermute | solution.py:947
  68.2 17.7 %all_to_all.62 = bf16[4,64,2048]{2,1,0:T(8,128)(2,1)} all-to-all(bf16[4,64,2048]{2,1,0:T(8,128)(2,1)S(1)} %shard_map.240), channel_id=1, replica_groups=mesh['head'=4,'blk'=8] {'head'}, dimensions={0} | all-to-all | bytes 2097152 | tf_op jit(solution)/shard_map/all_to_all | solution.py:84
  90.5 11.0 %collective-permute-done.refs_1_ = bf16[128,2048]{1,0:T(8,128)(2,1)S(1)} collective-permute-done((bf16[128,2048]{1,0:T(8,128)(2,1)S(1)}, bf16[128,2048]{1,0:T(8,128)(2,1)S(1)}, u32[]{:S(2)}, u32[]{:S(2)}) %collective-permute-start) | collective-permute-done | bytes 524320 | tf_op jit(solution)/shard_map/ppermute | solution.py:60
  102.9 3.8 collective-permute-done.8
  106.7 3.0 collective-permute-start.9
  116.8 6.0 fusion.61
  123.5 4.4 collective-permute-done.3.refs_2_
  137.0 3.4 fusion.5
  142.0 8.1 %shard_map.241 = (f32[512,768]{1,0:T(8,128)S(1)}, bf16[8,112,256]{2,1,0:T(8,128)(2,1)}, f32[512,128]{1,0:T(8,128)S(1)}, f32[8,128]{1,0:T(8,128)S(1)}) custom-call(s32[8]{0:T(128)S(1)} %stack.40.place_ref, f32[512,768]{1,0:T(8,128)S(1)} %slice.412.refs_0_.refs_4_.refs_3_, f32[512,256]{1,0:T(8,128)S(1)} %get-tuple-element.144.refs_1_, ...), custom_call_target="tpu_custom_call" | custom-call | flops 6000000000 | bytes 5705728 | tf_op jit(solution)/shard_map/pallas_call | solution.py:761
  152.1 5.2 all-to-all-start.5
  162.9 9.7 %collective-permute-done.11 = bf16[128,2048]{1,0:T(8,128)(2,1)} collective-permute-done((bf16[128,2048]{1,0:T(8,128)(2,1)S(1)}, bf16[128,2048]{1,0:T(8,128)(2,1)}, u32[]{:S(2)}, u32[]{:S(2)}) %collective-permute-start.11) | collective-permute-done | bytes 524320 | tf_op jit(solution)/shard_map/ppermute | solution.py:60
  172.5 19.5 %all-to-all-done.5 = bf16[8,512,128]{2,1,0:T(8,128)(2,1)S(1)} async-done(((bf16[8,512,128]{2,1,0:T(8,128)(2,1)}), bf16[8,512,128]{2,1,0:T(8,128)(2,1)S(1)}, u32[]{:S(2)}, u32[]{:S(2)}) %all-to-all-start.5) | async-done | bytes 1048608 | tf_op jit(solution)/shard_map/all_to_all | solution.py:1077
  192.0 6.4 all-to-all-start.3
  205.0 8.1 %all-to-all-done.3.refs_0_ = bf16[8,112,256]{2,1,0:T(8,128)(2,1)S(1)} async-done(((bf16[8,112,256]{2,1,0:T(8,128)(2,1)}), bf16[8,112,256]{2,1,0:T(8,128)(2,1)S(1)}, u32[]{:S(2)}, u32[]{:S(2)}) %all-to-all-start.3) | async-done | bytes 458784 | tf_op jit(solution)/shard_map/all_to_all | solution.py:1047
  214.5 6.7 all-to-all-start.4
  221.2 5.1 fusion.62.refs_0_
  230.1 12.7 %shard_map.245 = (f32[512,256]{1,0:T(8,128)S(1)}, f32[2,512,128]{2,1,0:T(8,128)S(1)}) custom-call(s32[3]{0:T(128)S(1)} %pad_add_fusion.4.refs_0_, bf16[512,256]{1,0:T(8,128)(2,1)S(1)} %get-tuple-element.74.refs_1_, s32[512,128]{1,0:T(8,128)S(1)} %broadcast_in_dim.23.refs_2_, bf16[8,512,128]{2,1,0:T(8,128)(2,1)S(1)} %get-tuple-element.146.refs_3_, ...), custom_call_target="tpu_custom_call" | custom-call | flops 20000000000 | bytes 4000000 | tf_op jit(solution)/shard_map/pallas_call | solution.py:785
  257.2 3.8 fusion.31
  262.5 2.7 collective-permute-done.15
  266.1 13.3 %collective-permute-done.16 = bf16[128,2048]{1,0:T(8,128)(2,1)S(1)} collective-permute-done((bf16[128,2048]{1,0:T(8,128)(2,1)S(1)}, bf16[128,2048]{1,0:T(8,128)(2,1)S(1)}, u32[]{:S(2)}, u32[]{:S(2)}) %collective-permute-start.16) | collective-permute-done | bytes 524320 | tf_op jit(solution)/shard_map/ppermute | solution.py:60
  281.4 12.6 %collective-permute-done.17 = bf16[128,2048]{1,0:T(8,128)(2,1)S(1)} collective-permute-done((bf16[128,2048]{1,0:T(8,128)(2,1)S(1)}, bf16[128,2048]{1,0:T(8,128)(2,1)S(1)}, u32[]{:S(2)}, u32[]{:S(2)}) %collective-permute-start.17) | collective-permute-done | bytes 524320 | tf_op jit(solution)/shard_map/ppermute | solution.py:60
  297.4 20.2 %all-gather.12.cloned.1.call-done = bf16[2048,2048]{1,0:T(8,128)(2,1)} async-done(((bf16[256,2048]{1,0:T(8,128)(2,1)}), bf16[2048,2048]{1,0:T(8,128)(2,1)}) %all-gather.12.cloned.1.call-update) | async-done | bytes 8388624 | tf_op jit(solution)/shard_map/all_gather | solution.py:45
  317.6 10.6 %fusion.63 = f32[512,2048]{1,0:T(8,128)} fusion(bf16[512,2048]{1,0:T(8,128)(2,1)} %constant_dynamic-update-slice_fusion.4, bf16[2048,2048]{1,0:T(8,128)(2,1)} %all-gather.12.cloned.1.call-done), kind=kOutput, calls=%fused_computation.171 | convolution fusion | flops 4294967296 | bytes 14680064 | tf_op jit(solution)/shard_map/dot_general | solution.py:1106
  328.1 38.8 %all-gather.14.cloned.1.call-done = bf16[1024,2048]{1,0:T(8,128)(2,1)} async-done(((bf16[128,2048]{1,0:T(8,128)(2,1)}), bf16[1024,2048]{1,0:T(8,128)(2,1)}) %all-gather.14.cloned.1.call-update) | async-done | bytes 4194320 | tf_op jit(solution)/shard_map/all_gather | solution.py:45
  366.9 8.6 %multiply_convert_fusion.1 = (bf16[512,1024]{1,0:T(8,128)(2,1)}, bf16[512,1024]{1,0:T(8,128)(2,1)}, bf16[512,1024]{1,0:T(8,128)(2,1)S(1)}) fusion(f32[512,2048]{1,0:T(8,128)} %fusion.63, bf16[512,2048]{1,0:T(8,128)(2,1)} %constant_dynamic-update-slice_fusion.refs_6_, bf16[1024,2048]{1,0:T(8,128)(2,1)} %all-gather.14.cloned.1.call-done), kind=kOutput, calls=%fused_computation.35 | convolution fusion | flops 2155347968 | bytes 13631488 | tf_op jit(solution)/shard_map/dot_general | solution.py:326
  376.5 4.4 convolution_convert_fusion.4.refs_4_
  382.8 7.8 %fusion.19 = f32[256,2048]{1,0:T(8,128)} fusion(bf16[2048,2048]{1,0:T(8,128)(2,1)} %all-gather.12.cloned.1.call-done, bf16[512,2048]{1,0:T(8,128)(2,1)S(1)} %pad_maximum_fusion), kind=kOutput, calls=%fused_computation.62 | convolution fusion | flops 2147483648 | bytes 11534336 | tf_op jit(solution)/shard_map/dot_general | solution.py:326
  390.7 8.4 %convolution_convert_fusion.1.refs_5_ = bf16[2048,2048]{1,0:T(8,128)(2,1)} fusion(bf16[512,2048]{1,0:T(8,128)(2,1)} %constant_dynamic-update-slice_fusion.4, bf16[512,2048]{1,0:T(8,128)(2,1)S(1)} %pad_maximum_fusion), kind=kOutput, calls=%fused_computation.3 | convolution fusion | flops 4299161600 | bytes 12582912 | tf_op jit(solution)/shard_map/dot_general | solution.py:320
  399.1 30.4 %reduce-scatter.6.cloned.1.call-done = bf16[128,2048]{1,0:T(8,128)(2,1)} async-done(((bf16[1024,2048]{1,0:T(8,128)(2,1)}), bf16[128,2048]{1,0:T(8,128)(2,1)}) %reduce-scatter.6.cloned.1.call-update) | async-done | bytes 524304 | tf_op jit(solution)/shard_map/reduce_scatter | solution.py:49
  429.5 6.1 convolution_convert_fusion.6
  435.8 2.6 collective-permute-done.20
  440.3 12.5 %collective-permute-done.21 = bf16[128,2048]{1,0:T(8,128)(2,1)S(1)} collective-permute-done((bf16[128,2048]{1,0:T(8,128)(2,1)S(1)}, bf16[128,2048]{1,0:T(8,128)(2,1)S(1)}, u32[]{:S(2)}, u32[]{:S(2)}) %collective-permute-start.21) | collective-permute-done | bytes 524320 | tf_op jit(solution)/shard_map/ppermute | solution.py:60
  456.8 11.8 %collective-permute-done.22 = bf16[128,2048]{1,0:T(8,128)(2,1)S(1)} collective-permute-done((bf16[128,2048]{1,0:T(8,128)(2,1)S(1)}, bf16[128,2048]{1,0:T(8,128)(2,1)S(1)}, u32[]{:S(2)}, u32[]{:S(2)}) %collective-permute-start.22) | collective-permute-done | bytes 524320 | tf_op jit(solution)/shard_map/ppermute | solution.py:60
  470.6 4.4 convolution_convert_fusion.3.refs_8_
  475.0 44.8 %reduce-scatter.8.cloned.1.call-done = bf16[256,2048]{1,0:T(8,128)(2,1)} async-done(((bf16[2048,2048]{1,0:T(8,128)(2,1)}), bf16[256,2048]{1,0:T(8,128)(2,1)}) %reduce-scatter.8.cloned.1.call-update) | async-done | bytes 1048592 | tf_op jit(solution)/shard_map/reduce_scatter | solution.py:49
  519.9 4.7 convolution_convert_fusion.5
  527.1 3.9 shard_map.249
  534.4 5.3 all-to-all-start.6
  547.5 9.9 %shard_map.251 = (f32[512,256]{1,0:T(8,128)S(1)}, bf16[8,512,128]{2,1,0:T(8,128)(2,1)S(1)}, bf16[8,512,128]{2,1,0:T(8,128)(2,1)S(1)}) custom-call(s32[3]{0:T(128)S(1)} %pad_add_fusion.4.refs_0_, bf16[512,256]{1,0:T(8,128)(2,1)S(1)} %copy-done.70, s32[512,128]{1,0:T(8,128)S(1)} %copy-done.56, bf16[8,512,128]{2,1,0:T(8,128)(2,1)S(1)} %copy-done.24, ...), custom_call_target="tpu_custom_call" | custom-call | flops 30000001024 | bytes 4000000 | tf_op jit(solution)/shard_map/pallas_call | solution.py:825
  559.7 5.3 multiply_reduce_fusion.1
  566.1 13.6 %reduce-scatter.10.cloned.1.call-done = bf16[128,2048]{1,0:T(8,128)(2,1)} async-done(((bf16[1024,2048]{1,0:T(8,128)(2,1)}), bf16[128,2048]{1,0:T(8,128)(2,1)}) %reduce-scatter.10.cloned.1.call-update) | async-done | bytes 524304 | tf_op jit(solution)/shard_map/reduce_scatter | solution.py:49
  579.7 3.6 fusion.29
  590.8 5.1 all-to-all-start.7
  595.9 2.8 add_convert_fusion.refs_11_
  598.7 3.1 collective-permute-done.26
  604.3 5.8 all-to-all-done.7
  610.1 6.6 all-to-all-start.8
  622.8 19.0 %shard_map.253 = (f32[512,768]{1,0:T(8,128)S(1)}, f32[512,256]{1,0:T(8,128)S(1)}, f32[512,256]{1,0:T(8,128)S(1)}, f32[512,128]{1,0:T(8,128)S(1)}, f32[512,128]{1,0:T(8,128)S(1)}) custom-call(s32[8]{0:T(128)S(1)} %stack.40.place_ref, f32[512,768]{1,0:T(8,128)S(1)} %copy-done.20, f32[512,256]{1,0:T(8,128)S(1)} %copy-done.41, f32[512,256]{1,0:T(8,128)S(1)} %copy-done.39, ...), custom_call_target="tpu_custom_call" | custom-call | flops 10000000000 | bytes 10488832 | tf_op jit(solution)/shard_map/pallas_call | solution.py:761
  643.9 3.4 multiply_reduce_fusion.5
  648.2 3.4 collective-permute-start.28
  668.7 6.5 multiply_reduce_fusion
  682.8 4.7 fusion.21
  693.0 2.5 collective-permute-start.36
  696.5 3.5 all-to-all-start.11
  701.7 3.9 fusion.23
  708.5 2.7 convolution_add_fusion.1
  711.2 3.3 all-to-all-done.11.refs_0_
  722.7 3.5 all-to-all-start.10
  727.4 15.2 %collective-permute-done.33 = bf16[128,2048]{1,0:T(8,128)(2,1)S(1)} collective-permute-done((bf16[128,2048]{1,0:T(8,128)(2,1)S(1)}, bf16[128,2048]{1,0:T(8,128)(2,1)S(1)}, u32[]{:S(2)}, u32[]{:S(2)}) %collective-permute-start.33) | collective-permute-done | bytes 524320 | tf_op jit(solution)/shard_map/ppermute | solution.py:1178
  743.7 6.5 all-to-all-done.10.refs_1_
  750.2 4.5 all-to-all-start.9
  758.5 5.7 all-to-all-done.9.refs_0_
  (539 shorter events, 171.0 us)
Async XLA Ops:
  7.2 109.6 %all-gather.6.cloned.1.call-start = ((), (), s32[]{:S(2)}) async-start(), calls=%async_computation.17 | async-start | bytes 5308416 | tf_op jit(solution)/shard_map/all_gather | solution.py:45
  9.6 57.8 %copy-start.13 = (f32[64,8192]{1,0:T(8,128)S(1)}, f32[64,8192]{1,0:T(8,128)}, u32[]{:S(2)}) copy-start(f32[64,8192]{1,0:T(8,128)} %refs_0_.2) | copy-start | bytes 6291460
  22.4 198.8 %all-gather.8.cloned.1.call-start = ((), (), s32[]{:S(2)}) async-start(), calls=%async_computation.18 | async-start | bytes 4718592 | tf_op jit(solution)/shard_map/all_gather | solution.py:45
  34.4 222.7 %all-gather.10.cloned.1.call-start = ((), (), s32[]{:S(2)}) async-start(), calls=%async_computation.19 | async-start | bytes 4718592 | tf_op jit(solution)/shard_map/all_gather | solution.py:45
  35.8 30.8 %collective-permute-start.14 = (bf16[128,2048]{1,0:T(8,128)(2,1)S(1)}, bf16[128,2048]{1,0:T(8,128)(2,1)S(1)}, u32[]{:S(2)}, u32[]{:S(2)}) collective-permute-start(bf16[128,2048]{1,0:T(8,128)(2,1)S(1)} %convert_element_type.153), channel_id=1, source_target_pairs={{0,0},{1,2},{2,8},{3,10},{4,16},{5,18},{6,24},{7,26},{8,4},{9,6},{... | collective-permute-start | bytes 1572872 | tf_op jit(solution)/shard_map/ppermute | solution.py:947
  67.4 250.2 %all-gather.12.cloned.1.call-start = ((), (), s32[]{:S(2)}) async-start(), calls=%async_computation.20 | async-start | bytes 9437184 | tf_op jit(solution)/shard_map/all_gather | solution.py:45
  68.2 34.4 %copy-start.134 = (f32[48]{0:T(128)S(1)}, f32[48]{0:T(128)}, u32[]{:S(2)}) copy-start(f32[48]{0:T(128)} %param.26) | copy-start | bytes 580
  68.2 34.5 %copy-start.139 = (f32[48]{0:T(128)S(1)}, f32[48]{0:T(128)}, u32[]{:S(2)}) copy-start(f32[48]{0:T(128)} %param.25) | copy-start | bytes 580
  68.2 34.6 %slice-start = ((f32[4,3584]{1,0:T(4,128)}), f32[4,512]{1,0:T(4,128)S(1)}, s32[]{:S(2)}) async-start(f32[4,3584]{1,0:T(4,128)} %param.23), calls=%async_computation.27 | async-start | bytes 16384 | tf_op jit(solution)/shard_map/slice | solution.py:988
  68.2 43.0 %copy-start.59 = (f32[2048]{0:T(1024)S(1)}, f32[2048]{0:T(1024)}, u32[]{:S(2)}) copy-start(f32[2048]{0:T(1024)} %param.21) | copy-start | bytes 24580
  86.3 16.1 %collective-permute-start.7 = (s32[4096]{0:T(1024)S(1)}, s32[4096]{0:T(1024)S(1)}, u32[]{:S(2)}, u32[]{:S(2)}) collective-permute-start(s32[4096]{0:T(1024)S(1)} %dynamic_update_slice.20), channel_id=1, source_target_pairs={{0,1},{1,0},{2,3},{3,2},{4,5},{5,4},{6,7},{7,6},{8,9},{9,8},{10,11... | collective-permute-start | bytes 49160 | tf_op jit(solution)/shard_map/ppermute | solution.py:885
  88.2 13.4 %collective-permute-start = (bf16[128,2048]{1,0:T(8,128)(2,1)S(1)}, bf16[128,2048]{1,0:T(8,128)(2,1)S(1)}, u32[]{:S(2)}, u32[]{:S(2)}) collective-permute-start(bf16[128,2048]{1,0:T(8,128)(2,1)S(1)} %bitcast.85), channel_id=1, source_target_pairs={{0,16},{8,24},{16,0},{24,8},{1,17},{9,25},{17,1},{25,9},{2,18},{10... | collective-permute-start | bytes 1572872 | tf_op jit(solution)/shard_map/ppermute | solution.py:60
  90.5 19.1 %collective-permute-start.1 = (bf16[128,2048]{1,0:T(8,128)(2,1)S(1)}, bf16[128,2048]{1,0:T(8,128)(2,1)S(1)}, u32[]{:S(2)}, u32[]{:S(2)}) collective-permute-start(bf16[128,2048]{1,0:T(8,128)(2,1)S(1)} %bitcast.86), channel_id=1, source_target_pairs={{0,8},{8,0},{16,24},{24,16},{1,9},{9,1},{17,25},{25,17},{2,10},{10... | collective-permute-start | bytes 1572872 | tf_op jit(solution)/shard_map/ppermute | solution.py:60
  101.6 8.9 %collective-permute-start.2 = (bf16[128,2048]{1,0:T(8,128)(2,1)S(1)}, bf16[128,2048]{1,0:T(8,128)(2,1)S(1)}, u32[]{:S(2)}, u32[]{:S(2)}) collective-permute-start(bf16[128,2048]{1,0:T(8,128)(2,1)S(1)} %collective-permute-done.refs_1_), channel_id=1, source_target_pairs={{0,8},{8,0},{16,24},{24,16},{1,9},{9,1},{17,25},{25,17},{2,10},{10... | collective-permute-start | bytes 1572872 | tf_op jit(solution)/shard_map/ppermute | solution.py:60
  102.6 4.1 collective-permute-start.8
  106.7 16.8 %collective-permute-start.9 = (s32[4096]{0:T(1024)S(1)}, s32[4096]{0:T(1024)S(1)}, u32[]{:S(2)}, u32[]{:S(2)}) collective-permute-start(s32[4096]{0:T(1024)S(1)} %add.236), channel_id=1, source_target_pairs={{0,4},{1,5},{2,6},{3,7},{4,0},{5,1},{6,2},{7,3},{8,12},{9,13},{10,... | collective-permute-start | bytes 49160 | tf_op jit(solution)/shard_map/ppermute | solution.py:885
  122.9 5.0 collective-permute-start.3
  123.5 4.6 collective-permute-start.4
  127.9 1.3 collective-permute-start.5
  130.0 6.7 collective-permute-start.6
  152.1 40.0 %all-to-all-start.5 = ((bf16[8,512,128]{2,1,0:T(8,128)(2,1)}), bf16[8,512,128]{2,1,0:T(8,128)(2,1)S(1)}, u32[]{:S(2)}, u32[]{:S(2)}) async-start(bf16[8,512,128]{2,1,0:T(8,128)(2,1)} %shard_map.244), calls=%async_computation.5 | async-start | bytes 2097152 | tf_op jit(solution)/shard_map/all_to_all | solution.py:1077
  160.0 12.5 %collective-permute-start.11 = (bf16[128,2048]{1,0:T(8,128)(2,1)S(1)}, bf16[128,2048]{1,0:T(8,128)(2,1)}, u32[]{:S(2)}, u32[]{:S(2)}) collective-permute-start(bf16[128,2048]{1,0:T(8,128)(2,1)S(1)} %bitcast.92), channel_id=1, source_target_pairs={{0,16},{8,24},{16,0},{24,8},{1,17},{9,25},{17,1},{25,9},{2,18},{10... | collective-permute-start | bytes 1572872 | tf_op jit(solution)/shard_map/ppermute | solution.py:60
  161.5 39.7 %collective-permute-start.12 = (bf16[128,2048]{1,0:T(8,128)(2,1)S(1)}, bf16[128,2048]{1,0:T(8,128)(2,1)}, u32[]{:S(2)}, u32[]{:S(2)}) collective-permute-start(bf16[128,2048]{1,0:T(8,128)(2,1)S(1)} %bitcast.93), channel_id=1, source_target_pairs={{0,8},{8,0},{16,24},{24,16},{1,9},{9,1},{17,25},{25,17},{2,10},{10... | collective-permute-start | bytes 1572872 | tf_op jit(solution)/shard_map/ppermute | solution.py:60
  172.5 30.6 %collective-permute-start.13 = (bf16[128,2048]{1,0:T(8,128)(2,1)}, bf16[128,2048]{1,0:T(8,128)(2,1)}, u32[]{:S(2)}, u32[]{:S(2)}) collective-permute-start(bf16[128,2048]{1,0:T(8,128)(2,1)} %collective-permute-done.11), channel_id=1, source_target_pairs={{0,8},{8,0},{16,24},{24,16},{1,9},{9,1},{17,25},{25,17},{2,10},{10... | collective-permute-start | bytes 1572872 | tf_op jit(solution)/shard_map/ppermute | solution.py:60
  192.0 21.0 %all-to-all-start.3 = ((bf16[8,112,256]{2,1,0:T(8,128)(2,1)}), bf16[8,112,256]{2,1,0:T(8,128)(2,1)S(1)}, u32[]{:S(2)}, u32[]{:S(2)}) async-start(bf16[8,112,256]{2,1,0:T(8,128)(2,1)} %get-tuple-element.71), calls=%async_computation.3 | async-start | bytes 917504 | tf_op jit(solution)/shard_map/all_to_all | solution.py:1047
  198.5 168.4 %all-gather.14.cloned.1.call-start = ((), (), s32[]{:S(2)}) async-start(), calls=%async_computation.21 | async-start | bytes 4718592 | tf_op jit(solution)/shard_map/all_gather | solution.py:45
  201.2 26.9 %collective-permute-start.10 = (bf16[8,512,128]{2,1,0:T(8,128)(2,1)S(1)}, bf16[8,512,128]{2,1,0:T(8,128)(2,1)}, u32[]{:S(2)}, u32[]{:S(2)}) collective-permute-start(bf16[8,512,128]{2,1,0:T(8,128)(2,1)S(1)} %all-to-all-done.5), channel_id=1, source_target_pairs={{0,8},{8,0},{16,24},{24,16},{1,9},{9,1},{17,25},{25,17},{2,10},{10... | collective-permute-start | bytes 3145736 | tf_op jit(solution)/shard_map/ppermute | solution.py:60
  214.5 32.6 %all-to-all-start.4 = ((bf16[8,96,256]{2,1,0:T(8,128)(2,1)}), bf16[8,96,256]{2,1,0:T(8,128)(2,1)S(1)}, u32[]{:S(2)}, u32[]{:S(2)}) async-start(bf16[8,96,256]{2,1,0:T(8,128)(2,1)} %shard_map.242.refs_5_), calls=%async_computation.4 | async-start | bytes 786432 | tf_op jit(solution)/shard_map/all_to_all | solution.py:1055
  221.2 208.3 %reduce-scatter.6.cloned.1.call-start = ((), (), s32[]{:S(2)}) async-start(), calls=%async_computation.22 | async-start | bytes 4718592 | tf_op jit(solution)/shard_map/reduce_scatter | solution.py:49
  261.0 4.2 collective-permute-start.15
  265.3 14.0 %collective-permute-start.16 = (bf16[128,2048]{1,0:T(8,128)(2,1)S(1)}, bf16[128,2048]{1,0:T(8,128)(2,1)S(1)}, u32[]{:S(2)}, u32[]{:S(2)}) collective-permute-start(bf16[128,2048]{1,0:T(8,128)(2,1)S(1)} %fusion.16), channel_id=1, source_target_pairs={{0,16},{8,24},{16,0},{24,8},{1,17},{9,25},{17,1},{25,9},{2,18},{10... | collective-permute-start | bytes 1572872 | tf_op jit(solution)/shard_map/ppermute | solution.py:60
  280.7 172.3 %copy-start.9 = (f32[128,2048]{1,0:T(8,128)}, f32[128,2048]{1,0:T(8,128)S(1)}, u32[]{:S(2)}) copy-start(f32[128,2048]{1,0:T(8,128)S(1)} %get-tuple-element.80.refs_1_) | copy-start | bytes 3145732
  280.7 13.3 %collective-permute-start.17 = (bf16[128,2048]{1,0:T(8,128)(2,1)S(1)}, bf16[128,2048]{1,0:T(8,128)(2,1)S(1)}, u32[]{:S(2)}, u32[]{:S(2)}) collective-permute-start(bf16[128,2048]{1,0:T(8,128)(2,1)S(1)} %get-tuple-element.81), channel_id=1, source_target_pairs={{0,16},{8,24},{16,0},{24,8},{1,17},{9,25},{17,1},{25,9},{2,18},{10... | collective-permute-start | bytes 1572872 | tf_op jit(solution)/shard_map/ppermute | solution.py:60
  281.4 14.3 %collective-permute-start.18 = (bf16[128,2048]{1,0:T(8,128)(2,1)S(1)}, bf16[128,2048]{1,0:T(8,128)(2,1)S(1)}, u32[]{:S(2)}, u32[]{:S(2)}) collective-permute-start(bf16[128,2048]{1,0:T(8,128)(2,1)S(1)} %get-tuple-element.81), channel_id=1, source_target_pairs={{0,8},{8,0},{16,24},{24,16},{1,9},{9,1},{17,25},{25,17},{2,10},{10... | collective-permute-start | bytes 1572872 | tf_op jit(solution)/shard_map/ppermute | solution.py:60
  294.0 2.6 collective-permute-start.19
  380.9 139.0 %reduce-scatter.8.cloned.1.call-start = ((), (), s32[]{:S(2)}) async-start(), calls=%async_computation.23 | async-start | bytes 9437184 | tf_op jit(solution)/shard_map/reduce_scatter | solution.py:49
  429.5 150.2 %reduce-scatter.10.cloned.1.call-start = ((), (), s32[]{:S(2)}) async-start(), calls=%async_computation.24 | async-start | bytes 4718592 | tf_op jit(solution)/shard_map/reduce_scatter | solution.py:49
  435.7 2.7 collective-permute-start.20
  438.8 14.0 %collective-permute-start.21 = (bf16[128,2048]{1,0:T(8,128)(2,1)S(1)}, bf16[128,2048]{1,0:T(8,128)(2,1)S(1)}, u32[]{:S(2)}, u32[]{:S(2)}) collective-permute-start(bf16[128,2048]{1,0:T(8,128)(2,1)S(1)} %fusion.14), channel_id=1, source_target_pairs={{0,16},{8,24},{16,0},{24,8},{1,17},{9,25},{17,1},{25,9},{2,18},{10... | collective-permute-start | bytes 1572872 | tf_op jit(solution)/shard_map/ppermute | solution.py:60
  455.4 13.2 %collective-permute-start.22 = (bf16[128,2048]{1,0:T(8,128)(2,1)S(1)}, bf16[128,2048]{1,0:T(8,128)(2,1)S(1)}, u32[]{:S(2)}, u32[]{:S(2)}) collective-permute-start(bf16[128,2048]{1,0:T(8,128)(2,1)S(1)} %get-tuple-element.87), channel_id=1, source_target_pairs={{0,16},{8,24},{16,0},{24,8},{1,17},{9,25},{17,1},{25,9},{2,18},{10... | collective-permute-start | bytes 1572872 | tf_op jit(solution)/shard_map/ppermute | solution.py:60
  456.8 11.9 %collective-permute-start.23 = (bf16[128,2048]{1,0:T(8,128)(2,1)S(1)}, bf16[128,2048]{1,0:T(8,128)(2,1)S(1)}, u32[]{:S(2)}, u32[]{:S(2)}) collective-permute-start(bf16[128,2048]{1,0:T(8,128)(2,1)S(1)} %get-tuple-element.87), channel_id=1, source_target_pairs={{0,8},{8,0},{16,24},{24,16},{1,9},{9,1},{17,25},{25,17},{2,10},{10... | collective-permute-start | bytes 1572872 | tf_op jit(solution)/shard_map/ppermute | solution.py:60
  468.6 1.9 collective-permute-start.24
  524.6 58.7 %collective-permute-start.25 = (bf16[256,2048]{1,0:T(8,128)(2,1)}, bf16[256,2048]{1,0:T(8,128)(2,1)}, u32[]{:S(2)}, u32[]{:S(2)}) collective-permute-start(bf16[256,2048]{1,0:T(8,128)(2,1)} %convolution_convert_fusion.5), channel_id=1, source_target_pairs={{0,8},{8,0},{16,24},{24,16},{1,9},{9,1},{17,25},{25,17},{2,10},{10... | collective-permute-start | bytes 3145736 | tf_op jit(solution)/shard_map/ppermute | solution.py:60
  534.4 54.8 %all-to-all-start.6 = ((bf16[8,112,256]{2,1,0:T(8,128)(2,1)}), bf16[8,112,256]{2,1,0:T(8,128)(2,1)S(1)}, u32[]{:S(2)}, u32[]{:S(2)}) async-start(bf16[8,112,256]{2,1,0:T(8,128)(2,1)} %get-tuple-element.92), calls=%async_computation.7 | async-start | bytes 917504 | tf_op jit(solution)/shard_map/all_to_all | solution.py:1047
  539.7 135.5 %reduce-scatter.12.cloned.1.call-start = ((), (), s32[]{:S(2)}) async-start(), calls=%async_computation.25 | async-start | bytes 4718592 | tf_op jit(solution)/shard_map/reduce_scatter | solution.py:49
  558.6 37.3 %collective-permute-start.27 = (bf16[8,512,128]{2,1,0:T(8,128)(2,1)}, bf16[8,512,128]{2,1,0:T(8,128)(2,1)}, u32[]{:S(2)}, u32[]{:S(2)}) collective-permute-start(bf16[8,512,128]{2,1,0:T(8,128)(2,1)} %broadcast_select_fusion), channel_id=1, source_target_pairs={{0,8},{8,0},{16,24},{24,16},{1,9},{9,1},{17,25},{25,17},{2,10},{10... | collective-permute-start | bytes 3145736 | tf_op jit(solution)/shard_map/ppermute | solution.py:60
  587.8 14.0 %collective-permute-start.26 = (bf16[128,2048]{1,0:T(8,128)(2,1)}, bf16[128,2048]{1,0:T(8,128)(2,1)}, u32[]{:S(2)}, u32[]{:S(2)}) collective-permute-start(bf16[128,2048]{1,0:T(8,128)(2,1)} %fusion.10), channel_id=1, source_target_pairs={{0,16},{8,24},{16,0},{24,8},{1,17},{9,25},{17,1},{25,9},{2,18},{10... | collective-permute-start | bytes 1572872 | tf_op jit(solution)/shard_map/ppermute | solution.py:60
  590.8 19.3 %all-to-all-start.7 = ((bf16[8,96,256]{2,1,0:T(8,128)(2,1)}), bf16[8,96,256]{2,1,0:T(8,128)(2,1)}, u32[]{:S(2)}, u32[]{:S(2)}) async-start(bf16[8,96,256]{2,1,0:T(8,128)(2,1)} %shard_map.250), calls=%async_computation.8 | async-start | bytes 786432 | tf_op jit(solution)/shard_map/all_to_all | solution.py:1055
  610.1 52.1 %all-to-all-start.8 = ((bf16[8,512,128]{2,1,0:T(8,128)(2,1)}), bf16[8,512,128]{2,1,0:T(8,128)(2,1)S(1)}, u32[]{:S(2)}, u32[]{:S(2)}) async-start(bf16[8,512,128]{2,1,0:T(8,128)(2,1)} %add_convert_fusion.refs_11_), calls=%async_computation.10 | async-start | bytes 2097152 | tf_op jit(solution)/shard_map/all_to_all | solution.py:1207
  616.6 133.6 %reduce-scatter.14.cloned.1.call-start = ((), (), s32[]{:S(2)}) async-start(), calls=%async_computation.26 | async-start | bytes 5308416 | tf_op jit(solution)/shard_map/reduce_scatter | solution.py:49
  648.2 5.7 collective-permute-start.28
  656.5 1.7 collective-permute-start.29
  659.0 5.8 collective-permute-start.30
  679.5 8.0 %collective-permute-start.34 = (f32[176,128]{1,0:T(8,128)S(1)}, f32[176,128]{1,0:T(8,128)S(1)}, u32[]{:S(2)}, u32[]{:S(2)}) collective-permute-start(f32[176,128]{1,0:T(8,128)S(1)} %pad_bitcast_fusion), channel_id=1, source_target_pairs={{0,8},{8,0},{16,24},{24,16},{1,9},{9,1},{17,25},{25,17},{2,10},{10... | collective-permute-start | bytes 270344 | tf_op jit(solution)/shard_map/ppermute | solution.py:885
  687.6 5.3 collective-permute-start.35
  690.3 28.1 %collective-permute-start.31 = (bf16[256,2048]{1,0:T(8,128)(2,1)}, bf16[256,2048]{1,0:T(8,128)(2,1)}, u32[]{:S(2)}, u32[]{:S(2)}) collective-permute-start(bf16[256,2048]{1,0:T(8,128)(2,1)} %fusion.6), channel_id=1, source_target_pairs={{0,8},{8,0},{16,24},{24,16},{1,9},{9,1},{17,25},{25,17},{2,10},{10... | collective-permute-start | bytes 3145736 | tf_op jit(solution)/shard_map/ppermute | solution.py:60
  693.0 7.1 collective-permute-start.36
  696.5 18.0 %all-to-all-start.11 = ((bf16[4,64,2048]{2,1,0:T(8,128)(2,1)}), bf16[4,64,2048]{2,1,0:T(8,128)(2,1)S(1)}, u32[]{:S(2)}, u32[]{:S(2)}) async-start(bf16[4,64,2048]{2,1,0:T(8,128)(2,1)} %bitcast.105), calls=%async_computation.16 | async-start | bytes 2097152 | tf_op jit(solution)/shard_map/all_to_all | solution.py:84
  700.1 7.2 collective-permute-start.37
  707.3 9.2 %collective-permute-start.38 = (f32[176,128]{1,0:T(8,128)S(1)}, f32[176,128]{1,0:T(8,128)S(1)}, u32[]{:S(2)}, u32[]{:S(2)}) collective-permute-start(f32[176,128]{1,0:T(8,128)S(1)} %add.279), channel_id=1, source_target_pairs={{0,4},{1,5},{2,6},{3,7},{4,0},{5,1},{6,2},{7,3},{8,12},{9,13},{10,... | collective-permute-start | bytes 270344 | tf_op jit(solution)/shard_map/ppermute | solution.py:885
  716.5 26.1 %collective-permute-start.33 = (bf16[128,2048]{1,0:T(8,128)(2,1)S(1)}, bf16[128,2048]{1,0:T(8,128)(2,1)S(1)}, u32[]{:S(2)}, u32[]{:S(2)}) collective-permute-start(bf16[128,2048]{1,0:T(8,128)(2,1)S(1)} %copy-done.138), channel_id=1, source_target_pairs={{0,0},{2,1},{8,2},{10,3},{16,4},{18,5},{24,6},{26,7},{4,8},{6,9},{... | collective-permute-start | bytes 1572872 | tf_op jit(solution)/shard_map/ppermute | solution.py:1178
  721.5 33.2 %collective-permute-start.32 = (bf16[128,2048]{1,0:T(8,128)(2,1)}, bf16[128,2048]{1,0:T(8,128)(2,1)S(1)}, u32[]{:S(2)}, u32[]{:S(2)}) collective-permute-start(bf16[128,2048]{1,0:T(8,128)(2,1)} %fusion.8), channel_id=1, source_target_pairs={{0,16},{8,24},{16,0},{24,8},{1,17},{9,25},{17,1},{25,9},{2,18},{10... | collective-permute-start | bytes 1572872 | tf_op jit(solution)/shard_map/ppermute | solution.py:60
  722.7 27.5 %all-to-all-start.10 = ((bf16[4,64,1024]{2,1,0:T(8,128)(2,1)}), bf16[4,64,1024]{2,1,0:T(8,128)(2,1)S(1)}, u32[]{:S(2)}, u32[]{:S(2)}) async-start(bf16[4,64,1024]{2,1,0:T(8,128)(2,1)} %bitcast.26), calls=%async_computation.15 | async-start | bytes 1048576 | tf_op jit(solution)/shard_map/all_to_all | solution.py:84
  750.2 14.0 %all-to-all-start.9 = ((bf16[4,64,1152]{2,1,0:T(8,128)(2,1)}), bf16[4,64,1152]{2,1,0:T(8,128)(2,1)S(1)}, u32[]{:S(2)}, u32[]{:S(2)}) async-start(bf16[4,64,1152]{2,1,0:T(8,128)(2,1)} %bitcast.106), calls=%async_computation.14 | async-start | bytes 1179648 | tf_op jit(solution)/shard_map/all_to_all | solution.py:84
  (138 other events, 864.3 us)
Sparse Core Ops, SparseCore 0:
  22.5 67.3 all-gather.5
  91.5 49.2 all-gather.7
  142.8 85.5 all-gather.9
  229.8 87.6 all-gather.11
  319.0 47.8 all-gather.13
  381.0 48.4 reduce-scatter.5
  431.8 88.0 reduce-scatter.7
  522.2 57.4 reduce-scatter.9
  581.9 78.3 reduce-scatter.11
  675.4 66.2 reduce-scatter.13

commit v4 on v3

--- a/solution.py
+++ b/solution.py
@@ -1075,7 +1075,7 @@
         [projected_rest, cosine_wide, sine_wide],
     )
     kv_blocks = lax.all_to_all(
-        after(kv_mine, state_sent), "blk", split_axis=0, concat_axis=0, tiled=True
+        kv_mine, "blk", split_axis=0, concat_axis=0, tiled=True
     )
     kv_beside = from_head(kv_blocks, 1)
     keys = jnp.where(even, kv_blocks, kv_beside)
@@ -1106,7 +1106,8 @@
     gate_up = jnp.dot(model_normed, weights_ffn, preferred_element_type=jnp.float32)
     gate_part, up_part = gate_up[:, :units], gate_up[:, units:]
     activated = (jax.nn.silu(gate_part) * up_part).astype(low)
-    grad_activated = times_transposed(model_cotangent, weights_down)
+    grad_down_low = outer_grad(activated, model_cotangent).astype(low)
+    grad_activated = times_transposed(model_cotangent, after(weights_down, grad_down_low))
     sigmoid_gate = jax.nn.sigmoid(gate_part)
     grad_gate_up = jnp.concatenate(
         [
@@ -1115,14 +1116,12 @@
         ],
         axis=1,
     ).astype(low)
-    grad_down_low = outer_grad(activated, model_cotangent).astype(low)
-    grad_down = scatter_blocks(grad_down_low)
+    grad_down = scatter_blocks(after(grad_down_low, weights_down))
     gate_up_late = after(grad_gate_up, grad_down_low)
     grad_norm_other = times_transposed(gate_up_late[pair_rows:], weights_ffn).astype(low)
     grad_norm_own = times_transposed(gate_up_late[:pair_rows], weights_ffn)
     grad_normed_two = scatter_pairs(grad_norm_own, grad_norm_other, low)
     grad_ffn_low = outer_grad(model_normed, after(grad_gate_up, grad_norm_own)).astype(low)
-    grad_ffn = scatter_blocks(after(grad_ffn_low, grad_down))
 
     grad_hidden, grad_hidden_low, grad_second = call(
         partial(back_two, ring=ring),
@@ -1141,6 +1140,7 @@
         after=[grad_down_low, grad_ffn_low],
         scratch=[pltpu.VMEM((row_count, D), jnp.float32)],
     )
+    grad_ffn = scatter_blocks(after(grad_ffn_low, grad_down, grad_hidden_low))
     span_grad_hidden = jnp.concatenate(gather_heads(after(grad_hidden_low, grad_down)))
     grad_heads = times_transposed(span_grad_hidden, weights_out).astype(low)
     grad_ssd, grad_gate, grad_sent, grad_skip_wide, grad_attended = call(
@@ -1174,11 +1174,7 @@
 
     grad_skip = grad_skip_wide[0].reshape(step_heads, MP).sum(axis=1)
     grad_out_low = outer_grad(mixer, span_grad_hidden).astype(low)
-    grad_out_sum = scatter_blocks(after(grad_out_low, grad_ffn))
-    grad_mix_weight = lax.ppermute(
-        grad_out_sum, ("head", "blk"), [(there, here) for here, there in out_pairs]
-    ).astype(jnp.float32)
-    later_grad, _ = chained(grad_sent, True)
+    later_grad, later_mine = chained(grad_sent, True)
 
     grad_query, grad_keys, grad_values = attention_back(
         view,
@@ -1201,11 +1197,15 @@
         [shaped((span_rows, rest_columns), low)],
         place,
         [grad_query, grad_gate, cosine_wide, sine_wide],
+        after=[later_mine],
     )[0]
     grad_rest_low = outer_grad(normed_one, grad_rest).astype(low)
-    grad_rest_in = scatter_blocks(after(grad_rest_low, grad_out_sum))
     grad_kv_parts = lax.all_to_all(kv_sums, "blk", split_axis=0, concat_axis=0, tiled=True)
 
+    grad_out_sum = scatter_blocks(after(grad_out_low, grad_ffn, grad_rest_low, kv_sums))
+    grad_mix_weight = lax.ppermute(
+        grad_out_sum, ("head", "blk"), [(there, here) for here, there in out_pairs]
+    ).astype(jnp.float32)
     grad_inner, grad_into, grad_outof, grad_step, grad_decay_line = call(
         ssd_back,
         [
@@ -1239,7 +1239,7 @@
     grad_raw, grad_step_shift, grad_rate = step_back(
         (grad_step[:, :step_heads], grad_decay_line[:, :step_heads])
     )
-    grad_inner = after(grad_inner, grad_ffn)
+    grad_inner = after(grad_inner, grad_kv_parts)
     grad_extended, grad_taps, grad_shift = conv_back(
         jnp.concatenate([grad_inner, grad_into, grad_outof], axis=1)
     )
@@ -1269,16 +1269,7 @@
         ],
     )[0]
     grad_conv_low = outer_grad(normed_one, grad_conv).astype(low)
-    grad_conv_in = scatter_blocks(after(grad_conv_low, grad_rest_in))
-    grad_proj_weight = call(
-        unpack_in,
-        [shaped(in_weight.shape, jnp.float32)],
-        place,
-        [
-            swap_heads(part.reshape(4, rows_in, -1))
-            for part in (grad_conv_in, grad_rest_in)
-        ],
-    )[0]
+    grad_rest_in = scatter_blocks(after(grad_rest_low, grad_out_sum, grad_taps))
     conv_moved, rest_moved = call(
         relative_order,
         [shaped((span_rows, conv_columns), low), shaped((span_rows, rest_columns), low)],
@@ -1294,7 +1285,7 @@
 
     grad_normed_other = back_in(slice(pair_rows, span_rows)).astype(low)
     grad_normed_own = back_in(slice(0, pair_rows))
-    grad_normed_other = after(grad_normed_other, grad_out_sum)
+    rest_swapped = swap_heads(grad_rest_in.reshape(4, rows_in, -1))
     grad_input = call(
         partial(back_one, ring=ring),
         [shaped((row_count, D), low)],
@@ -1305,11 +1296,12 @@
             grad_hidden,
             first_gain[None, :],
         ],
+        after=[rest_swapped, grad_ffn_weight],
         scratch=[pltpu.VMEM((row_count, D), jnp.float32)],
     )[0]
     first_line = jnp.sum(
         weights_conv.astype(jnp.float32) * grad_conv_low.astype(jnp.float32), axis=1
-    ) + jnp.sum(weights_rest.astype(jnp.float32) * grad_rest_low.astype(jnp.float32), axis=1)
+    ) + jnp.sum(weights_rest.astype(jnp.float32) * after(grad_rest_low, grad_conv_low).astype(jnp.float32), axis=1)
     first_line = first_line.reshape(blocks, 4, -1)
     first_line = jnp.stack([first_line[ring.index(k)] for k in range(blocks)], axis=1).reshape(D)
 
@@ -1338,6 +1330,13 @@
     line = jnp.concatenate([part.reshape(-1) for part in small])
     line = jnp.pad(line, (0, -line.shape[0] % 1024)).reshape(-1, 128)
     line = summed_over(summed_over(line, "head"), "blk").reshape(-1)
+    grad_conv_in = scatter_blocks(after(grad_conv_low, grad_rest_in, grad_normed_own))
+    grad_proj_weight = call(
+        unpack_in,
+        [shaped(in_weight.shape, jnp.float32)],
+        place,
+        [swap_heads(grad_conv_in.reshape(4, rows_in, -1)), rest_swapped],
+    )[0]
     summed_small = []
     at = 0
     for part in small:

time: 787 us -> 750 us (0.953)
  waiting for transfers between devices: 342 us -> 291 us
    reduce_scatter x5, waiting for transfers between devices: 88.9 us -> 56.2 us  [scatter_blocks(): lax.psum_scatter(partial_sums, 'blk', scatter_dimension=0, tiled=True, ax...]
    ppermute x27, waiting for transfers between devices: 90.1 us -> 64 us  [from_head(): lax.ppermute(shard, 'head', [(i, i ^ distance) for i in range(peers)])]
    ppermute x2, waiting for transfers between devices: 3.78 us -> 29.8 us  [passed_along(): return lax.ppermute(shard, axis, pairs)]
    all_to_all x1, waiting for transfers between devices: 19.5 us -> 0.01 us  [per_device(): lax.all_to_all(kv_mine, 'blk', split_axis=0, concat_axis=0, tiled=True)]
    ppermute x1, waiting for transfers between devices: 15.2 us -> 0.01 us  [per_device(): lax.ppermute(grad_out_sum, ('head', 'blk'), [(there, here) for here, ther...]
    all_gather x5, waiting for transfers between devices: 58.9 us -> 45.1 us  [gather_blocks(): lax.all_gather(shard, 'blk', axis=0, tiled=True, axis_index_groups=[ring_...]
    ppermute x8, waiting for transfers between devices: 7.61 us -> 17.3 us  [summed_over(): lax.ppermute(values_in, axis, [(i, i ^ by) for i in range(peers)])]
    all_to_all x1, waiting for transfers between devices: 0.01 us -> 9.25 us  [per_device(): lax.all_to_all(kv_sums, 'blk', split_axis=0, concat_axis=0, tiled=True)]
  transfers between devices with their start and end apart: 58 -> 58, of which waited for: 32 -> 33; matrix products, arithmetic and copies ran while one was open for 19% -> 22% of each run, Pallas kernels for 10% -> 10%
where the time goes in v4:
time: 750 us; the launch traced here: 737 us
  waiting for transfers between devices  291 us (39%)
  matrix products  96.3 us (13%)
  starting transfers between devices  83.7 us (11%)
  local copies, waits for them, and re-layouts  81.3 us (11%)
  Pallas kernels  76.8 us (10%)
  other arithmetic  47.3 us (6%)
  blocking collectives  43.7 us (6%)
  between operations  16.2 us (2%)
    unnamed x303, local copies, waits for them, and re-layouts  69.7 us
    ppermute x27, waiting for transfers between devices, from_head(): lax.ppermute(shard, 'head', [(i, i ^ distance) for i in range(peers)])  64 us
    reduce_scatter x5, waiting for transfers between devices, scatter_blocks(): lax.psum_scatter(partial_sums, 'blk', scatter_dimension=0, tiled=True, ax...  56.2 us
    pallas_call x20, Pallas kernels, call(): pl.pallas_call(body, out_shape=outputs, in_specs=[pl.BlockSpec(memory_spa...  53.9 us
    all_gather x5, waiting for transfers between devices, gather_blocks(): lax.all_gather(shard, 'blk', axis=0, tiled=True, axis_index_groups=[ring_...  45.1 us
    all_to_all x3, blocking collectives, swap_heads(): lax.all_to_all(pieces, 'head', split_axis=0, concat_axis=0, tiled=True)  43.7 us
    dot_general x8, matrix products, times_transposed(): lax.dot_general(grad_side, weight, (((1,), (1,)), ((), ())), preferred_el...  34.7 us
    dot_general x5, matrix products, outer_grad(): lax.dot_general(left_side, grad_side, (((0,), (0,)), ((), ())), preferred...  30.1 us
  transfers between devices with their start and end apart: 58, of which 33 were waited for; matrix products, arithmetic and copies ran while one was open for 22% of the time, Pallas kernels for 10%

profile of v4, /device:TPU:16, one launch (start us, length us, event | category | flops | bytes accessed | tf_op | source)
XLA Modules:
  0.0 736.5 jit_solution(2718302302607938190)
XLA Ops:
  9.6 12.9 %all_to_all.60 = bf16[4,64,1152]{2,1,0:T(8,128)(2,1)} all-to-all(bf16[4,64,1152]{2,1,0:T(8,128)(2,1)S(1)} %get-tuple-element.65), channel_id=1, replica_groups=mesh['head'=4,'blk'=8] {'head'}, dimensions={0} | all-to-all | bytes 1179648 | tf_op jit(solution)/shard_map/all_to_all | solution.py:84
  22.6 13.1 %all_to_all.61 = bf16[4,64,1024]{2,1,0:T(8,128)(2,1)} all-to-all(bf16[4,64,1024]{2,1,0:T(8,128)(2,1)} %copy-done.31), channel_id=1, replica_groups=mesh['head'=4,'blk'=8] {'head'}, dimensions={0} | all-to-all | bytes 1048576 | tf_op jit(solution)/shard_map/all_to_all | solution.py:84
  39.0 28.9 %collective-permute-done.14 = bf16[128,2048]{1,0:T(8,128)(2,1)S(1)} collective-permute-done((bf16[128,2048]{1,0:T(8,128)(2,1)S(1)}, bf16[128,2048]{1,0:T(8,128)(2,1)S(1)}, u32[]{:S(2)}, u32[]{:S(2)}) %collective-permute-start.14) | collective-permute-done | bytes 524320 | tf_op jit(solution)/shard_map/ppermute | solution.py:947
  69.5 17.7 %all_to_all.62 = bf16[4,64,2048]{2,1,0:T(8,128)(2,1)} all-to-all(bf16[4,64,2048]{2,1,0:T(8,128)(2,1)S(1)} %shard_map.240), channel_id=1, replica_groups=mesh['head'=4,'blk'=8] {'head'}, dimensions={0} | all-to-all | bytes 2097152 | tf_op jit(solution)/shard_map/all_to_all | solution.py:84
  93.0 3.1 collective-permute-done.8
  96.2 3.0 collective-permute-start.9
  102.1 3.0 collective-permute-done.refs_1_
  111.3 5.9 fusion.61
  119.5 8.1 %collective-permute-done.3.refs_2_ = bf16[512,128]{1,0:T(8,128)(2,1)S(1)} collective-permute-done((bf16[512,128]{1,0:T(8,128)(2,1)S(1)}, bf16[512,128]{1,0:T(8,128)(2,1)S(1)}, u32[]{:S(2)}, u32[]{:S(2)}) %collective-permute-start.3) | collective-permute-done | bytes 131104 | tf_op jit(solution)/shard_map/ppermute | solution.py:60
  133.3 7.1 all-to-all-start.5
  141.6 3.6 collective-permute-start.6
  146.4 29.1 %collective-permute-done.6 = bf16[3,1280]{1,0:T(4,128)(2,1)S(1)} collective-permute-done((bf16[3,1280]{1,0:T(4,128)(2,1)S(1)}, bf16[3,1280]{1,0:T(4,128)(2,1)S(1)}, u32[]{:S(2)}, u32[]{:S(2)}) %collective-permute-start.6) | collective-permute-done | bytes 7712 | tf_op jit(solution)/shard_map/ppermute | solution.py:34
  175.9 3.4 fusion.5
  181.1 8.1 %shard_map.241 = (f32[512,768]{1,0:T(8,128)S(1)}, bf16[8,112,256]{2,1,0:T(8,128)(2,1)}, f32[512,128]{1,0:T(8,128)S(1)}, f32[8,128]{1,0:T(8,128)S(1)}) custom-call(s32[8]{0:T(128)S(1)} %stack.40.place_ref, f32[512,768]{1,0:T(8,128)S(1)} %slice.412.refs_0_.refs_4_.refs_3_, f32[512,256]{1,0:T(8,128)S(1)} %get-tuple-element.145.refs_1_, ...), custom_call_target="tpu_custom_call" | custom-call | flops 6000000000 | bytes 5705728 | tf_op jit(solution)/shard_map/pallas_call | solution.py:761
  193.3 4.2 all-to-all-start.3
  204.1 8.9 %all-to-all-done.3.refs_0_ = bf16[8,112,256]{2,1,0:T(8,128)(2,1)S(1)} async-done(((bf16[8,112,256]{2,1,0:T(8,128)(2,1)}), bf16[8,112,256]{2,1,0:T(8,128)(2,1)S(1)}, u32[]{:S(2)}, u32[]{:S(2)}) %all-to-all-start.3) | async-done | bytes 458784 | tf_op jit(solution)/shard_map/all_to_all | solution.py:1047
  214.4 6.8 all-to-all-start.4
  221.3 5.3 fusion.62.refs_0_
  230.3 12.7 %shard_map.245 = (f32[512,256]{1,0:T(8,128)S(1)}, f32[2,512,128]{2,1,0:T(8,128)S(1)}) custom-call(s32[3]{0:T(128)S(1)} %pad_add_fusion.3.refs_0_, bf16[512,256]{1,0:T(8,128)(2,1)S(1)} %get-tuple-element.75.refs_1_, s32[512,128]{1,0:T(8,128)S(1)} %broadcast_in_dim.23.refs_2_, bf16[8,512,128]{2,1,0:T(8,128)(2,1)S(1)} %get-tuple-element.147.refs_3_, ...), custom_call_target="tpu_custom_call" | custom-call | flops 20000000000 | bytes 4000000 | tf_op jit(solution)/shard_map/pallas_call | solution.py:785
  257.0 3.8 fusion.31
  262.3 2.7 collective-permute-done.15
  265.2 14.0 %collective-permute-done.16 = bf16[128,2048]{1,0:T(8,128)(2,1)S(1)} collective-permute-done((bf16[128,2048]{1,0:T(8,128)(2,1)S(1)}, bf16[128,2048]{1,0:T(8,128)(2,1)S(1)}, u32[]{:S(2)}, u32[]{:S(2)}) %collective-permute-start.16) | collective-permute-done | bytes 524320 | tf_op jit(solution)/shard_map/ppermute | solution.py:60
  280.8 13.0 %collective-permute-done.17 = bf16[128,2048]{1,0:T(8,128)(2,1)S(1)} collective-permute-done((bf16[128,2048]{1,0:T(8,128)(2,1)S(1)}, bf16[128,2048]{1,0:T(8,128)(2,1)S(1)}, u32[]{:S(2)}, u32[]{:S(2)}) %collective-permute-start.17) | collective-permute-done | bytes 524320 | tf_op jit(solution)/shard_map/ppermute | solution.py:60
  297.2 11.9 %all-gather.12.cloned.1.call-done = bf16[2048,2048]{1,0:T(8,128)(2,1)} async-done(((bf16[256,2048]{1,0:T(8,128)(2,1)}), bf16[2048,2048]{1,0:T(8,128)(2,1)}) %all-gather.12.cloned.1.call-update) | async-done | bytes 8388624 | tf_op jit(solution)/shard_map/all_gather | solution.py:45
  309.1 8.0 %fusion.63 = f32[512,2048]{1,0:T(8,128)S(1)} fusion(bf16[512,2048]{1,0:T(8,128)(2,1)} %constant_dynamic-update-slice_fusion.4, bf16[2048,2048]{1,0:T(8,128)(2,1)} %all-gather.12.cloned.1.call-done), kind=kOutput, calls=%fused_computation.170 | convolution fusion | flops 4294967296 | bytes 14680064 | tf_op jit(solution)/shard_map/dot_general | solution.py:1106
  320.2 4.4 convolution_convert_fusion.4.refs_4_
  324.6 33.1 %all-gather.14.cloned.1.call-done = bf16[1024,2048]{1,0:T(8,128)(2,1)} async-done(((bf16[128,2048]{1,0:T(8,128)(2,1)}), bf16[1024,2048]{1,0:T(8,128)(2,1)}) %all-gather.14.cloned.1.call-update) | async-done | bytes 4194320 | tf_op jit(solution)/shard_map/all_gather | solution.py:45
  357.8 7.0 multiply_convert_fusion.1
  365.0 6.3 convolution_convert_fusion.6
  378.1 8.6 %convolution_convert_fusion.1.refs_5_ = bf16[2048,2048]{1,0:T(8,128)(2,1)} fusion(bf16[512,2048]{1,0:T(8,128)(2,1)} %constant_dynamic-update-slice_fusion.4, bf16[512,2048]{1,0:T(8,128)(2,1)S(1)} %pad_maximum_fusion), kind=kOutput, calls=%fused_computation.3 | convolution fusion | flops 4299161600 | bytes 12582912 | tf_op jit(solution)/shard_map/dot_general | solution.py:320
  386.7 4.2 collective-permute-done.21
  397.9 10.4 %reduce-scatter.6.cloned.1.call-done = bf16[128,2048]{1,0:T(8,128)(2,1)} async-done(((bf16[1024,2048]{1,0:T(8,128)(2,1)}), bf16[128,2048]{1,0:T(8,128)(2,1)}) %reduce-scatter.6.cloned.1.call-update) | async-done | bytes 524304 | tf_op jit(solution)/shard_map/reduce_scatter | solution.py:49
  409.9 12.2 %collective-permute-done.22 = bf16[128,2048]{1,0:T(8,128)(2,1)S(1)} collective-permute-done((bf16[128,2048]{1,0:T(8,128)(2,1)S(1)}, bf16[128,2048]{1,0:T(8,128)(2,1)S(1)}, u32[]{:S(2)}, u32[]{:S(2)}) %collective-permute-start.22) | collective-permute-done | bytes 524320 | tf_op jit(solution)/shard_map/ppermute | solution.py:60
  424.2 5.4 convolution_convert_fusion.7.refs_0_
  429.7 3.9 shard_map.249
  437.0 5.2 all-to-all-start.6
  442.3 6.1 convolution_convert_fusion.3.refs_8_
  455.7 10.1 %shard_map.251 = (f32[512,256]{1,0:T(8,128)S(1)}, bf16[8,512,128]{2,1,0:T(8,128)(2,1)S(1)}, bf16[8,512,128]{2,1,0:T(8,128)(2,1)S(1)}) custom-call(s32[3]{0:T(128)S(1)} %copy-done.64, bf16[512,256]{1,0:T(8,128)(2,1)S(1)} %copy-done.72, s32[512,128]{1,0:T(8,128)S(1)} %copy-done.56, bf16[8,512,128]{2,1,0:T(8,128)(2,1)S(1)} %copy-done.26, ...), custom_call_target="tpu_custom_call" | custom-call | flops 30000001024 | bytes 4000000 | tf_op jit(solution)/shard_map/pallas_call | solution.py:825
  472.8 4.4 convolution_convert_fusion.2.refs_12_
  480.8 26.8 %reduce-scatter.8.cloned.1.call-done = bf16[256,2048]{1,0:T(8,128)(2,1)} async-done(((bf16[2048,2048]{1,0:T(8,128)(2,1)}), bf16[256,2048]{1,0:T(8,128)(2,1)}) %reduce-scatter.8.cloned.1.call-update) | async-done | bytes 1048592 | tf_op jit(solution)/shard_map/reduce_scatter | solution.py:49
  507.7 4.6 convolution_convert_fusion.5
  514.9 5.1 all-to-all-start.7
  524.7 9.6 %all-to-all-done.7 = bf16[8,96,256]{2,1,0:T(8,128)(2,1)S(1)} async-done(((bf16[8,96,256]{2,1,0:T(8,128)(2,1)}), bf16[8,96,256]{2,1,0:T(8,128)(2,1)S(1)}, u32[]{:S(2)}, u32[]{:S(2)}) %all-to-all-start.7) | async-done | bytes 393248 | tf_op jit(solution)/shard_map/all_to_all | solution.py:1055
  535.0 6.5 all-to-all-start.8
  544.3 19.2 %shard_map.253 = (f32[512,768]{1,0:T(8,128)S(1)}, f32[512,256]{1,0:T(8,128)S(1)}, f32[512,256]{1,0:T(8,128)S(1)}, f32[512,128]{1,0:T(8,128)S(1)}, f32[512,128]{1,0:T(8,128)S(1)}) custom-call(s32[8]{0:T(128)S(1)} %stack.40.place_ref, f32[512,768]{1,0:T(8,128)S(1)} %copy-done.21, f32[512,256]{1,0:T(8,128)S(1)} %copy-done.37, f32[512,256]{1,0:T(8,128)S(1)} %copy-done.35, ...), custom_call_target="tpu_custom_call" | custom-call | flops 10000000000 | bytes 10488832 | tf_op jit(solution)/shard_map/pallas_call | solution.py:761
  566.9 9.2 %all-to-all-done.8.refs_6_ = bf16[8,512,128]{2,1,0:T(8,128)(2,1)S(1)} async-done(((bf16[8,512,128]{2,1,0:T(8,128)(2,1)}), bf16[8,512,128]{2,1,0:T(8,128)(2,1)S(1)}, u32[]{:S(2)}, u32[]{:S(2)}) %all-to-all-start.8) | async-done | bytes 1048608 | tf_op jit(solution)/shard_map/all_to_all | solution.py:1203
  578.8 5.2 multiply_reduce_fusion.5
  584.1 4.3 reduce-scatter.10.cloned.1.call-done
  591.1 4.3 collective-permute-start.28
  607.1 6.7 multiply_reduce_fusion
  617.0 4.8 fusion.23
  624.4 14.7 %reduce-scatter.12.cloned.1.call-done = bf16[256,1024]{1,0:T(8,128)(2,1)} async-done(((bf16[2048,1024]{1,0:T(8,128)(2,1)}), bf16[256,1024]{1,0:T(8,128)(2,1)}) %reduce-scatter.12.cloned.1.call-update) | async-done | bytes 524304 | tf_op jit(solution)/shard_map/reduce_scatter | solution.py:49
  641.9 4.0 fusion.21
  653.8 3.2 collective-permute-done.35
  658.6 3.1 collective-permute-done.36
  661.7 4.1 collective-permute-start.37
  665.8 4.9 collective-permute-done.37
  671.9 3.5 all-to-all-start.10
  684.0 6.3 all-to-all-done.10.refs_0_
  690.4 3.5 all-to-all-start.9
  695.0 3.7 collective-permute-start.33
  698.8 12.2 %all-to-all-done.9.refs_4_.refs_1_ = bf16[4,64,1024]{2,1,0:T(8,128)(2,1)S(1)} async-done(((bf16[4,64,1024]{2,1,0:T(8,128)(2,1)}), bf16[4,64,1024]{2,1,0:T(8,128)(2,1)S(1)}, u32[]{:S(2)}, u32[]{:S(2)}) %all-to-all-start.9) | async-done | bytes 524320 | tf_op jit(solution)/shard_map/all_to_all | solution.py:84
  711.0 3.5 all-to-all-start.11
  724.0 3.4 all-to-all-done.11.refs_0_
  (550 shorter events, 184.3 us)
Async XLA Ops:
  7.2 104.1 %all-gather.6.cloned.1.call-start = ((), (), s32[]{:S(2)}) async-start(), calls=%async_computation.17 | async-start | bytes 5308416 | tf_op jit(solution)/shard_map/all_gather | solution.py:45
  9.6 59.1 %copy-start.14 = (f32[64,8192]{1,0:T(8,128)S(1)}, f32[64,8192]{1,0:T(8,128)}, u32[]{:S(2)}) copy-start(f32[64,8192]{1,0:T(8,128)} %refs_0_.2) | copy-start | bytes 6291460
  22.6 198.7 %all-gather.8.cloned.1.call-start = ((), (), s32[]{:S(2)}) async-start(), calls=%async_computation.18 | async-start | bytes 4718592 | tf_op jit(solution)/shard_map/all_gather | solution.py:45
  35.7 221.3 %all-gather.10.cloned.1.call-start = ((), (), s32[]{:S(2)}) async-start(), calls=%async_computation.19 | async-start | bytes 4718592 | tf_op jit(solution)/shard_map/all_gather | solution.py:45
  37.0 30.8 %collective-permute-start.14 = (bf16[128,2048]{1,0:T(8,128)(2,1)S(1)}, bf16[128,2048]{1,0:T(8,128)(2,1)S(1)}, u32[]{:S(2)}, u32[]{:S(2)}) collective-permute-start(bf16[128,2048]{1,0:T(8,128)(2,1)S(1)} %convert_element_type.153), channel_id=1, source_target_pairs={{0,0},{1,2},{2,8},{3,10},{4,16},{5,18},{6,24},{7,26},{8,4},{9,6},{... | collective-permute-start | bytes 1572872 | tf_op jit(solution)/shard_map/ppermute | solution.py:947
  68.6 240.5 %all-gather.12.cloned.1.call-start = ((), (), s32[]{:S(2)}) async-start(), calls=%async_computation.20 | async-start | bytes 9437184 | tf_op jit(solution)/shard_map/all_gather | solution.py:45
  87.6 4.7 collective-permute-start.7
  91.8 13.3 %collective-permute-start = (bf16[128,2048]{1,0:T(8,128)(2,1)S(1)}, bf16[128,2048]{1,0:T(8,128)(2,1)S(1)}, u32[]{:S(2)}, u32[]{:S(2)}) collective-permute-start(bf16[128,2048]{1,0:T(8,128)(2,1)S(1)} %bitcast.85), channel_id=1, source_target_pairs={{0,16},{8,24},{16,0},{24,8},{1,17},{9,25},{17,1},{25,9},{2,18},{10... | collective-permute-start | bytes 1572872 | tf_op jit(solution)/shard_map/ppermute | solution.py:60
  92.4 3.7 collective-permute-start.8
  96.2 9.0 %collective-permute-start.9 = (s32[4096]{0:T(1024)S(1)}, s32[4096]{0:T(1024)S(1)}, u32[]{:S(2)}, u32[]{:S(2)}) collective-permute-start(s32[4096]{0:T(1024)S(1)} %add.236), channel_id=1, source_target_pairs={{0,4},{1,5},{2,6},{3,7},{4,0},{5,1},{6,2},{7,3},{8,12},{9,13},{10,... | collective-permute-start | bytes 49160 | tf_op jit(solution)/shard_map/ppermute | solution.py:885
  102.1 4.4 collective-permute-start.1
  105.1 1.9 collective-permute-start.2
  110.8 20.6 %collective-permute-start.11 = (bf16[128,2048]{1,0:T(8,128)(2,1)S(1)}, bf16[128,2048]{1,0:T(8,128)(2,1)}, u32[]{:S(2)}, u32[]{:S(2)}) collective-permute-start(bf16[128,2048]{1,0:T(8,128)(2,1)S(1)} %bitcast.92), channel_id=1, source_target_pairs={{0,16},{8,24},{16,0},{24,8},{1,17},{9,25},{17,1},{25,9},{2,18},{10... | collective-permute-start | bytes 1572872 | tf_op jit(solution)/shard_map/ppermute | solution.py:60
  117.2 10.3 %collective-permute-start.3 = (bf16[512,128]{1,0:T(8,128)(2,1)S(1)}, bf16[512,128]{1,0:T(8,128)(2,1)S(1)}, u32[]{:S(2)}, u32[]{:S(2)}) collective-permute-start(bf16[512,128]{1,0:T(8,128)(2,1)S(1)} %slice.402.refs_1_), channel_id=1, source_target_pairs={{0,16},{8,24},{16,0},{24,8},{1,17},{9,25},{17,1},{25,9},{2,18},{10... | collective-permute-start | bytes 393224 | tf_op jit(solution)/shard_map/ppermute | solution.py:60
  119.5 56.3 %copy-start.122 = (f32[512]{0:T(512)}, f32[512]{0:T(512)S(1)}, u32[]{:S(2)}) copy-start(f32[512]{0:T(512)S(1)} %get-tuple-element.136) | copy-start | bytes 6148
  119.5 21.0 %collective-permute-start.4 = (bf16[512,128]{1,0:T(8,128)(2,1)S(1)}, bf16[512,128]{1,0:T(8,128)(2,1)S(1)}, u32[]{:S(2)}, u32[]{:S(2)}) collective-permute-start(bf16[512,128]{1,0:T(8,128)(2,1)S(1)} %slice.402.refs_1_), channel_id=1, source_target_pairs={{0,8},{8,0},{16,24},{24,16},{1,9},{9,1},{17,25},{25,17},{2,10},{10... | collective-permute-start | bytes 393224 | tf_op jit(solution)/shard_map/ppermute | solution.py:60
  127.6 12.9 %collective-permute-start.5 = (bf16[512,128]{1,0:T(8,128)(2,1)S(1)}, bf16[512,128]{1,0:T(8,128)(2,1)}, u32[]{:S(2)}, u32[]{:S(2)}) collective-permute-start(bf16[512,128]{1,0:T(8,128)(2,1)S(1)} %collective-permute-done.3.refs_2_), channel_id=1, source_target_pairs={{0,8},{8,0},{16,24},{24,16},{1,9},{9,1},{17,25},{25,17},{2,10},{10... | collective-permute-start | bytes 393224 | tf_op jit(solution)/shard_map/ppermute | solution.py:60
  130.9 99.0 %copy-start.63 = (s32[3]{0:T(128)}, s32[3]{0:T(128)S(1)}, u32[]{:S(2)}) copy-start(s32[3]{0:T(128)S(1)} %pad_add_fusion.3.refs_0_) | copy-start | bytes 40
  130.9 69.4 %collective-permute-start.12 = (bf16[128,2048]{1,0:T(8,128)(2,1)S(1)}, bf16[128,2048]{1,0:T(8,128)(2,1)}, u32[]{:S(2)}, u32[]{:S(2)}) collective-permute-start(bf16[128,2048]{1,0:T(8,128)(2,1)S(1)} %bitcast.93), channel_id=1, source_target_pairs={{0,8},{8,0},{16,24},{24,16},{1,9},{9,1},{17,25},{25,17},{2,10},{10... | collective-permute-start | bytes 1572872 | tf_op jit(solution)/shard_map/ppermute | solution.py:60
  131.4 70.7 %collective-permute-start.13 = (bf16[128,2048]{1,0:T(8,128)(2,1)}, bf16[128,2048]{1,0:T(8,128)(2,1)}, u32[]{:S(2)}, u32[]{:S(2)}) collective-permute-start(bf16[128,2048]{1,0:T(8,128)(2,1)} %collective-permute-done.11), channel_id=1, source_target_pairs={{0,8},{8,0},{16,24},{24,16},{1,9},{9,1},{17,25},{25,17},{2,10},{10... | collective-permute-start | bytes 1572872 | tf_op jit(solution)/shard_map/ppermute | solution.py:60
  133.3 60.0 %all-to-all-start.5 = ((bf16[8,512,128]{2,1,0:T(8,128)(2,1)}), bf16[8,512,128]{2,1,0:T(8,128)(2,1)}, u32[]{:S(2)}, u32[]{:S(2)}) async-start(bf16[8,512,128]{2,1,0:T(8,128)(2,1)} %copy-done.9), calls=%async_computation.5 | async-start | bytes 2097152 | tf_op jit(solution)/shard_map/all_to_all | solution.py:1077
  141.6 34.0 %collective-permute-start.6 = (bf16[3,1280]{1,0:T(4,128)(2,1)S(1)}, bf16[3,1280]{1,0:T(4,128)(2,1)S(1)}, u32[]{:S(2)}, u32[]{:S(2)}) collective-permute-start(bf16[3,1280]{1,0:T(4,128)(2,1)S(1)} %slice.403), channel_id=1, source_target_pairs={{0,1},{1,2},{2,3},{3,4},{4,5},{5,6},{6,7},{8,9},{9,10},{10,11},{11... | collective-permute-start | bytes 23048 | tf_op jit(solution)/shard_map/ppermute | solution.py:34
  146.4 33.7 %copy-start.49 = (f32[512,128]{1,0:T(8,128)}, f32[512,128]{1,0:T(8,128)S(1)}, u32[]{:S(2)}) copy-start(f32[512,128]{1,0:T(8,128)S(1)} %pad.43.refs_3_) | copy-start | bytes 786436
  146.4 33.7 %copy-start.51 = (f32[512,128]{1,0:T(8,128)}, f32[512,128]{1,0:T(8,128)S(1)}, u32[]{:S(2)}) copy-start(f32[512,128]{1,0:T(8,128)S(1)} %pad.44.refs_4_) | copy-start | bytes 786436
  193.3 19.6 %all-to-all-start.3 = ((bf16[8,112,256]{2,1,0:T(8,128)(2,1)}), bf16[8,112,256]{2,1,0:T(8,128)(2,1)S(1)}, u32[]{:S(2)}, u32[]{:S(2)}) async-start(bf16[8,112,256]{2,1,0:T(8,128)(2,1)} %get-tuple-element.72), calls=%async_computation.3 | async-start | bytes 917504 | tf_op jit(solution)/shard_map/all_to_all | solution.py:1047
  197.5 160.2 %all-gather.14.cloned.1.call-start = ((), (), s32[]{:S(2)}) async-start(), calls=%async_computation.21 | async-start | bytes 4718592 | tf_op jit(solution)/shard_map/all_gather | solution.py:45
  200.3 28.0 %collective-permute-start.10 = (bf16[8,512,128]{2,1,0:T(8,128)(2,1)}, bf16[8,512,128]{2,1,0:T(8,128)(2,1)S(1)}, u32[]{:S(2)}, u32[]{:S(2)}) collective-permute-start(bf16[8,512,128]{2,1,0:T(8,128)(2,1)} %all-to-all-done.5), channel_id=1, source_target_pairs={{0,8},{8,0},{16,24},{24,16},{1,9},{9,1},{17,25},{25,17},{2,10},{10... | collective-permute-start | bytes 3145736 | tf_op jit(solution)/shard_map/ppermute | solution.py:60
  214.4 32.9 %all-to-all-start.4 = ((bf16[8,96,256]{2,1,0:T(8,128)(2,1)}), bf16[8,96,256]{2,1,0:T(8,128)(2,1)S(1)}, u32[]{:S(2)}, u32[]{:S(2)}) async-start(bf16[8,96,256]{2,1,0:T(8,128)(2,1)} %shard_map.242.refs_5_), calls=%async_computation.4 | async-start | bytes 786432 | tf_op jit(solution)/shard_map/all_to_all | solution.py:1055
  221.3 187.1 %reduce-scatter.6.cloned.1.call-start = ((), (), s32[]{:S(2)}) async-start(), calls=%async_computation.22 | async-start | bytes 4718592 | tf_op jit(solution)/shard_map/reduce_scatter | solution.py:49
  260.8 4.2 collective-permute-start.15
  265.1 14.0 %collective-permute-start.16 = (bf16[128,2048]{1,0:T(8,128)(2,1)S(1)}, bf16[128,2048]{1,0:T(8,128)(2,1)S(1)}, u32[]{:S(2)}, u32[]{:S(2)}) collective-permute-start(bf16[128,2048]{1,0:T(8,128)(2,1)S(1)} %fusion.16), channel_id=1, source_target_pairs={{0,16},{8,24},{16,0},{24,8},{1,17},{9,25},{17,1},{25,9},{2,18},{10... | collective-permute-start | bytes 1572872 | tf_op jit(solution)/shard_map/ppermute | solution.py:60
  280.5 112.2 %copy-start.7 = (f32[128,2048]{1,0:T(8,128)}, f32[128,2048]{1,0:T(8,128)S(1)}, u32[]{:S(2)}) copy-start(f32[128,2048]{1,0:T(8,128)S(1)} %get-tuple-element.80.refs_1_) | copy-start | bytes 3145732
  280.5 13.3 %collective-permute-start.17 = (bf16[128,2048]{1,0:T(8,128)(2,1)S(1)}, bf16[128,2048]{1,0:T(8,128)(2,1)S(1)}, u32[]{:S(2)}, u32[]{:S(2)}) collective-permute-start(bf16[128,2048]{1,0:T(8,128)(2,1)S(1)} %get-tuple-element.81), channel_id=1, source_target_pairs={{0,16},{8,24},{16,0},{24,8},{1,17},{9,25},{17,1},{25,9},{2,18},{10... | collective-permute-start | bytes 1572872 | tf_op jit(solution)/shard_map/ppermute | solution.py:60
  280.8 14.6 %collective-permute-start.18 = (bf16[128,2048]{1,0:T(8,128)(2,1)S(1)}, bf16[128,2048]{1,0:T(8,128)(2,1)S(1)}, u32[]{:S(2)}, u32[]{:S(2)}) collective-permute-start(bf16[128,2048]{1,0:T(8,128)(2,1)S(1)} %get-tuple-element.81), channel_id=1, source_target_pairs={{0,8},{8,0},{16,24},{24,16},{1,9},{9,1},{17,25},{25,17},{2,10},{10... | collective-permute-start | bytes 1572872 | tf_op jit(solution)/shard_map/ppermute | solution.py:60
  293.8 2.5 collective-permute-start.19
  357.8 149.8 %reduce-scatter.8.cloned.1.call-start = ((), (), s32[]{:S(2)}) async-start(), calls=%async_computation.23 | async-start | bytes 9437184 | tf_op jit(solution)/shard_map/reduce_scatter | solution.py:49
  371.3 2.7 collective-permute-start.20
  376.7 14.3 %collective-permute-start.21 = (bf16[128,2048]{1,0:T(8,128)(2,1)}, bf16[128,2048]{1,0:T(8,128)(2,1)S(1)}, u32[]{:S(2)}, u32[]{:S(2)}) collective-permute-start(bf16[128,2048]{1,0:T(8,128)(2,1)} %fusion.14), channel_id=1, source_target_pairs={{0,16},{8,24},{16,0},{24,8},{1,17},{9,25},{17,1},{25,9},{2,18},{10... | collective-permute-start | bytes 1572872 | tf_op jit(solution)/shard_map/ppermute | solution.py:60
  408.4 13.8 %collective-permute-start.22 = (bf16[128,2048]{1,0:T(8,128)(2,1)S(1)}, bf16[128,2048]{1,0:T(8,128)(2,1)S(1)}, u32[]{:S(2)}, u32[]{:S(2)}) collective-permute-start(bf16[128,2048]{1,0:T(8,128)(2,1)S(1)} %get-tuple-element.89), channel_id=1, source_target_pairs={{0,16},{8,24},{16,0},{24,8},{1,17},{9,25},{17,1},{25,9},{2,18},{10... | collective-permute-start | bytes 1572872 | tf_op jit(solution)/shard_map/ppermute | solution.py:60
  409.9 12.3 %collective-permute-start.23 = (bf16[128,2048]{1,0:T(8,128)(2,1)S(1)}, bf16[128,2048]{1,0:T(8,128)(2,1)S(1)}, u32[]{:S(2)}, u32[]{:S(2)}) collective-permute-start(bf16[128,2048]{1,0:T(8,128)(2,1)S(1)} %get-tuple-element.89), channel_id=1, source_target_pairs={{0,8},{8,0},{16,24},{24,16},{1,9},{9,1},{17,25},{25,17},{2,10},{10... | collective-permute-start | bytes 1572872 | tf_op jit(solution)/shard_map/ppermute | solution.py:60
  422.2 1.9 collective-permute-start.24
  437.0 30.7 %all-to-all-start.6 = ((bf16[8,112,256]{2,1,0:T(8,128)(2,1)}), bf16[8,112,256]{2,1,0:T(8,128)(2,1)}, u32[]{:S(2)}, u32[]{:S(2)}) async-start(bf16[8,112,256]{2,1,0:T(8,128)(2,1)} %get-tuple-element.94), calls=%async_computation.7 | async-start | bytes 917504 | tf_op jit(solution)/shard_map/all_to_all | solution.py:1047
  442.3 146.1 %reduce-scatter.10.cloned.1.call-start = ((), (), s32[]{:S(2)}) async-start(), calls=%async_computation.24 | async-start | bytes 4718592 | tf_op jit(solution)/shard_map/reduce_scatter | solution.py:49
  467.7 10.4 %collective-permute-start.27 = (bf16[8,512,128]{2,1,0:T(8,128)(2,1)}, bf16[8,512,128]{2,1,0:T(8,128)(2,1)}, u32[]{:S(2)}, u32[]{:S(2)}) collective-permute-start(bf16[8,512,128]{2,1,0:T(8,128)(2,1)} %broadcast_select_fusion), channel_id=1, source_target_pairs={{0,8},{8,0},{16,24},{24,16},{1,9},{9,1},{17,25},{25,17},{2,10},{10... | collective-permute-start | bytes 3145736 | tf_op jit(solution)/shard_map/ppermute | solution.py:60
  512.2 7.8 %collective-permute-start.25 = (bf16[256,2048]{1,0:T(8,128)(2,1)}, bf16[256,2048]{1,0:T(8,128)(2,1)S(1)}, u32[]{:S(2)}, u32[]{:S(2)}) collective-permute-start(bf16[256,2048]{1,0:T(8,128)(2,1)} %convolution_convert_fusion.5), channel_id=1, source_target_pairs={{0,8},{8,0},{16,24},{24,16},{1,9},{9,1},{17,25},{25,17},{2,10},{10... | collective-permute-start | bytes 3145736 | tf_op jit(solution)/shard_map/ppermute | solution.py:60
  514.9 19.3 %all-to-all-start.7 = ((bf16[8,96,256]{2,1,0:T(8,128)(2,1)}), bf16[8,96,256]{2,1,0:T(8,128)(2,1)S(1)}, u32[]{:S(2)}, u32[]{:S(2)}) async-start(bf16[8,96,256]{2,1,0:T(8,128)(2,1)} %shard_map.250.refs_4_), calls=%async_computation.8 | async-start | bytes 786432 | tf_op jit(solution)/shard_map/all_to_all | solution.py:1055
  523.2 18.3 %collective-permute-start.26 = (bf16[128,2048]{1,0:T(8,128)(2,1)}, bf16[128,2048]{1,0:T(8,128)(2,1)}, u32[]{:S(2)}, u32[]{:S(2)}) collective-permute-start(bf16[128,2048]{1,0:T(8,128)(2,1)} %fusion.10), channel_id=1, source_target_pairs={{0,16},{8,24},{16,0},{24,8},{1,17},{9,25},{17,1},{25,9},{2,18},{10... | collective-permute-start | bytes 1572872 | tf_op jit(solution)/shard_map/ppermute | solution.py:60
  535.0 41.1 %all-to-all-start.8 = ((bf16[8,512,128]{2,1,0:T(8,128)(2,1)}), bf16[8,512,128]{2,1,0:T(8,128)(2,1)S(1)}, u32[]{:S(2)}, u32[]{:S(2)}) async-start(bf16[8,512,128]{2,1,0:T(8,128)(2,1)} %add_convert_fusion.refs_11_), calls=%async_computation.9 | async-start | bytes 2097152 | tf_op jit(solution)/shard_map/all_to_all | solution.py:1203
  541.5 97.6 %reduce-scatter.12.cloned.1.call-start = ((), (), s32[]{:S(2)}) async-start(), calls=%async_computation.25 | async-start | bytes 4718592 | tf_op jit(solution)/shard_map/reduce_scatter | solution.py:49
  588.4 122.6 %reduce-scatter.14.cloned.1.call-start = ((), (), s32[]{:S(2)}) async-start(), calls=%async_computation.26 | async-start | bytes 5308416 | tf_op jit(solution)/shard_map/reduce_scatter | solution.py:49
  591.1 5.8 collective-permute-start.28
  598.9 1.6 collective-permute-start.29
  600.6 5.6 collective-permute-start.30
  648.3 30.0 %collective-permute-start.31 = (bf16[256,2048]{1,0:T(8,128)(2,1)}, bf16[256,2048]{1,0:T(8,128)(2,1)}, u32[]{:S(2)}, u32[]{:S(2)}) collective-permute-start(bf16[256,2048]{1,0:T(8,128)(2,1)} %fusion.6), channel_id=1, source_target_pairs={{0,8},{8,0},{16,24},{24,16},{1,9},{9,1},{17,25},{25,17},{2,10},{10... | collective-permute-start | bytes 3145736 | tf_op jit(solution)/shard_map/ppermute | solution.py:60
  650.9 1.4 collective-permute-start.34
  652.3 4.7 collective-permute-start.35
  657.1 4.6 collective-permute-start.36
  661.7 9.0 %collective-permute-start.37 = (f32[176,128]{1,0:T(8,128)S(1)}, f32[176,128]{1,0:T(8,128)S(1)}, u32[]{:S(2)}, u32[]{:S(2)}) collective-permute-start(f32[176,128]{1,0:T(8,128)S(1)} %add.278), channel_id=1, source_target_pairs={{0,2},{1,3},{2,0},{3,1},{4,6},{5,7},{6,4},{7,5},{8,10},{9,11},{10,... | collective-permute-start | bytes 270344 | tf_op jit(solution)/shard_map/ppermute | solution.py:885
  670.7 7.6 %collective-permute-start.38 = (f32[176,128]{1,0:T(8,128)S(1)}, f32[176,128]{1,0:T(8,128)S(1)}, u32[]{:S(2)}, u32[]{:S(2)}) collective-permute-start(f32[176,128]{1,0:T(8,128)S(1)} %add.279), channel_id=1, source_target_pairs={{0,4},{1,5},{2,6},{3,7},{4,0},{5,1},{6,2},{7,3},{8,12},{9,13},{10,... | collective-permute-start | bytes 270344 | tf_op jit(solution)/shard_map/ppermute | solution.py:885
  671.9 18.4 %all-to-all-start.10 = ((bf16[4,64,2048]{2,1,0:T(8,128)(2,1)}), bf16[4,64,2048]{2,1,0:T(8,128)(2,1)S(1)}, u32[]{:S(2)}, u32[]{:S(2)}) async-start(bf16[4,64,2048]{2,1,0:T(8,128)(2,1)} %bitcast.106), calls=%async_computation.14 | async-start | bytes 2097152 | tf_op jit(solution)/shard_map/all_to_all | solution.py:84
  681.3 33.2 %collective-permute-start.32 = (bf16[128,2048]{1,0:T(8,128)(2,1)}, bf16[128,2048]{1,0:T(8,128)(2,1)S(1)}, u32[]{:S(2)}, u32[]{:S(2)}) collective-permute-start(bf16[128,2048]{1,0:T(8,128)(2,1)} %fusion.8), channel_id=1, source_target_pairs={{0,16},{8,24},{16,0},{24,8},{1,17},{9,25},{17,1},{25,9},{2,18},{10... | collective-permute-start | bytes 1572872 | tf_op jit(solution)/shard_map/ppermute | solution.py:60
  690.4 20.6 %all-to-all-start.9 = ((bf16[4,64,1024]{2,1,0:T(8,128)(2,1)}), bf16[4,64,1024]{2,1,0:T(8,128)(2,1)S(1)}, u32[]{:S(2)}, u32[]{:S(2)}) async-start(bf16[4,64,1024]{2,1,0:T(8,128)(2,1)} %bitcast.24), calls=%async_computation.13 | async-start | bytes 1048576 | tf_op jit(solution)/shard_map/all_to_all | solution.py:84
  695.0 23.2 %collective-permute-start.33 = (bf16[128,2048]{1,0:T(8,128)(2,1)}, bf16[128,2048]{1,0:T(8,128)(2,1)}, u32[]{:S(2)}, u32[]{:S(2)}) collective-permute-start(bf16[128,2048]{1,0:T(8,128)(2,1)} %reduce-scatter.10.cloned.1.call-done), channel_id=1, source_target_pairs={{0,0},{2,1},{8,2},{10,3},{16,4},{18,5},{24,6},{26,7},{4,8},{6,9},{... | collective-permute-start | bytes 1572872 | tf_op jit(solution)/shard_map/ppermute | solution.py:1206
  711.0 16.5 %all-to-all-start.11 = ((bf16[4,64,1152]{2,1,0:T(8,128)(2,1)}), bf16[4,64,1152]{2,1,0:T(8,128)(2,1)S(1)}, u32[]{:S(2)}, u32[]{:S(2)}) async-start(bf16[4,64,1152]{2,1,0:T(8,128)(2,1)} %bitcast.107), calls=%async_computation.16 | async-start | bytes 1179648 | tf_op jit(solution)/shard_map/all_to_all | solution.py:84
  (142 other events, 954.6 us)
Sparse Core Ops, SparseCore 0:
  22.7 67.3 all-gather.5
  91.6 48.6 all-gather.7
  142.4 72.8 all-gather.9
  216.7 92.3 all-gather.11
  310.5 47.2 all-gather.13
  359.9 48.4 reduce-scatter.5
  410.6 96.9 reduce-scatter.7
  509.9 78.3 reduce-scatter.9
  590.6 48.3 reduce-scatter.11
  641.2 57.2 reduce-scatter.13

commit v5 on v4

--- a/solution.py
+++ b/solution.py
@@ -264,9 +264,40 @@
 
 def rope_kv(place_ref, in_ref, cosine_ref, sine_ref, out_ref):
     kv = in_ref[...]
-    kv = jnp.where(place_ref[1] == 0, turned(kv, cosine_ref[...], sine_ref[...]), kv).astype(low)
-    for k in range(out_ref.shape[0]):
-        out_ref[k] = kv
+    out_ref[...] = jnp.where(
+        place_ref[1] == 0, turned(kv, cosine_ref[...], sine_ref[...]), kv
+    ).astype(low)
+
+
+def kv_moves(span):
+    height = span * HD // D
+    return height, [(j * height, j * HD) for j in range(D // HD)]
+
+
+def pack_out(place_ref, out_rows_ref, kv_ref, packed_ref):
+    rows = out_rows_ref.shape[0]
+    packed_ref[:rows, :] = out_rows_ref[...]
+    height, moves = kv_moves(kv_ref.shape[0])
+    for begin, at in moves:
+        packed_ref[rows:, at : at + HD] = kv_ref[begin : begin + height, :]
+
+
+def unpack_out(place_ref, packed_ref, out_ref, kv_ref, *, ring):
+    rows = out_ref.shape[1]
+    height, moves = kv_moves(kv_ref.shape[1])
+    for i, k in enumerate(ring):
+        out_ref[i] = packed_ref[i, :rows, :]
+        for begin, at in moves:
+            kv_ref[k, begin : begin + height, :] = packed_ref[i, rows:, at : at + HD]
+
+
+def pack_out_grads(place_ref, out_ref, kv_ref, packed_ref, *, ring):
+    rows = out_ref.shape[1]
+    height, moves = kv_moves(kv_ref.shape[1])
+    for i, k in enumerate(ring):
+        packed_ref[i, :rows, :] = out_ref[i]
+        for begin, at in moves:
+            packed_ref[i, rows:, at : at + HD] = kv_ref[k, begin : begin + height, :]
 
 
 def rope_query(place_ref, in_ref, cosine_ref, sine_ref, query_ref, gate_ref):
@@ -299,12 +330,13 @@
     out_ref[:, :inner_columns] = inner_ref[...].astype(low)
     out_ref[:, inner_columns:step_at] = (near_ref[...] + far_ref[...].astype(jnp.float32)).astype(low)
     out_ref[:, step_at:kv_at] = step_ref[...].astype(low)
-    kv = kv_ref[0].astype(jnp.float32)
-    for k in range(1, kv_ref.shape[0]):
-        kv = kv + kv_ref[k].astype(jnp.float32)
-    out_ref[:, kv_at:] = jnp.where(
-        place_ref[1] == 0, turned(kv, cosine_ref[...], -sine_ref[...]), kv
-    ).astype(low)
+    height, moves = kv_moves(out_ref.shape[0])
+    for begin, at in moves:
+        rows = slice(begin, begin + height)
+        kv = kv_ref[:, at : at + HD].astype(jnp.float32)
+        out_ref[rows, kv_at:] = jnp.where(
+            place_ref[1] == 0, turned(kv, cosine_ref[rows, :], -sine_ref[rows, :]), kv
+        ).astype(low)
 
 
 def relative_order(place_ref, first_ref, second_ref, first_out, second_out):
@@ -945,7 +977,6 @@
     weights_rest = gather_blocks(rest_rows)
     gathered_tokens = gather_heads(after(tokens, conv_rows))
     out_rows = lax.ppermute(after(out_weight.astype(low), rest_rows), ("head", "blk"), out_pairs)
-    weights_out = gather_blocks(out_rows)
     rows_ffn = gate_up_weight.shape[0]
     units = FF // 4
     packed_ffn = call(
@@ -955,8 +986,6 @@
         [after(gate_up_weight, rest_rows)],
     )[0]
     ffn_rows = swap_heads(packed_ffn).reshape(-1, 2 * units)
-    weights_ffn = gather_blocks(after(ffn_rows, out_rows))
-    weights_down = gather_blocks(after(down_weight.astype(low), ffn_rows))
     model_cotangent = jnp.concatenate(gather_heads(after(cotangent, ffn_rows)))
 
     positions = block_index * span_rows + jnp.arange(span_rows, dtype=jnp.int32)
@@ -1011,7 +1040,7 @@
     projected = jnp.dot(normed_one, weights_conv, preferred_element_type=jnp.float32)
     kv_mine = call(
         rope_kv,
-        [shaped((blocks, span_rows, HD), low)],
+        [shaped((span_rows, HD), low)],
         place,
         [projected[:, kv_at:], cosine_wide, sine_wide],
     )[0]
@@ -1074,9 +1103,24 @@
         place,
         [projected_rest, cosine_wide, sine_wide],
     )
-    kv_blocks = lax.all_to_all(
-        kv_mine, "blk", split_axis=0, concat_axis=0, tiled=True
-    )
+    out_height = out_weight.shape[0] + span_rows * HD // D
+    out_packed = call(
+        pack_out, [shaped((out_height, D), low)], place, [out_rows, kv_mine]
+    )[0]
+    out_gathered = gather_blocks(after(out_packed, weights_rest, state_sent)).reshape(blocks, out_height, D)
+    weights_out, kv_blocks = call(
+        partial(unpack_out, ring=ring),
+        [
+            shaped((blocks, *out_weight.shape), low),
+            shaped((blocks, span_rows, HD), low),
+        ],
+        place,
+        [out_gathered],
+        after=[query_local, states_mine],
+    )
+    weights_out = weights_out.reshape(-1, D)
+    weights_ffn = gather_blocks(after(ffn_rows, out_gathered, query_local, states_mine))
+    weights_down = gather_blocks(after(down_weight.astype(low), weights_ffn))
     kv_beside = from_head(kv_blocks, 1)
     keys = jnp.where(even, kv_blocks, kv_beside)
     values = jnp.where(even, kv_beside, kv_blocks)
@@ -1157,11 +1201,12 @@
         scratch=[state_scratch],
         flops=2 * 10**9,
     )
+    ffn_swapped = swap_heads(grad_ffn.reshape(4, rows_ffn, 2 * units))
     grad_ffn_weight = call(
         partial(unpack_ffn, ring=ring),
         [shaped(gate_up_weight.shape, jnp.float32)],
         place,
-        [swap_heads(grad_ffn.reshape(4, rows_ffn, 2 * units))],
+        [ffn_swapped],
     )[0]
     activated_late = after(activated, span_grad_hidden)
     downed_other = jnp.dot(
@@ -1200,12 +1245,18 @@
         after=[later_mine],
     )[0]
     grad_rest_low = outer_grad(normed_one, grad_rest).astype(low)
-    grad_kv_parts = lax.all_to_all(kv_sums, "blk", split_axis=0, concat_axis=0, tiled=True)
-
-    grad_out_sum = scatter_blocks(after(grad_out_low, grad_ffn, grad_rest_low, kv_sums))
-    grad_mix_weight = lax.ppermute(
-        grad_out_sum, ("head", "blk"), [(there, here) for here, there in out_pairs]
-    ).astype(jnp.float32)
+
+    grad_out_packed = call(
+        partial(pack_out_grads, ring=ring),
+        [shaped((blocks, out_height, D), low)],
+        place,
+        [grad_out_low.reshape(blocks, -1, D), kv_sums],
+        after=[grad_rest_low],
+    )[0]
+    grad_out_sum = scatter_blocks(
+        after(grad_out_packed.reshape(-1, D), grad_ffn)
+    )
+    grad_kv = grad_out_sum[out_weight.shape[0] :]
     grad_inner, grad_into, grad_outof, grad_step, grad_decay_line = call(
         ssd_back,
         [
@@ -1229,7 +1280,7 @@
             state_in,
             later_grad,
         ],
-        after=[kv_sums, grad_rest_low, block_output],
+        after=[grad_out_packed, block_output],
         scratch=[
             pltpu.VMEM((span_rows // chunk + 1, inner_columns, NS), jnp.float32),
             state_scratch,
@@ -1239,7 +1290,6 @@
     grad_raw, grad_step_shift, grad_rate = step_back(
         (grad_step[:, :step_heads], grad_decay_line[:, :step_heads])
     )
-    grad_inner = after(grad_inner, grad_kv_parts)
     grad_extended, grad_taps, grad_shift = conv_back(
         jnp.concatenate([grad_inner, grad_into, grad_outof], axis=1)
     )
@@ -1265,11 +1315,12 @@
             in_lanes(grad_raw),
             cosine_wide,
             sine_wide,
-            grad_kv_parts,
+            grad_kv,
         ],
+        after=[ffn_swapped],
     )[0]
     grad_conv_low = outer_grad(normed_one, grad_conv).astype(low)
-    grad_rest_in = scatter_blocks(after(grad_rest_low, grad_out_sum, grad_taps))
+    grad_rest_in = scatter_blocks(after(grad_rest_low, grad_out_sum, grad_inner))
     conv_moved, rest_moved = call(
         relative_order,
         [shaped((span_rows, conv_columns), low), shaped((span_rows, rest_columns), low)],
@@ -1330,7 +1381,12 @@
     line = jnp.concatenate([part.reshape(-1) for part in small])
     line = jnp.pad(line, (0, -line.shape[0] % 1024)).reshape(-1, 128)
     line = summed_over(summed_over(line, "head"), "blk").reshape(-1)
-    grad_conv_in = scatter_blocks(after(grad_conv_low, grad_rest_in, grad_normed_own))
+    grad_conv_in = scatter_blocks(after(grad_conv_low, grad_rest_in))
+    grad_mix_weight = lax.ppermute(
+        after(grad_out_sum[: out_weight.shape[0]], grad_conv_in),
+        ("head", "blk"),
+        [(there, here) for here, there in out_pairs],
+    ).astype(jnp.float32)
     grad_proj_weight = call(
         unpack_in,
         [shaped(in_weight.shape, jnp.float32)],

time: 750 us -> 729 us (0.972)
  matrix products: 96.3 us -> 84.7 us
  starting transfers between devices: 83.7 us -> 72.6 us
  waiting for transfers between devices: 291 us -> 280 us
  Pallas kernels: 76.8 us -> 84.9 us
    all_gather x5, waiting for transfers between devices: 45.1 us -> 95.4 us  [gather_blocks(): lax.all_gather(shard, 'blk', axis=0, tiled=True, axis_index_groups=[ring_...]
    ppermute x2, waiting for transfers between devices: 29.8 us -> 0.91 us  [passed_along(): return lax.ppermute(shard, axis, pairs)]
    ppermute x27, waiting for transfers between devices: 64 us -> 86.9 us  [from_head(): lax.ppermute(shard, 'head', [(i, i ^ distance) for i in range(peers)])]
    all_to_all x0 -> x1, blocking collectives: none -> 21.9 us  [chained(): lax.all_to_all(payload, 'blk', split_axis=0, concat_axis=0, tiled=True)]
    all_to_all x3 -> x2, blocking collectives: 43.7 us -> 24.7 us  [swap_heads(): lax.all_to_all(pieces, 'head', split_axis=0, concat_axis=0, tiled=True)]
    ppermute x1, waiting for transfers between devices: 28.9 us -> 11.5 us  [per_device(): lax.ppermute(after(out_weight.astype(low), rest_rows), ('head', 'blk'), o...]
    all_to_all x2 -> x0, starting transfers between devices: 13.6 us -> none  [the longest x1 7.11 us: per_device(): lax.all_to_all(kv_mine, 'blk', split_axis=0, concat_axis=0, tiled=True)]
    all_to_all x2 -> x0, waiting for transfers between devices: 9.25 us -> none  [the longest x1 9.25 us: per_device(): lax.all_to_all(kv_sums, 'blk', split_axis=0, concat_axis=0, tiled=True)]
  transfers between devices with their start and end apart: 58 -> 56, of which waited for: 33 -> 33; matrix products, arithmetic and copies ran while one was open for 22% -> 21% of each run, Pallas kernels for 10% -> 12%
where the time goes in v5:
time: 729 us; the launch traced here: 718 us
  waiting for transfers between devices  280 us (38%)
  Pallas kernels  84.9 us (12%)
  matrix products  84.7 us (12%)
  local copies, waits for them, and re-layouts  82.3 us (11%)
  starting transfers between devices  72.6 us (10%)
  other arithmetic  50.7 us (7%)
  blocking collectives  46.6 us (6%)
  between operations  16.6 us (2%)
    all_gather x5, waiting for transfers between devices, gather_blocks(): lax.all_gather(shard, 'blk', axis=0, tiled=True, axis_index_groups=[ring_...  95.4 us
    ppermute x27, waiting for transfers between devices, from_head(): lax.ppermute(shard, 'head', [(i, i ^ distance) for i in range(peers)])  86.9 us
    unnamed x315, local copies, waits for them, and re-layouts  64.5 us
    pallas_call x23, Pallas kernels, call(): pl.pallas_call(body, out_shape=outputs, in_specs=[pl.BlockSpec(memory_spa...  62 us
    reduce_scatter x5, waiting for transfers between devices, scatter_blocks(): lax.psum_scatter(partial_sums, 'blk', scatter_dimension=0, tiled=True, ax...  58.1 us
    dot_general x8, matrix products, times_transposed(): lax.dot_general(grad_side, weight, (((1,), (1,)), ((), ())), preferred_el...  28.9 us
    dot_general x5, matrix products, outer_grad(): lax.dot_general(left_side, grad_side, (((0,), (0,)), ((), ())), preferred...  28.6 us
    all_to_all x2, blocking collectives, swap_heads(): lax.all_to_all(pieces, 'head', split_axis=0, concat_axis=0, tiled=True)  24.7 us
  transfers between devices with their start and end apart: 56, of which 33 were waited for; matrix products, arithmetic and copies ran while one was open for 21% of the time, Pallas kernels for 12%

profile of v5, /device:TPU:16, one launch (start us, length us, event | category | flops | bytes accessed | tf_op | source)
XLA Modules:
  0.0 718.1 jit_solution(2993872194878577600)
XLA Ops:
  9.7 12.8 %all_to_all.50 = bf16[4,64,1152]{2,1,0:T(8,128)(2,1)} all-to-all(bf16[4,64,1152]{2,1,0:T(8,128)(2,1)S(1)} %get-tuple-element.68), channel_id=1, replica_groups=mesh['head'=4,'blk'=8] {'head'}, dimensions={0} | all-to-all | bytes 1179648 | tf_op jit(solution)/shard_map/all_to_all | solution.py:84
  22.5 11.9 %all_to_all.51 = bf16[4,64,1024]{2,1,0:T(8,128)(2,1)} all-to-all(bf16[4,64,1024]{2,1,0:T(8,128)(2,1)S(1)} %get-tuple-element.71), channel_id=1, replica_groups=mesh['head'=4,'blk'=8] {'head'}, dimensions={0} | all-to-all | bytes 1048576 | tf_op jit(solution)/shard_map/all_to_all | solution.py:84
  39.3 10.5 %collective-permute-done.refs_1_ = bf16[128,2048]{1,0:T(8,128)(2,1)S(1)} collective-permute-done((bf16[128,2048]{1,0:T(8,128)(2,1)S(1)}, bf16[128,2048]{1,0:T(8,128)(2,1)S(1)}, u32[]{:S(2)}, u32[]{:S(2)}) %collective-permute-start) | collective-permute-done | bytes 524320 | tf_op jit(solution)/shard_map/ppermute | solution.py:60
  56.6 2.5 shard_map.238
  60.4 15.8 %all-gather.6.cloned.1.call-done = bf16[2048,1152]{1,0:T(8,128)(2,1)} async-done(((bf16[256,1152]{1,0:T(8,128)(2,1)}), bf16[2048,1152]{1,0:T(8,128)(2,1)}) %all-gather.6.cloned.1.call-update) | async-done | bytes 4718608 | tf_op jit(solution)/shard_map/all_gather | solution.py:45
  76.3 7.4 %fusion.61 = (bf16[512,1152]{1,0:T(8,128)(2,1)S(1)}, f32[512,1152]{1,0:T(8,128)}) fusion(bf16[512,2048]{1,0:T(8,128)(2,1)} %copy-done.16, bf16[2048,1152]{1,0:T(8,128)(2,1)} %all-gather.6.cloned.1.call-done), kind=kOutput, calls=%fused_computation.169 | convolution fusion | flops 2416508928 | bytes 10354688 | tf_op jit(solution)/shard_map/dot_general | solution.py:1040
  85.8 2.4 collective-permute-start.10
  91.9 4.2 all-to-all-start.2
  98.5 3.3 collective-permute-start.6
  106.1 11.5 %collective-permute-done.10.refs_0_ = bf16[128,2048]{1,0:T(8,128)(2,1)S(1)} collective-permute-done((bf16[128,2048]{1,0:T(8,128)(2,1)}, bf16[128,2048]{1,0:T(8,128)(2,1)S(1)}, u32[]{:S(2)}, u32[]{:S(2)}) %collective-permute-start.10) | collective-permute-done | bytes 524320 | tf_op jit(solution)/shard_map/ppermute | solution.py:979
  119.4 3.3 fusion.5
  127.6 7.3 %shard_map.241 = (f32[512,768]{1,0:T(8,128)S(1)}, bf16[8,112,256]{2,1,0:T(8,128)(2,1)S(1)}, f32[512,128]{1,0:T(8,128)S(1)}, f32[8,128]{1,0:T(8,128)S(1)}) custom-call(s32[8]{0:T(128)S(1)} %stack.40.place_ref, f32[512,768]{1,0:T(8,128)S(1)} %slice.420.refs_0_.refs_4_.refs_3_, f32[512,256]{1,0:T(8,128)S(1)} %copy-done.37, ...), custom_call_target="tpu_custom_call" | custom-call | flops 6000000000 | bytes 5705728 | tf_op jit(solution)/shard_map/pallas_call | solution.py:793
  137.6 2.5 all-gather.8.cloned.1.call-done
  140.2 21.9 %all_to_all.52.refs_0_ = bf16[8,112,256]{2,1,0:T(8,128)(2,1)S(1)} all-to-all(bf16[8,112,256]{2,1,0:T(8,128)(2,1)} %copy-done.42), channel_id=1, replica_groups=mesh['head'=4,'blk'=8] {'blk'}, dimensions={0} | all-to-all | bytes 917504 | tf_op jit(solution)/shard_map/all_to_all | solution.py:1076
  163.6 5.2 fusion.62.refs_0_
  170.6 36.5 %all-gather.10.cloned.1.call-done = bf16[1280,2048]{1,0:T(8,128)(2,1)} async-done(((bf16[160,2048]{1,0:T(8,128)(2,1)}), bf16[1280,2048]{1,0:T(8,128)(2,1)}) %all-gather.10.cloned.1.call-update) | async-done | bytes 5242896 | tf_op jit(solution)/shard_map/all_gather | solution.py:45
  211.5 3.8 shard_map.246
  217.2 6.6 collective-permute-done.12
  227.1 5.4 all-to-all-start.4
  235.2 12.8 %shard_map.247 = (f32[512,256]{1,0:T(8,128)S(1)}, f32[2,512,128]{2,1,0:T(8,128)S(1)}) custom-call(s32[3]{0:T(128)S(1)} %pad_add_fusion.4.refs_0_, bf16[512,256]{1,0:T(8,128)(2,1)S(1)} %copy-done.44, s32[512,128]{1,0:T(8,128)S(1)} %broadcast_in_dim.23.refs_2_, bf16[8,512,128]{2,1,0:T(8,128)(2,1)S(1)} %get-tuple-element.153.refs_3_, ...), custom_call_target="tpu_custom_call" | custom-call | flops 20000000000 | bytes 4000000 | tf_op jit(solution)/shard_map/pallas_call | solution.py:817
  262.1 40.5 %all-gather.12.cloned.1.call-done = bf16[2048,2048]{1,0:T(8,128)(2,1)} async-done(((bf16[256,2048]{1,0:T(8,128)(2,1)}), bf16[2048,2048]{1,0:T(8,128)(2,1)}) %all-gather.12.cloned.1.call-update) | async-done | bytes 8388624 | tf_op jit(solution)/shard_map/all_gather | solution.py:45
  302.9 3.7 fusion.31
  308.1 2.8 collective-permute-done.15
  312.5 12.5 %collective-permute-done.16 = bf16[128,2048]{1,0:T(8,128)(2,1)S(1)} collective-permute-done((bf16[128,2048]{1,0:T(8,128)(2,1)S(1)}, bf16[128,2048]{1,0:T(8,128)(2,1)S(1)}, u32[]{:S(2)}, u32[]{:S(2)}) %collective-permute-start.16) | collective-permute-done | bytes 524320 | tf_op jit(solution)/shard_map/ppermute | solution.py:60
  327.9 11.8 %collective-permute-done.17 = bf16[128,2048]{1,0:T(8,128)(2,1)S(1)} collective-permute-done((bf16[128,2048]{1,0:T(8,128)(2,1)S(1)}, bf16[128,2048]{1,0:T(8,128)(2,1)S(1)}, u32[]{:S(2)}, u32[]{:S(2)}) %collective-permute-start.17) | collective-permute-done | bytes 524320 | tf_op jit(solution)/shard_map/ppermute | solution.py:60
  342.9 4.6 fusion.63
  350.6 4.3 convolution_convert_fusion.4.refs_4_
  355.2 7.0 multiply_convert_fusion.1
  362.4 5.9 convolution_convert_fusion.6
  374.9 7.2 %convolution_convert_fusion.1.refs_5_ = bf16[2048,2048]{1,0:T(8,128)(2,1)} fusion(bf16[512,2048]{1,0:T(8,128)(2,1)S(1)} %copy-done.110, bf16[512,2048]{1,0:T(8,128)(2,1)S(1)} %pad_maximum_fusion), kind=kOutput, calls=%fused_computation.3 | convolution fusion | flops 4299161600 | bytes 12582912 | tf_op jit(solution)/shard_map/dot_general | solution.py:352
  382.2 5.6 collective-permute-done.21
  394.1 9.5 %reduce-scatter.6.cloned.1.call-done = bf16[128,2048]{1,0:T(8,128)(2,1)} async-done(((bf16[1024,2048]{1,0:T(8,128)(2,1)}), bf16[128,2048]{1,0:T(8,128)(2,1)}) %reduce-scatter.6.cloned.1.call-update) | async-done | bytes 524304 | tf_op jit(solution)/shard_map/reduce_scatter | solution.py:49
  405.1 12.3 %collective-permute-done.22 = bf16[128,2048]{1,0:T(8,128)(2,1)S(1)} collective-permute-done((bf16[128,2048]{1,0:T(8,128)(2,1)S(1)}, bf16[128,2048]{1,0:T(8,128)(2,1)S(1)}, u32[]{:S(2)}, u32[]{:S(2)}) %collective-permute-start.22) | collective-permute-done | bytes 524320 | tf_op jit(solution)/shard_map/ppermute | solution.py:60
  419.4 5.4 convolution_convert_fusion.7.refs_0_
  424.9 4.0 shard_map.251
  432.2 5.2 all-to-all-start.5
  437.5 6.2 convolution_convert_fusion.3.refs_8_
  443.8 10.2 %shard_map.253 = (f32[512,256]{1,0:T(8,128)S(1)}, bf16[8,512,128]{2,1,0:T(8,128)(2,1)S(1)}, bf16[8,512,128]{2,1,0:T(8,128)(2,1)S(1)}) custom-call(s32[3]{0:T(128)S(1)} %pad_add_fusion.4.refs_0_, bf16[512,256]{1,0:T(8,128)(2,1)S(1)} %copy-done.45, s32[512,128]{1,0:T(8,128)S(1)} %copy-done.57, bf16[8,512,128]{2,1,0:T(8,128)(2,1)S(1)} %copy-done.27, ...), custom_call_target="tpu_custom_call" | custom-call | flops 30000001024 | bytes 4000000 | tf_op jit(solution)/shard_map/pallas_call | solution.py:857
  459.6 4.4 convolution_convert_fusion.2.refs_2_
  469.7 3.3 shard_map.255.refs_11_
  473.0 29.9 %reduce-scatter.8.cloned.1.call-done = bf16[256,2048]{1,0:T(8,128)(2,1)} async-done(((bf16[2048,2048]{1,0:T(8,128)(2,1)}), bf16[256,2048]{1,0:T(8,128)(2,1)}) %reduce-scatter.8.cloned.1.call-update) | async-done | bytes 1048592 | tf_op jit(solution)/shard_map/reduce_scatter | solution.py:49
  504.1 3.6 convolution_convert_fusion.5
  514.4 5.1 all-to-all-start.6
  519.5 7.7 %collective-permute-done.26 = bf16[128,2048]{1,0:T(8,128)(2,1)} collective-permute-done((bf16[128,2048]{1,0:T(8,128)(2,1)}, bf16[128,2048]{1,0:T(8,128)(2,1)}, u32[]{:S(2)}, u32[]{:S(2)}) %collective-permute-start.26) | collective-permute-done | bytes 524320 | tf_op jit(solution)/shard_map/ppermute | solution.py:60
  527.2 2.7 fusion.13.refs_12_
  529.9 3.7 all-to-all-done.6
  541.1 18.7 %shard_map.256 = (f32[512,768]{1,0:T(8,128)S(1)}, f32[512,256]{1,0:T(8,128)S(1)}, f32[512,256]{1,0:T(8,128)S(1)}, f32[512,128]{1,0:T(8,128)S(1)}, f32[512,128]{1,0:T(8,128)S(1)}) custom-call(s32[8]{0:T(128)S(1)} %stack.40.place_ref, f32[512,768]{1,0:T(8,128)S(1)} %copy-done.21, f32[512,256]{1,0:T(8,128)S(1)} %copy-done.38, f32[512,256]{1,0:T(8,128)S(1)} %copy-done.36, ...), custom_call_target="tpu_custom_call" | custom-call | flops 10000000000 | bytes 10488832 | tf_op jit(solution)/shard_map/pallas_call | solution.py:793
  562.4 8.5 %reduce-scatter.10.cloned.1.call-done = bf16[160,2048]{1,0:T(8,128)(2,1)} async-done(((bf16[1280,2048]{1,0:T(8,128)(2,1)}), bf16[160,2048]{1,0:T(8,128)(2,1)}) %reduce-scatter.10.cloned.1.call-update) | async-done | bytes 655376 | tf_op jit(solution)/shard_map/reduce_scatter | solution.py:49
  574.2 4.8 multiply_reduce_fusion.5
  579.9 4.3 collective-permute-start.28
  587.9 3.7 all-to-all-start.7
  599.7 9.1 %collective-permute-done.30.refs_2_ = bf16[512,128]{1,0:T(8,128)(2,1)S(1)} collective-permute-done((bf16[512,128]{1,0:T(8,128)(2,1)S(1)}, bf16[512,128]{1,0:T(8,128)(2,1)S(1)}, u32[]{:S(2)}, u32[]{:S(2)}) %collective-permute-start.30) | collective-permute-done | bytes 131104 | tf_op jit(solution)/shard_map/ppermute | solution.py:60
  612.3 6.4 multiply_reduce_fusion
  619.7 2.4 reduce-scatter.12.cloned.1.call-done
  625.5 4.8 multiply_reduce_fusion.1
  634.3 4.1 fusion.21
  648.1 4.1 collective-permute-start.37
  653.8 3.2 collective-permute-done.37
  660.7 4.3 collective-permute-done.38
  669.1 3.5 all-to-all-start.8
  673.8 7.8 %reduce-scatter.14.cloned.1.call-done = bf16[256,1152]{1,0:T(8,128)(2,1)} async-done(((bf16[2048,1152]{1,0:T(8,128)(2,1)}), bf16[256,1152]{1,0:T(8,128)(2,1)}) %reduce-scatter.14.cloned.1.call-update) | async-done | bytes 589840 | tf_op jit(solution)/shard_map/reduce_scatter | solution.py:49
  684.3 5.4 all-to-all-start.9
  693.7 12.4 %all-to-all-done.9.refs_0_ = bf16[4,64,1152]{2,1,0:T(8,128)(2,1)} async-done(((bf16[4,64,1152]{2,1,0:T(8,128)(2,1)}), bf16[4,64,1152]{2,1,0:T(8,128)(2,1)}, u32[]{:S(2)}, u32[]{:S(2)}) %all-to-all-start.9) | async-done | bytes 589856 | tf_op jit(solution)/shard_map/all_to_all | solution.py:84
  706.2 2.6 shard_map.261
  (565 shorter events, 184.5 us)
Async XLA Ops:
  7.2 69.1 %all-gather.6.cloned.1.call-start = ((), (), s32[]{:S(2)}) async-start(), calls=%async_computation.15 | async-start | bytes 5308416 | tf_op jit(solution)/shard_map/all_gather | solution.py:45
  9.6 40.2 %copy-start.132 = (f32[4,3584]{1,0:T(4,128)S(1)}, f32[4,3584]{1,0:T(4,128)}, u32[]{:S(2)}) copy-start(f32[4,3584]{1,0:T(4,128)} %param.23) | copy-start | bytes 172036
  9.6 42.4 %copy-start.141 = (f32[48]{0:T(128)S(1)}, f32[48]{0:T(128)}, u32[]{:S(2)}) copy-start(f32[48]{0:T(128)} %param.26) | copy-start | bytes 580
  22.4 117.7 %all-gather.8.cloned.1.call-start = ((), (), s32[]{:S(2)}) async-start(), calls=%async_computation.16 | async-start | bytes 4718592 | tf_op jit(solution)/shard_map/all_gather | solution.py:45
  34.8 15.6 %collective-permute-start.7 = (s32[4096]{0:T(1024)S(1)}, s32[4096]{0:T(1024)S(1)}, u32[]{:S(2)}, u32[]{:S(2)}) collective-permute-start(s32[4096]{0:T(1024)S(1)} %dynamic_update_slice.20), channel_id=1, source_target_pairs={{0,1},{1,0},{2,3},{3,2},{4,5},{5,4},{6,7},{7,6},{8,9},{9,8},{10,11... | collective-permute-start | bytes 49160 | tf_op jit(solution)/shard_map/ppermute | solution.py:917
  36.4 13.4 %collective-permute-start = (bf16[128,2048]{1,0:T(8,128)(2,1)S(1)}, bf16[128,2048]{1,0:T(8,128)(2,1)S(1)}, u32[]{:S(2)}, u32[]{:S(2)}) collective-permute-start(bf16[128,2048]{1,0:T(8,128)(2,1)S(1)} %bitcast.89), channel_id=1, source_target_pairs={{0,16},{8,24},{16,0},{24,8},{1,17},{9,25},{17,1},{25,9},{2,18},{10... | collective-permute-start | bytes 1572872 | tf_op jit(solution)/shard_map/ppermute | solution.py:60
  39.3 17.3 %collective-permute-start.1 = (bf16[128,2048]{1,0:T(8,128)(2,1)S(1)}, bf16[128,2048]{1,0:T(8,128)(2,1)S(1)}, u32[]{:S(2)}, u32[]{:S(2)}) collective-permute-start(bf16[128,2048]{1,0:T(8,128)(2,1)S(1)} %bitcast.90), channel_id=1, source_target_pairs={{0,8},{8,0},{16,24},{24,16},{1,9},{9,1},{17,25},{25,17},{2,10},{10... | collective-permute-start | bytes 1572872 | tf_op jit(solution)/shard_map/ppermute | solution.py:60
  49.8 6.9 collective-permute-start.2
  50.6 5.6 collective-permute-start.8
  56.1 63.2 %copy-start.112 = (f32[1280]{0:T(1024)}, f32[1280]{0:T(1024)S(1)}, u32[]{:S(2)}) copy-start(f32[1280]{0:T(1024)S(1)} %get-tuple-element.128) | copy-start | bytes 15364
  56.1 29.1 %collective-permute-start.9 = (s32[4096]{0:T(1024)S(1)}, s32[4096]{0:T(1024)S(1)}, u32[]{:S(2)}, u32[]{:S(2)}) collective-permute-start(s32[4096]{0:T(1024)S(1)} %add.236), channel_id=1, source_target_pairs={{0,4},{1,5},{2,6},{3,7},{4,0},{5,1},{6,2},{7,3},{8,12},{9,13},{10,... | collective-permute-start | bytes 49160 | tf_op jit(solution)/shard_map/ppermute | solution.py:917
  83.7 5.7 collective-permute-start.3
  85.8 31.7 %collective-permute-start.10 = (bf16[128,2048]{1,0:T(8,128)(2,1)}, bf16[128,2048]{1,0:T(8,128)(2,1)S(1)}, u32[]{:S(2)}, u32[]{:S(2)}) collective-permute-start(bf16[128,2048]{1,0:T(8,128)(2,1)} %convert_element_type.153), channel_id=1, source_target_pairs={{0,0},{1,2},{2,8},{3,10},{4,16},{5,18},{6,24},{7,26},{8,4},{9,6},{... | collective-permute-start | bytes 1572872 | tf_op jit(solution)/shard_map/ppermute | solution.py:979
  88.3 9.4 %collective-permute-start.4 = (bf16[512,128]{1,0:T(8,128)(2,1)S(1)}, bf16[512,128]{1,0:T(8,128)(2,1)S(1)}, u32[]{:S(2)}, u32[]{:S(2)}) collective-permute-start(bf16[512,128]{1,0:T(8,128)(2,1)S(1)} %slice.410.refs_1_), channel_id=1, source_target_pairs={{0,8},{8,0},{16,24},{24,16},{1,9},{9,1},{17,25},{25,17},{2,10},{10... | collective-permute-start | bytes 393224 | tf_op jit(solution)/shard_map/ppermute | solution.py:60
  89.4 8.3 %collective-permute-start.5 = (bf16[512,128]{1,0:T(8,128)(2,1)S(1)}, bf16[512,128]{1,0:T(8,128)(2,1)S(1)}, u32[]{:S(2)}, u32[]{:S(2)}) collective-permute-start(bf16[512,128]{1,0:T(8,128)(2,1)S(1)} %collective-permute-done.3.refs_2_), channel_id=1, source_target_pairs={{0,8},{8,0},{16,24},{24,16},{1,9},{9,1},{17,25},{25,17},{2,10},{10... | collective-permute-start | bytes 393224 | tf_op jit(solution)/shard_map/ppermute | solution.py:60
  91.9 31.9 %all-to-all-start.2 = ((bf16[4,64,2048]{2,1,0:T(8,128)(2,1)}), bf16[4,64,2048]{2,1,0:T(8,128)(2,1)}, u32[]{:S(2)}, u32[]{:S(2)}) async-start(bf16[4,64,2048]{2,1,0:T(8,128)(2,1)} %shard_map.240), calls=%async_computation.2 | async-start | bytes 2097152 | tf_op jit(solution)/shard_map/all_to_all | solution.py:84
  96.1 111.0 %all-gather.10.cloned.1.call-start = ((), (), s32[]{:S(2)}) async-start(), calls=%async_computation.17 | async-start | bytes 5898240 | tf_op jit(solution)/shard_map/all_gather | solution.py:45
  98.5 20.5 %collective-permute-start.6 = (bf16[3,1280]{1,0:T(4,128)(2,1)S(1)}, bf16[3,1280]{1,0:T(4,128)(2,1)S(1)}, u32[]{:S(2)}, u32[]{:S(2)}) collective-permute-start(bf16[3,1280]{1,0:T(4,128)(2,1)S(1)} %slice.411), channel_id=1, source_target_pairs={{0,1},{1,2},{2,3},{3,4},{4,5},{5,6},{6,7},{8,9},{9,10},{10,11},{11... | collective-permute-start | bytes 23048 | tf_op jit(solution)/shard_map/ppermute | solution.py:34
  122.8 129.5 %copy-start.19 = (f32[512,768]{1,0:T(8,128)}, f32[512,768]{1,0:T(8,128)S(1)}, u32[]{:S(2)}) copy-start(f32[512,768]{1,0:T(8,128)S(1)} %slice.420.refs_0_.refs_4_.refs_3_) | copy-start | bytes 4718596
  140.2 162.4 %all-gather.12.cloned.1.call-start = ((), (), s32[]{:S(2)}) async-start(), calls=%async_computation.18 | async-start | bytes 9437184 | tf_op jit(solution)/shard_map/all_gather | solution.py:45
  168.8 40.6 %copy-start.120 = (s32[32,128]{1,0:T(8,128)S(1)}, s32[32,128]{1,0:T(8,128)}, u32[]{:S(2)}) copy-start(s32[32,128]{1,0:T(8,128)} %get-tuple-element.138) | copy-start | bytes 49156
  168.8 41.1 %copy-start.14 = (bf16[1,128,2048]{2,1,0:T(8,128)(2,1)S(1)}, bf16[1,128,2048]{2,1,0:T(8,128)(2,1)}, u32[]{:S(2)}) copy-start(bf16[1,128,2048]{2,1,0:T(8,128)(2,1)} %param.15) | copy-start | bytes 1572868
  170.6 44.7 %copy-start.43 = (bf16[512,256]{1,0:T(8,128)(2,1)}, bf16[512,256]{1,0:T(8,128)(2,1)S(1)}, u32[]{:S(2)}) copy-start(bf16[512,256]{1,0:T(8,128)(2,1)S(1)} %get-tuple-element.78.refs_1_) | copy-start | bytes 786436
  209.9 13.9 %collective-permute-start.12 = (bf16[128,2048]{1,0:T(8,128)(2,1)S(1)}, bf16[128,2048]{1,0:T(8,128)(2,1)S(1)}, u32[]{:S(2)}, u32[]{:S(2)}) collective-permute-start(bf16[128,2048]{1,0:T(8,128)(2,1)S(1)} %bitcast.95), channel_id=1, source_target_pairs={{0,16},{8,24},{16,0},{24,8},{1,17},{9,25},{17,1},{25,9},{2,18},{10... | collective-permute-start | bytes 1572872 | tf_op jit(solution)/shard_map/ppermute | solution.py:60
  211.5 12.5 %collective-permute-start.13 = (bf16[128,2048]{1,0:T(8,128)(2,1)S(1)}, bf16[128,2048]{1,0:T(8,128)(2,1)S(1)}, u32[]{:S(2)}, u32[]{:S(2)}) collective-permute-start(bf16[128,2048]{1,0:T(8,128)(2,1)S(1)} %bitcast.96), channel_id=1, source_target_pairs={{0,8},{8,0},{16,24},{24,16},{1,9},{9,1},{17,25},{25,17},{2,10},{10... | collective-permute-start | bytes 1572872 | tf_op jit(solution)/shard_map/ppermute | solution.py:60
  215.3 17.2 %collective-permute-start.11 = (bf16[8,512,128]{2,1,0:T(8,128)(2,1)}, bf16[8,512,128]{2,1,0:T(8,128)(2,1)}, u32[]{:S(2)}, u32[]{:S(2)}) collective-permute-start(bf16[8,512,128]{2,1,0:T(8,128)(2,1)} %get-tuple-element.81), channel_id=1, source_target_pairs={{0,8},{8,0},{16,24},{24,16},{1,9},{9,1},{17,25},{25,17},{2,10},{10... | collective-permute-start | bytes 3145736 | tf_op jit(solution)/shard_map/ppermute | solution.py:60
  223.9 1.9 collective-permute-start.14
  227.1 25.2 %all-to-all-start.4 = ((bf16[8,96,256]{2,1,0:T(8,128)(2,1)}), bf16[8,96,256]{2,1,0:T(8,128)(2,1)S(1)}, u32[]{:S(2)}, u32[]{:S(2)}) async-start(bf16[8,96,256]{2,1,0:T(8,128)(2,1)} %shard_map.242.refs_2_.refs_5_), calls=%async_computation.4 | async-start | bytes 786432 | tf_op jit(solution)/shard_map/all_to_all | solution.py:1084
  232.5 122.5 %all-gather.14.cloned.1.call-start = ((), (), s32[]{:S(2)}) async-start(), calls=%async_computation.19 | async-start | bytes 4718592 | tf_op jit(solution)/shard_map/all_gather | solution.py:45
  302.6 100.9 %reduce-scatter.6.cloned.1.call-start = ((), (), s32[]{:S(2)}) async-start(), calls=%async_computation.20 | async-start | bytes 4718592 | tf_op jit(solution)/shard_map/reduce_scatter | solution.py:49
  306.6 4.2 collective-permute-start.15
  311.0 14.0 %collective-permute-start.16 = (bf16[128,2048]{1,0:T(8,128)(2,1)S(1)}, bf16[128,2048]{1,0:T(8,128)(2,1)S(1)}, u32[]{:S(2)}, u32[]{:S(2)}) collective-permute-start(bf16[128,2048]{1,0:T(8,128)(2,1)S(1)} %fusion.16), channel_id=1, source_target_pairs={{0,16},{8,24},{16,0},{24,8},{1,17},{9,25},{17,1},{25,9},{2,18},{10... | collective-permute-start | bytes 1572872 | tf_op jit(solution)/shard_map/ppermute | solution.py:60
  326.3 63.2 %copy-start.9 = (f32[128,2048]{1,0:T(8,128)}, f32[128,2048]{1,0:T(8,128)S(1)}, u32[]{:S(2)}) copy-start(f32[128,2048]{1,0:T(8,128)S(1)} %get-tuple-element.86.refs_1_) | copy-start | bytes 3145732
  326.3 13.3 %collective-permute-start.17 = (bf16[128,2048]{1,0:T(8,128)(2,1)S(1)}, bf16[128,2048]{1,0:T(8,128)(2,1)S(1)}, u32[]{:S(2)}, u32[]{:S(2)}) collective-permute-start(bf16[128,2048]{1,0:T(8,128)(2,1)S(1)} %get-tuple-element.87), channel_id=1, source_target_pairs={{0,16},{8,24},{16,0},{24,8},{1,17},{9,25},{17,1},{25,9},{2,18},{10... | collective-permute-start | bytes 1572872 | tf_op jit(solution)/shard_map/ppermute | solution.py:60
  327.9 11.9 %collective-permute-start.18 = (bf16[128,2048]{1,0:T(8,128)(2,1)S(1)}, bf16[128,2048]{1,0:T(8,128)(2,1)S(1)}, u32[]{:S(2)}, u32[]{:S(2)}) collective-permute-start(bf16[128,2048]{1,0:T(8,128)(2,1)S(1)} %get-tuple-element.87), channel_id=1, source_target_pairs={{0,8},{8,0},{16,24},{24,16},{1,9},{9,1},{17,25},{25,17},{2,10},{10... | collective-permute-start | bytes 1572872 | tf_op jit(solution)/shard_map/ppermute | solution.py:60
  339.6 1.9 collective-permute-start.19
  355.0 147.9 %reduce-scatter.8.cloned.1.call-start = ((), (), s32[]{:S(2)}) async-start(), calls=%async_computation.21 | async-start | bytes 9437184 | tf_op jit(solution)/shard_map/reduce_scatter | solution.py:49
  368.3 2.7 collective-permute-start.20
  373.5 14.3 %collective-permute-start.21 = (bf16[128,2048]{1,0:T(8,128)(2,1)}, bf16[128,2048]{1,0:T(8,128)(2,1)S(1)}, u32[]{:S(2)}, u32[]{:S(2)}) collective-permute-start(bf16[128,2048]{1,0:T(8,128)(2,1)} %fusion.14), channel_id=1, source_target_pairs={{0,16},{8,24},{16,0},{24,8},{1,17},{9,25},{17,1},{25,9},{2,18},{10... | collective-permute-start | bytes 1572872 | tf_op jit(solution)/shard_map/ppermute | solution.py:60
  403.6 13.8 %collective-permute-start.22 = (bf16[128,2048]{1,0:T(8,128)(2,1)S(1)}, bf16[128,2048]{1,0:T(8,128)(2,1)S(1)}, u32[]{:S(2)}, u32[]{:S(2)}) collective-permute-start(bf16[128,2048]{1,0:T(8,128)(2,1)S(1)} %get-tuple-element.95), channel_id=1, source_target_pairs={{0,16},{8,24},{16,0},{24,8},{1,17},{9,25},{17,1},{25,9},{2,18},{10... | collective-permute-start | bytes 1572872 | tf_op jit(solution)/shard_map/ppermute | solution.py:60
  405.1 12.4 %collective-permute-start.23 = (bf16[128,2048]{1,0:T(8,128)(2,1)S(1)}, bf16[128,2048]{1,0:T(8,128)(2,1)S(1)}, u32[]{:S(2)}, u32[]{:S(2)}) collective-permute-start(bf16[128,2048]{1,0:T(8,128)(2,1)S(1)} %get-tuple-element.95), channel_id=1, source_target_pairs={{0,8},{8,0},{16,24},{24,16},{1,9},{9,1},{17,25},{25,17},{2,10},{10... | collective-permute-start | bytes 1572872 | tf_op jit(solution)/shard_map/ppermute | solution.py:60
  417.4 1.9 collective-permute-start.24
  432.2 22.9 %all-to-all-start.5 = ((bf16[8,112,256]{2,1,0:T(8,128)(2,1)}), bf16[8,112,256]{2,1,0:T(8,128)(2,1)S(1)}, u32[]{:S(2)}, u32[]{:S(2)}) async-start(bf16[8,112,256]{2,1,0:T(8,128)(2,1)} %get-tuple-element.100), calls=%async_computation.6 | async-start | bytes 917504 | tf_op jit(solution)/shard_map/all_to_all | solution.py:1076
  437.4 133.5 %reduce-scatter.10.cloned.1.call-start = ((), (), s32[]{:S(2)}) async-start(), calls=%async_computation.22 | async-start | bytes 5898240 | tf_op jit(solution)/shard_map/reduce_scatter | solution.py:49
  455.2 9.8 %collective-permute-start.27 = (bf16[8,512,128]{2,1,0:T(8,128)(2,1)}, bf16[8,512,128]{2,1,0:T(8,128)(2,1)}, u32[]{:S(2)}, u32[]{:S(2)}) collective-permute-start(bf16[8,512,128]{2,1,0:T(8,128)(2,1)} %broadcast_select_fusion), channel_id=1, source_target_pairs={{0,8},{8,0},{16,24},{24,16},{1,9},{9,1},{17,25},{25,17},{2,10},{10... | collective-permute-start | bytes 3145736 | tf_op jit(solution)/shard_map/ppermute | solution.py:60
  507.7 2.7 collective-permute-start.25
  512.9 14.3 %collective-permute-start.26 = (bf16[128,2048]{1,0:T(8,128)(2,1)}, bf16[128,2048]{1,0:T(8,128)(2,1)}, u32[]{:S(2)}, u32[]{:S(2)}) collective-permute-start(bf16[128,2048]{1,0:T(8,128)(2,1)} %fusion.10), channel_id=1, source_target_pairs={{0,16},{8,24},{16,0},{24,8},{1,17},{9,25},{17,1},{25,9},{2,18},{10... | collective-permute-start | bytes 1572872 | tf_op jit(solution)/shard_map/ppermute | solution.py:60
  514.4 19.3 %all-to-all-start.6 = ((bf16[8,96,256]{2,1,0:T(8,128)(2,1)}), bf16[8,96,256]{2,1,0:T(8,128)(2,1)}, u32[]{:S(2)}, u32[]{:S(2)}) async-start(bf16[8,96,256]{2,1,0:T(8,128)(2,1)} %shard_map.252.refs_4_), calls=%async_computation.7 | async-start | bytes 786432 | tf_op jit(solution)/shard_map/all_to_all | solution.py:1084
  519.5 102.7 %reduce-scatter.12.cloned.1.call-start = ((), (), s32[]{:S(2)}) async-start(), calls=%async_computation.23 | async-start | bytes 4718592 | tf_op jit(solution)/shard_map/reduce_scatter | solution.py:49
  579.9 6.0 collective-permute-start.28
  587.9 21.6 %all-to-all-start.7 = ((bf16[4,64,2048]{2,1,0:T(8,128)(2,1)}), bf16[4,64,2048]{2,1,0:T(8,128)(2,1)S(1)}, u32[]{:S(2)}, u32[]{:S(2)}) async-start(bf16[4,64,2048]{2,1,0:T(8,128)(2,1)} %bitcast.113), calls=%async_computation.10 | async-start | bytes 2097152 | tf_op jit(solution)/shard_map/all_to_all | solution.py:84
  591.6 90.0 %reduce-scatter.14.cloned.1.call-start = ((), (), s32[]{:S(2)}) async-start(), calls=%async_computation.24 | async-start | bytes 5308416 | tf_op jit(solution)/shard_map/reduce_scatter | solution.py:49
  592.3 1.8 collective-permute-start.29
  594.3 14.5 %collective-permute-start.30 = (bf16[512,128]{1,0:T(8,128)(2,1)S(1)}, bf16[512,128]{1,0:T(8,128)(2,1)S(1)}, u32[]{:S(2)}, u32[]{:S(2)}) collective-permute-start(bf16[512,128]{1,0:T(8,128)(2,1)S(1)} %get-tuple-element.154), channel_id=1, source_target_pairs={{0,16},{8,24},{16,0},{24,8},{1,17},{9,25},{17,1},{25,9},{2,18},{10... | collective-permute-start | bytes 393224 | tf_op jit(solution)/shard_map/ppermute | solution.py:60
  631.1 7.3 %collective-permute-start.34 = (f32[176,128]{1,0:T(8,128)S(1)}, f32[176,128]{1,0:T(8,128)S(1)}, u32[]{:S(2)}, u32[]{:S(2)}) collective-permute-start(f32[176,128]{1,0:T(8,128)S(1)} %pad_bitcast_fusion), channel_id=1, source_target_pairs={{0,8},{8,0},{16,24},{24,16},{1,9},{9,1},{17,25},{25,17},{2,10},{10... | collective-permute-start | bytes 270344 | tf_op jit(solution)/shard_map/ppermute | solution.py:917
  638.5 5.1 collective-permute-start.35
  641.3 23.7 %collective-permute-start.31 = (bf16[256,2048]{1,0:T(8,128)(2,1)S(1)}, bf16[256,2048]{1,0:T(8,128)(2,1)S(1)}, u32[]{:S(2)}, u32[]{:S(2)}) collective-permute-start(bf16[256,2048]{1,0:T(8,128)(2,1)S(1)} %fusion.6), channel_id=1, source_target_pairs={{0,8},{8,0},{16,24},{24,16},{1,9},{9,1},{17,25},{25,17},{2,10},{10... | collective-permute-start | bytes 3145736 | tf_op jit(solution)/shard_map/ppermute | solution.py:60
  643.5 4.6 collective-permute-start.36
  648.1 8.9 %collective-permute-start.37 = (f32[176,128]{1,0:T(8,128)S(1)}, f32[176,128]{1,0:T(8,128)S(1)}, u32[]{:S(2)}, u32[]{:S(2)}) collective-permute-start(f32[176,128]{1,0:T(8,128)S(1)} %add.278), channel_id=1, source_target_pairs={{0,2},{1,3},{2,0},{3,1},{4,6},{5,7},{6,4},{7,5},{8,10},{9,11},{10,... | collective-permute-start | bytes 270344 | tf_op jit(solution)/shard_map/ppermute | solution.py:917
  657.0 8.0 %collective-permute-start.38 = (f32[176,128]{1,0:T(8,128)S(1)}, f32[176,128]{1,0:T(8,128)S(1)}, u32[]{:S(2)}, u32[]{:S(2)}) collective-permute-start(f32[176,128]{1,0:T(8,128)S(1)} %add.279), channel_id=1, source_target_pairs={{0,4},{1,5},{2,6},{3,7},{4,0},{5,1},{6,2},{7,3},{8,12},{9,13},{10,... | collective-permute-start | bytes 270344 | tf_op jit(solution)/shard_map/ppermute | solution.py:917
  666.3 23.4 %collective-permute-start.32 = (bf16[128,2048]{1,0:T(8,128)(2,1)}, bf16[128,2048]{1,0:T(8,128)(2,1)}, u32[]{:S(2)}, u32[]{:S(2)}) collective-permute-start(bf16[128,2048]{1,0:T(8,128)(2,1)} %fusion.8), channel_id=1, source_target_pairs={{0,16},{8,24},{16,0},{24,8},{1,17},{9,25},{17,1},{25,9},{2,18},{10... | collective-permute-start | bytes 1572872 | tf_op jit(solution)/shard_map/ppermute | solution.py:60
  669.1 15.2 %all-to-all-start.8 = ((bf16[4,64,1024]{2,1,0:T(8,128)(2,1)}), bf16[4,64,1024]{2,1,0:T(8,128)(2,1)S(1)}, u32[]{:S(2)}, u32[]{:S(2)}) async-start(bf16[4,64,1024]{2,1,0:T(8,128)(2,1)} %bitcast.29), calls=%async_computation.12 | async-start | bytes 1048576 | tf_op jit(solution)/shard_map/all_to_all | solution.py:84
  681.6 27.2 %collective-permute-start.33 = (bf16[128,2048]{1,0:T(8,128)(2,1)}, bf16[128,2048]{1,0:T(8,128)(2,1)}, u32[]{:S(2)}, u32[]{:S(2)}) collective-permute-start(bf16[128,2048]{1,0:T(8,128)(2,1)} %slice.451), channel_id=1, source_target_pairs={{0,0},{2,1},{8,2},{10,3},{16,4},{18,5},{24,6},{26,7},{4,8},{6,9},{... | collective-permute-start | bytes 1572872 | tf_op jit(solution)/shard_map/ppermute | solution.py:1385
  684.3 21.9 %all-to-all-start.9 = ((bf16[4,64,1152]{2,1,0:T(8,128)(2,1)}), bf16[4,64,1152]{2,1,0:T(8,128)(2,1)}, u32[]{:S(2)}, u32[]{:S(2)}) async-start(bf16[4,64,1152]{2,1,0:T(8,128)(2,1)} %bitcast.114), calls=%async_computation.14 | async-start | bytes 1179648 | tf_op jit(solution)/shard_map/all_to_all | solution.py:84
  (146 other events, 963.2 us)
Sparse Core Ops, SparseCore 0:
  22.6 53.6 all-gather.5
  77.8 62.3 all-gather.7
  142.3 64.7 all-gather.9
  208.5 94.0 all-gather.11
  304.0 47.8 all-gather.13
  355.1 48.4 reduce-scatter.5
  405.8 96.9 reduce-scatter.7
  505.2 65.7 reduce-scatter.9
  573.3 48.8 reduce-scatter.11
  624.3 57.1 reduce-scatter.13

commit v6 on v5

--- a/solution.py
+++ b/solution.py
@@ -93,10 +93,12 @@
     for r in range(peers):
         if r < query_blocks * heads:
             group, slot = divmod(r, query_blocks)
+            turn = slot + mamba_blocks
         else:
-            group, slot = divmod(r - query_blocks * heads, mamba_blocks)
-            slot += query_blocks
-        pairs.append((r, group * len(ring) + ring[slot]))
+            group, turn = divmod(r - query_blocks * heads, mamba_blocks)
+            slot = turn + query_blocks
+        block = (mamba_blocks * group + turn) % len(ring) if len(ring) == 8 else ring[slot]
+        pairs.append((r, group * len(ring) + block))
     return pairs
 
 
@@ -509,26 +511,37 @@
     return pl.ds(pl.multiple_of(at * chunk, chunk), chunk)
 
 
+def mixer_lanes(place_ref, part, turned_columns):
+    if not turned_columns:
+        begin = (part + 2) % 8 * lanes
+        return slice(begin, begin + lanes)
+    block = lax.rem(6 * place_ref[0] + part, 8)
+    at = jnp.where(block % 2 == 0, block // 2, 7 - block // 2)
+    return pl.ds(pl.multiple_of(at * lanes, lanes), lanes)
+
+
 def ssd_finish(
     place_ref, y_ref, enter_ref, c_ref, state_ref, x_ref, z_ref, skip_ref, attended_ref,
-    ssd_ref, mixer_ref,
+    ssd_ref, mixer_ref, *, turned_columns,
 ):
     pairs = x_ref.shape[1] // lanes
-    width = attended_ref.shape[1]
 
     def body(index, carry):
         rows = chunk_rows(index)
         there = relative_rows(place_ref, index)
         outof = c_ref[rows, :].astype(low)
         entering = enter_ref[rows, :]
-        mixer_ref[there, :width] = attended_ref[rows, :].astype(low)
+        for half in range(2):
+            mixer_ref[there, mixer_lanes(place_ref, 6 + half, turned_columns)] = attended_ref[
+                rows, half * lanes : (half + 1) * lanes
+            ].astype(low)
         for pair in range(pairs):
             cols = slice(pair * lanes, (pair + 1) * lanes)
             ssd = y_ref[rows, cols] + spread(entering, pair) * dot_nt(outof, state_ref[cols, :])
             ssd_ref[rows, cols] = ssd
             gate = z_ref[rows, cols].astype(jnp.float32)
             total = ssd + skip_ref[:, cols] * x_ref[rows, cols]
-            mixer_ref[there, width + pair * lanes : width + (pair + 1) * lanes] = (
+            mixer_ref[there, mixer_lanes(place_ref, pair, turned_columns)] = (
                 total * gate / (1.0 + jnp.exp(-gate))
             ).astype(low)
         return carry
@@ -538,10 +551,9 @@
 
 def ssd_gate_back(
     place_ref, grad_ref, z_ref, ssd_ref, x_ref, skip_ref, enter_ref, c_ref, fac_ref,
-    dy_ref, dz_ref, sent_ref, dskip_ref, datt_ref, dstate_ref,
+    dy_ref, dz_ref, sent_ref, dskip_ref, datt_ref, dstate_ref, *, turned_columns,
 ):
     pairs = x_ref.shape[1] // lanes
-    width = datt_ref.shape[1]
     dstate_ref[...] = jnp.zeros_like(dstate_ref)
     dskip_ref[...] = jnp.zeros_like(dskip_ref)
 
@@ -550,14 +562,17 @@
         there = relative_rows(place_ref, index)
         outof = c_ref[rows, :].astype(low)
         entering = enter_ref[rows, :]
-        datt_ref[rows, :] = grad_ref[there, :width]
+        for half in range(2):
+            datt_ref[rows, half * lanes : (half + 1) * lanes] = grad_ref[
+                there, mixer_lanes(place_ref, 6 + half, turned_columns)
+            ]
         for pair in range(pairs):
             cols = slice(pair * lanes, (pair + 1) * lanes)
             gate = z_ref[rows, cols].astype(jnp.float32)
             sigmoid = 1.0 / (1.0 + jnp.exp(-gate))
-            grad = grad_ref[
-                there, width + pair * lanes : width + (pair + 1) * lanes
-            ].astype(jnp.float32)
+            grad = grad_ref[there, mixer_lanes(place_ref, pair, turned_columns)].astype(
+                jnp.float32
+            )
             x = x_ref[rows, cols]
             total = ssd_ref[rows, cols] + skip_ref[:, cols] * x
             dz_ref[rows, cols] = (
@@ -1129,7 +1144,7 @@
     )
 
     ssd, mixer = call(
-        ssd_finish,
+        partial(ssd_finish, turned_columns=blocks == 8),
         [tall, shaped((span_rows, query_columns + inner_columns), low)],
         place,
         [within, entering, outof_act, state_in, inner_act, gate_act, skip_wide, attended],
@@ -1188,7 +1203,7 @@
     span_grad_hidden = jnp.concatenate(gather_heads(after(grad_hidden_low, grad_down)))
     grad_heads = times_transposed(span_grad_hidden, weights_out).astype(low)
     grad_ssd, grad_gate, grad_sent, grad_skip_wide, grad_attended = call(
-        ssd_gate_back,
+        partial(ssd_gate_back, turned_columns=blocks == 8),
         [
             tall,
             tall_low,

time: 729 us -> 720 us (0.988)
  transfers between devices with their start and end apart: 56 -> 56, of which waited for: 33 -> 35; matrix products, arithmetic and copies ran while one was open for 21% -> 21% of each run, Pallas kernels for 12% -> 12%
where the time goes in v6:
time: 720 us; the launch traced here: 712 us
  waiting for transfers between devices  275 us (38%)
  Pallas kernels  84.9 us (12%)
  matrix products  84.7 us (12%)
  local copies, waits for them, and re-layouts  82.3 us (11%)
  starting transfers between devices  72.1 us (10%)
  other arithmetic  50.7 us (7%)
  blocking collectives  45.3 us (6%)
  between operations  16.6 us (2%)
    all_gather x5, waiting for transfers between devices, gather_blocks(): lax.all_gather(shard, 'blk', axis=0, tiled=True, axis_index_groups=[ring_...  95.8 us
    ppermute x27, waiting for transfers between devices, from_head(): lax.ppermute(shard, 'head', [(i, i ^ distance) for i in range(peers)])  87.5 us
    unnamed x315, local copies, waits for them, and re-layouts  64.5 us
    pallas_call x23, Pallas kernels, call(): pl.pallas_call(body, out_shape=outputs, in_specs=[pl.BlockSpec(memory_spa...  62 us
    reduce_scatter x5, waiting for transfers between devices, scatter_blocks(): lax.psum_scatter(partial_sums, 'blk', scatter_dimension=0, tiled=True, ax...  58.1 us
    dot_general x8, matrix products, times_transposed(): lax.dot_general(grad_side, weight, (((1,), (1,)), ((), ())), preferred_el...  28.9 us
    dot_general x5, matrix products, outer_grad(): lax.dot_general(left_side, grad_side, (((0,), (0,)), ((), ())), preferred...  28.6 us
    all_to_all x2, blocking collectives, swap_heads(): lax.all_to_all(pieces, 'head', split_axis=0, concat_axis=0, tiled=True)  24.7 us
  transfers between devices with their start and end apart: 56, of which 35 were waited for; matrix products, arithmetic and copies ran while one was open for 21% of the time, Pallas kernels for 12%

profile of v6, /device:TPU:16, one launch (start us, length us, event | category | flops | bytes accessed | tf_op | source)
XLA Modules:
  0.0 711.6 jit_solution(17055955548964059878)
XLA Ops:
  9.7 12.8 %all_to_all.50 = bf16[4,64,1152]{2,1,0:T(8,128)(2,1)} all-to-all(bf16[4,64,1152]{2,1,0:T(8,128)(2,1)S(1)} %get-tuple-element.68), channel_id=1, replica_groups=mesh['head'=4,'blk'=8] {'head'}, dimensions={0} | all-to-all | bytes 1179648 | tf_op jit(solution)/shard_map/all_to_all | solution.py:84
  22.5 11.9 %all_to_all.51 = bf16[4,64,1024]{2,1,0:T(8,128)(2,1)} all-to-all(bf16[4,64,1024]{2,1,0:T(8,128)(2,1)S(1)} %get-tuple-element.71), channel_id=1, replica_groups=mesh['head'=4,'blk'=8] {'head'}, dimensions={0} | all-to-all | bytes 1048576 | tf_op jit(solution)/shard_map/all_to_all | solution.py:84
  39.3 10.5 %collective-permute-done.refs_1_ = bf16[128,2048]{1,0:T(8,128)(2,1)S(1)} collective-permute-done((bf16[128,2048]{1,0:T(8,128)(2,1)S(1)}, bf16[128,2048]{1,0:T(8,128)(2,1)S(1)}, u32[]{:S(2)}, u32[]{:S(2)}) %collective-permute-start) | collective-permute-done | bytes 524320 | tf_op jit(solution)/shard_map/ppermute | solution.py:60
  56.6 2.5 shard_map.238
  60.4 15.8 %all-gather.6.cloned.1.call-done = bf16[2048,1152]{1,0:T(8,128)(2,1)} async-done(((bf16[256,1152]{1,0:T(8,128)(2,1)}), bf16[2048,1152]{1,0:T(8,128)(2,1)}) %all-gather.6.cloned.1.call-update) | async-done | bytes 4718608 | tf_op jit(solution)/shard_map/all_gather | solution.py:45
  76.3 7.4 %fusion.61 = (bf16[512,1152]{1,0:T(8,128)(2,1)S(1)}, f32[512,1152]{1,0:T(8,128)}) fusion(bf16[512,2048]{1,0:T(8,128)(2,1)} %copy-done.16, bf16[2048,1152]{1,0:T(8,128)(2,1)} %all-gather.6.cloned.1.call-done), kind=kOutput, calls=%fused_computation.169 | convolution fusion | flops 2416508928 | bytes 10354688 | tf_op jit(solution)/shard_map/dot_general | solution.py:1055
  85.8 2.4 collective-permute-start.10
  91.3 4.2 all-to-all-start.2
  97.9 3.9 collective-permute-start.6
  106.1 6.0 collective-permute-done.10.refs_0_
  114.8 3.3 fusion.5
  123.1 7.3 %shard_map.241 = (f32[512,768]{1,0:T(8,128)S(1)}, bf16[8,112,256]{2,1,0:T(8,128)(2,1)S(1)}, f32[512,128]{1,0:T(8,128)S(1)}, f32[8,128]{1,0:T(8,128)S(1)}) custom-call(s32[8]{0:T(128)S(1)} %stack.40.place_ref, f32[512,768]{1,0:T(8,128)S(1)} %slice.420.refs_0_.refs_4_.refs_3_, f32[512,256]{1,0:T(8,128)S(1)} %copy-done.37, ...), custom_call_target="tpu_custom_call" | custom-call | flops 6000000000 | bytes 5705728 | tf_op jit(solution)/shard_map/pallas_call | solution.py:808
  133.1 3.0 all-gather.8.cloned.1.call-done
  136.1 20.5 %all_to_all.52.refs_0_ = bf16[8,112,256]{2,1,0:T(8,128)(2,1)S(1)} all-to-all(bf16[8,112,256]{2,1,0:T(8,128)(2,1)} %copy-done.42), channel_id=1, replica_groups=mesh['head'=4,'blk'=8] {'blk'}, dimensions={0} | all-to-all | bytes 917504 | tf_op jit(solution)/shard_map/all_to_all | solution.py:1091
  158.2 5.2 fusion.62.refs_0_
  165.1 36.5 %all-gather.10.cloned.1.call-done = bf16[1280,2048]{1,0:T(8,128)(2,1)} async-done(((bf16[160,2048]{1,0:T(8,128)(2,1)}), bf16[1280,2048]{1,0:T(8,128)(2,1)}) %all-gather.10.cloned.1.call-update) | async-done | bytes 5242896 | tf_op jit(solution)/shard_map/all_gather | solution.py:45
  206.1 3.8 shard_map.246
  211.8 6.6 collective-permute-done.12
  221.7 5.4 all-to-all-start.4
  229.8 12.8 %shard_map.247 = (f32[512,256]{1,0:T(8,128)S(1)}, f32[2,512,128]{2,1,0:T(8,128)S(1)}) custom-call(s32[3]{0:T(128)S(1)} %pad_add_fusion.4.refs_0_, bf16[512,256]{1,0:T(8,128)(2,1)S(1)} %copy-done.44, s32[512,128]{1,0:T(8,128)S(1)} %broadcast_in_dim.23.refs_2_, bf16[8,512,128]{2,1,0:T(8,128)(2,1)S(1)} %get-tuple-element.153.refs_3_, ...), custom_call_target="tpu_custom_call" | custom-call | flops 20000000000 | bytes 4000000 | tf_op jit(solution)/shard_map/pallas_call | solution.py:832
  256.6 40.5 %all-gather.12.cloned.1.call-done = bf16[2048,2048]{1,0:T(8,128)(2,1)} async-done(((bf16[256,2048]{1,0:T(8,128)(2,1)}), bf16[2048,2048]{1,0:T(8,128)(2,1)}) %all-gather.12.cloned.1.call-update) | async-done | bytes 8388624 | tf_op jit(solution)/shard_map/all_gather | solution.py:45
  297.4 3.7 fusion.31
  302.6 2.8 collective-permute-done.15
  307.0 12.5 %collective-permute-done.16 = bf16[128,2048]{1,0:T(8,128)(2,1)S(1)} collective-permute-done((bf16[128,2048]{1,0:T(8,128)(2,1)S(1)}, bf16[128,2048]{1,0:T(8,128)(2,1)S(1)}, u32[]{:S(2)}, u32[]{:S(2)}) %collective-permute-start.16) | collective-permute-done | bytes 524320 | tf_op jit(solution)/shard_map/ppermute | solution.py:60
  322.4 11.8 %collective-permute-done.17 = bf16[128,2048]{1,0:T(8,128)(2,1)S(1)} collective-permute-done((bf16[128,2048]{1,0:T(8,128)(2,1)S(1)}, bf16[128,2048]{1,0:T(8,128)(2,1)S(1)}, u32[]{:S(2)}, u32[]{:S(2)}) %collective-permute-start.17) | collective-permute-done | bytes 524320 | tf_op jit(solution)/shard_map/ppermute | solution.py:60
  337.4 4.6 fusion.63
  345.2 4.3 convolution_convert_fusion.4.refs_4_
  349.8 7.0 multiply_convert_fusion.1
  356.9 5.9 convolution_convert_fusion.6
  369.5 7.2 %convolution_convert_fusion.1.refs_5_ = bf16[2048,2048]{1,0:T(8,128)(2,1)} fusion(bf16[512,2048]{1,0:T(8,128)(2,1)S(1)} %copy-done.110, bf16[512,2048]{1,0:T(8,128)(2,1)S(1)} %pad_maximum_fusion), kind=kOutput, calls=%fused_computation.3 | convolution fusion | flops 4299161600 | bytes 12582912 | tf_op jit(solution)/shard_map/dot_general | solution.py:354
  376.7 5.6 collective-permute-done.21
  388.6 9.4 %reduce-scatter.6.cloned.1.call-done = bf16[128,2048]{1,0:T(8,128)(2,1)} async-done(((bf16[1024,2048]{1,0:T(8,128)(2,1)}), bf16[128,2048]{1,0:T(8,128)(2,1)}) %reduce-scatter.6.cloned.1.call-update) | async-done | bytes 524304 | tf_op jit(solution)/shard_map/reduce_scatter | solution.py:49
  399.6 12.3 %collective-permute-done.22 = bf16[128,2048]{1,0:T(8,128)(2,1)S(1)} collective-permute-done((bf16[128,2048]{1,0:T(8,128)(2,1)S(1)}, bf16[128,2048]{1,0:T(8,128)(2,1)S(1)}, u32[]{:S(2)}, u32[]{:S(2)}) %collective-permute-start.22) | collective-permute-done | bytes 524320 | tf_op jit(solution)/shard_map/ppermute | solution.py:60
  413.9 5.4 convolution_convert_fusion.7.refs_0_
  419.4 4.0 shard_map.251
  426.8 5.2 all-to-all-start.5
  432.0 6.2 convolution_convert_fusion.3.refs_8_
  438.3 10.2 %shard_map.253 = (f32[512,256]{1,0:T(8,128)S(1)}, bf16[8,512,128]{2,1,0:T(8,128)(2,1)S(1)}, bf16[8,512,128]{2,1,0:T(8,128)(2,1)S(1)}) custom-call(s32[3]{0:T(128)S(1)} %pad_add_fusion.4.refs_0_, bf16[512,256]{1,0:T(8,128)(2,1)S(1)} %copy-done.45, s32[512,128]{1,0:T(8,128)S(1)} %copy-done.57, bf16[8,512,128]{2,1,0:T(8,128)(2,1)S(1)} %copy-done.27, ...), custom_call_target="tpu_custom_call" | custom-call | flops 30000001024 | bytes 4000000 | tf_op jit(solution)/shard_map/pallas_call | solution.py:872
  454.2 4.4 convolution_convert_fusion.2.refs_2_
  464.3 3.3 shard_map.255.refs_11_
  467.5 29.9 %reduce-scatter.8.cloned.1.call-done = bf16[256,2048]{1,0:T(8,128)(2,1)} async-done(((bf16[2048,2048]{1,0:T(8,128)(2,1)}), bf16[256,2048]{1,0:T(8,128)(2,1)}) %reduce-scatter.8.cloned.1.call-update) | async-done | bytes 1048592 | tf_op jit(solution)/shard_map/reduce_scatter | solution.py:49
  498.6 3.6 convolution_convert_fusion.5
  508.9 5.1 all-to-all-start.6
  514.1 7.7 %collective-permute-done.26 = bf16[128,2048]{1,0:T(8,128)(2,1)} collective-permute-done((bf16[128,2048]{1,0:T(8,128)(2,1)}, bf16[128,2048]{1,0:T(8,128)(2,1)}, u32[]{:S(2)}, u32[]{:S(2)}) %collective-permute-start.26) | collective-permute-done | bytes 524320 | tf_op jit(solution)/shard_map/ppermute | solution.py:60
  521.7 2.7 fusion.13.refs_12_
  524.5 3.7 all-to-all-done.6
  535.7 18.8 %shard_map.256 = (f32[512,768]{1,0:T(8,128)S(1)}, f32[512,256]{1,0:T(8,128)S(1)}, f32[512,256]{1,0:T(8,128)S(1)}, f32[512,128]{1,0:T(8,128)S(1)}, f32[512,128]{1,0:T(8,128)S(1)}) custom-call(s32[8]{0:T(128)S(1)} %stack.40.place_ref, f32[512,768]{1,0:T(8,128)S(1)} %copy-done.21, f32[512,256]{1,0:T(8,128)S(1)} %copy-done.38, f32[512,256]{1,0:T(8,128)S(1)} %copy-done.36, ...), custom_call_target="tpu_custom_call" | custom-call | flops 10000000000 | bytes 10488832 | tf_op jit(solution)/shard_map/pallas_call | solution.py:808
  557.0 8.5 %reduce-scatter.10.cloned.1.call-done = bf16[160,2048]{1,0:T(8,128)(2,1)} async-done(((bf16[1280,2048]{1,0:T(8,128)(2,1)}), bf16[160,2048]{1,0:T(8,128)(2,1)}) %reduce-scatter.10.cloned.1.call-update) | async-done | bytes 655376 | tf_op jit(solution)/shard_map/reduce_scatter | solution.py:49
  568.7 4.8 multiply_reduce_fusion.5
  574.4 4.3 collective-permute-start.28
  582.4 3.7 all-to-all-start.7
  594.3 9.1 %collective-permute-done.30.refs_2_ = bf16[512,128]{1,0:T(8,128)(2,1)S(1)} collective-permute-done((bf16[512,128]{1,0:T(8,128)(2,1)S(1)}, bf16[512,128]{1,0:T(8,128)(2,1)S(1)}, u32[]{:S(2)}, u32[]{:S(2)}) %collective-permute-start.30) | collective-permute-done | bytes 131104 | tf_op jit(solution)/shard_map/ppermute | solution.py:60
  606.8 6.4 multiply_reduce_fusion
  614.3 2.4 reduce-scatter.12.cloned.1.call-done
  620.0 4.8 multiply_reduce_fusion.1
  628.8 4.1 fusion.21
  642.7 4.1 collective-permute-start.37
  648.3 3.2 collective-permute-done.37
  655.2 4.3 collective-permute-done.38
  663.6 3.5 all-to-all-start.8
  668.3 7.8 %reduce-scatter.14.cloned.1.call-done = bf16[256,1152]{1,0:T(8,128)(2,1)} async-done(((bf16[2048,1152]{1,0:T(8,128)(2,1)}), bf16[256,1152]{1,0:T(8,128)(2,1)}) %reduce-scatter.14.cloned.1.call-update) | async-done | bytes 589840 | tf_op jit(solution)/shard_map/reduce_scatter | solution.py:49
  678.8 5.4 all-to-all-start.9
  688.3 11.3 %all-to-all-done.9.refs_0_ = bf16[4,64,1152]{2,1,0:T(8,128)(2,1)} async-done(((bf16[4,64,1152]{2,1,0:T(8,128)(2,1)}), bf16[4,64,1152]{2,1,0:T(8,128)(2,1)}, u32[]{:S(2)}, u32[]{:S(2)}) %all-to-all-start.9) | async-done | bytes 589856 | tf_op jit(solution)/shard_map/all_to_all | solution.py:84
  699.6 2.6 shard_map.261
  (565 shorter events, 184.9 us)
Async XLA Ops:
  7.2 69.1 %all-gather.6.cloned.1.call-start = ((), (), s32[]{:S(2)}) async-start(), calls=%async_computation.15 | async-start | bytes 5308416 | tf_op jit(solution)/shard_map/all_gather | solution.py:45
  9.6 40.2 %copy-start.132 = (f32[4,3584]{1,0:T(4,128)S(1)}, f32[4,3584]{1,0:T(4,128)}, u32[]{:S(2)}) copy-start(f32[4,3584]{1,0:T(4,128)} %param.23) | copy-start | bytes 172036
  9.6 42.4 %copy-start.141 = (f32[48]{0:T(128)S(1)}, f32[48]{0:T(128)}, u32[]{:S(2)}) copy-start(f32[48]{0:T(128)} %param.26) | copy-start | bytes 580
  22.4 113.6 %all-gather.8.cloned.1.call-start = ((), (), s32[]{:S(2)}) async-start(), calls=%async_computation.16 | async-start | bytes 4718592 | tf_op jit(solution)/shard_map/all_gather | solution.py:45
  34.8 15.6 %collective-permute-start.7 = (s32[4096]{0:T(1024)S(1)}, s32[4096]{0:T(1024)S(1)}, u32[]{:S(2)}, u32[]{:S(2)}) collective-permute-start(s32[4096]{0:T(1024)S(1)} %dynamic_update_slice.20), channel_id=1, source_target_pairs={{0,1},{1,0},{2,3},{3,2},{4,5},{5,4},{6,7},{7,6},{8,9},{9,8},{10,11... | collective-permute-start | bytes 49160 | tf_op jit(solution)/shard_map/ppermute | solution.py:932
  36.4 13.4 %collective-permute-start = (bf16[128,2048]{1,0:T(8,128)(2,1)S(1)}, bf16[128,2048]{1,0:T(8,128)(2,1)S(1)}, u32[]{:S(2)}, u32[]{:S(2)}) collective-permute-start(bf16[128,2048]{1,0:T(8,128)(2,1)S(1)} %bitcast.89), channel_id=1, source_target_pairs={{0,16},{8,24},{16,0},{24,8},{1,17},{9,25},{17,1},{25,9},{2,18},{10... | collective-permute-start | bytes 1572872 | tf_op jit(solution)/shard_map/ppermute | solution.py:60
  39.3 17.3 %collective-permute-start.1 = (bf16[128,2048]{1,0:T(8,128)(2,1)S(1)}, bf16[128,2048]{1,0:T(8,128)(2,1)S(1)}, u32[]{:S(2)}, u32[]{:S(2)}) collective-permute-start(bf16[128,2048]{1,0:T(8,128)(2,1)S(1)} %bitcast.90), channel_id=1, source_target_pairs={{0,8},{8,0},{16,24},{24,16},{1,9},{9,1},{17,25},{25,17},{2,10},{10... | collective-permute-start | bytes 1572872 | tf_op jit(solution)/shard_map/ppermute | solution.py:60
  49.8 6.9 collective-permute-start.2
  50.6 5.6 collective-permute-start.8
  56.1 58.6 %copy-start.112 = (f32[1280]{0:T(1024)}, f32[1280]{0:T(1024)S(1)}, u32[]{:S(2)}) copy-start(f32[1280]{0:T(1024)S(1)} %get-tuple-element.128) | copy-start | bytes 15364
  56.1 29.1 %collective-permute-start.9 = (s32[4096]{0:T(1024)S(1)}, s32[4096]{0:T(1024)S(1)}, u32[]{:S(2)}, u32[]{:S(2)}) collective-permute-start(s32[4096]{0:T(1024)S(1)} %add.236), channel_id=1, source_target_pairs={{0,4},{1,5},{2,6},{3,7},{4,0},{5,1},{6,2},{7,3},{8,12},{9,13},{10,... | collective-permute-start | bytes 49160 | tf_op jit(solution)/shard_map/ppermute | solution.py:932
  83.7 5.3 collective-permute-start.3
  85.8 26.3 %collective-permute-start.10 = (bf16[128,2048]{1,0:T(8,128)(2,1)}, bf16[128,2048]{1,0:T(8,128)(2,1)S(1)}, u32[]{:S(2)}, u32[]{:S(2)}) collective-permute-start(bf16[128,2048]{1,0:T(8,128)(2,1)} %convert_element_type.153), channel_id=1, source_target_pairs={{0,6},{1,7},{2,12},{3,13},{4,18},{5,19},{6,24},{7,25},{8,0},{9,1},... | collective-permute-start | bytes 1572872 | tf_op jit(solution)/shard_map/ppermute | solution.py:994
  88.4 8.8 %collective-permute-start.4 = (bf16[512,128]{1,0:T(8,128)(2,1)S(1)}, bf16[512,128]{1,0:T(8,128)(2,1)S(1)}, u32[]{:S(2)}, u32[]{:S(2)}) collective-permute-start(bf16[512,128]{1,0:T(8,128)(2,1)S(1)} %slice.410.refs_1_), channel_id=1, source_target_pairs={{0,8},{8,0},{16,24},{24,16},{1,9},{9,1},{17,25},{25,17},{2,10},{10... | collective-permute-start | bytes 393224 | tf_op jit(solution)/shard_map/ppermute | solution.py:60
  89.0 8.2 %collective-permute-start.5 = (bf16[512,128]{1,0:T(8,128)(2,1)S(1)}, bf16[512,128]{1,0:T(8,128)(2,1)S(1)}, u32[]{:S(2)}, u32[]{:S(2)}) collective-permute-start(bf16[512,128]{1,0:T(8,128)(2,1)S(1)} %collective-permute-done.3.refs_2_), channel_id=1, source_target_pairs={{0,8},{8,0},{16,24},{24,16},{1,9},{9,1},{17,25},{25,17},{2,10},{10... | collective-permute-start | bytes 393224 | tf_op jit(solution)/shard_map/ppermute | solution.py:60
  91.3 27.9 %all-to-all-start.2 = ((bf16[4,64,2048]{2,1,0:T(8,128)(2,1)}), bf16[4,64,2048]{2,1,0:T(8,128)(2,1)}, u32[]{:S(2)}, u32[]{:S(2)}) async-start(bf16[4,64,2048]{2,1,0:T(8,128)(2,1)} %shard_map.240), calls=%async_computation.2 | async-start | bytes 2097152 | tf_op jit(solution)/shard_map/all_to_all | solution.py:84
  95.6 106.1 %all-gather.10.cloned.1.call-start = ((), (), s32[]{:S(2)}) async-start(), calls=%async_computation.17 | async-start | bytes 5898240 | tf_op jit(solution)/shard_map/all_gather | solution.py:45
  97.9 16.6 %collective-permute-start.6 = (bf16[3,1280]{1,0:T(4,128)(2,1)S(1)}, bf16[3,1280]{1,0:T(4,128)(2,1)S(1)}, u32[]{:S(2)}, u32[]{:S(2)}) collective-permute-start(bf16[3,1280]{1,0:T(4,128)(2,1)S(1)} %slice.411), channel_id=1, source_target_pairs={{0,1},{1,2},{2,3},{3,4},{4,5},{5,6},{6,7},{8,9},{9,10},{10,11},{11... | collective-permute-start | bytes 23048 | tf_op jit(solution)/shard_map/ppermute | solution.py:34
  118.3 128.6 %copy-start.19 = (f32[512,768]{1,0:T(8,128)}, f32[512,768]{1,0:T(8,128)S(1)}, u32[]{:S(2)}) copy-start(f32[512,768]{1,0:T(8,128)S(1)} %slice.420.refs_0_.refs_4_.refs_3_) | copy-start | bytes 4718596
  136.1 161.1 %all-gather.12.cloned.1.call-start = ((), (), s32[]{:S(2)}) async-start(), calls=%async_computation.18 | async-start | bytes 9437184 | tf_op jit(solution)/shard_map/all_gather | solution.py:45
  163.4 40.6 %copy-start.120 = (s32[32,128]{1,0:T(8,128)S(1)}, s32[32,128]{1,0:T(8,128)}, u32[]{:S(2)}) copy-start(s32[32,128]{1,0:T(8,128)} %get-tuple-element.138) | copy-start | bytes 49156
  163.4 41.1 %copy-start.14 = (bf16[1,128,2048]{2,1,0:T(8,128)(2,1)S(1)}, bf16[1,128,2048]{2,1,0:T(8,128)(2,1)}, u32[]{:S(2)}) copy-start(bf16[1,128,2048]{2,1,0:T(8,128)(2,1)} %param.15) | copy-start | bytes 1572868
  165.1 44.7 %copy-start.43 = (bf16[512,256]{1,0:T(8,128)(2,1)}, bf16[512,256]{1,0:T(8,128)(2,1)S(1)}, u32[]{:S(2)}) copy-start(bf16[512,256]{1,0:T(8,128)(2,1)S(1)} %get-tuple-element.78.refs_1_) | copy-start | bytes 786436
  204.5 13.9 %collective-permute-start.12 = (bf16[128,2048]{1,0:T(8,128)(2,1)S(1)}, bf16[128,2048]{1,0:T(8,128)(2,1)S(1)}, u32[]{:S(2)}, u32[]{:S(2)}) collective-permute-start(bf16[128,2048]{1,0:T(8,128)(2,1)S(1)} %bitcast.95), channel_id=1, source_target_pairs={{0,16},{8,24},{16,0},{24,8},{1,17},{9,25},{17,1},{25,9},{2,18},{10... | collective-permute-start | bytes 1572872 | tf_op jit(solution)/shard_map/ppermute | solution.py:60
  206.0 12.5 %collective-permute-start.13 = (bf16[128,2048]{1,0:T(8,128)(2,1)S(1)}, bf16[128,2048]{1,0:T(8,128)(2,1)S(1)}, u32[]{:S(2)}, u32[]{:S(2)}) collective-permute-start(bf16[128,2048]{1,0:T(8,128)(2,1)S(1)} %bitcast.96), channel_id=1, source_target_pairs={{0,8},{8,0},{16,24},{24,16},{1,9},{9,1},{17,25},{25,17},{2,10},{10... | collective-permute-start | bytes 1572872 | tf_op jit(solution)/shard_map/ppermute | solution.py:60
  209.9 17.2 %collective-permute-start.11 = (bf16[8,512,128]{2,1,0:T(8,128)(2,1)}, bf16[8,512,128]{2,1,0:T(8,128)(2,1)}, u32[]{:S(2)}, u32[]{:S(2)}) collective-permute-start(bf16[8,512,128]{2,1,0:T(8,128)(2,1)} %get-tuple-element.81), channel_id=1, source_target_pairs={{0,8},{8,0},{16,24},{24,16},{1,9},{9,1},{17,25},{25,17},{2,10},{10... | collective-permute-start | bytes 3145736 | tf_op jit(solution)/shard_map/ppermute | solution.py:60
  218.4 1.9 collective-permute-start.14
  221.7 25.2 %all-to-all-start.4 = ((bf16[8,96,256]{2,1,0:T(8,128)(2,1)}), bf16[8,96,256]{2,1,0:T(8,128)(2,1)S(1)}, u32[]{:S(2)}, u32[]{:S(2)}) async-start(bf16[8,96,256]{2,1,0:T(8,128)(2,1)} %shard_map.242.refs_2_.refs_5_), calls=%async_computation.4 | async-start | bytes 786432 | tf_op jit(solution)/shard_map/all_to_all | solution.py:1099
  227.1 122.5 %all-gather.14.cloned.1.call-start = ((), (), s32[]{:S(2)}) async-start(), calls=%async_computation.19 | async-start | bytes 4718592 | tf_op jit(solution)/shard_map/all_gather | solution.py:45
  297.2 100.9 %reduce-scatter.6.cloned.1.call-start = ((), (), s32[]{:S(2)}) async-start(), calls=%async_computation.20 | async-start | bytes 4718592 | tf_op jit(solution)/shard_map/reduce_scatter | solution.py:49
  301.2 4.2 collective-permute-start.15
  305.5 14.0 %collective-permute-start.16 = (bf16[128,2048]{1,0:T(8,128)(2,1)S(1)}, bf16[128,2048]{1,0:T(8,128)(2,1)S(1)}, u32[]{:S(2)}, u32[]{:S(2)}) collective-permute-start(bf16[128,2048]{1,0:T(8,128)(2,1)S(1)} %fusion.16), channel_id=1, source_target_pairs={{0,16},{8,24},{16,0},{24,8},{1,17},{9,25},{17,1},{25,9},{2,18},{10... | collective-permute-start | bytes 1572872 | tf_op jit(solution)/shard_map/ppermute | solution.py:60
  320.9 63.2 %copy-start.9 = (f32[128,2048]{1,0:T(8,128)}, f32[128,2048]{1,0:T(8,128)S(1)}, u32[]{:S(2)}) copy-start(f32[128,2048]{1,0:T(8,128)S(1)} %get-tuple-element.86.refs_1_) | copy-start | bytes 3145732
  320.9 13.3 %collective-permute-start.17 = (bf16[128,2048]{1,0:T(8,128)(2,1)S(1)}, bf16[128,2048]{1,0:T(8,128)(2,1)S(1)}, u32[]{:S(2)}, u32[]{:S(2)}) collective-permute-start(bf16[128,2048]{1,0:T(8,128)(2,1)S(1)} %get-tuple-element.87), channel_id=1, source_target_pairs={{0,16},{8,24},{16,0},{24,8},{1,17},{9,25},{17,1},{25,9},{2,18},{10... | collective-permute-start | bytes 1572872 | tf_op jit(solution)/shard_map/ppermute | solution.py:60
  322.4 11.9 %collective-permute-start.18 = (bf16[128,2048]{1,0:T(8,128)(2,1)S(1)}, bf16[128,2048]{1,0:T(8,128)(2,1)S(1)}, u32[]{:S(2)}, u32[]{:S(2)}) collective-permute-start(bf16[128,2048]{1,0:T(8,128)(2,1)S(1)} %get-tuple-element.87), channel_id=1, source_target_pairs={{0,8},{8,0},{16,24},{24,16},{1,9},{9,1},{17,25},{25,17},{2,10},{10... | collective-permute-start | bytes 1572872 | tf_op jit(solution)/shard_map/ppermute | solution.py:60
  334.2 1.9 collective-permute-start.19
  349.5 147.9 %reduce-scatter.8.cloned.1.call-start = ((), (), s32[]{:S(2)}) async-start(), calls=%async_computation.21 | async-start | bytes 9437184 | tf_op jit(solution)/shard_map/reduce_scatter | solution.py:49
  362.8 2.7 collective-permute-start.20
  368.0 14.3 %collective-permute-start.21 = (bf16[128,2048]{1,0:T(8,128)(2,1)}, bf16[128,2048]{1,0:T(8,128)(2,1)S(1)}, u32[]{:S(2)}, u32[]{:S(2)}) collective-permute-start(bf16[128,2048]{1,0:T(8,128)(2,1)} %fusion.14), channel_id=1, source_target_pairs={{0,16},{8,24},{16,0},{24,8},{1,17},{9,25},{17,1},{25,9},{2,18},{10... | collective-permute-start | bytes 1572872 | tf_op jit(solution)/shard_map/ppermute | solution.py:60
  398.1 13.8 %collective-permute-start.22 = (bf16[128,2048]{1,0:T(8,128)(2,1)S(1)}, bf16[128,2048]{1,0:T(8,128)(2,1)S(1)}, u32[]{:S(2)}, u32[]{:S(2)}) collective-permute-start(bf16[128,2048]{1,0:T(8,128)(2,1)S(1)} %get-tuple-element.95), channel_id=1, source_target_pairs={{0,16},{8,24},{16,0},{24,8},{1,17},{9,25},{17,1},{25,9},{2,18},{10... | collective-permute-start | bytes 1572872 | tf_op jit(solution)/shard_map/ppermute | solution.py:60
  399.6 12.4 %collective-permute-start.23 = (bf16[128,2048]{1,0:T(8,128)(2,1)S(1)}, bf16[128,2048]{1,0:T(8,128)(2,1)S(1)}, u32[]{:S(2)}, u32[]{:S(2)}) collective-permute-start(bf16[128,2048]{1,0:T(8,128)(2,1)S(1)} %get-tuple-element.95), channel_id=1, source_target_pairs={{0,8},{8,0},{16,24},{24,16},{1,9},{9,1},{17,25},{25,17},{2,10},{10... | collective-permute-start | bytes 1572872 | tf_op jit(solution)/shard_map/ppermute | solution.py:60
  411.9 1.9 collective-permute-start.24
  426.8 22.9 %all-to-all-start.5 = ((bf16[8,112,256]{2,1,0:T(8,128)(2,1)}), bf16[8,112,256]{2,1,0:T(8,128)(2,1)S(1)}, u32[]{:S(2)}, u32[]{:S(2)}) async-start(bf16[8,112,256]{2,1,0:T(8,128)(2,1)} %get-tuple-element.100), calls=%async_computation.6 | async-start | bytes 917504 | tf_op jit(solution)/shard_map/all_to_all | solution.py:1091
  432.0 133.5 %reduce-scatter.10.cloned.1.call-start = ((), (), s32[]{:S(2)}) async-start(), calls=%async_computation.22 | async-start | bytes 5898240 | tf_op jit(solution)/shard_map/reduce_scatter | solution.py:49
  449.7 9.8 %collective-permute-start.27 = (bf16[8,512,128]{2,1,0:T(8,128)(2,1)}, bf16[8,512,128]{2,1,0:T(8,128)(2,1)}, u32[]{:S(2)}, u32[]{:S(2)}) collective-permute-start(bf16[8,512,128]{2,1,0:T(8,128)(2,1)} %broadcast_select_fusion), channel_id=1, source_target_pairs={{0,8},{8,0},{16,24},{24,16},{1,9},{9,1},{17,25},{25,17},{2,10},{10... | collective-permute-start | bytes 3145736 | tf_op jit(solution)/shard_map/ppermute | solution.py:60
  502.2 2.7 collective-permute-start.25
  507.5 14.3 %collective-permute-start.26 = (bf16[128,2048]{1,0:T(8,128)(2,1)}, bf16[128,2048]{1,0:T(8,128)(2,1)}, u32[]{:S(2)}, u32[]{:S(2)}) collective-permute-start(bf16[128,2048]{1,0:T(8,128)(2,1)} %fusion.10), channel_id=1, source_target_pairs={{0,16},{8,24},{16,0},{24,8},{1,17},{9,25},{17,1},{25,9},{2,18},{10... | collective-permute-start | bytes 1572872 | tf_op jit(solution)/shard_map/ppermute | solution.py:60
  508.9 19.3 %all-to-all-start.6 = ((bf16[8,96,256]{2,1,0:T(8,128)(2,1)}), bf16[8,96,256]{2,1,0:T(8,128)(2,1)}, u32[]{:S(2)}, u32[]{:S(2)}) async-start(bf16[8,96,256]{2,1,0:T(8,128)(2,1)} %shard_map.252.refs_4_), calls=%async_computation.7 | async-start | bytes 786432 | tf_op jit(solution)/shard_map/all_to_all | solution.py:1099
  514.0 102.7 %reduce-scatter.12.cloned.1.call-start = ((), (), s32[]{:S(2)}) async-start(), calls=%async_computation.23 | async-start | bytes 4718592 | tf_op jit(solution)/shard_map/reduce_scatter | solution.py:49
  574.4 6.0 collective-permute-start.28
  582.4 21.6 %all-to-all-start.7 = ((bf16[4,64,2048]{2,1,0:T(8,128)(2,1)}), bf16[4,64,2048]{2,1,0:T(8,128)(2,1)S(1)}, u32[]{:S(2)}, u32[]{:S(2)}) async-start(bf16[4,64,2048]{2,1,0:T(8,128)(2,1)} %bitcast.113), calls=%async_computation.10 | async-start | bytes 2097152 | tf_op jit(solution)/shard_map/all_to_all | solution.py:84
  586.1 90.0 %reduce-scatter.14.cloned.1.call-start = ((), (), s32[]{:S(2)}) async-start(), calls=%async_computation.24 | async-start | bytes 5308416 | tf_op jit(solution)/shard_map/reduce_scatter | solution.py:49
  586.9 1.8 collective-permute-start.29
  588.8 14.5 %collective-permute-start.30 = (bf16[512,128]{1,0:T(8,128)(2,1)S(1)}, bf16[512,128]{1,0:T(8,128)(2,1)S(1)}, u32[]{:S(2)}, u32[]{:S(2)}) collective-permute-start(bf16[512,128]{1,0:T(8,128)(2,1)S(1)} %get-tuple-element.154), channel_id=1, source_target_pairs={{0,16},{8,24},{16,0},{24,8},{1,17},{9,25},{17,1},{25,9},{2,18},{10... | collective-permute-start | bytes 393224 | tf_op jit(solution)/shard_map/ppermute | solution.py:60
  625.7 7.3 %collective-permute-start.34 = (f32[176,128]{1,0:T(8,128)S(1)}, f32[176,128]{1,0:T(8,128)S(1)}, u32[]{:S(2)}, u32[]{:S(2)}) collective-permute-start(f32[176,128]{1,0:T(8,128)S(1)} %pad_bitcast_fusion), channel_id=1, source_target_pairs={{0,8},{8,0},{16,24},{24,16},{1,9},{9,1},{17,25},{25,17},{2,10},{10... | collective-permute-start | bytes 270344 | tf_op jit(solution)/shard_map/ppermute | solution.py:932
  633.0 5.1 collective-permute-start.35
  635.9 23.7 %collective-permute-start.31 = (bf16[256,2048]{1,0:T(8,128)(2,1)S(1)}, bf16[256,2048]{1,0:T(8,128)(2,1)S(1)}, u32[]{:S(2)}, u32[]{:S(2)}) collective-permute-start(bf16[256,2048]{1,0:T(8,128)(2,1)S(1)} %fusion.6), channel_id=1, source_target_pairs={{0,8},{8,0},{16,24},{24,16},{1,9},{9,1},{17,25},{25,17},{2,10},{10... | collective-permute-start | bytes 3145736 | tf_op jit(solution)/shard_map/ppermute | solution.py:60
  638.1 4.6 collective-permute-start.36
  642.7 8.8 %collective-permute-start.37 = (f32[176,128]{1,0:T(8,128)S(1)}, f32[176,128]{1,0:T(8,128)S(1)}, u32[]{:S(2)}, u32[]{:S(2)}) collective-permute-start(f32[176,128]{1,0:T(8,128)S(1)} %add.278), channel_id=1, source_target_pairs={{0,2},{1,3},{2,0},{3,1},{4,6},{5,7},{6,4},{7,5},{8,10},{9,11},{10,... | collective-permute-start | bytes 270344 | tf_op jit(solution)/shard_map/ppermute | solution.py:932
  651.6 8.0 %collective-permute-start.38 = (f32[176,128]{1,0:T(8,128)S(1)}, f32[176,128]{1,0:T(8,128)S(1)}, u32[]{:S(2)}, u32[]{:S(2)}) collective-permute-start(f32[176,128]{1,0:T(8,128)S(1)} %add.279), channel_id=1, source_target_pairs={{0,4},{1,5},{2,6},{3,7},{4,0},{5,1},{6,2},{7,3},{8,12},{9,13},{10,... | collective-permute-start | bytes 270344 | tf_op jit(solution)/shard_map/ppermute | solution.py:932
  660.8 23.4 %collective-permute-start.32 = (bf16[128,2048]{1,0:T(8,128)(2,1)}, bf16[128,2048]{1,0:T(8,128)(2,1)}, u32[]{:S(2)}, u32[]{:S(2)}) collective-permute-start(bf16[128,2048]{1,0:T(8,128)(2,1)} %fusion.8), channel_id=1, source_target_pairs={{0,16},{8,24},{16,0},{24,8},{1,17},{9,25},{17,1},{25,9},{2,18},{10... | collective-permute-start | bytes 1572872 | tf_op jit(solution)/shard_map/ppermute | solution.py:60
  663.6 15.2 %all-to-all-start.8 = ((bf16[4,64,1024]{2,1,0:T(8,128)(2,1)}), bf16[4,64,1024]{2,1,0:T(8,128)(2,1)S(1)}, u32[]{:S(2)}, u32[]{:S(2)}) async-start(bf16[4,64,1024]{2,1,0:T(8,128)(2,1)} %bitcast.29), calls=%async_computation.12 | async-start | bytes 1048576 | tf_op jit(solution)/shard_map/all_to_all | solution.py:84
  676.1 26.1 %collective-permute-start.33 = (bf16[128,2048]{1,0:T(8,128)(2,1)}, bf16[128,2048]{1,0:T(8,128)(2,1)}, u32[]{:S(2)}, u32[]{:S(2)}) collective-permute-start(bf16[128,2048]{1,0:T(8,128)(2,1)} %slice.451), channel_id=1, source_target_pairs={{6,0},{7,1},{12,2},{13,3},{18,4},{19,5},{24,6},{25,7},{0,8},{1,9},... | collective-permute-start | bytes 1572872 | tf_op jit(solution)/shard_map/ppermute | solution.py:1400
  678.8 20.8 %all-to-all-start.9 = ((bf16[4,64,1152]{2,1,0:T(8,128)(2,1)}), bf16[4,64,1152]{2,1,0:T(8,128)(2,1)}, u32[]{:S(2)}, u32[]{:S(2)}) async-start(bf16[4,64,1152]{2,1,0:T(8,128)(2,1)} %bitcast.114), calls=%async_computation.14 | async-start | bytes 1179648 | tf_op jit(solution)/shard_map/all_to_all | solution.py:84
  (146 other events, 931.9 us)
Sparse Core Ops, SparseCore 0:
  22.6 53.6 all-gather.5
  77.8 58.2 all-gather.7
  138.2 63.4 all-gather.9
  203.0 94.0 all-gather.11
  298.5 47.8 all-gather.13
  349.7 48.3 reduce-scatter.5
  400.4 96.9 reduce-scatter.7
  499.7 65.7 reduce-scatter.9
  567.8 48.8 reduce-scatter.11
  618.9 57.1 reduce-scatter.13

commit v7 on v6

--- a/solution.py
+++ b/solution.py
@@ -1352,6 +1352,18 @@
     grad_normed_other = back_in(slice(pair_rows, span_rows)).astype(low)
     grad_normed_own = back_in(slice(0, pair_rows))
     rest_swapped = swap_heads(grad_rest_in.reshape(4, rows_in, -1))
+    grad_out_rows = grad_out_sum[: out_weight.shape[0]]
+
+    def to_owners(rows, along_heads):
+        pairs = [
+            (there, here)
+            for here, there in out_pairs
+            if (here % blocks == there % blocks) == along_heads
+        ]
+        return lax.ppermute(rows, ("head", "blk"), pairs)
+
+    grad_mix_early = to_owners(after(grad_out_rows, grad_rest_in), True)
+    grad_normed_own = after(grad_normed_own, rest_swapped, grad_mix_early)
     grad_input = call(
         partial(back_one, ring=ring),
         [shaped((row_count, D), low)],
@@ -1362,7 +1374,7 @@
             grad_hidden,
             first_gain[None, :],
         ],
-        after=[rest_swapped, grad_ffn_weight],
+        after=[grad_ffn_weight],
         scratch=[pltpu.VMEM((row_count, D), jnp.float32)],
     )[0]
     first_line = jnp.sum(
@@ -1397,11 +1409,8 @@
     line = jnp.pad(line, (0, -line.shape[0] % 1024)).reshape(-1, 128)
     line = summed_over(summed_over(line, "head"), "blk").reshape(-1)
     grad_conv_in = scatter_blocks(after(grad_conv_low, grad_rest_in))
-    grad_mix_weight = lax.ppermute(
-        after(grad_out_sum[: out_weight.shape[0]], grad_conv_in),
-        ("head", "blk"),
-        [(there, here) for here, there in out_pairs],
-    ).astype(jnp.float32)
+    grad_mix_late = to_owners(after(grad_out_rows, grad_conv_in), False)
+    grad_mix_weight = grad_mix_early.astype(jnp.float32) + grad_mix_late.astype(jnp.float32)
     grad_proj_weight = call(
         unpack_in,
         [shaped(in_weight.shape, jnp.float32)],

time: 720 us -> 716 us (level)
  waiting for transfers between devices: 275 us -> 260 us
    all_to_all x4, waiting for transfers between devices: 12.1 us -> 2.84 us  [swap_heads(): lax.all_to_all(pieces, 'head', split_axis=0, concat_axis=0, tiled=True)]
    ppermute x8, waiting for transfers between devices: 9.78 us -> 1.38 us  [summed_over(): lax.ppermute(values_in, axis, [(i, i ^ by) for i in range(peers)])]
    unnamed x315 -> x323, local copies, waits for them, and re-layouts: 64.5 us -> 66.1 us
  transfers between devices with their start and end apart: 56 -> 57, of which waited for: 35 -> 35; matrix products, arithmetic and copies ran while one was open for 21% -> 23% of each run, Pallas kernels for 12% -> 12%
where the time goes in v7:
time: 716 us; the launch traced here: 707 us
  waiting for transfers between devices  260 us (36%)
  matrix products  91.4 us (13%)
  Pallas kernels  84.4 us (12%)
  local copies, waits for them, and re-layouts  82.9 us (12%)
  starting transfers between devices  71.8 us (10%)
  other arithmetic  54.7 us (8%)
  blocking collectives  45.2 us (6%)
  between operations  16.6 us (2%)
    all_gather x5, waiting for transfers between devices, gather_blocks(): lax.all_gather(shard, 'blk', axis=0, tiled=True, axis_index_groups=[ring_...  96 us
    ppermute x27, waiting for transfers between devices, from_head(): lax.ppermute(shard, 'head', [(i, i ^ distance) for i in range(peers)])  89.4 us
    unnamed x323, local copies, waits for them, and re-layouts  66.1 us
    pallas_call x23, Pallas kernels, call(): pl.pallas_call(body, out_shape=outputs, in_specs=[pl.BlockSpec(memory_spa...  61.4 us
    reduce_scatter x5, waiting for transfers between devices, scatter_blocks(): lax.psum_scatter(partial_sums, 'blk', scatter_dimension=0, tiled=True, ax...  53.6 us
    dot_general x8, matrix products, times_transposed(): lax.dot_general(grad_side, weight, (((1,), (1,)), ((), ())), preferred_el...  35.7 us
    dot_general x5, matrix products, outer_grad(): lax.dot_general(left_side, grad_side, (((0,), (0,)), ((), ())), preferred...  28.6 us
    all_to_all x2, blocking collectives, swap_heads(): lax.all_to_all(pieces, 'head', split_axis=0, concat_axis=0, tiled=True)  24.7 us
  transfers between devices with their start and end apart: 57, of which 35 were waited for; matrix products, arithmetic and copies ran while one was open for 23% of the time, Pallas kernels for 12%

profile of v7, /device:TPU:16, one launch (start us, length us, event | category | flops | bytes accessed | tf_op | source)
XLA Modules:
  0.0 707.2 jit_solution(13049893924152230580)
XLA Ops:
  9.7 12.8 %all_to_all.50 = bf16[4,64,1152]{2,1,0:T(8,128)(2,1)} all-to-all(bf16[4,64,1152]{2,1,0:T(8,128)(2,1)S(1)} %get-tuple-element.70), channel_id=1, replica_groups=mesh['head'=4,'blk'=8] {'head'}, dimensions={0} | all-to-all | bytes 1179648 | tf_op jit(solution)/shard_map/all_to_all | solution.py:84
  22.5 11.9 %all_to_all.51 = bf16[4,64,1024]{2,1,0:T(8,128)(2,1)} all-to-all(bf16[4,64,1024]{2,1,0:T(8,128)(2,1)S(1)} %get-tuple-element.73), channel_id=1, replica_groups=mesh['head'=4,'blk'=8] {'head'}, dimensions={0} | all-to-all | bytes 1048576 | tf_op jit(solution)/shard_map/all_to_all | solution.py:84
  39.3 10.5 %collective-permute-done.refs_1_ = bf16[128,2048]{1,0:T(8,128)(2,1)S(1)} collective-permute-done((bf16[128,2048]{1,0:T(8,128)(2,1)S(1)}, bf16[128,2048]{1,0:T(8,128)(2,1)S(1)}, u32[]{:S(2)}, u32[]{:S(2)}) %collective-permute-start) | collective-permute-done | bytes 524320 | tf_op jit(solution)/shard_map/ppermute | solution.py:60
  56.6 2.5 shard_map.238
  60.3 15.9 %all-gather.6.cloned.1.call-done = bf16[2048,1152]{1,0:T(8,128)(2,1)} async-done(((bf16[256,1152]{1,0:T(8,128)(2,1)}), bf16[2048,1152]{1,0:T(8,128)(2,1)}) %all-gather.6.cloned.1.call-update) | async-done | bytes 4718608 | tf_op jit(solution)/shard_map/all_gather | solution.py:45
  76.3 7.4 %fusion.61 = (bf16[512,1152]{1,0:T(8,128)(2,1)S(1)}, f32[512,1152]{1,0:T(8,128)}) fusion(bf16[512,2048]{1,0:T(8,128)(2,1)} %copy-done.16, bf16[2048,1152]{1,0:T(8,128)(2,1)} %all-gather.6.cloned.1.call-done), kind=kOutput, calls=%fused_computation.170 | convolution fusion | flops 2416508928 | bytes 10354688 | tf_op jit(solution)/shard_map/dot_general | solution.py:1055
  91.3 4.3 all-to-all-start.2
  97.9 3.9 collective-permute-start.6
  106.1 6.0 collective-permute-done.10.refs_0_
  114.8 3.3 fusion.5
  123.1 7.3 %shard_map.241 = (f32[512,768]{1,0:T(8,128)S(1)}, bf16[8,112,256]{2,1,0:T(8,128)(2,1)S(1)}, f32[512,128]{1,0:T(8,128)S(1)}, f32[8,128]{1,0:T(8,128)S(1)}) custom-call(s32[8]{0:T(128)S(1)} %stack.40.place_ref, f32[512,768]{1,0:T(8,128)S(1)} %slice.420.refs_0_.refs_4_.refs_3_, f32[512,256]{1,0:T(8,128)S(1)} %copy-done.39, ...), custom_call_target="tpu_custom_call" | custom-call | flops 6000000000 | bytes 5705728 | tf_op jit(solution)/shard_map/pallas_call | solution.py:808
  133.0 3.0 all-gather.8.cloned.1.call-done
  136.1 20.5 %all_to_all.52.refs_0_ = bf16[8,112,256]{2,1,0:T(8,128)(2,1)S(1)} all-to-all(bf16[8,112,256]{2,1,0:T(8,128)(2,1)} %copy-done.44), channel_id=1, replica_groups=mesh['head'=4,'blk'=8] {'blk'}, dimensions={0} | all-to-all | bytes 917504 | tf_op jit(solution)/shard_map/all_to_all | solution.py:1091
  158.1 5.2 fusion.62.refs_0_
  165.1 36.5 %all-gather.10.cloned.1.call-done = bf16[1280,2048]{1,0:T(8,128)(2,1)} async-done(((bf16[160,2048]{1,0:T(8,128)(2,1)}), bf16[1280,2048]{1,0:T(8,128)(2,1)}) %all-gather.10.cloned.1.call-update) | async-done | bytes 5242896 | tf_op jit(solution)/shard_map/all_gather | solution.py:45
  206.1 3.8 shard_map.246
  211.8 6.6 collective-permute-done.12
  221.7 5.4 all-to-all-start.4
  229.8 12.8 %shard_map.247 = (f32[512,256]{1,0:T(8,128)S(1)}, f32[2,512,128]{2,1,0:T(8,128)S(1)}) custom-call(s32[3]{0:T(128)S(1)} %pad_add_fusion.4.refs_0_, bf16[512,256]{1,0:T(8,128)(2,1)S(1)} %copy-done.48, s32[512,128]{1,0:T(8,128)S(1)} %broadcast_in_dim.23.refs_2_, bf16[8,512,128]{2,1,0:T(8,128)(2,1)S(1)} %get-tuple-element.157.refs_3_, ...), custom_call_target="tpu_custom_call" | custom-call | flops 20000000000 | bytes 4000000 | tf_op jit(solution)/shard_map/pallas_call | solution.py:832
  256.6 40.6 %all-gather.12.cloned.1.call-done = bf16[2048,2048]{1,0:T(8,128)(2,1)} async-done(((bf16[256,2048]{1,0:T(8,128)(2,1)}), bf16[2048,2048]{1,0:T(8,128)(2,1)}) %all-gather.12.cloned.1.call-update) | async-done | bytes 8388624 | tf_op jit(solution)/shard_map/all_gather | solution.py:45
  297.4 3.7 fusion.31
  302.6 2.8 collective-permute-done.15
  307.0 12.5 %collective-permute-done.16 = bf16[128,2048]{1,0:T(8,128)(2,1)S(1)} collective-permute-done((bf16[128,2048]{1,0:T(8,128)(2,1)S(1)}, bf16[128,2048]{1,0:T(8,128)(2,1)S(1)}, u32[]{:S(2)}, u32[]{:S(2)}) %collective-permute-start.16) | collective-permute-done | bytes 524320 | tf_op jit(solution)/shard_map/ppermute | solution.py:60
  322.4 11.8 %collective-permute-done.17 = bf16[128,2048]{1,0:T(8,128)(2,1)S(1)} collective-permute-done((bf16[128,2048]{1,0:T(8,128)(2,1)S(1)}, bf16[128,2048]{1,0:T(8,128)(2,1)S(1)}, u32[]{:S(2)}, u32[]{:S(2)}) %collective-permute-start.17) | collective-permute-done | bytes 524320 | tf_op jit(solution)/shard_map/ppermute | solution.py:60
  337.4 4.6 fusion.63
  345.1 4.4 convolution_convert_fusion.4.refs_4_
  349.8 7.0 multiply_convert_fusion.1
  356.9 5.9 convolution_convert_fusion.6
  369.5 7.2 %convolution_convert_fusion.1.refs_5_ = bf16[2048,2048]{1,0:T(8,128)(2,1)} fusion(bf16[512,2048]{1,0:T(8,128)(2,1)S(1)} %copy-done.114, bf16[512,2048]{1,0:T(8,128)(2,1)S(1)} %pad_maximum_fusion), kind=kOutput, calls=%fused_computation.3 | convolution fusion | flops 4299161600 | bytes 12582912 | tf_op jit(solution)/shard_map/dot_general | solution.py:354
  376.7 5.6 collective-permute-done.21
  388.7 9.4 %reduce-scatter.6.cloned.1.call-done = bf16[128,2048]{1,0:T(8,128)(2,1)} async-done(((bf16[1024,2048]{1,0:T(8,128)(2,1)}), bf16[128,2048]{1,0:T(8,128)(2,1)}) %reduce-scatter.6.cloned.1.call-update) | async-done | bytes 524304 | tf_op jit(solution)/shard_map/reduce_scatter | solution.py:49
  399.7 12.3 %collective-permute-done.22 = bf16[128,2048]{1,0:T(8,128)(2,1)S(1)} collective-permute-done((bf16[128,2048]{1,0:T(8,128)(2,1)S(1)}, bf16[128,2048]{1,0:T(8,128)(2,1)S(1)}, u32[]{:S(2)}, u32[]{:S(2)}) %collective-permute-start.22) | collective-permute-done | bytes 524320 | tf_op jit(solution)/shard_map/ppermute | solution.py:60
  413.9 5.4 convolution_convert_fusion.7.refs_0_
  419.4 4.0 shard_map.251
  426.7 5.2 all-to-all-start.5
  432.0 6.2 convolution_convert_fusion.3.refs_8_
  438.3 10.2 %shard_map.253 = (f32[512,256]{1,0:T(8,128)S(1)}, bf16[8,512,128]{2,1,0:T(8,128)(2,1)S(1)}, bf16[8,512,128]{2,1,0:T(8,128)(2,1)S(1)}) custom-call(s32[3]{0:T(128)S(1)} %pad_add_fusion.4.refs_0_, bf16[512,256]{1,0:T(8,128)(2,1)S(1)} %copy-done.49, s32[512,128]{1,0:T(8,128)S(1)} %copy-done.61, bf16[8,512,128]{2,1,0:T(8,128)(2,1)S(1)} %copy-done.29, ...), custom_call_target="tpu_custom_call" | custom-call | flops 30000001024 | bytes 4000000 | tf_op jit(solution)/shard_map/pallas_call | solution.py:872
  454.2 4.4 convolution_convert_fusion.2.refs_2_
  464.2 3.3 shard_map.255.refs_11_
  467.5 29.9 %reduce-scatter.8.cloned.1.call-done = bf16[256,2048]{1,0:T(8,128)(2,1)} async-done(((bf16[2048,2048]{1,0:T(8,128)(2,1)}), bf16[256,2048]{1,0:T(8,128)(2,1)}) %reduce-scatter.8.cloned.1.call-update) | async-done | bytes 1048592 | tf_op jit(solution)/shard_map/reduce_scatter | solution.py:49
  498.6 3.6 convolution_convert_fusion.5
  508.9 5.2 all-to-all-start.6
  514.1 7.7 %collective-permute-done.26 = bf16[128,2048]{1,0:T(8,128)(2,1)} collective-permute-done((bf16[128,2048]{1,0:T(8,128)(2,1)}, bf16[128,2048]{1,0:T(8,128)(2,1)}, u32[]{:S(2)}, u32[]{:S(2)}) %collective-permute-start.26) | collective-permute-done | bytes 524320 | tf_op jit(solution)/shard_map/ppermute | solution.py:60
  521.7 2.7 fusion.13.refs_12_
  524.5 3.8 all-to-all-done.6
  535.7 18.7 %shard_map.256 = (f32[512,768]{1,0:T(8,128)S(1)}, f32[512,256]{1,0:T(8,128)S(1)}, f32[512,256]{1,0:T(8,128)S(1)}, f32[512,128]{1,0:T(8,128)S(1)}, f32[512,128]{1,0:T(8,128)S(1)}) custom-call(s32[8]{0:T(128)S(1)} %stack.40.place_ref, f32[512,768]{1,0:T(8,128)S(1)} %copy-done.23, f32[512,256]{1,0:T(8,128)S(1)} %copy-done.40, f32[512,256]{1,0:T(8,128)S(1)} %copy-done.38, ...), custom_call_target="tpu_custom_call" | custom-call | flops 10000000000 | bytes 10488832 | tf_op jit(solution)/shard_map/pallas_call | solution.py:808
  557.0 8.5 %reduce-scatter.10.cloned.1.call-done = bf16[160,2048]{1,0:T(8,128)(2,1)} async-done(((bf16[1280,2048]{1,0:T(8,128)(2,1)}), bf16[160,2048]{1,0:T(8,128)(2,1)}) %reduce-scatter.10.cloned.1.call-update) | async-done | bytes 655376 | tf_op jit(solution)/shard_map/reduce_scatter | solution.py:49
  568.7 4.8 multiply_reduce_fusion.5
  574.4 4.3 collective-permute-start.28
  582.4 3.7 all-to-all-start.7
  594.3 9.1 %collective-permute-done.30.refs_2_ = bf16[512,128]{1,0:T(8,128)(2,1)S(1)} collective-permute-done((bf16[512,128]{1,0:T(8,128)(2,1)S(1)}, bf16[512,128]{1,0:T(8,128)(2,1)S(1)}, u32[]{:S(2)}, u32[]{:S(2)}) %collective-permute-start.30) | collective-permute-done | bytes 131104 | tf_op jit(solution)/shard_map/ppermute | solution.py:60
  606.8 6.4 multiply_reduce_fusion
  614.2 2.5 reduce-scatter.12.cloned.1.call-done
  620.0 4.8 multiply_reduce_fusion.1
  628.9 4.4 fusion.21
  643.0 4.1 collective-permute-start.38
  649.2 2.9 fusion.23
  653.3 3.5 all-to-all-start.8
  656.8 5.6 convolution_add_fusion.1
  662.4 2.9 convert_element_type.183
  672.8 3.3 reduce-scatter.14.cloned.1.call-done
  676.1 3.5 all-to-all-start.9
  686.9 2.6 all-to-all-done.9.refs_0_
  692.6 5.1 collective-permute-done.34
  (575 shorter events, 191.2 us)
Async XLA Ops:
  7.2 69.1 %all-gather.6.cloned.1.call-start = ((), (), s32[]{:S(2)}) async-start(), calls=%async_computation.15 | async-start | bytes 5308416 | tf_op jit(solution)/shard_map/all_gather | solution.py:45
  9.6 42.4 %copy-start.145 = (f32[48]{0:T(128)S(1)}, f32[48]{0:T(128)}, u32[]{:S(2)}) copy-start(f32[48]{0:T(128)} %param.26) | copy-start | bytes 580
  22.4 113.6 %all-gather.8.cloned.1.call-start = ((), (), s32[]{:S(2)}) async-start(), calls=%async_computation.16 | async-start | bytes 4718592 | tf_op jit(solution)/shard_map/all_gather | solution.py:45
  34.8 15.6 %collective-permute-start.7 = (s32[4096]{0:T(1024)S(1)}, s32[4096]{0:T(1024)S(1)}, u32[]{:S(2)}, u32[]{:S(2)}) collective-permute-start(s32[4096]{0:T(1024)S(1)} %dynamic_update_slice.20), channel_id=1, source_target_pairs={{0,1},{1,0},{2,3},{3,2},{4,5},{5,4},{6,7},{7,6},{8,9},{9,8},{10,11... | collective-permute-start | bytes 49160 | tf_op jit(solution)/shard_map/ppermute | solution.py:932
  36.4 13.4 %collective-permute-start = (bf16[128,2048]{1,0:T(8,128)(2,1)S(1)}, bf16[128,2048]{1,0:T(8,128)(2,1)S(1)}, u32[]{:S(2)}, u32[]{:S(2)}) collective-permute-start(bf16[128,2048]{1,0:T(8,128)(2,1)S(1)} %bitcast.89), channel_id=1, source_target_pairs={{0,16},{8,24},{16,0},{24,8},{1,17},{9,25},{17,1},{25,9},{2,18},{10... | collective-permute-start | bytes 1572872 | tf_op jit(solution)/shard_map/ppermute | solution.py:60
  39.3 17.3 %collective-permute-start.1 = (bf16[128,2048]{1,0:T(8,128)(2,1)S(1)}, bf16[128,2048]{1,0:T(8,128)(2,1)S(1)}, u32[]{:S(2)}, u32[]{:S(2)}) collective-permute-start(bf16[128,2048]{1,0:T(8,128)(2,1)S(1)} %bitcast.90), channel_id=1, source_target_pairs={{0,8},{8,0},{16,24},{24,16},{1,9},{9,1},{17,25},{25,17},{2,10},{10... | collective-permute-start | bytes 1572872 | tf_op jit(solution)/shard_map/ppermute | solution.py:60
  49.8 6.8 collective-permute-start.2
  50.5 5.5 collective-permute-start.8
  56.1 58.7 %copy-start.116 = (f32[1280]{0:T(1024)}, f32[1280]{0:T(1024)S(1)}, u32[]{:S(2)}) copy-start(f32[1280]{0:T(1024)S(1)} %get-tuple-element.132) | copy-start | bytes 15364
  56.1 29.1 %collective-permute-start.9 = (s32[4096]{0:T(1024)S(1)}, s32[4096]{0:T(1024)S(1)}, u32[]{:S(2)}, u32[]{:S(2)}) collective-permute-start(s32[4096]{0:T(1024)S(1)} %add.239), channel_id=1, source_target_pairs={{0,4},{1,5},{2,6},{3,7},{4,0},{5,1},{6,2},{7,3},{8,12},{9,13},{10,... | collective-permute-start | bytes 49160 | tf_op jit(solution)/shard_map/ppermute | solution.py:932
  83.7 5.3 collective-permute-start.3
  85.8 26.3 %collective-permute-start.10 = (bf16[128,2048]{1,0:T(8,128)(2,1)}, bf16[128,2048]{1,0:T(8,128)(2,1)S(1)}, u32[]{:S(2)}, u32[]{:S(2)}) collective-permute-start(bf16[128,2048]{1,0:T(8,128)(2,1)} %convert_element_type.156), channel_id=1, source_target_pairs={{0,6},{1,7},{2,12},{3,13},{4,18},{5,19},{6,24},{7,25},{8,0},{9,1},... | collective-permute-start | bytes 1572872 | tf_op jit(solution)/shard_map/ppermute | solution.py:994
  88.4 8.8 %collective-permute-start.4 = (bf16[512,128]{1,0:T(8,128)(2,1)S(1)}, bf16[512,128]{1,0:T(8,128)(2,1)S(1)}, u32[]{:S(2)}, u32[]{:S(2)}) collective-permute-start(bf16[512,128]{1,0:T(8,128)(2,1)S(1)} %slice.410.refs_1_), channel_id=1, source_target_pairs={{0,8},{8,0},{16,24},{24,16},{1,9},{9,1},{17,25},{25,17},{2,10},{10... | collective-permute-start | bytes 393224 | tf_op jit(solution)/shard_map/ppermute | solution.py:60
  89.0 8.2 %collective-permute-start.5 = (bf16[512,128]{1,0:T(8,128)(2,1)S(1)}, bf16[512,128]{1,0:T(8,128)(2,1)S(1)}, u32[]{:S(2)}, u32[]{:S(2)}) collective-permute-start(bf16[512,128]{1,0:T(8,128)(2,1)S(1)} %collective-permute-done.3.refs_2_), channel_id=1, source_target_pairs={{0,8},{8,0},{16,24},{24,16},{1,9},{9,1},{17,25},{25,17},{2,10},{10... | collective-permute-start | bytes 393224 | tf_op jit(solution)/shard_map/ppermute | solution.py:60
  91.3 27.9 %all-to-all-start.2 = ((bf16[4,64,2048]{2,1,0:T(8,128)(2,1)}), bf16[4,64,2048]{2,1,0:T(8,128)(2,1)}, u32[]{:S(2)}, u32[]{:S(2)}) async-start(bf16[4,64,2048]{2,1,0:T(8,128)(2,1)} %shard_map.240), calls=%async_computation.2 | async-start | bytes 2097152 | tf_op jit(solution)/shard_map/all_to_all | solution.py:84
  95.6 106.1 %all-gather.10.cloned.1.call-start = ((), (), s32[]{:S(2)}) async-start(), calls=%async_computation.17 | async-start | bytes 5898240 | tf_op jit(solution)/shard_map/all_gather | solution.py:45
  97.9 16.5 %collective-permute-start.6 = (bf16[3,1280]{1,0:T(4,128)(2,1)S(1)}, bf16[3,1280]{1,0:T(4,128)(2,1)S(1)}, u32[]{:S(2)}, u32[]{:S(2)}) collective-permute-start(bf16[3,1280]{1,0:T(4,128)(2,1)S(1)} %slice.411), channel_id=1, source_target_pairs={{0,1},{1,2},{2,3},{3,4},{4,5},{5,6},{6,7},{8,9},{9,10},{10,11},{11... | collective-permute-start | bytes 23048 | tf_op jit(solution)/shard_map/ppermute | solution.py:34
  118.3 128.5 %copy-start.21 = (f32[512,768]{1,0:T(8,128)}, f32[512,768]{1,0:T(8,128)S(1)}, u32[]{:S(2)}) copy-start(f32[512,768]{1,0:T(8,128)S(1)} %slice.420.refs_0_.refs_4_.refs_3_) | copy-start | bytes 4718596
  136.1 161.1 %all-gather.12.cloned.1.call-start = ((), (), s32[]{:S(2)}) async-start(), calls=%async_computation.18 | async-start | bytes 9437184 | tf_op jit(solution)/shard_map/all_gather | solution.py:45
  163.4 40.7 %copy-start.124 = (s32[32,128]{1,0:T(8,128)S(1)}, s32[32,128]{1,0:T(8,128)}, u32[]{:S(2)}) copy-start(s32[32,128]{1,0:T(8,128)} %get-tuple-element.142) | copy-start | bytes 49156
  163.4 41.1 %copy-start.14 = (bf16[1,128,2048]{2,1,0:T(8,128)(2,1)S(1)}, bf16[1,128,2048]{2,1,0:T(8,128)(2,1)}, u32[]{:S(2)}) copy-start(bf16[1,128,2048]{2,1,0:T(8,128)(2,1)} %param.15) | copy-start | bytes 1572868
  165.1 44.8 %copy-start.47 = (bf16[512,256]{1,0:T(8,128)(2,1)}, bf16[512,256]{1,0:T(8,128)(2,1)S(1)}, u32[]{:S(2)}) copy-start(bf16[512,256]{1,0:T(8,128)(2,1)S(1)} %get-tuple-element.80.refs_1_) | copy-start | bytes 786436
  204.4 13.9 %collective-permute-start.12 = (bf16[128,2048]{1,0:T(8,128)(2,1)S(1)}, bf16[128,2048]{1,0:T(8,128)(2,1)S(1)}, u32[]{:S(2)}, u32[]{:S(2)}) collective-permute-start(bf16[128,2048]{1,0:T(8,128)(2,1)S(1)} %bitcast.95), channel_id=1, source_target_pairs={{0,16},{8,24},{16,0},{24,8},{1,17},{9,25},{17,1},{25,9},{2,18},{10... | collective-permute-start | bytes 1572872 | tf_op jit(solution)/shard_map/ppermute | solution.py:60
  206.0 12.5 %collective-permute-start.13 = (bf16[128,2048]{1,0:T(8,128)(2,1)S(1)}, bf16[128,2048]{1,0:T(8,128)(2,1)S(1)}, u32[]{:S(2)}, u32[]{:S(2)}) collective-permute-start(bf16[128,2048]{1,0:T(8,128)(2,1)S(1)} %bitcast.96), channel_id=1, source_target_pairs={{0,8},{8,0},{16,24},{24,16},{1,9},{9,1},{17,25},{25,17},{2,10},{10... | collective-permute-start | bytes 1572872 | tf_op jit(solution)/shard_map/ppermute | solution.py:60
  209.9 17.2 %collective-permute-start.11 = (bf16[8,512,128]{2,1,0:T(8,128)(2,1)}, bf16[8,512,128]{2,1,0:T(8,128)(2,1)}, u32[]{:S(2)}, u32[]{:S(2)}) collective-permute-start(bf16[8,512,128]{2,1,0:T(8,128)(2,1)} %get-tuple-element.83), channel_id=1, source_target_pairs={{0,8},{8,0},{16,24},{24,16},{1,9},{9,1},{17,25},{25,17},{2,10},{10... | collective-permute-start | bytes 3145736 | tf_op jit(solution)/shard_map/ppermute | solution.py:60
  218.4 1.9 collective-permute-start.14
  221.7 25.1 %all-to-all-start.4 = ((bf16[8,96,256]{2,1,0:T(8,128)(2,1)}), bf16[8,96,256]{2,1,0:T(8,128)(2,1)S(1)}, u32[]{:S(2)}, u32[]{:S(2)}) async-start(bf16[8,96,256]{2,1,0:T(8,128)(2,1)} %shard_map.242.refs_2_.refs_5_), calls=%async_computation.4 | async-start | bytes 786432 | tf_op jit(solution)/shard_map/all_to_all | solution.py:1099
  227.0 122.5 %all-gather.14.cloned.1.call-start = ((), (), s32[]{:S(2)}) async-start(), calls=%async_computation.19 | async-start | bytes 4718592 | tf_op jit(solution)/shard_map/all_gather | solution.py:45
  297.2 100.9 %reduce-scatter.6.cloned.1.call-start = ((), (), s32[]{:S(2)}) async-start(), calls=%async_computation.20 | async-start | bytes 4718592 | tf_op jit(solution)/shard_map/reduce_scatter | solution.py:49
  301.2 4.2 collective-permute-start.15
  305.5 14.0 %collective-permute-start.16 = (bf16[128,2048]{1,0:T(8,128)(2,1)S(1)}, bf16[128,2048]{1,0:T(8,128)(2,1)S(1)}, u32[]{:S(2)}, u32[]{:S(2)}) collective-permute-start(bf16[128,2048]{1,0:T(8,128)(2,1)S(1)} %fusion.16), channel_id=1, source_target_pairs={{0,16},{8,24},{16,0},{24,8},{1,17},{9,25},{17,1},{25,9},{2,18},{10... | collective-permute-start | bytes 1572872 | tf_op jit(solution)/shard_map/ppermute | solution.py:60
  320.9 63.2 %copy-start.9 = (f32[128,2048]{1,0:T(8,128)}, f32[128,2048]{1,0:T(8,128)S(1)}, u32[]{:S(2)}) copy-start(f32[128,2048]{1,0:T(8,128)S(1)} %get-tuple-element.88.refs_1_) | copy-start | bytes 3145732
  320.9 13.3 %collective-permute-start.17 = (bf16[128,2048]{1,0:T(8,128)(2,1)S(1)}, bf16[128,2048]{1,0:T(8,128)(2,1)S(1)}, u32[]{:S(2)}, u32[]{:S(2)}) collective-permute-start(bf16[128,2048]{1,0:T(8,128)(2,1)S(1)} %get-tuple-element.89), channel_id=1, source_target_pairs={{0,16},{8,24},{16,0},{24,8},{1,17},{9,25},{17,1},{25,9},{2,18},{10... | collective-permute-start | bytes 1572872 | tf_op jit(solution)/shard_map/ppermute | solution.py:60
  322.4 11.9 %collective-permute-start.18 = (bf16[128,2048]{1,0:T(8,128)(2,1)S(1)}, bf16[128,2048]{1,0:T(8,128)(2,1)S(1)}, u32[]{:S(2)}, u32[]{:S(2)}) collective-permute-start(bf16[128,2048]{1,0:T(8,128)(2,1)S(1)} %get-tuple-element.89), channel_id=1, source_target_pairs={{0,8},{8,0},{16,24},{24,16},{1,9},{9,1},{17,25},{25,17},{2,10},{10... | collective-permute-start | bytes 1572872 | tf_op jit(solution)/shard_map/ppermute | solution.py:60
  334.2 1.9 collective-permute-start.19
  349.5 147.8 %reduce-scatter.8.cloned.1.call-start = ((), (), s32[]{:S(2)}) async-start(), calls=%async_computation.21 | async-start | bytes 9437184 | tf_op jit(solution)/shard_map/reduce_scatter | solution.py:49
  362.8 2.7 collective-permute-start.20
  368.0 14.3 %collective-permute-start.21 = (bf16[128,2048]{1,0:T(8,128)(2,1)}, bf16[128,2048]{1,0:T(8,128)(2,1)S(1)}, u32[]{:S(2)}, u32[]{:S(2)}) collective-permute-start(bf16[128,2048]{1,0:T(8,128)(2,1)} %fusion.14), channel_id=1, source_target_pairs={{0,16},{8,24},{16,0},{24,8},{1,17},{9,25},{17,1},{25,9},{2,18},{10... | collective-permute-start | bytes 1572872 | tf_op jit(solution)/shard_map/ppermute | solution.py:60
  398.1 13.8 %collective-permute-start.22 = (bf16[128,2048]{1,0:T(8,128)(2,1)S(1)}, bf16[128,2048]{1,0:T(8,128)(2,1)S(1)}, u32[]{:S(2)}, u32[]{:S(2)}) collective-permute-start(bf16[128,2048]{1,0:T(8,128)(2,1)S(1)} %get-tuple-element.97), channel_id=1, source_target_pairs={{0,16},{8,24},{16,0},{24,8},{1,17},{9,25},{17,1},{25,9},{2,18},{10... | collective-permute-start | bytes 1572872 | tf_op jit(solution)/shard_map/ppermute | solution.py:60
  399.7 12.4 %collective-permute-start.23 = (bf16[128,2048]{1,0:T(8,128)(2,1)S(1)}, bf16[128,2048]{1,0:T(8,128)(2,1)S(1)}, u32[]{:S(2)}, u32[]{:S(2)}) collective-permute-start(bf16[128,2048]{1,0:T(8,128)(2,1)S(1)} %get-tuple-element.97), channel_id=1, source_target_pairs={{0,8},{8,0},{16,24},{24,16},{1,9},{9,1},{17,25},{25,17},{2,10},{10... | collective-permute-start | bytes 1572872 | tf_op jit(solution)/shard_map/ppermute | solution.py:60
  411.9 1.9 collective-permute-start.24
  426.7 22.9 %all-to-all-start.5 = ((bf16[8,112,256]{2,1,0:T(8,128)(2,1)}), bf16[8,112,256]{2,1,0:T(8,128)(2,1)S(1)}, u32[]{:S(2)}, u32[]{:S(2)}) async-start(bf16[8,112,256]{2,1,0:T(8,128)(2,1)} %get-tuple-element.102), calls=%async_computation.6 | async-start | bytes 917504 | tf_op jit(solution)/shard_map/all_to_all | solution.py:1091
  431.9 133.6 %reduce-scatter.10.cloned.1.call-start = ((), (), s32[]{:S(2)}) async-start(), calls=%async_computation.22 | async-start | bytes 5898240 | tf_op jit(solution)/shard_map/reduce_scatter | solution.py:49
  449.7 9.8 %collective-permute-start.27 = (bf16[8,512,128]{2,1,0:T(8,128)(2,1)}, bf16[8,512,128]{2,1,0:T(8,128)(2,1)}, u32[]{:S(2)}, u32[]{:S(2)}) collective-permute-start(bf16[8,512,128]{2,1,0:T(8,128)(2,1)} %broadcast_select_fusion), channel_id=1, source_target_pairs={{0,8},{8,0},{16,24},{24,16},{1,9},{9,1},{17,25},{25,17},{2,10},{10... | collective-permute-start | bytes 3145736 | tf_op jit(solution)/shard_map/ppermute | solution.py:60
  502.2 2.7 collective-permute-start.25
  507.4 14.3 %collective-permute-start.26 = (bf16[128,2048]{1,0:T(8,128)(2,1)}, bf16[128,2048]{1,0:T(8,128)(2,1)}, u32[]{:S(2)}, u32[]{:S(2)}) collective-permute-start(bf16[128,2048]{1,0:T(8,128)(2,1)} %fusion.10), channel_id=1, source_target_pairs={{0,16},{8,24},{16,0},{24,8},{1,17},{9,25},{17,1},{25,9},{2,18},{10... | collective-permute-start | bytes 1572872 | tf_op jit(solution)/shard_map/ppermute | solution.py:60
  508.9 19.3 %all-to-all-start.6 = ((bf16[8,96,256]{2,1,0:T(8,128)(2,1)}), bf16[8,96,256]{2,1,0:T(8,128)(2,1)}, u32[]{:S(2)}, u32[]{:S(2)}) async-start(bf16[8,96,256]{2,1,0:T(8,128)(2,1)} %shard_map.252.refs_4_), calls=%async_computation.7 | async-start | bytes 786432 | tf_op jit(solution)/shard_map/all_to_all | solution.py:1099
  514.1 102.7 %reduce-scatter.12.cloned.1.call-start = ((), (), s32[]{:S(2)}) async-start(), calls=%async_computation.23 | async-start | bytes 4718592 | tf_op jit(solution)/shard_map/reduce_scatter | solution.py:49
  574.4 6.0 collective-permute-start.28
  582.4 21.6 %all-to-all-start.7 = ((bf16[4,64,2048]{2,1,0:T(8,128)(2,1)}), bf16[4,64,2048]{2,1,0:T(8,128)(2,1)S(1)}, u32[]{:S(2)}, u32[]{:S(2)}) async-start(bf16[4,64,2048]{2,1,0:T(8,128)(2,1)} %bitcast.113), calls=%async_computation.10 | async-start | bytes 2097152 | tf_op jit(solution)/shard_map/all_to_all | solution.py:84
  586.1 90.0 %reduce-scatter.14.cloned.1.call-start = ((), (), s32[]{:S(2)}) async-start(), calls=%async_computation.24 | async-start | bytes 5308416 | tf_op jit(solution)/shard_map/reduce_scatter | solution.py:49
  586.9 1.8 collective-permute-start.29
  588.8 14.5 %collective-permute-start.30 = (bf16[512,128]{1,0:T(8,128)(2,1)S(1)}, bf16[512,128]{1,0:T(8,128)(2,1)S(1)}, u32[]{:S(2)}, u32[]{:S(2)}) collective-permute-start(bf16[512,128]{1,0:T(8,128)(2,1)S(1)} %get-tuple-element.158), channel_id=1, source_target_pairs={{0,16},{8,24},{16,0},{24,8},{1,17},{9,25},{17,1},{25,9},{2,18},{10... | collective-permute-start | bytes 393224 | tf_op jit(solution)/shard_map/ppermute | solution.py:60
  625.7 7.6 %collective-permute-start.35 = (f32[176,128]{1,0:T(8,128)S(1)}, f32[176,128]{1,0:T(8,128)S(1)}, u32[]{:S(2)}, u32[]{:S(2)}) collective-permute-start(f32[176,128]{1,0:T(8,128)S(1)} %pad_bitcast_fusion), channel_id=1, source_target_pairs={{0,8},{8,0},{16,24},{24,16},{1,9},{9,1},{17,25},{25,17},{2,10},{10... | collective-permute-start | bytes 270344 | tf_op jit(solution)/shard_map/ppermute | solution.py:932
  633.3 5.1 collective-permute-start.36
  637.1 25.3 %collective-permute-start.32 = (bf16[256,2048]{1,0:T(8,128)(2,1)}, bf16[256,2048]{1,0:T(8,128)(2,1)}, u32[]{:S(2)}, u32[]{:S(2)}) collective-permute-start(bf16[256,2048]{1,0:T(8,128)(2,1)} %fusion.6), channel_id=1, source_target_pairs={{0,8},{8,0},{16,24},{24,16},{1,9},{9,1},{17,25},{25,17},{2,10},{10... | collective-permute-start | bytes 3145736 | tf_op jit(solution)/shard_map/ppermute | solution.py:60
  638.4 4.6 collective-permute-start.37
  643.0 9.1 %collective-permute-start.38 = (f32[176,128]{1,0:T(8,128)S(1)}, f32[176,128]{1,0:T(8,128)S(1)}, u32[]{:S(2)}, u32[]{:S(2)}) collective-permute-start(f32[176,128]{1,0:T(8,128)S(1)} %add.282), channel_id=1, source_target_pairs={{0,2},{1,3},{2,0},{3,1},{4,6},{5,7},{6,4},{7,5},{8,10},{9,11},{10,... | collective-permute-start | bytes 270344 | tf_op jit(solution)/shard_map/ppermute | solution.py:932
  647.1 19.3 %collective-permute-start.31 = (bf16[128,2048]{1,0:T(8,128)(2,1)S(1)}, bf16[128,2048]{1,0:T(8,128)(2,1)}, u32[]{:S(2)}, u32[]{:S(2)}) collective-permute-start(bf16[128,2048]{1,0:T(8,128)(2,1)S(1)} %slice.447), channel_id=1, source_target_pairs={{0,8},{1,9},{2,10},{3,11},{4,12},{5,13},{14,14},{15,15},{8,16},{9,... | collective-permute-start | bytes 1572872 | tf_op jit(solution)/shard_map/ppermute | solution.py:1363
  652.1 10.4 %collective-permute-start.39 = (f32[176,128]{1,0:T(8,128)S(1)}, f32[176,128]{1,0:T(8,128)S(1)}, u32[]{:S(2)}, u32[]{:S(2)}) collective-permute-start(f32[176,128]{1,0:T(8,128)S(1)} %add.283), channel_id=1, source_target_pairs={{0,4},{1,5},{2,6},{3,7},{4,0},{5,1},{6,2},{7,3},{8,12},{9,13},{10,... | collective-permute-start | bytes 270344 | tf_op jit(solution)/shard_map/ppermute | solution.py:932
  653.3 12.3 %all-to-all-start.8 = ((bf16[4,64,1024]{2,1,0:T(8,128)(2,1)}), bf16[4,64,1024]{2,1,0:T(8,128)(2,1)S(1)}, u32[]{:S(2)}, u32[]{:S(2)}) async-start(bf16[4,64,1024]{2,1,0:T(8,128)(2,1)} %bitcast.29), calls=%async_computation.12 | async-start | bytes 1048576 | tf_op jit(solution)/shard_map/all_to_all | solution.py:84
  668.6 14.4 %collective-permute-start.33 = (bf16[128,2048]{1,0:T(8,128)(2,1)}, bf16[128,2048]{1,0:T(8,128)(2,1)}, u32[]{:S(2)}, u32[]{:S(2)}) collective-permute-start(bf16[128,2048]{1,0:T(8,128)(2,1)} %fusion.8), channel_id=1, source_target_pairs={{0,16},{8,24},{16,0},{24,8},{1,17},{9,25},{17,1},{25,9},{2,18},{10... | collective-permute-start | bytes 1572872 | tf_op jit(solution)/shard_map/ppermute | solution.py:60
  676.1 13.4 %all-to-all-start.9 = ((bf16[4,64,1152]{2,1,0:T(8,128)(2,1)}), bf16[4,64,1152]{2,1,0:T(8,128)(2,1)S(1)}, u32[]{:S(2)}, u32[]{:S(2)}) async-start(bf16[4,64,1152]{2,1,0:T(8,128)(2,1)} %bitcast.114), calls=%async_computation.14 | async-start | bytes 1179648 | tf_op jit(solution)/shard_map/all_to_all | solution.py:84
  679.6 18.0 %collective-permute-start.34 = (bf16[128,2048]{1,0:T(8,128)(2,1)}, bf16[128,2048]{1,0:T(8,128)(2,1)}, u32[]{:S(2)}, u32[]{:S(2)}) collective-permute-start(bf16[128,2048]{1,0:T(8,128)(2,1)} %copy-done.111), channel_id=1, source_target_pairs={{6,0},{7,1},{12,2},{13,3},{18,4},{19,5},{24,6},{25,7}} | collective-permute-start | bytes 1572872 | tf_op jit(solution)/shard_map/ppermute | solution.py:1363
  (151 other events, 1008.7 us)
Sparse Core Ops, SparseCore 0:
  22.6 53.6 all-gather.5
  77.8 58.2 all-gather.7
  138.2 63.4 all-gather.9
  203.0 94.0 all-gather.11
  298.5 47.8 all-gather.13
  349.7 48.3 reduce-scatter.5
  400.4 96.9 reduce-scatter.7
  499.7 65.7 reduce-scatter.9
  567.8 48.8 reduce-scatter.11
  618.9 57.2 reduce-scatter.13

commit v8 on v7

--- a/solution.py
+++ b/solution.py
@@ -1416,6 +1416,7 @@
         [shaped(in_weight.shape, jnp.float32)],
         place,
         [swap_heads(grad_conv_in.reshape(4, rows_in, -1)), rest_swapped],
+        after=[grad_mix_weight],
     )[0]
     summed_small = []
     at = 0

time: 716 us -> 720 us (level)
    unnamed x323 -> x321, local copies, waits for them, and re-layouts: 66.1 us -> 64.3 us
  transfers between devices with their start and end apart: 57 -> 57, of which waited for: 35 -> 36; matrix products, arithmetic and copies ran while one was open for 23% -> 23% of each run, Pallas kernels for 12% -> 12%
where the time goes in v8:
time: 720 us; the launch traced here: 710 us
  waiting for transfers between devices  265 us (37%)
  matrix products  91.4 us (13%)
  Pallas kernels  84.4 us (12%)
  local copies, waits for them, and re-layouts  81.1 us (11%)
  starting transfers between devices  71.7 us (10%)
  other arithmetic  53.7 us (7%)
  blocking collectives  45.3 us (6%)
  between operations  16.6 us (2%)
    all_gather x5, waiting for transfers between devices, gather_blocks(): lax.all_gather(shard, 'blk', axis=0, tiled=True, axis_index_groups=[ring_...  96 us
    ppermute x27, waiting for transfers between devices, from_head(): lax.ppermute(shard, 'head', [(i, i ^ distance) for i in range(peers)])  92.1 us
    unnamed x321, local copies, waits for them, and re-layouts  64.3 us
    pallas_call x23, Pallas kernels, call(): pl.pallas_call(body, out_shape=outputs, in_specs=[pl.BlockSpec(memory_spa...  61.4 us
    reduce_scatter x5, waiting for transfers between devices, scatter_blocks(): lax.psum_scatter(partial_sums, 'blk', scatter_dimension=0, tiled=True, ax...  54.4 us
    dot_general x8, matrix products, times_transposed(): lax.dot_general(grad_side, weight, (((1,), (1,)), ((), ())), preferred_el...  35.7 us
    dot_general x5, matrix products, outer_grad(): lax.dot_general(left_side, grad_side, (((0,), (0,)), ((), ())), preferred...  28.6 us
    all_to_all x2, blocking collectives, swap_heads(): lax.all_to_all(pieces, 'head', split_axis=0, concat_axis=0, tiled=True)  24.7 us
  transfers between devices with their start and end apart: 57, of which 36 were waited for; matrix products, arithmetic and copies ran while one was open for 23% of the time, Pallas kernels for 12%

profile of v8, /device:TPU:16, one launch (start us, length us, event | category | flops | bytes accessed | tf_op | source)
XLA Modules:
  0.0 709.7 jit_solution(14699308934914252022)
XLA Ops:
  9.7 12.8 %all_to_all.50 = bf16[4,64,1152]{2,1,0:T(8,128)(2,1)} all-to-all(bf16[4,64,1152]{2,1,0:T(8,128)(2,1)S(1)} %get-tuple-element.70), channel_id=1, replica_groups=mesh['head'=4,'blk'=8] {'head'}, dimensions={0} | all-to-all | bytes 1179648 | tf_op jit(solution)/shard_map/all_to_all | solution.py:84
  22.5 11.9 %all_to_all.51 = bf16[4,64,1024]{2,1,0:T(8,128)(2,1)} all-to-all(bf16[4,64,1024]{2,1,0:T(8,128)(2,1)S(1)} %get-tuple-element.73), channel_id=1, replica_groups=mesh['head'=4,'blk'=8] {'head'}, dimensions={0} | all-to-all | bytes 1048576 | tf_op jit(solution)/shard_map/all_to_all | solution.py:84
  39.3 10.5 %collective-permute-done.refs_1_ = bf16[128,2048]{1,0:T(8,128)(2,1)S(1)} collective-permute-done((bf16[128,2048]{1,0:T(8,128)(2,1)S(1)}, bf16[128,2048]{1,0:T(8,128)(2,1)S(1)}, u32[]{:S(2)}, u32[]{:S(2)}) %collective-permute-start) | collective-permute-done | bytes 524320 | tf_op jit(solution)/shard_map/ppermute | solution.py:60
  60.4 15.9 %all-gather.6.cloned.1.call-done = bf16[2048,1152]{1,0:T(8,128)(2,1)} async-done(((bf16[256,1152]{1,0:T(8,128)(2,1)}), bf16[2048,1152]{1,0:T(8,128)(2,1)}) %all-gather.6.cloned.1.call-update) | async-done | bytes 4718608 | tf_op jit(solution)/shard_map/all_gather | solution.py:45
  76.3 7.4 %fusion.61 = (bf16[512,1152]{1,0:T(8,128)(2,1)S(1)}, f32[512,1152]{1,0:T(8,128)}) fusion(bf16[512,2048]{1,0:T(8,128)(2,1)} %copy-done.17, bf16[2048,1152]{1,0:T(8,128)(2,1)} %all-gather.6.cloned.1.call-done), kind=kOutput, calls=%fused_computation.170 | convolution fusion | flops 2416508928 | bytes 10354688 | tf_op jit(solution)/shard_map/dot_general | solution.py:1055
  91.3 4.3 all-to-all-start.2
  97.9 3.9 collective-permute-start.6
  106.1 6.0 collective-permute-done.10.refs_0_
  114.8 3.3 fusion.5
  123.1 7.3 %shard_map.241 = (f32[512,768]{1,0:T(8,128)S(1)}, bf16[8,112,256]{2,1,0:T(8,128)(2,1)S(1)}, f32[512,128]{1,0:T(8,128)S(1)}, f32[8,128]{1,0:T(8,128)S(1)}) custom-call(s32[8]{0:T(128)S(1)} %stack.40.place_ref, f32[512,768]{1,0:T(8,128)S(1)} %slice.420.refs_0_.refs_4_.refs_3_, f32[512,256]{1,0:T(8,128)S(1)} %copy-done.38, ...), custom_call_target="tpu_custom_call" | custom-call | flops 6000000000 | bytes 5705728 | tf_op jit(solution)/shard_map/pallas_call | solution.py:808
  133.0 3.0 all-gather.8.cloned.1.call-done
  136.1 20.5 %all_to_all.52.refs_0_ = bf16[8,112,256]{2,1,0:T(8,128)(2,1)S(1)} all-to-all(bf16[8,112,256]{2,1,0:T(8,128)(2,1)} %copy-done.43), channel_id=1, replica_groups=mesh['head'=4,'blk'=8] {'blk'}, dimensions={0} | all-to-all | bytes 917504 | tf_op jit(solution)/shard_map/all_to_all | solution.py:1091
  158.2 5.2 fusion.62.refs_0_
  165.1 36.5 %all-gather.10.cloned.1.call-done = bf16[1280,2048]{1,0:T(8,128)(2,1)} async-done(((bf16[160,2048]{1,0:T(8,128)(2,1)}), bf16[1280,2048]{1,0:T(8,128)(2,1)}) %all-gather.10.cloned.1.call-update) | async-done | bytes 5242896 | tf_op jit(solution)/shard_map/all_gather | solution.py:45
  206.1 3.8 shard_map.246
  211.8 6.6 collective-permute-done.12
  221.7 5.4 all-to-all-start.4
  229.8 12.8 %shard_map.247 = (f32[512,256]{1,0:T(8,128)S(1)}, f32[2,512,128]{2,1,0:T(8,128)S(1)}) custom-call(s32[3]{0:T(128)S(1)} %pad_add_fusion.4.refs_0_, bf16[512,256]{1,0:T(8,128)(2,1)S(1)} %copy-done.47, s32[512,128]{1,0:T(8,128)S(1)} %broadcast_in_dim.23.refs_2_, bf16[8,512,128]{2,1,0:T(8,128)(2,1)S(1)} %get-tuple-element.157.refs_3_, ...), custom_call_target="tpu_custom_call" | custom-call | flops 20000000000 | bytes 4000000 | tf_op jit(solution)/shard_map/pallas_call | solution.py:832
  256.6 40.6 %all-gather.12.cloned.1.call-done = bf16[2048,2048]{1,0:T(8,128)(2,1)} async-done(((bf16[256,2048]{1,0:T(8,128)(2,1)}), bf16[2048,2048]{1,0:T(8,128)(2,1)}) %all-gather.12.cloned.1.call-update) | async-done | bytes 8388624 | tf_op jit(solution)/shard_map/all_gather | solution.py:45
  297.4 3.7 fusion.31
  302.6 2.8 collective-permute-done.15
  307.0 12.5 %collective-permute-done.16 = bf16[128,2048]{1,0:T(8,128)(2,1)S(1)} collective-permute-done((bf16[128,2048]{1,0:T(8,128)(2,1)S(1)}, bf16[128,2048]{1,0:T(8,128)(2,1)S(1)}, u32[]{:S(2)}, u32[]{:S(2)}) %collective-permute-start.16) | collective-permute-done | bytes 524320 | tf_op jit(solution)/shard_map/ppermute | solution.py:60
  322.4 11.8 %collective-permute-done.17 = bf16[128,2048]{1,0:T(8,128)(2,1)S(1)} collective-permute-done((bf16[128,2048]{1,0:T(8,128)(2,1)S(1)}, bf16[128,2048]{1,0:T(8,128)(2,1)S(1)}, u32[]{:S(2)}, u32[]{:S(2)}) %collective-permute-start.17) | collective-permute-done | bytes 524320 | tf_op jit(solution)/shard_map/ppermute | solution.py:60
  337.4 4.6 fusion.63
  345.2 4.3 convolution_convert_fusion.4.refs_4_
  349.8 7.0 multiply_convert_fusion.1
  356.9 5.9 convolution_convert_fusion.6
  369.5 7.2 %convolution_convert_fusion.1.refs_5_ = bf16[2048,2048]{1,0:T(8,128)(2,1)} fusion(bf16[512,2048]{1,0:T(8,128)(2,1)S(1)} %copy-done.113, bf16[512,2048]{1,0:T(8,128)(2,1)S(1)} %pad_maximum_fusion), kind=kOutput, calls=%fused_computation.3 | convolution fusion | flops 4299161600 | bytes 12582912 | tf_op jit(solution)/shard_map/dot_general | solution.py:354
  376.7 5.6 collective-permute-done.21
  388.7 9.4 %reduce-scatter.6.cloned.1.call-done = bf16[128,2048]{1,0:T(8,128)(2,1)} async-done(((bf16[1024,2048]{1,0:T(8,128)(2,1)}), bf16[128,2048]{1,0:T(8,128)(2,1)}) %reduce-scatter.6.cloned.1.call-update) | async-done | bytes 524304 | tf_op jit(solution)/shard_map/reduce_scatter | solution.py:49
  399.7 12.3 %collective-permute-done.22 = bf16[128,2048]{1,0:T(8,128)(2,1)S(1)} collective-permute-done((bf16[128,2048]{1,0:T(8,128)(2,1)S(1)}, bf16[128,2048]{1,0:T(8,128)(2,1)S(1)}, u32[]{:S(2)}, u32[]{:S(2)}) %collective-permute-start.22) | collective-permute-done | bytes 524320 | tf_op jit(solution)/shard_map/ppermute | solution.py:60
  413.9 5.4 convolution_convert_fusion.7.refs_0_
  419.4 4.0 shard_map.251
  426.8 5.2 all-to-all-start.5
  432.0 6.2 convolution_convert_fusion.3.refs_8_
  438.3 10.2 %shard_map.253 = (f32[512,256]{1,0:T(8,128)S(1)}, bf16[8,512,128]{2,1,0:T(8,128)(2,1)S(1)}, bf16[8,512,128]{2,1,0:T(8,128)(2,1)S(1)}) custom-call(s32[3]{0:T(128)S(1)} %pad_add_fusion.4.refs_0_, bf16[512,256]{1,0:T(8,128)(2,1)S(1)} %copy-done.48, s32[512,128]{1,0:T(8,128)S(1)} %copy-done.60, bf16[8,512,128]{2,1,0:T(8,128)(2,1)S(1)} %copy-done.28, ...), custom_call_target="tpu_custom_call" | custom-call | flops 30000001024 | bytes 4000000 | tf_op jit(solution)/shard_map/pallas_call | solution.py:872
  454.2 4.4 convolution_convert_fusion.2.refs_2_
  464.2 3.3 shard_map.255.refs_11_
  467.5 29.9 %reduce-scatter.8.cloned.1.call-done = bf16[256,2048]{1,0:T(8,128)(2,1)} async-done(((bf16[2048,2048]{1,0:T(8,128)(2,1)}), bf16[256,2048]{1,0:T(8,128)(2,1)}) %reduce-scatter.8.cloned.1.call-update) | async-done | bytes 1048592 | tf_op jit(solution)/shard_map/reduce_scatter | solution.py:49
  498.6 3.6 convolution_convert_fusion.5
  508.9 5.1 all-to-all-start.6
  514.1 7.7 %collective-permute-done.26 = bf16[128,2048]{1,0:T(8,128)(2,1)} collective-permute-done((bf16[128,2048]{1,0:T(8,128)(2,1)}, bf16[128,2048]{1,0:T(8,128)(2,1)}, u32[]{:S(2)}, u32[]{:S(2)}) %collective-permute-start.26) | collective-permute-done | bytes 524320 | tf_op jit(solution)/shard_map/ppermute | solution.py:60
  521.7 2.7 fusion.13.refs_12_
  524.5 3.7 all-to-all-done.6
  535.7 18.7 %shard_map.256 = (f32[512,768]{1,0:T(8,128)S(1)}, f32[512,256]{1,0:T(8,128)S(1)}, f32[512,256]{1,0:T(8,128)S(1)}, f32[512,128]{1,0:T(8,128)S(1)}, f32[512,128]{1,0:T(8,128)S(1)}) custom-call(s32[8]{0:T(128)S(1)} %stack.40.place_ref, f32[512,768]{1,0:T(8,128)S(1)} %copy-done.22, f32[512,256]{1,0:T(8,128)S(1)} %copy-done.39, f32[512,256]{1,0:T(8,128)S(1)} %copy-done.37, ...), custom_call_target="tpu_custom_call" | custom-call | flops 10000000000 | bytes 10488832 | tf_op jit(solution)/shard_map/pallas_call | solution.py:808
  557.0 8.5 %reduce-scatter.10.cloned.1.call-done = bf16[160,2048]{1,0:T(8,128)(2,1)} async-done(((bf16[1280,2048]{1,0:T(8,128)(2,1)}), bf16[160,2048]{1,0:T(8,128)(2,1)}) %reduce-scatter.10.cloned.1.call-update) | async-done | bytes 655376 | tf_op jit(solution)/shard_map/reduce_scatter | solution.py:49
  568.7 4.8 multiply_reduce_fusion.5
  574.4 4.3 collective-permute-start.28
  582.4 3.7 all-to-all-start.7
  594.2 9.1 %collective-permute-done.30.refs_2_ = bf16[512,128]{1,0:T(8,128)(2,1)S(1)} collective-permute-done((bf16[512,128]{1,0:T(8,128)(2,1)S(1)}, bf16[512,128]{1,0:T(8,128)(2,1)S(1)}, u32[]{:S(2)}, u32[]{:S(2)}) %collective-permute-start.30) | collective-permute-done | bytes 131104 | tf_op jit(solution)/shard_map/ppermute | solution.py:60
  606.8 6.4 multiply_reduce_fusion
  614.2 2.5 reduce-scatter.12.cloned.1.call-done
  620.0 4.8 multiply_reduce_fusion.1
  628.9 4.4 fusion.21
  643.0 4.1 collective-permute-start.38
  649.2 2.9 fusion.23
  653.3 3.5 all-to-all-start.8
  656.8 5.6 convolution_add_fusion.1
  662.5 2.9 convert_element_type.183
  672.0 4.1 reduce-scatter.14.cloned.1.call-done
  677.5 4.6 collective-permute-done.33
  686.1 3.5 all-to-all-start.9
  689.6 4.6 collective-permute-done.34
  695.6 4.8 all-to-all-done.9.refs_0_
  (573 shorter events, 189.1 us)
Async XLA Ops:
  7.2 69.1 %all-gather.6.cloned.1.call-start = ((), (), s32[]{:S(2)}) async-start(), calls=%async_computation.15 | async-start | bytes 5308416 | tf_op jit(solution)/shard_map/all_gather | solution.py:45
  9.6 42.5 %copy-start.144 = (f32[48]{0:T(128)S(1)}, f32[48]{0:T(128)}, u32[]{:S(2)}) copy-start(f32[48]{0:T(128)} %param.26) | copy-start | bytes 580
  22.5 113.6 %all-gather.8.cloned.1.call-start = ((), (), s32[]{:S(2)}) async-start(), calls=%async_computation.16 | async-start | bytes 4718592 | tf_op jit(solution)/shard_map/all_gather | solution.py:45
  34.8 15.6 %collective-permute-start.7 = (s32[4096]{0:T(1024)S(1)}, s32[4096]{0:T(1024)S(1)}, u32[]{:S(2)}, u32[]{:S(2)}) collective-permute-start(s32[4096]{0:T(1024)S(1)} %dynamic_update_slice.20), channel_id=1, source_target_pairs={{0,1},{1,0},{2,3},{3,2},{4,5},{5,4},{6,7},{7,6},{8,9},{9,8},{10,11... | collective-permute-start | bytes 49160 | tf_op jit(solution)/shard_map/ppermute | solution.py:932
  36.4 13.4 %collective-permute-start = (bf16[128,2048]{1,0:T(8,128)(2,1)S(1)}, bf16[128,2048]{1,0:T(8,128)(2,1)S(1)}, u32[]{:S(2)}, u32[]{:S(2)}) collective-permute-start(bf16[128,2048]{1,0:T(8,128)(2,1)S(1)} %bitcast.89), channel_id=1, source_target_pairs={{0,16},{8,24},{16,0},{24,8},{1,17},{9,25},{17,1},{25,9},{2,18},{10... | collective-permute-start | bytes 1572872 | tf_op jit(solution)/shard_map/ppermute | solution.py:60
  39.3 17.3 %collective-permute-start.1 = (bf16[128,2048]{1,0:T(8,128)(2,1)S(1)}, bf16[128,2048]{1,0:T(8,128)(2,1)S(1)}, u32[]{:S(2)}, u32[]{:S(2)}) collective-permute-start(bf16[128,2048]{1,0:T(8,128)(2,1)S(1)} %bitcast.90), channel_id=1, source_target_pairs={{0,8},{8,0},{16,24},{24,16},{1,9},{9,1},{17,25},{25,17},{2,10},{10... | collective-permute-start | bytes 1572872 | tf_op jit(solution)/shard_map/ppermute | solution.py:60
  49.8 6.9 collective-permute-start.2
  50.6 5.6 collective-permute-start.8
  56.1 58.6 %copy-start.115 = (f32[1280]{0:T(1024)}, f32[1280]{0:T(1024)S(1)}, u32[]{:S(2)}) copy-start(f32[1280]{0:T(1024)S(1)} %get-tuple-element.132) | copy-start | bytes 15364
  56.2 29.1 %collective-permute-start.9 = (s32[4096]{0:T(1024)S(1)}, s32[4096]{0:T(1024)S(1)}, u32[]{:S(2)}, u32[]{:S(2)}) collective-permute-start(s32[4096]{0:T(1024)S(1)} %add.239), channel_id=1, source_target_pairs={{0,4},{1,5},{2,6},{3,7},{4,0},{5,1},{6,2},{7,3},{8,12},{9,13},{10,... | collective-permute-start | bytes 49160 | tf_op jit(solution)/shard_map/ppermute | solution.py:932
  83.7 5.3 collective-permute-start.3
  85.8 26.3 %collective-permute-start.10 = (bf16[128,2048]{1,0:T(8,128)(2,1)}, bf16[128,2048]{1,0:T(8,128)(2,1)S(1)}, u32[]{:S(2)}, u32[]{:S(2)}) collective-permute-start(bf16[128,2048]{1,0:T(8,128)(2,1)} %convert_element_type.156), channel_id=1, source_target_pairs={{0,6},{1,7},{2,12},{3,13},{4,18},{5,19},{6,24},{7,25},{8,0},{9,1},... | collective-permute-start | bytes 1572872 | tf_op jit(solution)/shard_map/ppermute | solution.py:994
  88.4 8.8 %collective-permute-start.4 = (bf16[512,128]{1,0:T(8,128)(2,1)S(1)}, bf16[512,128]{1,0:T(8,128)(2,1)S(1)}, u32[]{:S(2)}, u32[]{:S(2)}) collective-permute-start(bf16[512,128]{1,0:T(8,128)(2,1)S(1)} %slice.410.refs_1_), channel_id=1, source_target_pairs={{0,8},{8,0},{16,24},{24,16},{1,9},{9,1},{17,25},{25,17},{2,10},{10... | collective-permute-start | bytes 393224 | tf_op jit(solution)/shard_map/ppermute | solution.py:60
  89.0 8.2 %collective-permute-start.5 = (bf16[512,128]{1,0:T(8,128)(2,1)S(1)}, bf16[512,128]{1,0:T(8,128)(2,1)S(1)}, u32[]{:S(2)}, u32[]{:S(2)}) collective-permute-start(bf16[512,128]{1,0:T(8,128)(2,1)S(1)} %collective-permute-done.3.refs_2_), channel_id=1, source_target_pairs={{0,8},{8,0},{16,24},{24,16},{1,9},{9,1},{17,25},{25,17},{2,10},{10... | collective-permute-start | bytes 393224 | tf_op jit(solution)/shard_map/ppermute | solution.py:60
  91.3 27.9 %all-to-all-start.2 = ((bf16[4,64,2048]{2,1,0:T(8,128)(2,1)}), bf16[4,64,2048]{2,1,0:T(8,128)(2,1)}, u32[]{:S(2)}, u32[]{:S(2)}) async-start(bf16[4,64,2048]{2,1,0:T(8,128)(2,1)} %shard_map.240), calls=%async_computation.2 | async-start | bytes 2097152 | tf_op jit(solution)/shard_map/all_to_all | solution.py:84
  95.6 106.1 %all-gather.10.cloned.1.call-start = ((), (), s32[]{:S(2)}) async-start(), calls=%async_computation.17 | async-start | bytes 5898240 | tf_op jit(solution)/shard_map/all_gather | solution.py:45
  97.9 16.6 %collective-permute-start.6 = (bf16[3,1280]{1,0:T(4,128)(2,1)S(1)}, bf16[3,1280]{1,0:T(4,128)(2,1)S(1)}, u32[]{:S(2)}, u32[]{:S(2)}) collective-permute-start(bf16[3,1280]{1,0:T(4,128)(2,1)S(1)} %slice.411), channel_id=1, source_target_pairs={{0,1},{1,2},{2,3},{3,4},{4,5},{5,6},{6,7},{8,9},{9,10},{10,11},{11... | collective-permute-start | bytes 23048 | tf_op jit(solution)/shard_map/ppermute | solution.py:34
  118.3 128.5 %copy-start.20 = (f32[512,768]{1,0:T(8,128)}, f32[512,768]{1,0:T(8,128)S(1)}, u32[]{:S(2)}) copy-start(f32[512,768]{1,0:T(8,128)S(1)} %slice.420.refs_0_.refs_4_.refs_3_) | copy-start | bytes 4718596
  136.1 161.1 %all-gather.12.cloned.1.call-start = ((), (), s32[]{:S(2)}) async-start(), calls=%async_computation.18 | async-start | bytes 9437184 | tf_op jit(solution)/shard_map/all_gather | solution.py:45
  163.4 40.7 %copy-start.123 = (s32[32,128]{1,0:T(8,128)S(1)}, s32[32,128]{1,0:T(8,128)}, u32[]{:S(2)}) copy-start(s32[32,128]{1,0:T(8,128)} %get-tuple-element.142) | copy-start | bytes 49156
  163.4 41.1 %copy-start.15 = (bf16[1,128,2048]{2,1,0:T(8,128)(2,1)S(1)}, bf16[1,128,2048]{2,1,0:T(8,128)(2,1)}, u32[]{:S(2)}) copy-start(bf16[1,128,2048]{2,1,0:T(8,128)(2,1)} %param.15) | copy-start | bytes 1572868
  165.1 44.8 %copy-start.46 = (bf16[512,256]{1,0:T(8,128)(2,1)}, bf16[512,256]{1,0:T(8,128)(2,1)S(1)}, u32[]{:S(2)}) copy-start(bf16[512,256]{1,0:T(8,128)(2,1)S(1)} %get-tuple-element.80.refs_1_) | copy-start | bytes 786436
  204.5 13.9 %collective-permute-start.12 = (bf16[128,2048]{1,0:T(8,128)(2,1)S(1)}, bf16[128,2048]{1,0:T(8,128)(2,1)S(1)}, u32[]{:S(2)}, u32[]{:S(2)}) collective-permute-start(bf16[128,2048]{1,0:T(8,128)(2,1)S(1)} %bitcast.95), channel_id=1, source_target_pairs={{0,16},{8,24},{16,0},{24,8},{1,17},{9,25},{17,1},{25,9},{2,18},{10... | collective-permute-start | bytes 1572872 | tf_op jit(solution)/shard_map/ppermute | solution.py:60
  206.0 12.5 %collective-permute-start.13 = (bf16[128,2048]{1,0:T(8,128)(2,1)S(1)}, bf16[128,2048]{1,0:T(8,128)(2,1)S(1)}, u32[]{:S(2)}, u32[]{:S(2)}) collective-permute-start(bf16[128,2048]{1,0:T(8,128)(2,1)S(1)} %bitcast.96), channel_id=1, source_target_pairs={{0,8},{8,0},{16,24},{24,16},{1,9},{9,1},{17,25},{25,17},{2,10},{10... | collective-permute-start | bytes 1572872 | tf_op jit(solution)/shard_map/ppermute | solution.py:60
  209.9 17.2 %collective-permute-start.11 = (bf16[8,512,128]{2,1,0:T(8,128)(2,1)}, bf16[8,512,128]{2,1,0:T(8,128)(2,1)}, u32[]{:S(2)}, u32[]{:S(2)}) collective-permute-start(bf16[8,512,128]{2,1,0:T(8,128)(2,1)} %get-tuple-element.83), channel_id=1, source_target_pairs={{0,8},{8,0},{16,24},{24,16},{1,9},{9,1},{17,25},{25,17},{2,10},{10... | collective-permute-start | bytes 3145736 | tf_op jit(solution)/shard_map/ppermute | solution.py:60
  218.4 1.9 collective-permute-start.14
  221.7 25.1 %all-to-all-start.4 = ((bf16[8,96,256]{2,1,0:T(8,128)(2,1)}), bf16[8,96,256]{2,1,0:T(8,128)(2,1)S(1)}, u32[]{:S(2)}, u32[]{:S(2)}) async-start(bf16[8,96,256]{2,1,0:T(8,128)(2,1)} %shard_map.242.refs_2_.refs_5_), calls=%async_computation.4 | async-start | bytes 786432 | tf_op jit(solution)/shard_map/all_to_all | solution.py:1099
  227.1 122.5 %all-gather.14.cloned.1.call-start = ((), (), s32[]{:S(2)}) async-start(), calls=%async_computation.19 | async-start | bytes 4718592 | tf_op jit(solution)/shard_map/all_gather | solution.py:45
  297.2 100.9 %reduce-scatter.6.cloned.1.call-start = ((), (), s32[]{:S(2)}) async-start(), calls=%async_computation.20 | async-start | bytes 4718592 | tf_op jit(solution)/shard_map/reduce_scatter | solution.py:49
  301.2 4.2 collective-permute-start.15
  305.5 14.0 %collective-permute-start.16 = (bf16[128,2048]{1,0:T(8,128)(2,1)S(1)}, bf16[128,2048]{1,0:T(8,128)(2,1)S(1)}, u32[]{:S(2)}, u32[]{:S(2)}) collective-permute-start(bf16[128,2048]{1,0:T(8,128)(2,1)S(1)} %fusion.16), channel_id=1, source_target_pairs={{0,16},{8,24},{16,0},{24,8},{1,17},{9,25},{17,1},{25,9},{2,18},{10... | collective-permute-start | bytes 1572872 | tf_op jit(solution)/shard_map/ppermute | solution.py:60
  320.9 63.2 %copy-start.10 = (f32[128,2048]{1,0:T(8,128)}, f32[128,2048]{1,0:T(8,128)S(1)}, u32[]{:S(2)}) copy-start(f32[128,2048]{1,0:T(8,128)S(1)} %get-tuple-element.88.refs_1_) | copy-start | bytes 3145732
  320.9 13.3 %collective-permute-start.17 = (bf16[128,2048]{1,0:T(8,128)(2,1)S(1)}, bf16[128,2048]{1,0:T(8,128)(2,1)S(1)}, u32[]{:S(2)}, u32[]{:S(2)}) collective-permute-start(bf16[128,2048]{1,0:T(8,128)(2,1)S(1)} %get-tuple-element.89), channel_id=1, source_target_pairs={{0,16},{8,24},{16,0},{24,8},{1,17},{9,25},{17,1},{25,9},{2,18},{10... | collective-permute-start | bytes 1572872 | tf_op jit(solution)/shard_map/ppermute | solution.py:60
  322.4 11.9 %collective-permute-start.18 = (bf16[128,2048]{1,0:T(8,128)(2,1)S(1)}, bf16[128,2048]{1,0:T(8,128)(2,1)S(1)}, u32[]{:S(2)}, u32[]{:S(2)}) collective-permute-start(bf16[128,2048]{1,0:T(8,128)(2,1)S(1)} %get-tuple-element.89), channel_id=1, source_target_pairs={{0,8},{8,0},{16,24},{24,16},{1,9},{9,1},{17,25},{25,17},{2,10},{10... | collective-permute-start | bytes 1572872 | tf_op jit(solution)/shard_map/ppermute | solution.py:60
  334.2 1.9 collective-permute-start.19
  349.5 147.9 %reduce-scatter.8.cloned.1.call-start = ((), (), s32[]{:S(2)}) async-start(), calls=%async_computation.21 | async-start | bytes 9437184 | tf_op jit(solution)/shard_map/reduce_scatter | solution.py:49
  362.8 2.7 collective-permute-start.20
  368.0 14.3 %collective-permute-start.21 = (bf16[128,2048]{1,0:T(8,128)(2,1)}, bf16[128,2048]{1,0:T(8,128)(2,1)S(1)}, u32[]{:S(2)}, u32[]{:S(2)}) collective-permute-start(bf16[128,2048]{1,0:T(8,128)(2,1)} %fusion.14), channel_id=1, source_target_pairs={{0,16},{8,24},{16,0},{24,8},{1,17},{9,25},{17,1},{25,9},{2,18},{10... | collective-permute-start | bytes 1572872 | tf_op jit(solution)/shard_map/ppermute | solution.py:60
  398.1 13.8 %collective-permute-start.22 = (bf16[128,2048]{1,0:T(8,128)(2,1)S(1)}, bf16[128,2048]{1,0:T(8,128)(2,1)S(1)}, u32[]{:S(2)}, u32[]{:S(2)}) collective-permute-start(bf16[128,2048]{1,0:T(8,128)(2,1)S(1)} %get-tuple-element.97), channel_id=1, source_target_pairs={{0,16},{8,24},{16,0},{24,8},{1,17},{9,25},{17,1},{25,9},{2,18},{10... | collective-permute-start | bytes 1572872 | tf_op jit(solution)/shard_map/ppermute | solution.py:60
  399.7 12.4 %collective-permute-start.23 = (bf16[128,2048]{1,0:T(8,128)(2,1)S(1)}, bf16[128,2048]{1,0:T(8,128)(2,1)S(1)}, u32[]{:S(2)}, u32[]{:S(2)}) collective-permute-start(bf16[128,2048]{1,0:T(8,128)(2,1)S(1)} %get-tuple-element.97), channel_id=1, source_target_pairs={{0,8},{8,0},{16,24},{24,16},{1,9},{9,1},{17,25},{25,17},{2,10},{10... | collective-permute-start | bytes 1572872 | tf_op jit(solution)/shard_map/ppermute | solution.py:60
  411.9 1.9 collective-permute-start.24
  426.8 22.9 %all-to-all-start.5 = ((bf16[8,112,256]{2,1,0:T(8,128)(2,1)}), bf16[8,112,256]{2,1,0:T(8,128)(2,1)S(1)}, u32[]{:S(2)}, u32[]{:S(2)}) async-start(bf16[8,112,256]{2,1,0:T(8,128)(2,1)} %get-tuple-element.102), calls=%async_computation.6 | async-start | bytes 917504 | tf_op jit(solution)/shard_map/all_to_all | solution.py:1091
  431.9 133.6 %reduce-scatter.10.cloned.1.call-start = ((), (), s32[]{:S(2)}) async-start(), calls=%async_computation.22 | async-start | bytes 5898240 | tf_op jit(solution)/shard_map/reduce_scatter | solution.py:49
  449.7 9.8 %collective-permute-start.27 = (bf16[8,512,128]{2,1,0:T(8,128)(2,1)}, bf16[8,512,128]{2,1,0:T(8,128)(2,1)}, u32[]{:S(2)}, u32[]{:S(2)}) collective-permute-start(bf16[8,512,128]{2,1,0:T(8,128)(2,1)} %broadcast_select_fusion), channel_id=1, source_target_pairs={{0,8},{8,0},{16,24},{24,16},{1,9},{9,1},{17,25},{25,17},{2,10},{10... | collective-permute-start | bytes 3145736 | tf_op jit(solution)/shard_map/ppermute | solution.py:60
  502.2 2.7 collective-permute-start.25
  507.5 14.3 %collective-permute-start.26 = (bf16[128,2048]{1,0:T(8,128)(2,1)}, bf16[128,2048]{1,0:T(8,128)(2,1)}, u32[]{:S(2)}, u32[]{:S(2)}) collective-permute-start(bf16[128,2048]{1,0:T(8,128)(2,1)} %fusion.10), channel_id=1, source_target_pairs={{0,16},{8,24},{16,0},{24,8},{1,17},{9,25},{17,1},{25,9},{2,18},{10... | collective-permute-start | bytes 1572872 | tf_op jit(solution)/shard_map/ppermute | solution.py:60
  508.9 19.3 %all-to-all-start.6 = ((bf16[8,96,256]{2,1,0:T(8,128)(2,1)}), bf16[8,96,256]{2,1,0:T(8,128)(2,1)}, u32[]{:S(2)}, u32[]{:S(2)}) async-start(bf16[8,96,256]{2,1,0:T(8,128)(2,1)} %shard_map.252.refs_4_), calls=%async_computation.7 | async-start | bytes 786432 | tf_op jit(solution)/shard_map/all_to_all | solution.py:1099
  514.1 102.7 %reduce-scatter.12.cloned.1.call-start = ((), (), s32[]{:S(2)}) async-start(), calls=%async_computation.23 | async-start | bytes 4718592 | tf_op jit(solution)/shard_map/reduce_scatter | solution.py:49
  574.4 6.0 collective-permute-start.28
  582.4 21.6 %all-to-all-start.7 = ((bf16[4,64,2048]{2,1,0:T(8,128)(2,1)}), bf16[4,64,2048]{2,1,0:T(8,128)(2,1)S(1)}, u32[]{:S(2)}, u32[]{:S(2)}) async-start(bf16[4,64,2048]{2,1,0:T(8,128)(2,1)} %bitcast.113), calls=%async_computation.10 | async-start | bytes 2097152 | tf_op jit(solution)/shard_map/all_to_all | solution.py:84
  586.1 90.0 %reduce-scatter.14.cloned.1.call-start = ((), (), s32[]{:S(2)}) async-start(), calls=%async_computation.24 | async-start | bytes 5308416 | tf_op jit(solution)/shard_map/reduce_scatter | solution.py:49
  586.8 1.8 collective-permute-start.29
  588.8 14.5 %collective-permute-start.30 = (bf16[512,128]{1,0:T(8,128)(2,1)S(1)}, bf16[512,128]{1,0:T(8,128)(2,1)S(1)}, u32[]{:S(2)}, u32[]{:S(2)}) collective-permute-start(bf16[512,128]{1,0:T(8,128)(2,1)S(1)} %get-tuple-element.158), channel_id=1, source_target_pairs={{0,16},{8,24},{16,0},{24,8},{1,17},{9,25},{17,1},{25,9},{2,18},{10... | collective-permute-start | bytes 393224 | tf_op jit(solution)/shard_map/ppermute | solution.py:60
  625.7 7.6 %collective-permute-start.35 = (f32[176,128]{1,0:T(8,128)S(1)}, f32[176,128]{1,0:T(8,128)S(1)}, u32[]{:S(2)}, u32[]{:S(2)}) collective-permute-start(f32[176,128]{1,0:T(8,128)S(1)} %pad_bitcast_fusion), channel_id=1, source_target_pairs={{0,8},{8,0},{16,24},{24,16},{1,9},{9,1},{17,25},{25,17},{2,10},{10... | collective-permute-start | bytes 270344 | tf_op jit(solution)/shard_map/ppermute | solution.py:932
  633.3 5.1 collective-permute-start.36
  637.1 25.3 %collective-permute-start.32 = (bf16[256,2048]{1,0:T(8,128)(2,1)}, bf16[256,2048]{1,0:T(8,128)(2,1)}, u32[]{:S(2)}, u32[]{:S(2)}) collective-permute-start(bf16[256,2048]{1,0:T(8,128)(2,1)} %fusion.6), channel_id=1, source_target_pairs={{0,8},{8,0},{16,24},{24,16},{1,9},{9,1},{17,25},{25,17},{2,10},{10... | collective-permute-start | bytes 3145736 | tf_op jit(solution)/shard_map/ppermute | solution.py:60
  638.4 4.6 collective-permute-start.37
  643.0 9.2 %collective-permute-start.38 = (f32[176,128]{1,0:T(8,128)S(1)}, f32[176,128]{1,0:T(8,128)S(1)}, u32[]{:S(2)}, u32[]{:S(2)}) collective-permute-start(f32[176,128]{1,0:T(8,128)S(1)} %add.282), channel_id=1, source_target_pairs={{0,2},{1,3},{2,0},{3,1},{4,6},{5,7},{6,4},{7,5},{8,10},{9,11},{10,... | collective-permute-start | bytes 270344 | tf_op jit(solution)/shard_map/ppermute | solution.py:932
  647.1 18.5 %collective-permute-start.31 = (bf16[128,2048]{1,0:T(8,128)(2,1)S(1)}, bf16[128,2048]{1,0:T(8,128)(2,1)}, u32[]{:S(2)}, u32[]{:S(2)}) collective-permute-start(bf16[128,2048]{1,0:T(8,128)(2,1)S(1)} %slice.447), channel_id=1, source_target_pairs={{0,8},{1,9},{2,10},{3,11},{4,12},{5,13},{14,14},{15,15},{8,16},{9,... | collective-permute-start | bytes 1572872 | tf_op jit(solution)/shard_map/ppermute | solution.py:1363
  652.2 10.2 %collective-permute-start.39 = (f32[176,128]{1,0:T(8,128)S(1)}, f32[176,128]{1,0:T(8,128)S(1)}, u32[]{:S(2)}, u32[]{:S(2)}) collective-permute-start(f32[176,128]{1,0:T(8,128)S(1)} %add.283), channel_id=1, source_target_pairs={{0,4},{1,5},{2,6},{3,7},{4,0},{5,1},{6,2},{7,3},{8,12},{9,13},{10,... | collective-permute-start | bytes 270344 | tf_op jit(solution)/shard_map/ppermute | solution.py:932
  653.3 12.3 %all-to-all-start.8 = ((bf16[4,64,1024]{2,1,0:T(8,128)(2,1)}), bf16[4,64,1024]{2,1,0:T(8,128)(2,1)S(1)}, u32[]{:S(2)}, u32[]{:S(2)}) async-start(bf16[4,64,1024]{2,1,0:T(8,128)(2,1)} %bitcast.29), calls=%async_computation.12 | async-start | bytes 1048576 | tf_op jit(solution)/shard_map/all_to_all | solution.py:84
  667.8 14.4 %collective-permute-start.33 = (bf16[128,2048]{1,0:T(8,128)(2,1)}, bf16[128,2048]{1,0:T(8,128)(2,1)}, u32[]{:S(2)}, u32[]{:S(2)}) collective-permute-start(bf16[128,2048]{1,0:T(8,128)(2,1)} %fusion.8), channel_id=1, source_target_pairs={{0,16},{8,24},{16,0},{24,8},{1,17},{9,25},{17,1},{25,9},{2,18},{10... | collective-permute-start | bytes 1572872 | tf_op jit(solution)/shard_map/ppermute | solution.py:60
  676.1 18.1 %collective-permute-start.34 = (bf16[128,2048]{1,0:T(8,128)(2,1)}, bf16[128,2048]{1,0:T(8,128)(2,1)}, u32[]{:S(2)}, u32[]{:S(2)}) collective-permute-start(bf16[128,2048]{1,0:T(8,128)(2,1)} %copy-done.110), channel_id=1, source_target_pairs={{6,0},{7,1},{12,2},{13,3},{18,4},{19,5},{24,6},{25,7}} | collective-permute-start | bytes 1572872 | tf_op jit(solution)/shard_map/ppermute | solution.py:1363
  686.1 14.2 %all-to-all-start.9 = ((bf16[4,64,1152]{2,1,0:T(8,128)(2,1)}), bf16[4,64,1152]{2,1,0:T(8,128)(2,1)S(1)}, u32[]{:S(2)}, u32[]{:S(2)}) async-start(bf16[4,64,1152]{2,1,0:T(8,128)(2,1)} %bitcast.114), calls=%async_computation.14 | async-start | bytes 1179648 | tf_op jit(solution)/shard_map/all_to_all | solution.py:84
  (150 other events, 1015.9 us)
Sparse Core Ops, SparseCore 0:
  22.6 53.6 all-gather.5
  77.8 58.2 all-gather.7
  138.2 63.4 all-gather.9
  203.0 94.0 all-gather.11
  298.5 47.8 all-gather.13
  349.7 48.3 reduce-scatter.5
  400.4 96.9 reduce-scatter.7
  499.7 65.7 reduce-scatter.9
  567.8 48.8 reduce-scatter.11
  618.9 57.1 reduce-scatter.13
